TPU v7x, 512 devices: a whole 4x4x16 slice. The times are simulated.
512 devices in a mesh: gx: 64 (over z, y_hi, core), gy: 8 (over x, y_lo).
Axes of the slice: x: 4, y: 4 (y_hi: 2, y_lo: 2; y = y_hi * 2 + y_lo), z: 16, core: 2. Of those that a mesh axis runs over, the one named last changes fastest.
Arguments:
- points: float32 [65536, 512], P(('gx', 'gy')), may hold values from -16 to 16, as said below
- block_cell: int32 [65536], P(('gx', 'gy')), may hold values from 0 to 511
- block_mat: int32 [65536], P(('gx', 'gy')), may hold values from 0 to 7
- density: float32 [8], replicated, may hold values from 1 to 3
- shear_modulus: float32 [8], replicated, may hold values from 0.5 to 4
- lame_modulus: float32 [8], replicated, may hold values from 0.5 to 4
- mig_slot_a: int32 [32768], P(('gx', 'gy')), may hold values from 0 to 63, as said below
- mig_dest_a: int32 [32768], P(('gx', 'gy')), may hold values from 0 to 511, as said below
- mig_cell_a: int32 [32768], P(('gx', 'gy')), may hold values from 0 to 511, as said below
- mig_slot_b: int32 [32768], P(('gx', 'gy')), may hold values from 64 to 127, as said below
- mig_dest_b: int32 [32768], P(('gx', 'gy')), may hold values from 0 to 511, as said below
- mig_cell_b: int32 [32768], P(('gx', 'gy')), may hold values from 0 to 511, as said below
Outputs:
- final_points: float32 [131072, 512], P(('gx', 'gy'))
- final_cells: int32 [131072], P(('gx', 'gy'))
- final_materials: int32 [131072], P(('gx', 'gy'))
Inputs may be any that keep to these rules, and one draw needn't show every extreme that they name: `points`: components 0 and 1 of every point lie in [0, 1]; peak pressures are 0 or more. `mig_slot_a`: the slots named by one device's list are distinct and lie below 64. `mig_slot_b`: the slots named by one device's list are distinct and lie in [64, 128). `mig_dest_a`: each entry names the device itself (the block stays) or an existing face neighbour (gx +- 1 or gy +- 1); at most 16 entries of one device name the same neighbour, and some device names one neighbour exactly 16 times. `mig_dest_b`: as for the first list. `mig_cell_a`: A cell local to the destination device. `mig_cell_b`: A cell local to the destination device.
All inputs are finite; a program needn't handle non-finite values.
Results may differ from a plain program's by a relative error of at most 0.0003.
Values sent between devices are 32-bit elements; how exact they have to be, the bound alone decides.
No kernel may reach another device: no remote copies, remote signals or barrier semaphores. Data moves between devices by JAX's collectives and lax.ppermute only.
A program may use at most 64 MiB of HBM per device.

v0:
```python
import jax
import jax.numpy as jnp
from jax import lax
from jax.experimental import pallas as pl
from jax.experimental.pallas import tpu as pltpu
from jax.sharding import PartitionSpec as P

CX = 16
CY = 32
BLOCK = 64
NMAT = 8
MCAP = 16
LANES = 128
SUB = 8
ROWS = 160
HALO = 24
TOP = CX * SUB
MSG = MCAP + SUB

TIME_STEP = 0.2
MASS_FLOOR = 0.25
VOLUME = 1.0 / BLOCK
VMEM_LIMIT = 12 * 1024 * 1024

IN_VMEM = pl.BlockSpec(memory_space=pltpu.VMEM)
IN_SMEM = pl.BlockSpec(memory_space=pltpu.SMEM)
F32 = jnp.float32
BF16 = jnp.bfloat16
NN = (((1,), (0,)), ((), ()))
NT = (((1,), (1,)), ((), ()))


def call(kernel, outs, scratch, in_specs, *operands):
    return pl.pallas_call(
        kernel,
        out_shape=tuple(jax.ShapeDtypeStruct(shape, dtype) for shape, dtype in outs),
        in_specs=in_specs,
        out_specs=tuple(IN_VMEM for _ in outs),
        scratch_shapes=scratch,
        compiler_params=pltpu.CompilerParams(vmem_limit_bytes=VMEM_LIMIT),
    )(*operands)


def swap(value, axis, first):
    count = lax.axis_size(axis)
    pairs = []
    for low in range(first, count - 1, 2):
        pairs += [(low, low + 1), (low + 1, low)]
    return lax.ppermute(value, axis, pairs)


def iota(shape, dim):
    return lax.broadcasted_iota(jnp.int32, shape, dim)


def thirds(value):
    high = value.astype(BF16)
    rest = value - high.astype(F32)
    middle = rest.astype(BF16)
    low = (rest - middle.astype(F32)).astype(BF16)
    return (high, middle, low)


def product(parts, onehot, dims):
    total = None
    for part in parts:
        term = lax.dot_general(part, onehot, dims, preferred_element_type=F32)
        total = term if total is None else total + term
    return total


def stencil(u):
    p = jnp.maximum(0.25 - u, 0.0)
    q = jnp.maximum(u - 0.75, 0.0)
    p2 = p * p
    q2 = q * q
    weight = (p2, (1.0 - u) - 2.0 * p2 + q2, u + p2 - 2.0 * q2, q2)
    slope = (-2.0 * p, 4.0 * p + 2.0 * q - 1.0, 1.0 - 2.0 * p - 4.0 * q, 2.0 * q)
    return (weight, slope)


def by_material(materials, table):
    value = jnp.zeros(materials.shape, F32)
    for index in range(NMAT):
        value = jnp.where(materials == index, table[index], value)
    return value


def column_onehot(cells):
    cross = jnp.broadcast_to(cells & (CY - 1), (LANES, LANES))
    column = iota((LANES, LANES), 0)
    return [(column == cross + b).astype(F32).astype(BF16) for b in range(4)]


def row_masks(cells):
    depth = jnp.broadcast_to(cells >> 5, (SUB, LANES))
    return [depth == index for index in range(CX)]


def node_terms(load, chunks, rho):
    sub = iota((SUB, LANES), 0)
    scale = jnp.where(sub < 3, jnp.broadcast_to(rho * VOLUME, (SUB, LANES)), -VOLUME)
    scale = jnp.where(sub < 5, scale, 0.0)
    stencils = [(stencil(load(0, k)), stencil(load(1, k))) for k in range(chunks)]
    terms = [[None] * 4 for _ in range(4)]
    for b in range(4):
        acc = [[None] * 5 for _ in range(4)]
        for k in range(chunks):
            (weight_x, slope_x), (weight_y, slope_y) = stencils[k]
            wy, dy = weight_y[b], slope_y[b]
            sxy = load(6, k)
            y1 = wy * load(2, k)
            y2 = wy * load(3, k)
            y3 = wy * load(4, k)
            y4 = wy * sxy
            y5 = dy * sxy
            y6 = dy * load(5, k)
            for a in range(4):
                wx, dx = weight_x[a], slope_x[a]
                new = (wx * wy, wx * y1, wx * y2, dx * y3 + wx * y5, dx * y4 + wx * y6)
                acc[a] = [n if o is None else o + n for o, n in zip(acc[a], new)]
        for a in range(4):
            packed = jnp.zeros((SUB, LANES), F32)
            for q in range(5):
                total = jnp.sum(acc[a][q], axis=0, keepdims=True)
                packed = jnp.where(sub == q, jnp.broadcast_to(total, (SUB, LANES)), packed)
            terms[a][b] = packed * scale
    return terms


def spread_rows(terms, masks, left_ref, lane):
    zero = jnp.zeros((SUB, LANES), F32)
    for b in range(4):
        for x in range(ROWS // SUB):
            total = zero
            for a in range(4):
                if 0 <= x - a < CX:
                    total = total + jnp.where(masks[x - a], terms[a][b], zero)
            left_ref[x * SUB : (x + 1) * SUB, lane + b * LANES : lane + (b + 1) * LANES] = total


def parity(axis):
    return (lax.axis_index(axis) & 1) == 1


def emit_sums(left_ref, onehots, sums_ref, inner_ref, outer_ref):
    sums = product(thirds(left_ref[...]), jnp.concatenate(onehots, axis=1), NT)
    sums_ref[...] = sums
    odd = parity("gx")
    bottom, top = (sums[0:HALO], sums[TOP : TOP + HALO])
    inner_ref[...] = jnp.where(odd, bottom, top)
    outer_ref[...] = jnp.where(odd, top, bottom)


def sums_one(points_ref, meta_ref, density_ref, sums_ref, inner_ref, outer_ref, turned_ref, left_ref):
    turned_ref[...] = points_ref[...].T
    cells = meta_ref[0:1, :]
    rho = by_material(meta_ref[1:2, :], density_ref)
    load = lambda c, k: turned_ref[c * BLOCK + k * SUB : c * BLOCK + (k + 1) * SUB, :]
    terms = node_terms(load, BLOCK // SUB, rho)
    spread_rows(terms, row_masks(cells), left_ref, 0)
    emit_sums(left_ref, column_onehot(cells), sums_ref, inner_ref, outer_ref)


def regions(from_inner_x, from_outer_x, from_inner_y, from_outer_y):
    odd_x, odd_y = (parity("gx"), parity("gy"))
    return (
        jnp.where(odd_x, from_inner_x, from_outer_x),
        jnp.where(odd_x, from_outer_x, from_inner_x),
        jnp.where(odd_y, from_inner_y, from_outer_y),
        jnp.where(odd_y, from_outer_y, from_inner_y),
    )


def arrived_meta(boxes):
    packed = boxes[0][MCAP:MSG, 0:LANES]
    for index in range(1, 4):
        packed = packed + pltpu.roll(boxes[index][MCAP:MSG, 0:LANES], MCAP * index, 1)
    packed = packed + pltpu.roll(packed, 4 * MCAP, 1)
    sub = iota((SUB, LANES), 0)
    return packed.astype(jnp.int32) - (sub == 1).astype(jnp.int32)


def sums_two(
    kept_ref, meta_ref, xi_ref, xo_ref, yi_ref, yo_ref, density_ref,
    sums_ref, inner_ref, outer_ref, turned_ref, new_meta_ref,
    left_ref, wide_ref,
):
    boxes = regions(xi_ref[...], xo_ref[...], yi_ref[...], yo_ref[...])
    new_meta = arrived_meta(boxes)
    new_meta_ref[...] = new_meta
    rows = jnp.concatenate([box[0:MCAP] for box in boxes], axis=0)
    wide_ref[...] = jnp.concatenate([rows, jnp.zeros_like(rows)], axis=0).T
    half = BLOCK // 2
    for c in range(8):
        first = wide_ref[c * BLOCK : c * BLOCK + half, :]
        second = wide_ref[c * BLOCK + half : (c + 1) * BLOCK, :]
        turned_ref[c * half : (c + 1) * half, :] = first + pltpu.roll(second, BLOCK, 1)
    onehots = []
    for lane, chunks, ref, cells, mats in (
        (0, BLOCK // SUB, kept_ref, meta_ref[0:1, :], meta_ref[1:2, :]),
        (4 * LANES, half // SUB, turned_ref, new_meta[0:1], new_meta[1:2]),
    ):
        stride = chunks * SUB
        load = lambda c, k: ref[c * stride + k * SUB : c * stride + (k + 1) * SUB, :]
        terms = node_terms(load, chunks, by_material(mats, density_ref))
        spread_rows(terms, row_masks(cells), left_ref, lane)
        onehots += column_onehot(cells)
    emit_sums(left_ref, onehots, sums_ref, inner_ref, outer_ref)


def merge_depth(sums_ref, from_inner_ref, from_outer_ref, merged_ref, inner_ref, outer_ref):
    odd = parity("gx")
    from_inner, from_outer = (from_inner_ref[...], from_outer_ref[...])
    merged_ref[...] = sums_ref[...]
    merged_ref[0:HALO] = sums_ref[0:HALO] + jnp.where(odd, from_inner, from_outer)
    merged_ref[TOP : TOP + HALO] = sums_ref[TOP : TOP + HALO] + jnp.where(odd, from_outer, from_inner)
    lane = iota((SUB, LANES), 1)
    low = jnp.zeros((SUB, LANES), F32)
    high = jnp.zeros((SUB, LANES), F32)
    for x in range(CX + 3):
        row = merged_ref[x * SUB : (x + 1) * SUB, :]
        here = (lane >= 3 * x) & (lane < 3 * x + 3)
        shift = 3 * x
        low = jnp.where(here, pltpu.roll(row, shift, 1) if shift else row, low)
        high = jnp.where(here, pltpu.roll(row, (shift - CY) % LANES, 1), high)
    odd_y = parity("gy")
    inner_ref[...] = jnp.where(odd_y, low, high)
    outer_ref[...] = jnp.where(odd_y, high, low)


def node_velocity(merged_ref, from_inner_ref, from_outer_ref, velocity_ref):
    odd_y = parity("gy")
    from_inner, from_outer = (from_inner_ref[...], from_outer_ref[...])
    low = jnp.where(odd_y, from_inner, from_outer)
    high = jnp.where(odd_y, from_outer, from_inner)
    lane = iota((SUB, LANES), 1)
    total_x = CX * lax.axis_size("gx")
    total_y = CY * lax.axis_size("gy")
    base_x = lax.axis_index("gx") * CX - 1
    node_y = lax.axis_index("gy") * CY - 1 + lane
    inside_y = (node_y > 0) & (node_y < total_y - 1)
    for x in range(ROWS // SUB):
        row = merged_ref[x * SUB : (x + 1) * SUB, :]
        if x < CX + 3:
            shift = 3 * x
            row = row + jnp.where(lane < 3, pltpu.roll(low, (-shift) % LANES, 1) if shift else low, 0.0)
            row = row + jnp.where(
                (lane >= CY) & (lane < CY + 3), pltpu.roll(high, (CY - shift) % LANES, 1), 0.0
            )
        mass = jnp.maximum(jnp.broadcast_to(row[0:1], (SUB, LANES)), MASS_FLOOR)
        value = (row + TIME_STEP * pltpu.roll(row, SUB - 2, 0)) / mass
        node_x = base_x + x
        inside_x = (node_x > 0) & (node_x < total_x - 1)
        velocity_ref[x * SUB : (x + 1) * SUB, :] = jnp.where(inside_y & inside_x, value, 0.0)


def gathered(velocity_parts, cells):
    masks = row_masks(cells)
    near = [[None] * 4 for _ in range(4)]
    for b, onehot in enumerate(column_onehot(cells)):
        column = product(velocity_parts, onehot, NN)
        for a in range(4):
            total = jnp.zeros((SUB, LANES), F32)
            for x in range(CX):
                total = jnp.where(masks[x], column[(x + a) * SUB : (x + a + 1) * SUB], total)
            near[a][b] = total
    return near


def move_points(load, store, chunks, near, materials, shear_ref, lame_ref):
    wide = lambda row: jnp.broadcast_to(row, (SUB, LANES))
    twice_shear = wide(2.0 * by_material(materials, shear_ref))
    lame = wide(by_material(materials, lame_ref))
    alive = wide(materials) >= 0
    for k in range(chunks):
        u, v = (load(0, k), load(1, k))
        weight_x, slope_x = stencil(u)
        weight_y, slope_y = stencil(v)
        speed, along, across = ([], [], [])
        for row in (1, 2):
            value = rate_x = rate_y = None
            for a in range(4):
                inner = slant = None
                for b in range(4):
                    node = wide(near[a][b][row : row + 1])
                    term, tilt = (weight_y[b] * node, slope_y[b] * node)
                    inner = term if b == 0 else inner + term
                    slant = tilt if b == 0 else slant + tilt
                add = (weight_x[a] * inner, slope_x[a] * inner, weight_x[a] * slant)
                if a == 0:
                    value, rate_x, rate_y = add
                else:
                    value, rate_x, rate_y = (value + add[0], rate_x + add[1], rate_y + add[2])
            speed.append(value)
            along.append(rate_x)
            across.append(rate_y)
        rate_xx, rate_yy = (along[0], across[1])
        rate_xy = 0.5 * (across[0] + along[1])
        spherical = lame * (rate_xx + rate_yy)
        stress_xx = load(4, k) + TIME_STEP * (twice_shear * rate_xx + spherical)
        stress_yy = load(5, k) + TIME_STEP * (twice_shear * rate_yy + spherical)
        stress_xy = load(6, k) + TIME_STEP * twice_shear * rate_xy
        fresh = (
            jnp.clip(u + TIME_STEP * speed[0], 0.0, 1.0),
            jnp.clip(v + TIME_STEP * speed[1], 0.0, 1.0),
            speed[0],
            speed[1],
            stress_xx,
            stress_yy,
            stress_xy,
            jnp.maximum(load(7, k), -0.5 * (stress_xx + stress_yy)),
        )
        for c in range(8):
            store(c, k, jnp.where(alive, fresh[c], 0.0))


def outgoing(fresh, cells, materials, list_ref, message_refs):
    across = lax.axis_size("gy")
    gx, gy = (lax.axis_index("gx"), lax.axis_index("gy"))
    home = gx * across + gy
    step_x = across - 2 * across * (gx & 1)
    step_y = 1 - 2 * (gy & 1)
    slots, dests, places = (list_ref[0:1, :], list_ref[1:2, :], list_ref[2:3, :])
    dest = jnp.broadcast_to(dests, (2 * SUB, LANES))
    sub = iota((2 * SUB, LANES), 0)
    matched = jnp.zeros((2 * SUB, LANES), F32)
    for o, target in enumerate((home + step_x, home - step_x, home + step_y, home - step_y)):
        matched = jnp.where((sub == o) & (dest == target), 1.0, matched)
    square = (LANES, LANES)
    earlier = (iota(square, 0) < iota(square, 1)).astype(F32).astype(BF16)
    rank = lax.dot_general(matched.astype(BF16), earlier, NN, preferred_element_type=F32)
    place_rank = iota((MCAP, LANES), 0).astype(F32)
    placing = []
    for o in range(4):
        hit = jnp.broadcast_to(rank[o : o + 1], (MCAP, LANES)) == place_rank
        placing.append(jnp.where(hit, jnp.broadcast_to(matched[o : o + 1], (MCAP, LANES)), 0.0))
    placing.append(jnp.zeros((LANES - 4 * MCAP, LANES), F32))
    placing = jnp.concatenate(placing, axis=0).astype(BF16)
    holds = (iota(square, 0) == jnp.broadcast_to(slots, square)).astype(F32).astype(BF16)
    moving = jnp.where((dest >= 0) & (dest != home), 1.0, 0.0).astype(BF16)
    vacated = lax.dot_general(moving, holds, NT, preferred_element_type=F32)[0:1] > 0.5
    chosen = lax.dot_general(placing, holds, NT, preferred_element_type=F32).astype(BF16)
    listed = jnp.where(sub == 0, jnp.broadcast_to(places >> 5, dest.shape), 0)
    listed = jnp.where(sub == 1, jnp.broadcast_to(places & (CY - 1), dest.shape), listed)
    listed = lax.dot_general(listed.astype(F32).astype(BF16), placing, NT, preferred_element_type=F32)
    kinds = jnp.broadcast_to(materials + 1, dest.shape).astype(F32).astype(BF16)
    kinds = lax.dot_general(kinds, chosen, NT, preferred_element_type=F32)
    new_cells = jnp.broadcast_to(listed[0:1] * float(CY) + listed[1:2], (SUB, LANES))
    new_kinds = jnp.broadcast_to(kinds[0:1], (SUB, LANES))
    low_sub, lane = (iota((SUB, LANES), 0), iota((SUB, LANES), 1))
    tags = jnp.where(low_sub == 0, new_cells, jnp.where(low_sub == 1, new_kinds, 0.0))
    total = None
    for part in thirds(fresh):
        term = lax.dot_general(chosen[0 : 4 * MCAP], part, NN, preferred_element_type=F32)
        total = term if total is None else total + term
    for o, ref in enumerate(message_refs):
        ref[0:MCAP, :] = total[o * MCAP : (o + 1) * MCAP]
        tag = pltpu.roll(tags, LANES - o * MCAP, 1) if o else tags
        ref[MCAP:MSG, 0:LANES] = jnp.where(lane < MCAP, tag, 0.0)
        ref[MCAP:MSG, LANES:] = jnp.zeros((SUB, 8 * BLOCK - LANES), F32)
    return vacated


def vacate(meta, vacated):
    sub = iota((SUB, LANES), 0)
    gone = jnp.broadcast_to(vacated.astype(F32), (SUB, LANES)) > 0.5
    return jnp.where(gone, jnp.where(sub == 1, -1, 0), meta)


def advance_one(
    turned_ref, meta_ref, list_ref, merged_ref, yi_ref, yo_ref, shear_ref, lame_ref,
    kept_ref, kept_meta_ref, m0_ref, m1_ref, m2_ref, m3_ref,
    velocity_ref, fresh_ref,
):
    node_velocity(merged_ref, yi_ref, yo_ref, velocity_ref)
    parts = thirds(velocity_ref[...])
    meta = meta_ref[...]
    cells, materials = (meta[0:1], meta[1:2])
    at = lambda c, k: slice(c * BLOCK + k * SUB, c * BLOCK + (k + 1) * SUB)

    def store(c, k, value):
        fresh_ref[at(c, k), :] = value

    load = lambda c, k: turned_ref[at(c, k), :]
    move_points(load, store, BLOCK // SUB, gathered(parts, cells), materials, shear_ref, lame_ref)
    fresh = fresh_ref[...]
    vacated = outgoing(fresh.T, cells, materials, list_ref, (m0_ref, m1_ref, m2_ref, m3_ref))
    gone = jnp.broadcast_to(vacated.astype(F32), fresh.shape) > 0.5
    kept_ref[...] = jnp.where(gone, 0.0, fresh)
    kept_meta_ref[...] = vacate(meta, vacated)


def advance_two(
    kept_ref, meta_ref, turned_ref, new_meta_ref, list_ref, merged_ref, yi_ref, yo_ref, shear_ref, lame_ref,
    old_ref, new_ref, old_meta_ref, m0_ref, m1_ref, m2_ref, m3_ref,
    velocity_ref, fresh_ref, wide_ref,
):
    node_velocity(merged_ref, yi_ref, yo_ref, velocity_ref)
    parts = thirds(velocity_ref[...])
    meta = meta_ref[...]
    cells, materials = (meta[0:1], meta[1:2])
    at = lambda c, k: slice(c * BLOCK + k * SUB, c * BLOCK + (k + 1) * SUB)

    def store(c, k, value):
        fresh_ref[at(c, k), :] = value

    load = lambda c, k: kept_ref[at(c, k), :]
    move_points(load, store, BLOCK // SUB, gathered(parts, cells), materials, shear_ref, lame_ref)
    fresh = fresh_ref[...]
    rows = fresh.T
    vacated = outgoing(rows, cells, materials, list_ref, (m0_ref, m1_ref, m2_ref, m3_ref))
    gone = jnp.broadcast_to(vacated.astype(F32), fresh.shape) > 0.5
    old_ref[...] = jnp.where(gone, 0.0, fresh).T
    old_meta_ref[...] = vacate(meta, vacated)

    half = BLOCK // 2
    new_cells, new_materials = (new_meta_ref[0:1, :], new_meta_ref[1:2, :])

    def store_new(c, k, value):
        wide_ref[c * BLOCK + k * SUB : c * BLOCK + (k + 1) * SUB, :] = value
        wide_ref[c * BLOCK + half + k * SUB : c * BLOCK + half + (k + 1) * SUB, :] = pltpu.roll(value, BLOCK, 1)

    load_new = lambda c, k: turned_ref[c * half + k * SUB : c * half + (k + 1) * SUB, :]
    near = gathered(parts, new_cells)
    move_points(load_new, store_new, half // SUB, near, new_materials, shear_ref, lame_ref)
    new_ref[...] = wide_ref[...].T[0 : 4 * MCAP]


def assemble(
    old_ref, new_ref, old_meta_ref, new_meta_ref, xi_ref, xo_ref, yi_ref, yo_ref,
    points_ref, cells_ref, mats_ref,
):
    old, new = (old_ref.shape[0], 4 * MCAP)
    points_ref[0:old, :] = old_ref[...]
    points_ref[old : old + new, :] = new_ref[...]
    boxes = regions(xi_ref[...], xo_ref[...], yi_ref[...], yo_ref[...])
    for index, box in enumerate(boxes):
        start = old + new + index * MCAP
        points_ref[start : start + MCAP, :] = box[0:MCAP]
    last_meta = arrived_meta(boxes)
    lane = iota((1, LANES), 1)
    for row, ref in ((0, cells_ref), (1, mats_ref)):
        ref[0:1, :] = old_meta_ref[row : row + 1, :]
        ref[1:2, :] = jnp.where(lane < new, new_meta_ref[row : row + 1, :], last_meta[row : row + 1])


def shards(
    points,
    block_cell,
    block_mat,
    density,
    shear_modulus,
    lame_modulus,
    mig_slot_a,
    mig_dest_a,
    mig_cell_a,
    mig_slot_b,
    mig_dest_b,
    mig_cell_b,
):
    wide = 8 * BLOCK
    I32 = jnp.int32
    blank = jnp.zeros((LANES,), I32)
    meta = jnp.stack([block_cell, block_mat] + [blank] * 6)
    lists = []
    for entries in ((mig_slot_a, mig_dest_a, mig_cell_a), (mig_slot_b, mig_dest_b, mig_cell_b)):
        rows = [jnp.pad(e, (0, LANES - e.shape[0]), constant_values=-1) for e in entries]
        lists.append(jnp.stack(rows + [blank] * 5))

    halo = ((HALO, LANES), F32)
    tile = ((SUB, LANES), F32)
    tags = ((SUB, LANES), I32)
    grid = ((ROWS, LANES), F32)
    message = ((MSG, wide), F32)
    turned_form = ((wide, LANES), F32)
    half_form = ((wide // 2, LANES), F32)

    def exchange_sums(sums, inner, outer):
        from_inner, from_outer = (swap(inner, "gx", 0), swap(outer, "gx", 1))
        merged, inner, outer = call(
            merge_depth, (grid, tile, tile), (), (IN_VMEM,) * 3, sums, from_inner, from_outer
        )
        return (merged, swap(inner, "gy", 0), swap(outer, "gy", 1))

    def exchange_blocks(messages):
        return (
            swap(messages[0], "gx", 0),
            swap(messages[1], "gx", 1),
            swap(messages[2], "gy", 0),
            swap(messages[3], "gy", 1),
        )

    sums, inner, outer, turned = call(
        sums_one,
        (grid, halo, halo, turned_form),
        (pltpu.VMEM((ROWS, 4 * LANES), F32),),
        (IN_VMEM, IN_VMEM, IN_SMEM),
        points, meta, density,
    )
    merged, from_inner, from_outer = exchange_sums(sums, inner, outer)
    kept, kept_meta, *messages = call(
        advance_one,
        (turned_form, tags) + (message,) * 4,
        (pltpu.VMEM((ROWS, LANES), F32), pltpu.VMEM((wide, LANES), F32)),
        (IN_VMEM,) * 6 + (IN_SMEM,) * 2,
        turned, meta, lists[0], merged, from_inner, from_outer, shear_modulus, lame_modulus,
    )
    arrived = exchange_blocks(messages)
    sums, inner, outer, turned, new_meta = call(
        sums_two,
        (grid, halo, halo, half_form, tags),
        (pltpu.VMEM((ROWS, 8 * LANES), F32), pltpu.VMEM((wide, LANES), F32)),
        (IN_VMEM,) * 6 + (IN_SMEM,),
        kept, kept_meta, *arrived, density,
    )
    merged, from_inner, from_outer = exchange_sums(sums, inner, outer)
    old, new, old_meta, *messages = call(
        advance_two,
        (((LANES, wide), F32), ((4 * MCAP, wide), F32), tags) + (message,) * 4,
        (
            pltpu.VMEM((ROWS, LANES), F32),
            pltpu.VMEM((wide, LANES), F32),
            pltpu.VMEM((wide, LANES), F32),
        ),
        (IN_VMEM,) * 8 + (IN_SMEM,) * 2,
        kept, kept_meta, turned, new_meta, lists[1], merged, from_inner, from_outer, shear_modulus, lame_modulus,
    )
    arrived = exchange_blocks(messages)
    final_points, cells, mats = call(
        assemble,
        (((2 * LANES, wide), F32), ((2, LANES), I32), ((2, LANES), I32)),
        (),
        (IN_VMEM,) * 8,
        old, new, old_meta, new_meta, *arrived,
    )
    return (final_points, cells.reshape(-1), mats.reshape(-1))


def solution(mesh):
    split = P(("gx", "gy"))
    rows = P(("gx", "gy"), None)
    return jax.shard_map(
        shards,
        mesh=mesh,
        in_specs=(rows, split, split, P(), P(), P()) + (split,) * 6,
        out_specs=(rows, split, split),
        check_vma=False,
    )
```

profile of v0, /device:TPU:412, one launch (start us, length us, event | category | flops | bytes accessed | tf_op | source)
XLA Modules:
  0.0 82.3 jit_solution(18287533835691510069)
XLA Ops:
  0.7 0.6 copy-done.8
  2.0 0.9 %copy-done = f32[128,512]{1,0:T(8,128)S(1)} copy-done((f32[128,512]{1,0:T(8,128)S(1)}, f32[128,512]{1,0:T(8,128)}, u32[]{:S(2)}) %copy-start) | copy-done | bytes 262168
  3.0 1.4 %shard_map.139 = (f32[160,128]{1,0:T(8,128)S(1)}, f32[24,128]{1,0:T(8,128)S(1)}, f32[24,128]{1,0:T(8,128)S(1)}, f32[512,128]{1,0:T(8,128)S(1)}) custom-call(f32[128,512]{1,0:T(8,128)S(1)} %copy-done, s32[8,128]{1,0:T(8,128)S(1)} %pad_add_fusion.meta_ref, f32[8]{0:T(128)S(1)} %copy-done.1), custom_call_target="tpu_custom_call" | custom-call | tf_op jit(solution)/shard_map/pallas_call | solution.py:34
  4.4 1.9 %collective-permute-start = (f32[24,128]{1,0:T(8,128)S(1)}, f32[24,128]{1,0:T(8,128)S(1)}, u32[]{:S(2)}, u32[]{:S(2)}) collective-permute-start(f32[24,128]{1,0:T(8,128)S(1)} %get-tuple-element.36), channel_id=1, source_target_pairs={{0,8},{8,0},{16,24},{24,16},{32,40},{40,32},{48,56},{56,48},{64,72... | collective-permute-start | bytes 36872 | tf_op jit(solution)/shard_map/ppermute | solution.py:49
  6.3 3.2 %collective-permute-start.1 = (f32[24,128]{1,0:T(8,128)S(1)}, f32[24,128]{1,0:T(8,128)S(1)}, u32[]{:S(2)}, u32[]{:S(2)}) collective-permute-start(f32[24,128]{1,0:T(8,128)S(1)} %get-tuple-element.37), channel_id=1, source_target_pairs={{8,16},{16,8},{24,32},{32,24},{40,48},{48,40},{56,64},{64,56},{72,... | collective-permute-start | bytes 36872 | tf_op jit(solution)/shard_map/ppermute | solution.py:49
  9.6 3.2 %collective-permute-done.1.from_outer_ref = f32[24,128]{1,0:T(8,128)S(1)} collective-permute-done((f32[24,128]{1,0:T(8,128)S(1)}, f32[24,128]{1,0:T(8,128)S(1)}, u32[]{:S(2)}, u32[]{:S(2)}) %collective-permute-start.1) | collective-permute-done | bytes 12320 | tf_op jit(solution)/shard_map/ppermute | solution.py:49
  13.0 2.7 %collective-permute-start.2 = (f32[8,128]{1,0:T(8,128)S(1)}, f32[8,128]{1,0:T(8,128)S(1)}, u32[]{:S(2)}, u32[]{:S(2)}) collective-permute-start(f32[8,128]{1,0:T(8,128)S(1)} %get-tuple-element.39), channel_id=1, source_target_pairs={{0,1},{1,0},{2,3},{3,2},{4,5},{5,4},{6,7},{7,6},{8,9},{9,8},{10,11... | collective-permute-start | bytes 12296 | tf_op jit(solution)/shard_map/ppermute | solution.py:49
  15.6 3.8 %collective-permute-start.3 = (f32[8,128]{1,0:T(8,128)S(1)}, f32[8,128]{1,0:T(8,128)S(1)}, u32[]{:S(2)}, u32[]{:S(2)}) collective-permute-start(f32[8,128]{1,0:T(8,128)S(1)} %get-tuple-element.40), channel_id=1, source_target_pairs={{1,2},{2,1},{3,4},{4,3},{5,6},{6,5},{9,10},{10,9},{11,12},{12,11},... | collective-permute-start | bytes 12296 | tf_op jit(solution)/shard_map/ppermute | solution.py:49
  19.5 2.5 %collective-permute-done.3.yo_ref = f32[8,128]{1,0:T(8,128)S(1)} collective-permute-done((f32[8,128]{1,0:T(8,128)S(1)}, f32[8,128]{1,0:T(8,128)S(1)}, u32[]{:S(2)}, u32[]{:S(2)}) %collective-permute-start.3) | collective-permute-done | bytes 4128 | tf_op jit(solution)/shard_map/ppermute | solution.py:49
  22.0 0.7 copy-done.2
  22.7 1.4 %shard_map.141 = (f32[512,128]{1,0:T(8,128)S(1)}, s32[8,128]{1,0:T(8,128)S(1)}, f32[24,512]{1,0:T(8,128)S(1)}, f32[24,512]{1,0:T(8,128)S(1)}, f32[24,512]{1,0:T(8,128)S(1)}, /*index=5*/f32[24,512]{1,0:T(8,128)S(1)}) custom-call(f32[512,128]{1,0:T(8,128)S(1)} %get-tuple-element.34.turned_ref, s32[8,128]{1,0:T(8,128)S(1)} %pad_add_fusion.meta_ref, ...), custom_call_target="tpu_custom_call" | custom-call | tf_op jit(solution)/shard_map/pallas_call | solution.py:34
  24.1 2.0 %collective-permute-start.4 = (f32[24,512]{1,0:T(8,128)S(1)}, f32[24,512]{1,0:T(8,128)S(1)}, u32[]{:S(2)}, u32[]{:S(2)}) collective-permute-start(f32[24,512]{1,0:T(8,128)S(1)} %get-tuple-element.43), channel_id=1, source_target_pairs={{0,8},{8,0},{16,24},{24,16},{32,40},{40,32},{48,56},{56,48},{64,72... | collective-permute-start | bytes 147464 | tf_op jit(solution)/shard_map/ppermute | solution.py:49
  26.2 5.0 %collective-permute-start.5 = (f32[24,512]{1,0:T(8,128)S(1)}, f32[24,512]{1,0:T(8,128)S(1)}, u32[]{:S(2)}, u32[]{:S(2)}) collective-permute-start(f32[24,512]{1,0:T(8,128)S(1)} %get-tuple-element.44), channel_id=1, source_target_pairs={{8,16},{16,8},{24,32},{32,24},{40,48},{48,40},{56,64},{64,56},{72,... | collective-permute-start | bytes 147464 | tf_op jit(solution)/shard_map/ppermute | solution.py:49
  31.1 2.9 %collective-permute-start.6 = (f32[24,512]{1,0:T(8,128)S(1)}, f32[24,512]{1,0:T(8,128)S(1)}, u32[]{:S(2)}, u32[]{:S(2)}) collective-permute-start(f32[24,512]{1,0:T(8,128)S(1)} %get-tuple-element.45), channel_id=1, source_target_pairs={{0,1},{1,0},{2,3},{3,2},{4,5},{5,4},{6,7},{7,6},{8,9},{9,8},{10,11... | collective-permute-start | bytes 147464 | tf_op jit(solution)/shard_map/ppermute | solution.py:49
  34.0 2.6 %collective-permute-start.7 = (f32[24,512]{1,0:T(8,128)S(1)}, f32[24,512]{1,0:T(8,128)S(1)}, u32[]{:S(2)}, u32[]{:S(2)}) collective-permute-start(f32[24,512]{1,0:T(8,128)S(1)} %get-tuple-element.46), channel_id=1, source_target_pairs={{1,2},{2,1},{3,4},{4,3},{5,6},{6,5},{9,10},{10,9},{11,12},{12,11},... | collective-permute-start | bytes 147464 | tf_op jit(solution)/shard_map/ppermute | solution.py:49
  37.1 3.8 %collective-permute-done.7.yo_ref = f32[24,512]{1,0:T(8,128)S(1)} collective-permute-done((f32[24,512]{1,0:T(8,128)S(1)}, f32[24,512]{1,0:T(8,128)S(1)}, u32[]{:S(2)}, u32[]{:S(2)}) %collective-permute-start.7) | collective-permute-done | bytes 49184 | tf_op jit(solution)/shard_map/ppermute | solution.py:49
  40.9 1.8 %shard_map.142 = (f32[160,128]{1,0:T(8,128)S(1)}, f32[24,128]{1,0:T(8,128)S(1)}, f32[24,128]{1,0:T(8,128)S(1)}, f32[256,128]{1,0:T(8,128)S(1)}, s32[8,128]{1,0:T(8,128)S(1)}) custom-call(f32[512,128]{1,0:T(8,128)S(1)} %get-tuple-element.41.kept_ref, s32[8,128]{1,0:T(8,128)S(1)} %get-tuple-element.42.meta_ref, f32[24,512]{1,0:T(8,128)S(1)} %collective-permute-done.4.xi_ref, ...), custom_call_target="tpu_custom_call" | custom-call | tf_op jit(solution)/shard_map/pallas_call | solution.py:34
  42.8 1.9 %collective-permute-start.8 = (f32[24,128]{1,0:T(8,128)S(1)}, f32[24,128]{1,0:T(8,128)S(1)}, u32[]{:S(2)}, u32[]{:S(2)}) collective-permute-start(f32[24,128]{1,0:T(8,128)S(1)} %get-tuple-element.50), channel_id=1, source_target_pairs={{0,8},{8,0},{16,24},{24,16},{32,40},{40,32},{48,56},{56,48},{64,72... | collective-permute-start | bytes 36872 | tf_op jit(solution)/shard_map/ppermute | solution.py:49
  44.7 5.7 %collective-permute-start.9 = (f32[24,128]{1,0:T(8,128)S(1)}, f32[24,128]{1,0:T(8,128)S(1)}, u32[]{:S(2)}, u32[]{:S(2)}) collective-permute-start(f32[24,128]{1,0:T(8,128)S(1)} %get-tuple-element.51), channel_id=1, source_target_pairs={{8,16},{16,8},{24,32},{32,24},{40,48},{48,40},{56,64},{64,56},{72,... | collective-permute-start | bytes 36872 | tf_op jit(solution)/shard_map/ppermute | solution.py:49
  50.5 1.3 %collective-permute-done.9.from_outer_ref = f32[24,128]{1,0:T(8,128)S(1)} collective-permute-done((f32[24,128]{1,0:T(8,128)S(1)}, f32[24,128]{1,0:T(8,128)S(1)}, u32[]{:S(2)}, u32[]{:S(2)}) %collective-permute-start.9) | collective-permute-done | bytes 12320 | tf_op jit(solution)/shard_map/ppermute | solution.py:49
  51.9 2.3 %collective-permute-start.10 = (f32[8,128]{1,0:T(8,128)S(1)}, f32[8,128]{1,0:T(8,128)S(1)}, u32[]{:S(2)}, u32[]{:S(2)}) collective-permute-start(f32[8,128]{1,0:T(8,128)S(1)} %get-tuple-element.53), channel_id=1, source_target_pairs={{0,1},{1,0},{2,3},{3,2},{4,5},{5,4},{6,7},{7,6},{8,9},{9,8},{10,11... | collective-permute-start | bytes 12296 | tf_op jit(solution)/shard_map/ppermute | solution.py:49
  54.3 1.9 %collective-permute-start.11 = (f32[8,128]{1,0:T(8,128)S(1)}, f32[8,128]{1,0:T(8,128)S(1)}, u32[]{:S(2)}, u32[]{:S(2)}) collective-permute-start(f32[8,128]{1,0:T(8,128)S(1)} %get-tuple-element.54), channel_id=1, source_target_pairs={{1,2},{2,1},{3,4},{4,3},{5,6},{6,5},{9,10},{10,9},{11,12},{12,11},... | collective-permute-start | bytes 12296 | tf_op jit(solution)/shard_map/ppermute | solution.py:49
  56.3 1.2 %collective-permute-done.10.yi_ref = f32[8,128]{1,0:T(8,128)S(1)} collective-permute-done((f32[8,128]{1,0:T(8,128)S(1)}, f32[8,128]{1,0:T(8,128)S(1)}, u32[]{:S(2)}, u32[]{:S(2)}) %collective-permute-start.10) | collective-permute-done | bytes 4128 | tf_op jit(solution)/shard_map/ppermute | solution.py:49
  57.4 3.3 %collective-permute-done.11.yo_ref = f32[8,128]{1,0:T(8,128)S(1)} collective-permute-done((f32[8,128]{1,0:T(8,128)S(1)}, f32[8,128]{1,0:T(8,128)S(1)}, u32[]{:S(2)}, u32[]{:S(2)}) %collective-permute-start.11) | collective-permute-done | bytes 4128 | tf_op jit(solution)/shard_map/ppermute | solution.py:49
  60.7 1.8 %shard_map.144 = (f32[128,512]{1,0:T(8,128)S(1)}, f32[64,512]{1,0:T(8,128)S(1)}, s32[8,128]{1,0:T(8,128)S(1)}, f32[24,512]{1,0:T(8,128)S(1)}, f32[24,512]{1,0:T(...) custom-call(f32[512,128]{1,0:T(8,128)S(1)} %get-tuple-element.41.kept_ref, ...), custom_call_target="tpu_custom_call" | custom-call | tf_op jit(solution)/shard_map/pallas_call | solution.py:34
  62.5 2.0 %collective-permute-start.12 = (f32[24,512]{1,0:T(8,128)S(1)}, f32[24,512]{1,0:T(8,128)S(1)}, u32[]{:S(2)}, u32[]{:S(2)}) collective-permute-start(f32[24,512]{1,0:T(8,128)S(1)} %get-tuple-element.58), channel_id=1, source_target_pairs={{0,8},{8,0},{16,24},{24,16},{32,40},{40,32},{48,56},{56,48},{64,72... | collective-permute-start | bytes 147464 | tf_op jit(solution)/shard_map/ppermute | solution.py:49
  64.5 6.8 %collective-permute-start.13 = (f32[24,512]{1,0:T(8,128)S(1)}, f32[24,512]{1,0:T(8,128)S(1)}, u32[]{:S(2)}, u32[]{:S(2)}) collective-permute-start(f32[24,512]{1,0:T(8,128)S(1)} %get-tuple-element.59), channel_id=1, source_target_pairs={{8,16},{16,8},{24,32},{32,24},{40,48},{48,40},{56,64},{64,56},{72,... | collective-permute-start | bytes 147464 | tf_op jit(solution)/shard_map/ppermute | solution.py:49
  71.4 3.2 %collective-permute-start.14 = (f32[24,512]{1,0:T(8,128)S(1)}, f32[24,512]{1,0:T(8,128)S(1)}, u32[]{:S(2)}, u32[]{:S(2)}) collective-permute-start(f32[24,512]{1,0:T(8,128)S(1)} %get-tuple-element.60), channel_id=1, source_target_pairs={{0,1},{1,0},{2,3},{3,2},{4,5},{5,4},{6,7},{7,6},{8,9},{9,8},{10,11... | collective-permute-start | bytes 147464 | tf_op jit(solution)/shard_map/ppermute | solution.py:49
  74.6 1.9 %collective-permute-start.15 = (f32[24,512]{1,0:T(8,128)S(1)}, f32[24,512]{1,0:T(8,128)S(1)}, u32[]{:S(2)}, u32[]{:S(2)}) collective-permute-start(f32[24,512]{1,0:T(8,128)S(1)} %get-tuple-element.61), channel_id=1, source_target_pairs={{1,2},{2,1},{3,4},{4,3},{5,6},{6,5},{9,10},{10,9},{11,12},{12,11},... | collective-permute-start | bytes 147464 | tf_op jit(solution)/shard_map/ppermute | solution.py:49
  76.5 1.4 %collective-permute-done.14.yi_ref = f32[24,512]{1,0:T(8,128)S(1)} collective-permute-done((f32[24,512]{1,0:T(8,128)S(1)}, f32[24,512]{1,0:T(8,128)S(1)}, u32[]{:S(2)}, u32[]{:S(2)}) %collective-permute-start.14) | collective-permute-done | bytes 49184 | tf_op jit(solution)/shard_map/ppermute | solution.py:49
  77.9 3.6 %collective-permute-done.15.yo_ref = f32[24,512]{1,0:T(8,128)S(1)} collective-permute-done((f32[24,512]{1,0:T(8,128)S(1)}, f32[24,512]{1,0:T(8,128)S(1)}, u32[]{:S(2)}, u32[]{:S(2)}) %collective-permute-start.15) | collective-permute-done | bytes 49184 | tf_op jit(solution)/shard_map/ppermute | solution.py:49
  81.5 0.9 %shard_map.145 = (f32[256,512]{1,0:T(8,128)}, s32[2,128]{1,0:T(2,128)}, s32[2,128]{1,0:T(2,128)}) custom-call(f32[128,512]{1,0:T(8,128)S(1)} %get-tuple-element.55.old_ref, f32[64,512]{1,0:T(8,128)S(1)} %get-tuple-element.56.new_ref, s32[8,128]{1,0:T(8,128)S(1)} %get-tuple-element.57.old_meta_ref, s32[8,128]{1,0:T(8,128)S(1)} %get-tuple-element.48.new_meta_ref, ...), custom_call_target="tpu_custom_call" | custom-call | tf_op jit(solution)/shard_map/pallas_call | solution.py:34
  (42 shorter events, 1.6 us)
Async XLA Ops:
  0.7 0.7 copy-start.8
  0.7 0.7 copy-start.9
  1.4 0.7 copy-start.1
  2.0 0.9 %copy-start = (f32[128,512]{1,0:T(8,128)S(1)}, f32[128,512]{1,0:T(8,128)}, u32[]{:S(2)}) copy-start(f32[128,512]{1,0:T(8,128)} %points_ref.1) | copy-start | bytes 786436
  4.4 5.2 %copy-start.4 = (s32[64]{0:T(128)S(1)}, s32[64]{0:T(128)}, u32[]{:S(2)}) copy-start(s32[64]{0:T(128)} %param.20) | copy-start | bytes 772
  4.4 5.2 %copy-start.5 = (s32[64]{0:T(128)S(1)}, s32[64]{0:T(128)}, u32[]{:S(2)}) copy-start(s32[64]{0:T(128)} %param.19) | copy-start | bytes 772
  4.4 5.2 %collective-permute-start = (f32[24,128]{1,0:T(8,128)S(1)}, f32[24,128]{1,0:T(8,128)S(1)}, u32[]{:S(2)}, u32[]{:S(2)}) collective-permute-start(f32[24,128]{1,0:T(8,128)S(1)} %get-tuple-element.36), channel_id=1, source_target_pairs={{0,8},{8,0},{16,24},{24,16},{32,40},{40,32},{48,56},{56,48},{64,72... | collective-permute-start | bytes 36872 | tf_op jit(solution)/shard_map/ppermute | solution.py:49
  6.3 6.5 %collective-permute-start.1 = (f32[24,128]{1,0:T(8,128)S(1)}, f32[24,128]{1,0:T(8,128)S(1)}, u32[]{:S(2)}, u32[]{:S(2)}) collective-permute-start(f32[24,128]{1,0:T(8,128)S(1)} %get-tuple-element.37), channel_id=1, source_target_pairs={{8,16},{16,8},{24,32},{32,24},{40,48},{48,40},{56,64},{64,56},{72,... | collective-permute-start | bytes 36872 | tf_op jit(solution)/shard_map/ppermute | solution.py:49
  12.9 6.5 %copy-start.10 = (s32[64]{0:T(128)S(1)}, s32[64]{0:T(128)}, u32[]{:S(2)}) copy-start(s32[64]{0:T(128)} %param.18) | copy-start | bytes 772
  13.0 6.6 %collective-permute-start.2 = (f32[8,128]{1,0:T(8,128)S(1)}, f32[8,128]{1,0:T(8,128)S(1)}, u32[]{:S(2)}, u32[]{:S(2)}) collective-permute-start(f32[8,128]{1,0:T(8,128)S(1)} %get-tuple-element.39), channel_id=1, source_target_pairs={{0,1},{1,0},{2,3},{3,2},{4,5},{5,4},{6,7},{7,6},{8,9},{9,8},{10,11... | collective-permute-start | bytes 12296 | tf_op jit(solution)/shard_map/ppermute | solution.py:49
  15.6 6.4 %collective-permute-start.3 = (f32[8,128]{1,0:T(8,128)S(1)}, f32[8,128]{1,0:T(8,128)S(1)}, u32[]{:S(2)}, u32[]{:S(2)}) collective-permute-start(f32[8,128]{1,0:T(8,128)S(1)} %get-tuple-element.40), channel_id=1, source_target_pairs={{1,2},{2,1},{3,4},{4,3},{5,6},{6,5},{9,10},{10,9},{11,12},{12,11},... | collective-permute-start | bytes 12296 | tf_op jit(solution)/shard_map/ppermute | solution.py:49
  22.0 0.7 copy-start.2
  22.0 0.7 copy-start.3
  24.1 12.5 %collective-permute-start.4 = (f32[24,512]{1,0:T(8,128)S(1)}, f32[24,512]{1,0:T(8,128)S(1)}, u32[]{:S(2)}, u32[]{:S(2)}) collective-permute-start(f32[24,512]{1,0:T(8,128)S(1)} %get-tuple-element.43), channel_id=1, source_target_pairs={{0,8},{8,0},{16,24},{24,16},{32,40},{40,32},{48,56},{56,48},{64,72... | collective-permute-start | bytes 147464 | tf_op jit(solution)/shard_map/ppermute | solution.py:49
  26.2 10.4 %collective-permute-start.5 = (f32[24,512]{1,0:T(8,128)S(1)}, f32[24,512]{1,0:T(8,128)S(1)}, u32[]{:S(2)}, u32[]{:S(2)}) collective-permute-start(f32[24,512]{1,0:T(8,128)S(1)} %get-tuple-element.44), channel_id=1, source_target_pairs={{8,16},{16,8},{24,32},{32,24},{40,48},{48,40},{56,64},{64,56},{72,... | collective-permute-start | bytes 147464 | tf_op jit(solution)/shard_map/ppermute | solution.py:49
  31.1 6.0 %collective-permute-start.6 = (f32[24,512]{1,0:T(8,128)S(1)}, f32[24,512]{1,0:T(8,128)S(1)}, u32[]{:S(2)}, u32[]{:S(2)}) collective-permute-start(f32[24,512]{1,0:T(8,128)S(1)} %get-tuple-element.45), channel_id=1, source_target_pairs={{0,1},{1,0},{2,3},{3,2},{4,5},{5,4},{6,7},{7,6},{8,9},{9,8},{10,11... | collective-permute-start | bytes 147464 | tf_op jit(solution)/shard_map/ppermute | solution.py:49
  34.0 6.9 %collective-permute-start.7 = (f32[24,512]{1,0:T(8,128)S(1)}, f32[24,512]{1,0:T(8,128)S(1)}, u32[]{:S(2)}, u32[]{:S(2)}) collective-permute-start(f32[24,512]{1,0:T(8,128)S(1)} %get-tuple-element.46), channel_id=1, source_target_pairs={{1,2},{2,1},{3,4},{4,3},{5,6},{6,5},{9,10},{10,9},{11,12},{12,11},... | collective-permute-start | bytes 147464 | tf_op jit(solution)/shard_map/ppermute | solution.py:49
  42.7 7.7 %copy-start.6 = (s32[64]{0:T(128)S(1)}, s32[64]{0:T(128)}, u32[]{:S(2)}) copy-start(s32[64]{0:T(128)} %param.23) | copy-start | bytes 772
  42.7 7.7 %copy-start.7 = (s32[64]{0:T(128)S(1)}, s32[64]{0:T(128)}, u32[]{:S(2)}) copy-start(s32[64]{0:T(128)} %param.22) | copy-start | bytes 772
  42.8 7.7 %collective-permute-start.8 = (f32[24,128]{1,0:T(8,128)S(1)}, f32[24,128]{1,0:T(8,128)S(1)}, u32[]{:S(2)}, u32[]{:S(2)}) collective-permute-start(f32[24,128]{1,0:T(8,128)S(1)} %get-tuple-element.50), channel_id=1, source_target_pairs={{0,8},{8,0},{16,24},{24,16},{32,40},{40,32},{48,56},{56,48},{64,72... | collective-permute-start | bytes 36872 | tf_op jit(solution)/shard_map/ppermute | solution.py:49
  44.7 7.1 %collective-permute-start.9 = (f32[24,128]{1,0:T(8,128)S(1)}, f32[24,128]{1,0:T(8,128)S(1)}, u32[]{:S(2)}, u32[]{:S(2)}) collective-permute-start(f32[24,128]{1,0:T(8,128)S(1)} %get-tuple-element.51), channel_id=1, source_target_pairs={{8,16},{16,8},{24,32},{32,24},{40,48},{48,40},{56,64},{64,56},{72,... | collective-permute-start | bytes 36872 | tf_op jit(solution)/shard_map/ppermute | solution.py:49
  51.9 4.3 %copy-start.11 = (s32[64]{0:T(128)S(1)}, s32[64]{0:T(128)}, u32[]{:S(2)}) copy-start(s32[64]{0:T(128)} %param.21) | copy-start | bytes 772
  51.9 5.5 %collective-permute-start.10 = (f32[8,128]{1,0:T(8,128)S(1)}, f32[8,128]{1,0:T(8,128)S(1)}, u32[]{:S(2)}, u32[]{:S(2)}) collective-permute-start(f32[8,128]{1,0:T(8,128)S(1)} %get-tuple-element.53), channel_id=1, source_target_pairs={{0,1},{1,0},{2,3},{3,2},{4,5},{5,4},{6,7},{7,6},{8,9},{9,8},{10,11... | collective-permute-start | bytes 12296 | tf_op jit(solution)/shard_map/ppermute | solution.py:49
  54.3 6.4 %collective-permute-start.11 = (f32[8,128]{1,0:T(8,128)S(1)}, f32[8,128]{1,0:T(8,128)S(1)}, u32[]{:S(2)}, u32[]{:S(2)}) collective-permute-start(f32[8,128]{1,0:T(8,128)S(1)} %get-tuple-element.54), channel_id=1, source_target_pairs={{1,2},{2,1},{3,4},{4,3},{5,6},{6,5},{9,10},{10,9},{11,12},{12,11},... | collective-permute-start | bytes 12296 | tf_op jit(solution)/shard_map/ppermute | solution.py:49
  62.5 14.0 %collective-permute-start.12 = (f32[24,512]{1,0:T(8,128)S(1)}, f32[24,512]{1,0:T(8,128)S(1)}, u32[]{:S(2)}, u32[]{:S(2)}) collective-permute-start(f32[24,512]{1,0:T(8,128)S(1)} %get-tuple-element.58), channel_id=1, source_target_pairs={{0,8},{8,0},{16,24},{24,16},{32,40},{40,32},{48,56},{56,48},{64,72... | collective-permute-start | bytes 147464 | tf_op jit(solution)/shard_map/ppermute | solution.py:49
  64.5 12.0 %collective-permute-start.13 = (f32[24,512]{1,0:T(8,128)S(1)}, f32[24,512]{1,0:T(8,128)S(1)}, u32[]{:S(2)}, u32[]{:S(2)}) collective-permute-start(f32[24,512]{1,0:T(8,128)S(1)} %get-tuple-element.59), channel_id=1, source_target_pairs={{8,16},{16,8},{24,32},{32,24},{40,48},{48,40},{56,64},{64,56},{72,... | collective-permute-start | bytes 147464 | tf_op jit(solution)/shard_map/ppermute | solution.py:49
  71.4 6.5 %collective-permute-start.14 = (f32[24,512]{1,0:T(8,128)S(1)}, f32[24,512]{1,0:T(8,128)S(1)}, u32[]{:S(2)}, u32[]{:S(2)}) collective-permute-start(f32[24,512]{1,0:T(8,128)S(1)} %get-tuple-element.60), channel_id=1, source_target_pairs={{0,1},{1,0},{2,3},{3,2},{4,5},{5,4},{6,7},{7,6},{8,9},{9,8},{10,11... | collective-permute-start | bytes 147464 | tf_op jit(solution)/shard_map/ppermute | solution.py:49
  74.6 6.9 %collective-permute-start.15 = (f32[24,512]{1,0:T(8,128)S(1)}, f32[24,512]{1,0:T(8,128)S(1)}, u32[]{:S(2)}, u32[]{:S(2)}) collective-permute-start(f32[24,512]{1,0:T(8,128)S(1)} %get-tuple-element.61), channel_id=1, source_target_pairs={{1,2},{2,1},{3,4},{4,3},{5,6},{6,5},{9,10},{10,9},{11,12},{12,11},... | collective-permute-start | bytes 147464 | tf_op jit(solution)/shard_map/ppermute | solution.py:49
where the time goes:
time: 82.9 us; the launch traced here: 82.3 us
  starting transfers between devices  50 us (60%)
  waiting for transfers between devices  20.7 us (25%)
  Pallas kernels  7.5 us (9%)
  local copies, waits for them, and re-layouts  3.05 us (4%)
  between operations  1 us (1%)
    ppermute x16, starting transfers between devices, swap(): return lax.ppermute(value, axis, pairs)  50 us
    ppermute x16, waiting for transfers between devices, swap(): return lax.ppermute(value, axis, pairs)  20.7 us
    pallas_call x7, Pallas kernels, call(): pl.pallas_call(kernel, out_shape=tuple((jax.ShapeDtypeStruct(shape, dtype...  7.5 us
    unnamed x24, local copies, waits for them, and re-layouts  2.91 us
  transfers between devices with their start and end apart: 16, of which 9 were waited for; matrix products, arithmetic and copies ran while one was open for 0% of the time, Pallas kernels for 0%

commit v1 on v0

--- a/solution.py
+++ b/solution.py
@@ -23,21 +23,23 @@
 VMEM_LIMIT = 12 * 1024 * 1024
 
 IN_VMEM = pl.BlockSpec(memory_space=pltpu.VMEM)
-IN_SMEM = pl.BlockSpec(memory_space=pltpu.SMEM)
+IN_HBM = pl.BlockSpec(memory_space=pltpu.HBM)
 F32 = jnp.float32
 BF16 = jnp.bfloat16
 NN = (((1,), (0,)), ((), ()))
 NT = (((1,), (1,)), ((), ()))
 
 
-def call(kernel, outs, scratch, in_specs, *operands):
+def call(kernel, outs, scratch, in_specs, *operands, out_specs=None, aliases=None):
     return pl.pallas_call(
         kernel,
         out_shape=tuple(jax.ShapeDtypeStruct(shape, dtype) for shape, dtype in outs),
         in_specs=in_specs,
-        out_specs=tuple(IN_VMEM for _ in outs),
+        out_specs=out_specs or tuple(IN_VMEM for _ in outs),
         scratch_shapes=scratch,
+        input_output_aliases=aliases or {},
         compiler_params=pltpu.CompilerParams(vmem_limit_bytes=VMEM_LIMIT),
+        cost_estimate=pl.CostEstimate(flops=1 << 22, bytes_accessed=1 << 19, transcendentals=0),
     )(*operands)
 
 
@@ -79,10 +81,11 @@
     return (weight, slope)
 
 
-def by_material(materials, table):
+def by_material(materials, tables_ref, which):
     value = jnp.zeros(materials.shape, F32)
     for index in range(NMAT):
-        value = jnp.where(materials == index, table[index], value)
+        row = which * NMAT + index
+        value = jnp.where(materials == index, tables_ref[row : row + 1, :], value)
     return value
 
 
@@ -143,8 +146,10 @@
     return (lax.axis_index(axis) & 1) == 1
 
 
-def emit_sums(left_ref, onehots, sums_ref, inner_ref, outer_ref):
+def emit_sums(left_ref, onehots, more_ref, sums_ref, inner_ref, outer_ref):
     sums = product(thirds(left_ref[...]), jnp.concatenate(onehots, axis=1), NT)
+    if more_ref is not None:
+        sums = sums + more_ref[...]
     sums_ref[...] = sums
     odd = parity("gx")
     bottom, top = (sums[0:HALO], sums[TOP : TOP + HALO])
@@ -152,14 +157,36 @@
     outer_ref[...] = jnp.where(odd, top, bottom)
 
 
-def sums_one(points_ref, meta_ref, density_ref, sums_ref, inner_ref, outer_ref, turned_ref, left_ref):
+def turn(points_ref, turned_ref):
     turned_ref[...] = points_ref[...].T
-    cells = meta_ref[0:1, :]
-    rho = by_material(meta_ref[1:2, :], density_ref)
+
+
+def sums_one(
+    turned_ref, cells_ref, mats_ref, density_ref, shear_ref, lame_ref,
+    sums_ref, inner_ref, outer_ref, tables_ref, meta_ref,
+    left_ref,
+):
+    for which, table_ref in enumerate((density_ref, shear_ref, lame_ref)):
+        table = table_ref[...]
+        for index in range(NMAT):
+            row = which * NMAT + index
+            tables_ref[row : row + 1, :] = jnp.broadcast_to(table[:, index : index + 1], (1, LANES))
+    cells, materials = (cells_ref[...], mats_ref[...])
+    meta_ref[0:1, :] = cells
+    meta_ref[1:2, :] = materials
+    rho = by_material(materials, tables_ref, 0)
     load = lambda c, k: turned_ref[c * BLOCK + k * SUB : c * BLOCK + (k + 1) * SUB, :]
     terms = node_terms(load, BLOCK // SUB, rho)
     spread_rows(terms, row_masks(cells), left_ref, 0)
-    emit_sums(left_ref, column_onehot(cells), sums_ref, inner_ref, outer_ref)
+    emit_sums(left_ref, column_onehot(cells), None, sums_ref, inner_ref, outer_ref)
+
+
+def join_lists(*refs):
+    *list_refs, lists_ref = refs
+    for index, ref in enumerate(list_refs):
+        row = ref[...]
+        rest = jnp.full((1, LANES - row.shape[1]), -1, jnp.int32)
+        lists_ref[index : index + 1, :] = jnp.concatenate([row, rest], axis=1)
 
 
 def regions(from_inner_x, from_outer_x, from_inner_y, from_outer_y):
@@ -173,21 +200,31 @@
 
 
 def arrived_meta(boxes):
-    packed = boxes[0][MCAP:MSG, 0:LANES]
+    packed = boxes[0]
     for index in range(1, 4):
-        packed = packed + pltpu.roll(boxes[index][MCAP:MSG, 0:LANES], MCAP * index, 1)
+        packed = packed + pltpu.roll(boxes[index], MCAP * index, 1)
     packed = packed + pltpu.roll(packed, 4 * MCAP, 1)
     sub = iota((SUB, LANES), 0)
     return packed.astype(jnp.int32) - (sub == 1).astype(jnp.int32)
 
 
+def sums_kept(fresh_ref, kept_meta_ref, tables_ref, sums_ref, kept_ref, left_ref):
+    cells, materials = (kept_meta_ref[0:1, :], kept_meta_ref[1:2, :])
+    alive = jnp.broadcast_to(materials, fresh_ref.shape) >= 0
+    kept_ref[...] = jnp.where(alive, fresh_ref[...], 0.0)
+    load = lambda c, k: kept_ref[c * BLOCK + k * SUB : c * BLOCK + (k + 1) * SUB, :]
+    terms = node_terms(load, BLOCK // SUB, by_material(materials, tables_ref, 0))
+    spread_rows(terms, row_masks(cells), left_ref, 0)
+    sums_ref[...] = product(thirds(left_ref[...]), jnp.concatenate(column_onehot(cells), axis=1), NT)
+
+
 def sums_two(
-    kept_ref, meta_ref, xi_ref, xo_ref, yi_ref, yo_ref, density_ref,
+    kept_sums_ref, xo_ref, yo_ref, yi_ref, xi_ref, tables_ref,
     sums_ref, inner_ref, outer_ref, turned_ref, new_meta_ref,
     left_ref, wide_ref,
 ):
     boxes = regions(xi_ref[...], xo_ref[...], yi_ref[...], yo_ref[...])
-    new_meta = arrived_meta(boxes)
+    new_meta = arrived_meta([box[MCAP:MSG, 0:LANES] for box in boxes])
     new_meta_ref[...] = new_meta
     rows = jnp.concatenate([box[0:MCAP] for box in boxes], axis=0)
     wide_ref[...] = jnp.concatenate([rows, jnp.zeros_like(rows)], axis=0).T
@@ -196,20 +233,14 @@
         first = wide_ref[c * BLOCK : c * BLOCK + half, :]
         second = wide_ref[c * BLOCK + half : (c + 1) * BLOCK, :]
         turned_ref[c * half : (c + 1) * half, :] = first + pltpu.roll(second, BLOCK, 1)
-    onehots = []
-    for lane, chunks, ref, cells, mats in (
-        (0, BLOCK // SUB, kept_ref, meta_ref[0:1, :], meta_ref[1:2, :]),
-        (4 * LANES, half // SUB, turned_ref, new_meta[0:1], new_meta[1:2]),
-    ):
-        stride = chunks * SUB
-        load = lambda c, k: ref[c * stride + k * SUB : c * stride + (k + 1) * SUB, :]
-        terms = node_terms(load, chunks, by_material(mats, density_ref))
-        spread_rows(terms, row_masks(cells), left_ref, lane)
-        onehots += column_onehot(cells)
-    emit_sums(left_ref, onehots, sums_ref, inner_ref, outer_ref)
-
-
-def merge_depth(sums_ref, from_inner_ref, from_outer_ref, merged_ref, inner_ref, outer_ref):
+    cells, materials = (new_meta[0:1], new_meta[1:2])
+    load = lambda c, k: turned_ref[c * half + k * SUB : c * half + (k + 1) * SUB, :]
+    terms = node_terms(load, half // SUB, by_material(materials, tables_ref, 0))
+    spread_rows(terms, row_masks(cells), left_ref, 0)
+    emit_sums(left_ref, column_onehot(cells), kept_sums_ref, sums_ref, inner_ref, outer_ref)
+
+
+def merge_depth(sums_ref, from_outer_ref, from_inner_ref, merged_ref, inner_ref, outer_ref):
     odd = parity("gx")
     from_inner, from_outer = (from_inner_ref[...], from_outer_ref[...])
     merged_ref[...] = sums_ref[...]
@@ -268,10 +299,10 @@
     return near
 
 
-def move_points(load, store, chunks, near, materials, shear_ref, lame_ref):
+def move_points(load, store, chunks, near, materials, tables_ref):
     wide = lambda row: jnp.broadcast_to(row, (SUB, LANES))
-    twice_shear = wide(2.0 * by_material(materials, shear_ref))
-    lame = wide(by_material(materials, lame_ref))
+    twice_shear = wide(2.0 * by_material(materials, tables_ref, 1))
+    lame = wide(by_material(materials, tables_ref, 2))
     alive = wide(materials) >= 0
     for k in range(chunks):
         u, v = (load(0, k), load(1, k))
@@ -315,13 +346,13 @@
             store(c, k, jnp.where(alive, fresh[c], 0.0))
 
 
-def outgoing(fresh, cells, materials, list_ref, message_refs):
+def outgoing(fresh, materials, lists, message_refs):
     across = lax.axis_size("gy")
     gx, gy = (lax.axis_index("gx"), lax.axis_index("gy"))
     home = gx * across + gy
     step_x = across - 2 * across * (gx & 1)
     step_y = 1 - 2 * (gy & 1)
-    slots, dests, places = (list_ref[0:1, :], list_ref[1:2, :], list_ref[2:3, :])
+    slots, dests, places = (lists[0:1], lists[1:2], lists[2:3])
     dest = jnp.broadcast_to(dests, (2 * SUB, LANES))
     sub = iota((2 * SUB, LANES), 0)
     matched = jnp.zeros((2 * SUB, LANES), F32)
@@ -362,87 +393,104 @@
     return vacated
 
 
-def vacate(meta, vacated):
-    sub = iota((SUB, LANES), 0)
+def vacate(cells, materials, vacated):
+    first = iota((SUB, LANES), 0) == 0
     gone = jnp.broadcast_to(vacated.astype(F32), (SUB, LANES)) > 0.5
-    return jnp.where(gone, jnp.where(sub == 1, -1, 0), meta)
-
-
-def advance_one(
-    turned_ref, meta_ref, list_ref, merged_ref, yi_ref, yo_ref, shear_ref, lame_ref,
-    kept_ref, kept_meta_ref, m0_ref, m1_ref, m2_ref, m3_ref,
-    velocity_ref, fresh_ref,
-):
+    meta = jnp.where(first, jnp.broadcast_to(cells, gone.shape), jnp.broadcast_to(materials, gone.shape))
+    return jnp.where(gone, jnp.where(first, 0, -1), meta)
+
+
+def advance_old(load, meta_ref, lists, merged_ref, yo_ref, yi_ref, tables_ref, outs, velocity_ref):
+    fresh_ref, kept_meta_ref, *message_refs = outs
+    cells, materials = (meta_ref[0:1, :], meta_ref[1:2, :])
     node_velocity(merged_ref, yi_ref, yo_ref, velocity_ref)
-    parts = thirds(velocity_ref[...])
-    meta = meta_ref[...]
-    cells, materials = (meta[0:1], meta[1:2])
     at = lambda c, k: slice(c * BLOCK + k * SUB, c * BLOCK + (k + 1) * SUB)
 
     def store(c, k, value):
         fresh_ref[at(c, k), :] = value
 
-    load = lambda c, k: turned_ref[at(c, k), :]
-    move_points(load, store, BLOCK // SUB, gathered(parts, cells), materials, shear_ref, lame_ref)
-    fresh = fresh_ref[...]
-    vacated = outgoing(fresh.T, cells, materials, list_ref, (m0_ref, m1_ref, m2_ref, m3_ref))
-    gone = jnp.broadcast_to(vacated.astype(F32), fresh.shape) > 0.5
-    kept_ref[...] = jnp.where(gone, 0.0, fresh)
-    kept_meta_ref[...] = vacate(meta, vacated)
+    near = gathered(thirds(velocity_ref[...]), cells)
+    move_points(lambda c, k: load(at(c, k)), store, BLOCK // SUB, near, materials, tables_ref)
+    vacated = outgoing(fresh_ref[...].T, materials, lists, message_refs)
+    kept_meta_ref[...] = vacate(cells, materials, vacated)
+
+
+def advance_one(
+    turned_ref, meta_ref, lists_ref, merged_ref, yo_ref, yi_ref, tables_ref,
+    fresh_ref, kept_meta_ref, m0_ref, m1_ref, m2_ref, m3_ref,
+    velocity_ref,
+):
+    advance_old(
+        lambda rows: turned_ref[rows, :], meta_ref, lists_ref[0:3, :], merged_ref, yo_ref, yi_ref, tables_ref,
+        (fresh_ref, kept_meta_ref, m0_ref, m1_ref, m2_ref, m3_ref), velocity_ref,
+    )
 
 
 def advance_two(
-    kept_ref, meta_ref, turned_ref, new_meta_ref, list_ref, merged_ref, yi_ref, yo_ref, shear_ref, lame_ref,
-    old_ref, new_ref, old_meta_ref, m0_ref, m1_ref, m2_ref, m3_ref,
-    velocity_ref, fresh_ref, wide_ref,
+    kept_ref, meta_ref, lists_ref, merged_ref, yo_ref, yi_ref, tables_ref,
+    fresh_ref, old_meta_ref, velocity_ref, m0_ref, m1_ref, m2_ref, m3_ref,
 ):
-    node_velocity(merged_ref, yi_ref, yo_ref, velocity_ref)
-    parts = thirds(velocity_ref[...])
-    meta = meta_ref[...]
-    cells, materials = (meta[0:1], meta[1:2])
-    at = lambda c, k: slice(c * BLOCK + k * SUB, c * BLOCK + (k + 1) * SUB)
+    advance_old(
+        lambda rows: kept_ref[rows, :], meta_ref, lists_ref[3:6, :], merged_ref, yo_ref, yi_ref, tables_ref,
+        (fresh_ref, old_meta_ref, m0_ref, m1_ref, m2_ref, m3_ref), velocity_ref,
+    )
+
+
+def settle(
+    fresh_ref, old_meta_ref, velocity_ref, turned_ref, new_meta_ref, tables_ref,
+    points_ref,
+    old_ref, wide_ref, new_ref, sems,
+):
+    alive = jnp.broadcast_to(old_meta_ref[1:2, :], fresh_ref.shape) >= 0
+    old_ref[...] = jnp.where(alive, fresh_ref[...], 0.0).T
+    old, new = (LANES, 4 * MCAP)
+    first = pltpu.make_async_copy(old_ref, points_ref.at[0:old], sems.at[0])
+    first.start()
+    half = BLOCK // 2
+    cells, materials = (new_meta_ref[0:1, :], new_meta_ref[1:2, :])
 
     def store(c, k, value):
-        fresh_ref[at(c, k), :] = value
-
-    load = lambda c, k: kept_ref[at(c, k), :]
-    move_points(load, store, BLOCK // SUB, gathered(parts, cells), materials, shear_ref, lame_ref)
-    fresh = fresh_ref[...]
-    rows = fresh.T
-    vacated = outgoing(rows, cells, materials, list_ref, (m0_ref, m1_ref, m2_ref, m3_ref))
-    gone = jnp.broadcast_to(vacated.astype(F32), fresh.shape) > 0.5
-    old_ref[...] = jnp.where(gone, 0.0, fresh).T
-    old_meta_ref[...] = vacate(meta, vacated)
-
-    half = BLOCK // 2
-    new_cells, new_materials = (new_meta_ref[0:1, :], new_meta_ref[1:2, :])
-
-    def store_new(c, k, value):
         wide_ref[c * BLOCK + k * SUB : c * BLOCK + (k + 1) * SUB, :] = value
         wide_ref[c * BLOCK + half + k * SUB : c * BLOCK + half + (k + 1) * SUB, :] = pltpu.roll(value, BLOCK, 1)
 
-    load_new = lambda c, k: turned_ref[c * half + k * SUB : c * half + (k + 1) * SUB, :]
-    near = gathered(parts, new_cells)
-    move_points(load_new, store_new, half // SUB, near, new_materials, shear_ref, lame_ref)
-    new_ref[...] = wide_ref[...].T[0 : 4 * MCAP]
+    load = lambda c, k: turned_ref[c * half + k * SUB : c * half + (k + 1) * SUB, :]
+    near = gathered(thirds(velocity_ref[...]), cells)
+    move_points(load, store, half // SUB, near, materials, tables_ref)
+    new_ref[...] = wide_ref[...].T[0:new]
+    second = pltpu.make_async_copy(new_ref, points_ref.at[old : old + new], sems.at[1])
+    second.start()
+    first.wait()
+    second.wait()
 
 
 def assemble(
-    old_ref, new_ref, old_meta_ref, new_meta_ref, xi_ref, xo_ref, yi_ref, yo_ref,
+    part_ref, old_meta_ref, new_meta_ref, xo_ref, yo_ref, yi_ref, xi_ref,
     points_ref, cells_ref, mats_ref,
+    tags_ref, sems,
 ):
-    old, new = (old_ref.shape[0], 4 * MCAP)
-    points_ref[0:old, :] = old_ref[...]
-    points_ref[old : old + new, :] = new_ref[...]
-    boxes = regions(xi_ref[...], xo_ref[...], yi_ref[...], yo_ref[...])
-    for index, box in enumerate(boxes):
-        start = old + new + index * MCAP
-        points_ref[start : start + MCAP, :] = box[0:MCAP]
-    last_meta = arrived_meta(boxes)
+    del part_ref
+    new = 4 * MCAP
+    base = points_ref.shape[0] - new
+    odd_x, odd_y = (lax.axis_index("gx") & 1, lax.axis_index("gy") & 1)
+    copies = []
+    for index, (ref, region) in enumerate(
+        ((xo_ref, odd_x), (yo_ref, 2 + odd_y), (yi_ref, 3 - odd_y), (xi_ref, 1 - odd_x))
+    ):
+        start = pl.multiple_of(base + region * MCAP, MCAP)
+        copies.append(
+            pltpu.make_async_copy(ref.at[0:MCAP, :], points_ref.at[pl.ds(start, MCAP), :], sems.at[index])
+        )
+        copies[-1].start()
+    tiles = [ref[MCAP:MSG, 0:LANES] for ref in (xi_ref, xo_ref, yi_ref, yo_ref)]
+    last_meta = arrived_meta(regions(*tiles))
     lane = iota((1, LANES), 1)
     for row, ref in ((0, cells_ref), (1, mats_ref)):
-        ref[0:1, :] = old_meta_ref[row : row + 1, :]
-        ref[1:2, :] = jnp.where(lane < new, new_meta_ref[row : row + 1, :], last_meta[row : row + 1])
+        tags_ref[row, 0:1, :] = old_meta_ref[row : row + 1, :]
+        tags_ref[row, 1:2, :] = jnp.where(lane < new, new_meta_ref[row : row + 1, :], last_meta[row : row + 1])
+        copies.append(pltpu.make_async_copy(tags_ref.at[row], ref, sems.at[4 + row]))
+        copies[-1].start()
+    for copy in copies:
+        copy.wait()
 
 
 def shards(
@@ -461,12 +509,10 @@
 ):
     wide = 8 * BLOCK
     I32 = jnp.int32
-    blank = jnp.zeros((LANES,), I32)
-    meta = jnp.stack([block_cell, block_mat] + [blank] * 6)
-    lists = []
-    for entries in ((mig_slot_a, mig_dest_a, mig_cell_a), (mig_slot_b, mig_dest_b, mig_cell_b)):
-        rows = [jnp.pad(e, (0, LANES - e.shape[0]), constant_values=-1) for e in entries]
-        lists.append(jnp.stack(rows + [blank] * 5))
+    row = lambda value: value.reshape(1, -1)
+    cells, mats = (row(block_cell), row(block_mat))
+    list_a = (row(mig_slot_a), row(mig_dest_a), row(mig_cell_a))
+    list_b = (row(mig_slot_b), row(mig_dest_b), row(mig_cell_b))
 
     halo = ((HALO, LANES), F32)
     tile = ((SUB, LANES), F32)
@@ -475,66 +521,88 @@
     message = ((MSG, wide), F32)
     turned_form = ((wide, LANES), F32)
     half_form = ((wide // 2, LANES), F32)
+    scratch = lambda form: pltpu.VMEM(*form)
+    left = pltpu.VMEM((ROWS, 4 * LANES), F32)
 
     def exchange_sums(sums, inner, outer):
-        from_inner, from_outer = (swap(inner, "gx", 0), swap(outer, "gx", 1))
+        from_outer = swap(outer, "gx", 1)
+        from_inner = swap(inner, "gx", 0)
         merged, inner, outer = call(
-            merge_depth, (grid, tile, tile), (), (IN_VMEM,) * 3, sums, from_inner, from_outer
+            merge_depth, (grid, tile, tile), (), (IN_VMEM,) * 3, sums, from_outer, from_inner
         )
-        return (merged, swap(inner, "gy", 0), swap(outer, "gy", 1))
+        from_outer = swap(outer, "gy", 1)
+        from_inner = swap(inner, "gy", 0)
+        return (merged, from_outer, from_inner)
 
     def exchange_blocks(messages):
-        return (
-            swap(messages[0], "gx", 0),
-            swap(messages[1], "gx", 1),
-            swap(messages[2], "gy", 0),
-            swap(messages[3], "gy", 1),
-        )
-
-    sums, inner, outer, turned = call(
+        xi, xo, yi, yo = messages
+        xo = swap(xo, "gx", 1)
+        yo = swap(yo, "gy", 1)
+        yi = swap(yi, "gy", 0)
+        xi = swap(xi, "gx", 0)
+        return (xo, yo, yi, xi)
+
+    (lists,) = call(join_lists, (tags,), (), (IN_VMEM,) * 6, *list_a, *list_b)
+    (turned,) = call(turn, (turned_form,), (), (IN_VMEM,), points)
+    sums, inner, outer, tables, meta = call(
         sums_one,
-        (grid, halo, halo, turned_form),
-        (pltpu.VMEM((ROWS, 4 * LANES), F32),),
-        (IN_VMEM, IN_VMEM, IN_SMEM),
-        points, meta, density,
-    )
-    merged, from_inner, from_outer = exchange_sums(sums, inner, outer)
-    kept, kept_meta, *messages = call(
+        (grid, halo, halo, ((3 * NMAT, LANES), F32), tags),
+        (left,),
+        (IN_VMEM,) * 6,
+        turned, cells, mats, row(density), row(shear_modulus), row(lame_modulus),
+    )
+    merged, from_outer, from_inner = exchange_sums(sums, inner, outer)
+    fresh, kept_meta, *messages = call(
         advance_one,
         (turned_form, tags) + (message,) * 4,
-        (pltpu.VMEM((ROWS, LANES), F32), pltpu.VMEM((wide, LANES), F32)),
-        (IN_VMEM,) * 6 + (IN_SMEM,) * 2,
-        turned, meta, lists[0], merged, from_inner, from_outer, shear_modulus, lame_modulus,
+        (scratch(grid),),
+        (IN_VMEM,) * 7,
+        turned, meta, lists, merged, from_outer, from_inner, tables,
     )
     arrived = exchange_blocks(messages)
+    kept_sums, kept = call(
+        sums_kept, (grid, turned_form), (left,), (IN_VMEM,) * 3, fresh, kept_meta, tables
+    )
     sums, inner, outer, turned, new_meta = call(
         sums_two,
         (grid, halo, halo, half_form, tags),
-        (pltpu.VMEM((ROWS, 8 * LANES), F32), pltpu.VMEM((wide, LANES), F32)),
-        (IN_VMEM,) * 6 + (IN_SMEM,),
-        kept, kept_meta, *arrived, density,
-    )
-    merged, from_inner, from_outer = exchange_sums(sums, inner, outer)
-    old, new, old_meta, *messages = call(
+        (left, scratch(turned_form)),
+        (IN_VMEM,) * 6,
+        kept_sums, *arrived, tables,
+    )
+    merged, from_outer, from_inner = exchange_sums(sums, inner, outer)
+    fresh, old_meta, velocity, *messages = call(
         advance_two,
-        (((LANES, wide), F32), ((4 * MCAP, wide), F32), tags) + (message,) * 4,
+        (turned_form, tags, grid) + (message,) * 4,
+        (),
+        (IN_VMEM,) * 7,
+        kept, kept_meta, lists, merged, from_outer, from_inner, tables,
+    )
+    arrived = exchange_blocks(messages)
+    final_form = ((2 * LANES, wide), F32)
+    (part,) = call(
+        settle,
+        (final_form,),
         (
-            pltpu.VMEM((ROWS, LANES), F32),
-            pltpu.VMEM((wide, LANES), F32),
-            pltpu.VMEM((wide, LANES), F32),
+            pltpu.VMEM((LANES, wide), F32),
+            scratch(turned_form),
+            pltpu.VMEM((4 * MCAP, wide), F32),
+            pltpu.SemaphoreType.DMA((2,)),
         ),
-        (IN_VMEM,) * 8 + (IN_SMEM,) * 2,
-        kept, kept_meta, turned, new_meta, lists[1], merged, from_inner, from_outer, shear_modulus, lame_modulus,
-    )
-    arrived = exchange_blocks(messages)
-    final_points, cells, mats = call(
+        (IN_VMEM,) * 6,
+        fresh, old_meta, velocity, turned, new_meta, tables,
+        out_specs=(IN_HBM,),
+    )
+    final_points, final_cells, final_mats = call(
         assemble,
-        (((2 * LANES, wide), F32), ((2, LANES), I32), ((2, LANES), I32)),
-        (),
-        (IN_VMEM,) * 8,
-        old, new, old_meta, new_meta, *arrived,
-    )
-    return (final_points, cells.reshape(-1), mats.reshape(-1))
+        (final_form, ((2, LANES), I32), ((2, LANES), I32)),
+        (pltpu.VMEM((2, 2, LANES), I32), pltpu.SemaphoreType.DMA((6,))),
+        (IN_HBM,) + (IN_VMEM,) * 6,
+        part, old_meta, new_meta, *arrived,
+        out_specs=(IN_HBM,) * 3,
+        aliases={0: 0},
+    )
+    return (final_points, final_cells.reshape(-1), final_mats.reshape(-1))
 
 
 def solution(mesh):

time: 82.9 us -> 70.4 us (0.85)
  the two profiles are of different devices: /device:TPU:412 before, /device:TPU:389 now
where the time goes in v1:
time: 70.4 us; the launch traced here: 69.8 us
  starting transfers between devices  56.8 us (81%)
  Pallas kernels  6.37 us (9%)
  waiting for transfers between devices  3.36 us (5%)
  local copies, waits for them, and re-layouts  2.31 us (3%)
  between operations  0.99 us (1%)
    ppermute x16, starting transfers between devices, swap(): return lax.ppermute(value, axis, pairs)  56.8 us
    pallas_call x11, Pallas kernels, call(): pl.pallas_call(kernel, out_shape=tuple((jax.ShapeDtypeStruct(shape, dtype...  6.37 us
    ppermute x16, waiting for transfers between devices, swap(): return lax.ppermute(value, axis, pairs)  3.36 us
    unnamed x24, local copies, waits for them, and re-layouts  2.31 us
  transfers between devices with their start and end apart: 16, of which 6 were waited for; matrix products, arithmetic and copies ran while one was open for 0% of the time, Pallas kernels for 3%

profile of v1, /device:TPU:389, one launch (start us, length us, event | category | flops | bytes accessed | tf_op | source)
XLA Modules:
  0.0 69.8 jit_solution(9531092563394766568)
XLA Ops:
  0.6 0.9 %copy-done = f32[128,512]{1,0:T(8,128)S(1)} copy-done((f32[128,512]{1,0:T(8,128)S(1)}, f32[128,512]{1,0:T(8,128)}, u32[]{:S(2)}) %copy-start) | copy-done | bytes 262168
  1.6 0.1 shard_map.139.turned_ref
  1.8 0.6 copy-done.4
  2.4 0.7 %shard_map.140 = (f32[160,128]{1,0:T(8,128)S(1)}, f32[24,128]{1,0:T(8,128)S(1)}, f32[24,128]{1,0:T(8,128)S(1)}, f32[24,128]{1,0:T(8,128)S(1)}, s32[8,128]{1,0:T(8,128)S(1)}) custom-call(f32[512,128]{1,0:T(8,128)S(1)} %shard_map.139.turned_ref, s32[1,128]{1,0:T(1,128)S(1)} %bitcast.13, s32[1,128]{1,0:T(1,128)S(1)} %bitcast.14, f32[1,8]{1,0:T(1,128)S(1)} %bitcast.15, ...), custom_call_target="tpu_custom_call" | custom-call | flops 4194304 | bytes 524288 | tf_op jit(solution)/shard_map/pallas_call | solution.py:34
  3.2 5.4 %collective-permute-start = (f32[24,128]{1,0:T(8,128)S(1)}, f32[24,128]{1,0:T(8,128)S(1)}, u32[]{:S(2)}, u32[]{:S(2)}) collective-permute-start(f32[24,128]{1,0:T(8,128)S(1)} %get-tuple-element.39), channel_id=1, source_target_pairs={{8,16},{16,8},{24,32},{32,24},{40,48},{48,40},{56,64},{64,56},{72,... | collective-permute-start | bytes 36872 | tf_op jit(solution)/shard_map/ppermute | solution.py:51
  8.6 3.4 %collective-permute-start.1 = (f32[24,128]{1,0:T(8,128)S(1)}, f32[24,128]{1,0:T(8,128)S(1)}, u32[]{:S(2)}, u32[]{:S(2)}) collective-permute-start(f32[24,128]{1,0:T(8,128)S(1)} %get-tuple-element.40), channel_id=1, source_target_pairs={{0,8},{8,0},{16,24},{24,16},{32,40},{40,32},{48,56},{56,48},{64,72... | collective-permute-start | bytes 36872 | tf_op jit(solution)/shard_map/ppermute | solution.py:51
  12.0 0.8 %collective-permute-done.1.from_inner_ref = f32[24,128]{1,0:T(8,128)S(1)} collective-permute-done((f32[24,128]{1,0:T(8,128)S(1)}, f32[24,128]{1,0:T(8,128)S(1)}, u32[]{:S(2)}, u32[]{:S(2)}) %collective-permute-start.1) | collective-permute-done | bytes 12320 | tf_op jit(solution)/shard_map/ppermute | solution.py:51
  12.9 2.3 %collective-permute-start.2 = (f32[8,128]{1,0:T(8,128)S(1)}, f32[8,128]{1,0:T(8,128)S(1)}, u32[]{:S(2)}, u32[]{:S(2)}) collective-permute-start(f32[8,128]{1,0:T(8,128)S(1)} %get-tuple-element.42), channel_id=1, source_target_pairs={{1,2},{2,1},{3,4},{4,3},{5,6},{6,5},{9,10},{10,9},{11,12},{12,11},... | collective-permute-start | bytes 12296 | tf_op jit(solution)/shard_map/ppermute | solution.py:51
  15.2 3.6 %collective-permute-start.3 = (f32[8,128]{1,0:T(8,128)S(1)}, f32[8,128]{1,0:T(8,128)S(1)}, u32[]{:S(2)}, u32[]{:S(2)}) collective-permute-start(f32[8,128]{1,0:T(8,128)S(1)} %get-tuple-element.43), channel_id=1, source_target_pairs={{0,1},{1,0},{2,3},{3,2},{4,5},{5,4},{6,7},{7,6},{8,9},{9,8},{10,11... | collective-permute-start | bytes 12296 | tf_op jit(solution)/shard_map/ppermute | solution.py:51
  18.9 0.6 copy-done.9
  19.6 0.2 collective-permute-done.3.yi_ref
  19.8 0.9 %shard_map.143 = (f32[512,128]{1,0:T(8,128)S(1)}, s32[8,128]{1,0:T(8,128)S(1)}, f32[24,512]{1,0:T(8,128)S(1)}, f32[24,512]{1,0:T(8,128)S(1)}, f32[24,512]{1,0:T(8,128)S(1)}, /*index=5*/f32[24,512]{1,0:T(8,128)S(1)}) custom-call(f32[512,128]{1,0:T(8,128)S(1)} %shard_map.139.turned_ref, s32[8,128]{1,0:T(8,128)S(1)} %get-tuple-element.37.meta_ref, ...), custom_call_target="tpu_custom_call" | custom-call | flops 4194304 | bytes 524288 | tf_op jit(solution)/shard_map/pallas_call | solution.py:34
  20.7 4.1 %collective-permute-start.4 = (f32[24,512]{1,0:T(8,128)S(1)}, f32[24,512]{1,0:T(8,128)S(1)}, u32[]{:S(2)}, u32[]{:S(2)}) collective-permute-start(f32[24,512]{1,0:T(8,128)S(1)} %get-tuple-element.49), channel_id=1, source_target_pairs={{8,16},{16,8},{24,32},{32,24},{40,48},{48,40},{56,64},{64,56},{72,... | collective-permute-start | bytes 147464 | tf_op jit(solution)/shard_map/ppermute | solution.py:51
  24.8 2.7 %collective-permute-start.5 = (f32[24,512]{1,0:T(8,128)S(1)}, f32[24,512]{1,0:T(8,128)S(1)}, u32[]{:S(2)}, u32[]{:S(2)}) collective-permute-start(f32[24,512]{1,0:T(8,128)S(1)} %get-tuple-element.50), channel_id=1, source_target_pairs={{1,2},{2,1},{3,4},{4,3},{5,6},{6,5},{9,10},{10,9},{11,12},{12,11},... | collective-permute-start | bytes 147464 | tf_op jit(solution)/shard_map/ppermute | solution.py:51
  27.5 3.5 %collective-permute-start.6 = (f32[24,512]{1,0:T(8,128)S(1)}, f32[24,512]{1,0:T(8,128)S(1)}, u32[]{:S(2)}, u32[]{:S(2)}) collective-permute-start(f32[24,512]{1,0:T(8,128)S(1)} %get-tuple-element.51), channel_id=1, source_target_pairs={{0,1},{1,0},{2,3},{3,2},{4,5},{5,4},{6,7},{7,6},{8,9},{9,8},{10,11... | collective-permute-start | bytes 147464 | tf_op jit(solution)/shard_map/ppermute | solution.py:51
  31.0 4.6 %collective-permute-start.7 = (f32[24,512]{1,0:T(8,128)S(1)}, f32[24,512]{1,0:T(8,128)S(1)}, u32[]{:S(2)}, u32[]{:S(2)}) collective-permute-start(f32[24,512]{1,0:T(8,128)S(1)} %get-tuple-element.52), channel_id=1, source_target_pairs={{0,8},{8,0},{16,24},{24,16},{32,40},{40,32},{48,56},{56,48},{64,72... | collective-permute-start | bytes 147464 | tf_op jit(solution)/shard_map/ppermute | solution.py:51
  35.6 0.8 %shard_map.144 = (f32[160,128]{1,0:T(8,128)S(1)}, f32[512,128]{1,0:T(8,128)S(1)}) custom-call(f32[512,128]{1,0:T(8,128)S(1)} %get-tuple-element.45.fresh_ref, s32[8,128]{1,0:T(8,128)S(1)} %get-tuple-element.46.kept_meta_ref.meta_ref, f32[24,128]{1,0:T(8,128)S(1)} %get-tuple-element.44.tables_ref), custom_call_target="tpu_custom_call" | custom-call | flops 4194304 | bytes 524288 | tf_op jit(solution)/shard_map/pallas_call | solution.py:34
  36.5 0.8 %shard_map.145 = (f32[160,128]{1,0:T(8,128)S(1)}, f32[24,128]{1,0:T(8,128)S(1)}, f32[24,128]{1,0:T(8,128)S(1)}, f32[256,128]{1,0:T(8,128)S(1)}, s32[8,128]{1,0:T(8,128)S(1)}) custom-call(f32[160,128]{1,0:T(8,128)S(1)} %get-tuple-element.48.kept_sums_ref, f32[24,512]{1,0:T(8,128)S(1)} %collective-permute-done.4.xo_ref, ...), custom_call_target="tpu_custom_call" | custom-call | flops 4194304 | bytes 524288 | tf_op jit(solution)/shard_map/pallas_call | solution.py:34
  37.3 2.1 %collective-permute-start.8 = (f32[24,128]{1,0:T(8,128)S(1)}, f32[24,128]{1,0:T(8,128)S(1)}, u32[]{:S(2)}, u32[]{:S(2)}) collective-permute-start(f32[24,128]{1,0:T(8,128)S(1)} %get-tuple-element.54), channel_id=1, source_target_pairs={{8,16},{16,8},{24,32},{32,24},{40,48},{48,40},{56,64},{64,56},{72,... | collective-permute-start | bytes 36872 | tf_op jit(solution)/shard_map/ppermute | solution.py:51
  39.4 4.3 %collective-permute-start.9 = (f32[24,128]{1,0:T(8,128)S(1)}, f32[24,128]{1,0:T(8,128)S(1)}, u32[]{:S(2)}, u32[]{:S(2)}) collective-permute-start(f32[24,128]{1,0:T(8,128)S(1)} %get-tuple-element.55), channel_id=1, source_target_pairs={{0,8},{8,0},{16,24},{24,16},{32,40},{40,32},{48,56},{56,48},{64,72... | collective-permute-start | bytes 36872 | tf_op jit(solution)/shard_map/ppermute | solution.py:51
  43.8 0.7 %collective-permute-done.9.from_inner_ref = f32[24,128]{1,0:T(8,128)S(1)} collective-permute-done((f32[24,128]{1,0:T(8,128)S(1)}, f32[24,128]{1,0:T(8,128)S(1)}, u32[]{:S(2)}, u32[]{:S(2)}) %collective-permute-start.9) | collective-permute-done | bytes 12320 | tf_op jit(solution)/shard_map/ppermute | solution.py:51
  44.5 0.1 shard_map.146
  44.6 2.7 %collective-permute-start.10 = (f32[8,128]{1,0:T(8,128)S(1)}, f32[8,128]{1,0:T(8,128)S(1)}, u32[]{:S(2)}, u32[]{:S(2)}) collective-permute-start(f32[8,128]{1,0:T(8,128)S(1)} %get-tuple-element.57), channel_id=1, source_target_pairs={{1,2},{2,1},{3,4},{4,3},{5,6},{6,5},{9,10},{10,9},{11,12},{12,11},... | collective-permute-start | bytes 12296 | tf_op jit(solution)/shard_map/ppermute | solution.py:51
  47.3 3.2 %collective-permute-start.11 = (f32[8,128]{1,0:T(8,128)S(1)}, f32[8,128]{1,0:T(8,128)S(1)}, u32[]{:S(2)}, u32[]{:S(2)}) collective-permute-start(f32[8,128]{1,0:T(8,128)S(1)} %get-tuple-element.58), channel_id=1, source_target_pairs={{0,1},{1,0},{2,3},{3,2},{4,5},{5,4},{6,7},{7,6},{8,9},{9,8},{10,11... | collective-permute-start | bytes 12296 | tf_op jit(solution)/shard_map/ppermute | solution.py:51
  50.5 1.4 %collective-permute-done.11.yi_ref = f32[8,128]{1,0:T(8,128)S(1)} collective-permute-done((f32[8,128]{1,0:T(8,128)S(1)}, f32[8,128]{1,0:T(8,128)S(1)}, u32[]{:S(2)}, u32[]{:S(2)}) %collective-permute-start.11) | collective-permute-done | bytes 4128 | tf_op jit(solution)/shard_map/ppermute | solution.py:51
  51.9 0.9 %shard_map.147 = (f32[512,128]{1,0:T(8,128)S(1)}, s32[8,128]{1,0:T(8,128)S(1)}, f32[160,128]{1,0:T(8,128)S(1)}, f32[24,512]{1,0:T(8,128)S(1)}, f32[24,512]{1,0:T...) custom-call(f32[512,128]{1,0:T(8,128)S(1)} %get-tuple-element.47.kept_ref, ...), custom_call_target="tpu_custom_call" | custom-call | flops 4194304 | bytes 524288 | tf_op jit(solution)/shard_map/pallas_call | solution.py:34
  52.9 3.7 %collective-permute-start.12 = (f32[24,512]{1,0:T(8,128)S(1)}, f32[24,512]{1,0:T(8,128)S(1)}, u32[]{:S(2)}, u32[]{:S(2)}) collective-permute-start(f32[24,512]{1,0:T(8,128)S(1)} %get-tuple-element.64), channel_id=1, source_target_pairs={{8,16},{16,8},{24,32},{32,24},{40,48},{48,40},{56,64},{64,56},{72,... | collective-permute-start | bytes 147464 | tf_op jit(solution)/shard_map/ppermute | solution.py:51
  56.6 3.2 %collective-permute-start.13 = (f32[24,512]{1,0:T(8,128)S(1)}, f32[24,512]{1,0:T(8,128)S(1)}, u32[]{:S(2)}, u32[]{:S(2)}) collective-permute-start(f32[24,512]{1,0:T(8,128)S(1)} %get-tuple-element.65), channel_id=1, source_target_pairs={{1,2},{2,1},{3,4},{4,3},{5,6},{6,5},{9,10},{10,9},{11,12},{12,11},... | collective-permute-start | bytes 147464 | tf_op jit(solution)/shard_map/ppermute | solution.py:51
  59.8 3.0 %collective-permute-start.14 = (f32[24,512]{1,0:T(8,128)S(1)}, f32[24,512]{1,0:T(8,128)S(1)}, u32[]{:S(2)}, u32[]{:S(2)}) collective-permute-start(f32[24,512]{1,0:T(8,128)S(1)} %get-tuple-element.66), channel_id=1, source_target_pairs={{0,1},{1,0},{2,3},{3,2},{4,5},{5,4},{6,7},{7,6},{8,9},{9,8},{10,11... | collective-permute-start | bytes 147464 | tf_op jit(solution)/shard_map/ppermute | solution.py:51
  62.8 5.0 %collective-permute-start.15 = (f32[24,512]{1,0:T(8,128)S(1)}, f32[24,512]{1,0:T(8,128)S(1)}, u32[]{:S(2)}, u32[]{:S(2)}) collective-permute-start(f32[24,512]{1,0:T(8,128)S(1)} %get-tuple-element.67), channel_id=1, source_target_pairs={{0,8},{8,0},{16,24},{24,16},{32,40},{40,32},{48,56},{56,48},{64,72... | collective-permute-start | bytes 147464 | tf_op jit(solution)/shard_map/ppermute | solution.py:51
  67.8 1.2 %shard_map.148.part_ref = f32[256,512]{1,0:T(8,128)} custom-call(f32[512,128]{1,0:T(8,128)S(1)} %get-tuple-element.59.fresh_ref, s32[8,128]{1,0:T(8,128)S(1)} %get-tuple-element.60.old_meta_ref, f32[160,128]{1,0:T(8,128)S(1)} %get-tuple-element.61.velocity_ref, f32[256,128]{1,0:T(8,128)S(1)} %get-tuple-element.62.turned_ref, ...), custom_call_target="tpu_custom_call" | custom-call | flops 4194304 | bytes 524288 | tf_op jit(solution)/shard_map/pallas_call | solution.py:34
  69.0 0.8 %shard_map.149 = (f32[256,512]{1,0:T(8,128)}, s32[2,128]{1,0:T(2,128)}, s32[2,128]{1,0:T(2,128)}) custom-call(f32[256,512]{1,0:T(8,128)} %shard_map.148.part_ref, s32[8,128]{1,0:T(8,128)S(1)} %get-tuple-element.60.old_meta_ref, s32[8,128]{1,0:T(8,128)S(1)} %get-tuple-element.63.new_meta_ref, ...), custom_call_target="tpu_custom_call", output_to_operand_aliasing={{0}: (0, {})} | custom-call | flops 4194304 | bytes 524288 | tf_op jit(solution)/shard_map/pallas_call | solution.py:34
  (35 shorter events, 0.5 us)
Async XLA Ops:
  0.6 1.0 %copy-start = (f32[128,512]{1,0:T(8,128)S(1)}, f32[128,512]{1,0:T(8,128)}, u32[]{:S(2)}) copy-start(f32[128,512]{1,0:T(8,128)} %points_ref.1) | copy-start | bytes 786436
  1.7 0.7 copy-start.4
  1.7 0.7 copy-start.5
  1.7 0.7 copy-start.1
  1.7 0.7 copy-start.2
  1.8 0.7 copy-start.3
  3.2 8.8 %collective-permute-start = (f32[24,128]{1,0:T(8,128)S(1)}, f32[24,128]{1,0:T(8,128)S(1)}, u32[]{:S(2)}, u32[]{:S(2)}) collective-permute-start(f32[24,128]{1,0:T(8,128)S(1)} %get-tuple-element.39), channel_id=1, source_target_pairs={{8,16},{16,8},{24,32},{32,24},{40,48},{48,40},{56,64},{64,56},{72,... | collective-permute-start | bytes 36872 | tf_op jit(solution)/shard_map/ppermute | solution.py:51
  8.6 4.2 %collective-permute-start.1 = (f32[24,128]{1,0:T(8,128)S(1)}, f32[24,128]{1,0:T(8,128)S(1)}, u32[]{:S(2)}, u32[]{:S(2)}) collective-permute-start(f32[24,128]{1,0:T(8,128)S(1)} %get-tuple-element.40), channel_id=1, source_target_pairs={{0,8},{8,0},{16,24},{24,16},{32,40},{40,32},{48,56},{56,48},{64,72... | collective-permute-start | bytes 36872 | tf_op jit(solution)/shard_map/ppermute | solution.py:51
  12.9 6.7 %collective-permute-start.2 = (f32[8,128]{1,0:T(8,128)S(1)}, f32[8,128]{1,0:T(8,128)S(1)}, u32[]{:S(2)}, u32[]{:S(2)}) collective-permute-start(f32[8,128]{1,0:T(8,128)S(1)} %get-tuple-element.42), channel_id=1, source_target_pairs={{1,2},{2,1},{3,4},{4,3},{5,6},{6,5},{9,10},{10,9},{11,12},{12,11},... | collective-permute-start | bytes 12296 | tf_op jit(solution)/shard_map/ppermute | solution.py:51
  15.2 4.6 %collective-permute-start.3 = (f32[8,128]{1,0:T(8,128)S(1)}, f32[8,128]{1,0:T(8,128)S(1)}, u32[]{:S(2)}, u32[]{:S(2)}) collective-permute-start(f32[8,128]{1,0:T(8,128)S(1)} %get-tuple-element.43), channel_id=1, source_target_pairs={{0,1},{1,0},{2,3},{3,2},{4,5},{5,4},{6,7},{7,6},{8,9},{9,8},{10,11... | collective-permute-start | bytes 12296 | tf_op jit(solution)/shard_map/ppermute | solution.py:51
  18.8 0.7 copy-start.9
  18.8 0.7 copy-start.10
  18.8 0.7 copy-start.11
  18.9 0.7 copy-start.6
  18.9 0.7 copy-start.7
  18.9 0.7 copy-start.8
  20.7 15.7 %collective-permute-start.4 = (f32[24,512]{1,0:T(8,128)S(1)}, f32[24,512]{1,0:T(8,128)S(1)}, u32[]{:S(2)}, u32[]{:S(2)}) collective-permute-start(f32[24,512]{1,0:T(8,128)S(1)} %get-tuple-element.49), channel_id=1, source_target_pairs={{8,16},{16,8},{24,32},{32,24},{40,48},{48,40},{56,64},{64,56},{72,... | collective-permute-start | bytes 147464 | tf_op jit(solution)/shard_map/ppermute | solution.py:51
  24.8 11.7 %collective-permute-start.5 = (f32[24,512]{1,0:T(8,128)S(1)}, f32[24,512]{1,0:T(8,128)S(1)}, u32[]{:S(2)}, u32[]{:S(2)}) collective-permute-start(f32[24,512]{1,0:T(8,128)S(1)} %get-tuple-element.50), channel_id=1, source_target_pairs={{1,2},{2,1},{3,4},{4,3},{5,6},{6,5},{9,10},{10,9},{11,12},{12,11},... | collective-permute-start | bytes 147464 | tf_op jit(solution)/shard_map/ppermute | solution.py:51
  27.5 9.0 %collective-permute-start.6 = (f32[24,512]{1,0:T(8,128)S(1)}, f32[24,512]{1,0:T(8,128)S(1)}, u32[]{:S(2)}, u32[]{:S(2)}) collective-permute-start(f32[24,512]{1,0:T(8,128)S(1)} %get-tuple-element.51), channel_id=1, source_target_pairs={{0,1},{1,0},{2,3},{3,2},{4,5},{5,4},{6,7},{7,6},{8,9},{9,8},{10,11... | collective-permute-start | bytes 147464 | tf_op jit(solution)/shard_map/ppermute | solution.py:51
  31.0 5.5 %collective-permute-start.7 = (f32[24,512]{1,0:T(8,128)S(1)}, f32[24,512]{1,0:T(8,128)S(1)}, u32[]{:S(2)}, u32[]{:S(2)}) collective-permute-start(f32[24,512]{1,0:T(8,128)S(1)} %get-tuple-element.52), channel_id=1, source_target_pairs={{0,8},{8,0},{16,24},{24,16},{32,40},{40,32},{48,56},{56,48},{64,72... | collective-permute-start | bytes 147464 | tf_op jit(solution)/shard_map/ppermute | solution.py:51
  37.3 6.5 %collective-permute-start.8 = (f32[24,128]{1,0:T(8,128)S(1)}, f32[24,128]{1,0:T(8,128)S(1)}, u32[]{:S(2)}, u32[]{:S(2)}) collective-permute-start(f32[24,128]{1,0:T(8,128)S(1)} %get-tuple-element.54), channel_id=1, source_target_pairs={{8,16},{16,8},{24,32},{32,24},{40,48},{48,40},{56,64},{64,56},{72,... | collective-permute-start | bytes 36872 | tf_op jit(solution)/shard_map/ppermute | solution.py:51
  39.4 5.1 %collective-permute-start.9 = (f32[24,128]{1,0:T(8,128)S(1)}, f32[24,128]{1,0:T(8,128)S(1)}, u32[]{:S(2)}, u32[]{:S(2)}) collective-permute-start(f32[24,128]{1,0:T(8,128)S(1)} %get-tuple-element.55), channel_id=1, source_target_pairs={{0,8},{8,0},{16,24},{24,16},{32,40},{40,32},{48,56},{56,48},{64,72... | collective-permute-start | bytes 36872 | tf_op jit(solution)/shard_map/ppermute | solution.py:51
  44.6 5.9 %collective-permute-start.10 = (f32[8,128]{1,0:T(8,128)S(1)}, f32[8,128]{1,0:T(8,128)S(1)}, u32[]{:S(2)}, u32[]{:S(2)}) collective-permute-start(f32[8,128]{1,0:T(8,128)S(1)} %get-tuple-element.57), channel_id=1, source_target_pairs={{1,2},{2,1},{3,4},{4,3},{5,6},{6,5},{9,10},{10,9},{11,12},{12,11},... | collective-permute-start | bytes 12296 | tf_op jit(solution)/shard_map/ppermute | solution.py:51
  47.3 4.6 %collective-permute-start.11 = (f32[8,128]{1,0:T(8,128)S(1)}, f32[8,128]{1,0:T(8,128)S(1)}, u32[]{:S(2)}, u32[]{:S(2)}) collective-permute-start(f32[8,128]{1,0:T(8,128)S(1)} %get-tuple-element.58), channel_id=1, source_target_pairs={{0,1},{1,0},{2,3},{3,2},{4,5},{5,4},{6,7},{7,6},{8,9},{9,8},{10,11... | collective-permute-start | bytes 12296 | tf_op jit(solution)/shard_map/ppermute | solution.py:51
  52.9 16.1 %collective-permute-start.12 = (f32[24,512]{1,0:T(8,128)S(1)}, f32[24,512]{1,0:T(8,128)S(1)}, u32[]{:S(2)}, u32[]{:S(2)}) collective-permute-start(f32[24,512]{1,0:T(8,128)S(1)} %get-tuple-element.64), channel_id=1, source_target_pairs={{8,16},{16,8},{24,32},{32,24},{40,48},{48,40},{56,64},{64,56},{72,... | collective-permute-start | bytes 147464 | tf_op jit(solution)/shard_map/ppermute | solution.py:51
  56.6 12.4 %collective-permute-start.13 = (f32[24,512]{1,0:T(8,128)S(1)}, f32[24,512]{1,0:T(8,128)S(1)}, u32[]{:S(2)}, u32[]{:S(2)}) collective-permute-start(f32[24,512]{1,0:T(8,128)S(1)} %get-tuple-element.65), channel_id=1, source_target_pairs={{1,2},{2,1},{3,4},{4,3},{5,6},{6,5},{9,10},{10,9},{11,12},{12,11},... | collective-permute-start | bytes 147464 | tf_op jit(solution)/shard_map/ppermute | solution.py:51
  59.8 9.2 %collective-permute-start.14 = (f32[24,512]{1,0:T(8,128)S(1)}, f32[24,512]{1,0:T(8,128)S(1)}, u32[]{:S(2)}, u32[]{:S(2)}) collective-permute-start(f32[24,512]{1,0:T(8,128)S(1)} %get-tuple-element.66), channel_id=1, source_target_pairs={{0,1},{1,0},{2,3},{3,2},{4,5},{5,4},{6,7},{7,6},{8,9},{9,8},{10,11... | collective-permute-start | bytes 147464 | tf_op jit(solution)/shard_map/ppermute | solution.py:51
  62.8 6.2 %collective-permute-start.15 = (f32[24,512]{1,0:T(8,128)S(1)}, f32[24,512]{1,0:T(8,128)S(1)}, u32[]{:S(2)}, u32[]{:S(2)}) collective-permute-start(f32[24,512]{1,0:T(8,128)S(1)} %get-tuple-element.67), channel_id=1, source_target_pairs={{0,8},{8,0},{16,24},{24,16},{32,40},{40,32},{48,56},{56,48},{64,72... | collective-permute-start | bytes 147464 | tf_op jit(solution)/shard_map/ppermute | solution.py:51

commit v2 on v1

v2 whole, which is shorter than its diff:
```python
import jax
import jax.numpy as jnp
from jax import lax
from jax.experimental import pallas as pl
from jax.experimental.pallas import tpu as pltpu
from jax.sharding import PartitionSpec as P

CX = 16
CY = 32
BLOCK = 64
NMAT = 8
MCAP = 16
LANES = 128
SUB = 8
ROWS = 160
HALO = 24
TOP = CX * SUB
MSG = MCAP + SUB
DEPTHS = CX + 3
PACK = 96
NEAR = 16
SLOT = PACK + NEAR
CROSS_MSG = SUB + 2 * MCAP
SPAN = 3 * CY + 3

TIME_STEP = 0.2
MASS_FLOOR = 0.25
VOLUME = 1.0 / BLOCK
VMEM_LIMIT = 12 * 1024 * 1024

IN_VMEM = pl.BlockSpec(memory_space=pltpu.VMEM)
IN_HBM = pl.BlockSpec(memory_space=pltpu.HBM)
F32 = jnp.float32
BF16 = jnp.bfloat16
NN = (((1,), (0,)), ((), ()))
NT = (((1,), (1,)), ((), ()))


def call(kernel, outs, scratch, in_specs, *operands, out_specs=None, aliases=None):
    return pl.pallas_call(
        kernel,
        out_shape=tuple(jax.ShapeDtypeStruct(shape, dtype) for shape, dtype in outs),
        in_specs=in_specs,
        out_specs=out_specs or tuple(IN_VMEM for _ in outs),
        scratch_shapes=scratch,
        input_output_aliases=aliases or {},
        compiler_params=pltpu.CompilerParams(vmem_limit_bytes=VMEM_LIMIT),
        cost_estimate=pl.CostEstimate(flops=1 << 22, bytes_accessed=1 << 19, transcendentals=0),
    )(*operands)


def swap(value, axis, first):
    count = lax.axis_size(axis)
    pairs = []
    for low in range(first, count - 1, 2):
        pairs += [(low, low + 1), (low + 1, low)]
    return lax.ppermute(value, axis, pairs)


def iota(shape, dim):
    return lax.broadcasted_iota(jnp.int32, shape, dim)


def thirds(value):
    high = value.astype(BF16)
    rest = value - high.astype(F32)
    middle = rest.astype(BF16)
    low = (rest - middle.astype(F32)).astype(BF16)
    return (high, middle, low)


def product(parts, onehot, dims):
    total = None
    for part in parts:
        term = lax.dot_general(part, onehot, dims, preferred_element_type=F32)
        total = term if total is None else total + term
    return total


def stencil(u):
    p = jnp.maximum(0.25 - u, 0.0)
    q = jnp.maximum(u - 0.75, 0.0)
    p2 = p * p
    q2 = q * q
    weight = (p2, (1.0 - u) - 2.0 * p2 + q2, u + p2 - 2.0 * q2, q2)
    slope = (-2.0 * p, 4.0 * p + 2.0 * q - 1.0, 1.0 - 2.0 * p - 4.0 * q, 2.0 * q)
    return (weight, slope)


def by_material(materials, tables_ref, which):
    value = jnp.zeros(materials.shape, F32)
    for index in range(NMAT):
        row = which * NMAT + index
        value = jnp.where(materials == index, tables_ref[row : row + 1, :], value)
    return value


def column_onehot(column_of):
    first = jnp.broadcast_to(column_of, (LANES, LANES))
    column = iota((LANES, LANES), 0)
    return [(column == first + b).astype(F32).astype(BF16) for b in range(4)]


def row_masks(depth_of):
    depth = jnp.broadcast_to(depth_of, (SUB, LANES))
    return [depth == index for index in range(CX)]


def node_terms(load, chunks, rho, alive):
    sub = iota((SUB, LANES), 0)
    scale = jnp.where(sub < 3, jnp.broadcast_to(rho * VOLUME, (SUB, LANES)), -VOLUME)
    scale = jnp.where((sub < 5) & jnp.broadcast_to(alive, (SUB, LANES)), scale, 0.0)
    stencils = [(stencil(load(0, k)), stencil(load(1, k))) for k in range(chunks)]
    terms = [[None] * 4 for _ in range(4)]
    for b in range(4):
        acc = [[None] * 5 for _ in range(4)]
        for k in range(chunks):
            (weight_x, slope_x), (weight_y, slope_y) = stencils[k]
            wy, dy = weight_y[b], slope_y[b]
            sxy = load(6, k)
            y1 = wy * load(2, k)
            y2 = wy * load(3, k)
            y3 = wy * load(4, k)
            y4 = wy * sxy
            y5 = dy * sxy
            y6 = dy * load(5, k)
            for a in range(4):
                wx, dx = weight_x[a], slope_x[a]
                new = (wx * wy, wx * y1, wx * y2, dx * y3 + wx * y5, dx * y4 + wx * y6)
                acc[a] = [n if o is None else o + n for o, n in zip(acc[a], new)]
        for a in range(4):
            packed = jnp.zeros((SUB, LANES), F32)
            for q in range(5):
                total = jnp.sum(acc[a][q], axis=0, keepdims=True)
                packed = jnp.where(sub == q, jnp.broadcast_to(total, (SUB, LANES)), packed)
            terms[a][b] = packed * scale
    return terms


def spread_rows(terms, masks, left_ref):
    zero = jnp.zeros((SUB, LANES), F32)
    for b in range(4):
        for x in range(ROWS // SUB):
            total = zero
            for a in range(4):
                if 0 <= x - a < CX:
                    total = total + jnp.where(masks[x - a], terms[a][b], zero)
            left_ref[x * SUB : (x + 1) * SUB, b * LANES : (b + 1) * LANES] = total


def parity(axis):
    return (lax.axis_index(axis) & 1) == 1


def emit_sums(left_ref, onehots, more_ref, sums_ref, inner_ref, outer_ref):
    sums = product(thirds(left_ref[...]), jnp.concatenate(onehots, axis=1), NT)
    if more_ref is not None:
        sums = sums + more_ref[...]
    sums_ref[...] = sums
    odd = parity("gx")
    bottom, top = (sums[0:HALO], sums[TOP : TOP + HALO])
    inner_ref[...] = jnp.where(odd, bottom, top)
    outer_ref[...] = jnp.where(odd, top, bottom)


def turn(points_ref, turned_ref):
    turned_ref[...] = points_ref[...].T


def sums_one(
    turned_ref, cells_ref, mats_ref, density_ref, shear_ref, lame_ref,
    sums_ref, inner_ref, outer_ref, tables_ref, meta_ref,
    left_ref,
):
    for which, table_ref in enumerate((density_ref, shear_ref, lame_ref)):
        table = table_ref[...]
        for index in range(NMAT):
            row = which * NMAT + index
            tables_ref[row : row + 1, :] = jnp.broadcast_to(table[:, index : index + 1], (1, LANES))
    cells, materials = (cells_ref[...], mats_ref[...])
    meta_ref[0:1, :] = cells
    meta_ref[1:2, :] = materials
    rho = by_material(materials, tables_ref, 0)
    load = lambda c, k: turned_ref[c * BLOCK + k * SUB : c * BLOCK + (k + 1) * SUB, :]
    terms = node_terms(load, BLOCK // SUB, rho, materials >= 0)
    spread_rows(terms, row_masks(cells >> 5), left_ref)
    emit_sums(left_ref, column_onehot(cells & (CY - 1)), None, sums_ref, inner_ref, outer_ref)


def join_lists(*refs):
    *list_refs, lists_ref = refs
    for index, ref in enumerate(list_refs):
        row = ref[...]
        rest = jnp.full((1, LANES - row.shape[1]), -1, jnp.int32)
        lists_ref[index : index + 1, :] = jnp.concatenate([row, rest], axis=1)


def by_side(inner, outer, odd):
    return (jnp.where(odd, inner, outer), jnp.where(odd, outer, inner))


def matches(dests, targets):
    dest = jnp.broadcast_to(dests, (2 * SUB, LANES))
    sub = iota(dest.shape, 0)
    matched = jnp.zeros(dest.shape, F32)
    for o, target in enumerate(targets):
        matched = jnp.where((sub == o) & (dest == target), 1.0, matched)
    square = (LANES, LANES)
    earlier = (iota(square, 0) < iota(square, 1)).astype(F32).astype(BF16)
    rank = lax.dot_general(matched.astype(BF16), earlier, NN, preferred_element_type=F32)
    return (matched, rank)


def placing_rows(matched, rank, groups):
    blank = jnp.zeros((MCAP, LANES), F32)
    place = iota((MCAP, LANES), 0).astype(F32)
    rows = []
    for o in groups:
        if o is None:
            rows.append(blank)
            continue
        hit = jnp.broadcast_to(rank[o : o + 1], blank.shape) == place
        rows.append(jnp.where(hit, jnp.broadcast_to(matched[o : o + 1], blank.shape), 0.0))
    rows += [blank] * (LANES // MCAP - len(groups))
    return jnp.concatenate(rows, axis=0).astype(BF16)


def holding(slots):
    square = (LANES, LANES)
    return (iota(square, 0) == jnp.broadcast_to(slots, square)).astype(F32).astype(BF16)


def small_rows(*rows):
    sub = iota((2 * SUB, LANES), 0)
    value = jnp.zeros((2 * SUB, LANES), F32)
    for index, row in enumerate(rows):
        value = jnp.where(sub == index, jnp.broadcast_to(row.astype(F32), value.shape), value)
    return value.astype(BF16)


def turned_to(small, onehot):
    return lax.dot_general(small, onehot, NT, preferred_element_type=F32)


def tag_tile(*rows):
    sub = iota((SUB, LANES), 0)
    tile = jnp.zeros((SUB, LANES), F32)
    for index, row in enumerate(rows):
        tile = jnp.where(sub == index, jnp.broadcast_to(row, tile.shape), tile)
    return tile


def home_and_steps():
    across = lax.axis_size("gy")
    gx, gy = (lax.axis_index("gx"), lax.axis_index("gy"))
    return (gx * across + gy, across - 2 * across * (gx & 1), 1 - 2 * (gy & 1))


def pick_cross(points_ref, meta_ref, lists_ref, rows_ref, tags_ref, chosen_ref):
    home, _, step_y = home_and_steps()
    chosen = places = None
    for first, groups in ((0, (0, None, 1, None)), (3, (None, 0, None, 1))):
        matched, rank = matches(lists_ref[first + 1 : first + 2, :], (home + step_y, home - step_y))
        placing = placing_rows(matched, rank, groups)
        part = turned_to(placing, holding(lists_ref[first : first + 1, :]))
        cell = lists_ref[first + 2 : first + 3, :]
        place = turned_to(small_rows(cell >> 5, cell & (CY - 1)), placing)
        chosen = part if chosen is None else chosen + part
        places = place if places is None else places + place
    chosen_ref[...] = chosen
    onehot = chosen.astype(BF16)
    cells, materials = (meta_ref[0:1, :], meta_ref[1:2, :])
    found = turned_to(small_rows(materials + 1, cells >> 5, cells & (CY - 1)), onehot)
    tags_ref[...] = tag_tile(
        places[0:1] * float(CY) + places[1:2], found[0:1], found[1:2] * float(CY) + found[2:3]
    )
    total = None
    for part in thirds(points_ref[...]):
        term = lax.dot_general(onehot[0 : 4 * MCAP], part, NN, preferred_element_type=F32)
        total = term if total is None else total + term
    rows_ref[...] = total


def merge_rows(sums_ref, from_outer_ref, from_inner_ref, merged_ref):
    from_low, from_high = by_side(from_inner_ref[...], from_outer_ref[...], parity("gx"))
    merged_ref[...] = sums_ref[...]
    merged_ref[0:HALO] = sums_ref[0:HALO] + from_low
    merged_ref[TOP : TOP + HALO] = sums_ref[TOP : TOP + HALO] + from_high


def merge_one(
    sums_ref, from_outer_ref, from_inner_ref, rows_ref, tags_ref,
    merged_ref, inner_ref, outer_ref,
):
    merge_rows(sums_ref, from_outer_ref, from_inner_ref, merged_ref)
    lane = iota((SUB, LANES), 1)
    low = jnp.zeros((SUB, LANES), F32)
    high = jnp.zeros((SUB, LANES), F32)
    for x in range(DEPTHS):
        row = merged_ref[x * SUB : (x + 1) * SUB, :]
        here = (lane >= 3 * x) & (lane < 3 * x + 3)
        shift = 3 * x
        low = jnp.where(here, pltpu.roll(row, shift, 1) if shift else row, low)
        high = jnp.where(here, pltpu.roll(row, (shift - CY) % LANES, 1), high)
    to_inner, to_outer = by_side(low, high, parity("gy"))
    movers = 2 * MCAP
    tags = tags_ref[...]
    for ref, halo, tag, first in (
        (inner_ref, to_inner, tags, 0),
        (outer_ref, to_outer, pltpu.roll(tags, LANES - movers, 1), movers),
    ):
        ref[0:SUB, 0:LANES] = halo
        ref[0:SUB, LANES : 2 * LANES] = jnp.where(lane < movers, tag, 0.0)
        ref[0:SUB, 2 * LANES :] = jnp.zeros((SUB, 8 * BLOCK - 2 * LANES), F32)
        ref[SUB:CROSS_MSG, :] = rows_ref[first : first + movers, :]


def merge_two(sums_ref, from_outer_ref, from_inner_ref, near_ref, slots_ref, merged_ref, slot_ref):
    merge_rows(sums_ref, from_outer_ref, from_inner_ref, merged_ref)
    slot_ref[PACK - SUB : PACK, :] = jnp.zeros((SUB, LANES), F32)
    for x in range(DEPTHS):
        slot_ref[5 * x : 5 * x + 5, :] = merged_ref[x * SUB : x * SUB + 5, :]
    slot_ref[PACK:SLOT, :] = near_ref[...]
    value = slot_ref[...]
    for index in range(slots_ref.shape[0]):
        slots_ref[index] = value


def put_velocity(row, x, node_y, velocity_ref):
    node_x = lax.axis_index("gx") * CX - 1 + x
    inside_x = (node_x > 0) & (node_x < CX * lax.axis_size("gx") - 1)
    inside_y = (node_y > 0) & (node_y < CY * lax.axis_size("gy") - 1)
    mass = jnp.maximum(jnp.broadcast_to(row[0:1], (SUB, LANES)), MASS_FLOOR)
    value = (row + TIME_STEP * pltpu.roll(row, SUB - 2, 0)) / mass
    velocity_ref[x * SUB : (x + 1) * SUB, :] = jnp.where(inside_y & inside_x, value, 0.0)


def velocity_one(merged_ref, from_inner, from_outer, velocity_ref):
    low, high = by_side(from_inner, from_outer, parity("gy"))
    lane = iota((SUB, LANES), 1)
    node_y = lax.axis_index("gy") * CY - 1 + lane
    for x in range(DEPTHS):
        row = merged_ref[x * SUB : (x + 1) * SUB, :]
        shift = 3 * x
        row = row + jnp.where(lane < 3, pltpu.roll(low, LANES - shift, 1) if shift else low, 0.0)
        row = row + jnp.where(
            (lane >= CY) & (lane < CY + 3), pltpu.roll(high, (CY - shift) % LANES, 1), 0.0
        )
        put_velocity(row, x, node_y, velocity_ref)
    velocity_ref[DEPTHS * SUB :, :] = jnp.zeros((ROWS - DEPTHS * SUB, LANES), F32)


def velocity_two(slots_ref, packed_ref, velocity_ref):
    gy = lax.axis_index("gy")
    lane = iota((PACK, LANES), 1)
    total = jnp.zeros((PACK, LANES), F32)
    for index in range(slots_ref.shape[0]):
        shift = CY * (index - gy)
        moved = pltpu.roll(slots_ref[index, 0:PACK, :], shift & (LANES - 1), 1)
        valid = (lane >= shift) & (lane < SPAN + shift) & (lane < SPAN)
        total = total + jnp.where(valid, moved, 0.0)
    packed_ref[0:PACK, :] = total
    packed_ref[PACK:, :] = jnp.zeros((packed_ref.shape[0] - PACK, LANES), F32)
    node_y = (gy - 1) * CY - 1 + iota((SUB, LANES), 1)
    for x in range(DEPTHS):
        put_velocity(packed_ref[5 * x : 5 * x + SUB, :], x, node_y, velocity_ref)
    velocity_ref[DEPTHS * SUB :, :] = jnp.zeros((ROWS - DEPTHS * SUB, LANES), F32)


def gathered(velocity_parts, depth_of, column_of):
    masks = row_masks(depth_of)
    near = [[None] * 4 for _ in range(4)]
    for b, onehot in enumerate(column_onehot(column_of)):
        column = product(velocity_parts, onehot, NN)
        for a in range(4):
            total = jnp.zeros((SUB, LANES), F32)
            for x in range(CX):
                total = jnp.where(masks[x], column[(x + a) * SUB : (x + a + 1) * SUB], total)
            near[a][b] = total
    return near


def move_points(load, store, chunks, node_of, materials, tables_ref):
    wide = lambda row: jnp.broadcast_to(row, (SUB, LANES))
    twice_shear = wide(2.0 * by_material(materials, tables_ref, 1))
    lame = wide(by_material(materials, tables_ref, 2))
    alive = wide(materials) >= 0
    for k in range(chunks):
        u, v = (load(0, k), load(1, k))
        weight_x, slope_x = stencil(u)
        weight_y, slope_y = stencil(v)
        speed, along, across = ([], [], [])
        for component in range(2):
            value = rate_x = rate_y = None
            for a in range(4):
                inner = slant = None
                for b in range(4):
                    node = wide(node_of(a, b, component))
                    term, tilt = (weight_y[b] * node, slope_y[b] * node)
                    inner = term if b == 0 else inner + term
                    slant = tilt if b == 0 else slant + tilt
                add = (weight_x[a] * inner, slope_x[a] * inner, weight_x[a] * slant)
                if a == 0:
                    value, rate_x, rate_y = add
                else:
                    value, rate_x, rate_y = (value + add[0], rate_x + add[1], rate_y + add[2])
            speed.append(value)
            along.append(rate_x)
            across.append(rate_y)
        rate_xx, rate_yy = (along[0], across[1])
        rate_xy = 0.5 * (across[0] + along[1])
        spherical = lame * (rate_xx + rate_yy)
        stress_xx = load(4, k) + TIME_STEP * (twice_shear * rate_xx + spherical)
        stress_yy = load(5, k) + TIME_STEP * (twice_shear * rate_yy + spherical)
        stress_xy = load(6, k) + TIME_STEP * twice_shear * rate_xy
        fresh = (
            jnp.clip(u + TIME_STEP * speed[0], 0.0, 1.0),
            jnp.clip(v + TIME_STEP * speed[1], 0.0, 1.0),
            speed[0],
            speed[1],
            stress_xx,
            stress_yy,
            stress_xy,
            jnp.maximum(load(7, k), -0.5 * (stress_xx + stress_yy)),
        )
        for c in range(8):
            store(c, k, jnp.where(alive, fresh[c], 0.0))


def node_getter(near):
    return lambda a, b, component: near[a][b][component + 1 : component + 2]


def emit_movers(fresh, materials, lists, far_ref, near_ref):
    home, step_x, _ = home_and_steps()
    slots, dests, cell = (lists[0:1], lists[1:2], lists[2:3])
    matched, rank = matches(dests, (home - step_x, home + step_x))
    placing = placing_rows(matched, rank, (0, 1))
    chosen = turned_to(placing, holding(slots)).astype(BF16)
    places = turned_to(small_rows(cell >> 5, cell & (CY - 1)), placing)
    kinds = turned_to(small_rows(materials + 1), chosen)
    tags = tag_tile(places[0:1] * float(CY) + places[1:2], kinds[0:1])
    total = None
    for part in thirds(fresh):
        term = lax.dot_general(chosen[0 : 2 * MCAP], part, NN, preferred_element_type=F32)
        total = term if total is None else total + term
    lane = iota((SUB, LANES), 1)
    for o, ref in enumerate((far_ref, near_ref)):
        ref[0:MCAP, :] = total[o * MCAP : (o + 1) * MCAP]
        tag = pltpu.roll(tags, LANES - o * MCAP, 1) if o else tags
        ref[MCAP:MSG, 0:LANES] = jnp.where(lane < MCAP, tag, 0.0)
        ref[MCAP:MSG, LANES:] = jnp.zeros((SUB, 8 * BLOCK - LANES), F32)


def departures(cells, materials, lists):
    home, _, _ = home_and_steps()
    slots, dests, cell = (lists[0:1], lists[1:2], lists[2:3])
    moving = (dests >= 0) & (dests != home)
    low, high = (dests == home - 1, dests == home + 1)
    cross = jnp.where(low | high, 1, 0)
    column = (cell & (CY - 1)) + jnp.where(high, 2 * CY, 0)
    entries = small_rows(jnp.where(moving, 1, 0), cross, cross * (cell >> 5), cross * column)
    found = turned_to(entries, holding(slots)).astype(jnp.int32)
    gone, across = (found[0:1] > 0, found[1:2] > 0)
    sub = iota((SUB, LANES), 0)
    wide = lambda value: jnp.broadcast_to(value, (SUB, LANES))
    kept = jnp.where(
        sub == 0,
        wide(jnp.where(gone, 0, cells)),
        wide(jnp.where(gone, -1, materials)),
    )
    target = jnp.where(
        sub == 0,
        wide(jnp.where(across, found[2:3], cells >> 5)),
        jnp.where(
            sub == 1,
            wide(jnp.where(across, found[3:4], (cells & (CY - 1)) + CY)),
            wide(jnp.where(gone & ~across, -1, materials)),
        ),
    )
    return (kept, target)


def rows_at(ref, c, k, stride):
    return ref[c * stride + k * SUB : c * stride + (k + 1) * SUB, :]


def advance_one(
    turned_ref, meta_ref, lists_ref, merged_ref, yo_ref, yi_ref, tables_ref, chosen_ref,
    fresh_ref, kept_meta_ref, target_ref, near_ref, far_message_ref, near_message_ref,
    velocity_ref, nodes_ref,
):
    velocity_one(merged_ref, yi_ref[0:SUB, 0:LANES], yo_ref[0:SUB, 0:LANES], velocity_ref)
    cells, materials = (meta_ref[0:1, :], meta_ref[1:2, :])

    def store(c, k, value):
        fresh_ref[c * BLOCK + k * SUB : c * BLOCK + (k + 1) * SUB, :] = value

    near = gathered(thirds(velocity_ref[...]), cells >> 5, cells & (CY - 1))
    load = lambda c, k: rows_at(turned_ref, c, k, BLOCK)
    move_points(load, store, BLOCK // SUB, node_getter(near), materials, tables_ref)
    emit_movers(fresh_ref[...].T, materials, lists_ref[0:3, :], far_message_ref, near_message_ref)
    kept, target = departures(cells, materials, lists_ref[0:3, :])
    kept_meta_ref[...] = kept
    target_ref[...] = target
    for a in range(4):
        for b in range(4):
            row = 2 * (4 * a + b)
            nodes_ref[row : row + 2, :] = near[a][b][1:3]
    nodes = product(thirds(nodes_ref[...]), chosen_ref[...].astype(BF16), NT)
    near_ref[...] = nodes[0:NEAR] + pltpu.roll(nodes[NEAR:], LANES // 2, 1)


def sums_kept(fresh_ref, target_ref, tables_ref, sums_ref, left_ref):
    depth, column, materials = (target_ref[0:1, :], target_ref[1:2, :], target_ref[2:3, :])
    load = lambda c, k: rows_at(fresh_ref, c, k, BLOCK)
    rho = by_material(materials, tables_ref, 0)
    terms = node_terms(load, BLOCK // SUB, rho, materials >= 0)
    spread_rows(terms, row_masks(depth), left_ref)
    sums_ref[...] = product(thirds(left_ref[...]), jnp.concatenate(column_onehot(column), axis=1), NT)


def packed_blocks(rows, wide_ref, turned_ref):
    count = rows.shape[0]
    fill = jnp.zeros((LANES - count, rows.shape[1]), F32)
    wide_ref[...] = jnp.concatenate([rows, fill], axis=0).T
    stride = BLOCK * count // LANES
    for c in range(8):
        total = wide_ref[c * BLOCK : c * BLOCK + stride, :]
        for group in range(1, LANES // count):
            start = c * BLOCK + group * stride
            total = total + pltpu.roll(wide_ref[start : start + stride, :], count * group, 1)
        turned_ref[c * stride : (c + 1) * stride, :] = total


def unpacked_blocks(turned_ref, count, wide_ref):
    stride = BLOCK * count // LANES
    for c in range(8):
        value = turned_ref[c * stride : (c + 1) * stride, :]
        for group in range(LANES // count):
            start = c * BLOCK + group * stride
            shift = (LANES - count * group) % LANES
            wide_ref[start : start + stride, :] = pltpu.roll(value, shift, 1) if shift else value
    return wide_ref[...].T[0:count]


def repeated(tile, count):
    while count < LANES:
        tile = tile + pltpu.roll(tile, count, 1)
        count *= 2
    return tile


def arrived_tags(from_inner, from_outer):
    low, high = by_side(from_inner, from_outer, parity("gx"))
    packed = repeated(low + pltpu.roll(high, MCAP, 1), 2 * MCAP)
    return packed.astype(jnp.int32) - (iota((SUB, LANES), 0) == 1).astype(jnp.int32)


def sums_two(
    kept_sums_ref, xo_ref, xi_ref, tables_ref,
    sums_ref, inner_ref, outer_ref, turned_ref, new_meta_ref,
    left_ref, wide_ref,
):
    new_meta = arrived_tags(xi_ref[MCAP:MSG, 0:LANES], xo_ref[MCAP:MSG, 0:LANES])
    new_meta_ref[...] = new_meta
    low, high = by_side(xi_ref[0:MCAP, :], xo_ref[0:MCAP, :], parity("gx"))
    packed_blocks(jnp.concatenate([low, high], axis=0), wide_ref, turned_ref)
    cells, materials = (new_meta[0:1], new_meta[1:2])
    stride = turned_ref.shape[0] // 8
    load = lambda c, k: rows_at(turned_ref, c, k, stride)
    rho = by_material(materials, tables_ref, 0)
    terms = node_terms(load, stride // SUB, rho, materials >= 0)
    spread_rows(terms, row_masks(cells >> 5), left_ref)
    onehots = column_onehot((cells & (CY - 1)) + CY)
    emit_sums(left_ref, onehots, kept_sums_ref, sums_ref, inner_ref, outer_ref)


def advance_two(
    kept_ref, meta_ref, lists_ref, slots_ref, tables_ref,
    fresh_ref, old_meta_ref, velocity_ref, far_message_ref, near_message_ref,
    packed_ref,
):
    velocity_two(slots_ref, packed_ref, velocity_ref)
    cells, materials = (meta_ref[0:1, :], meta_ref[1:2, :])

    def store(c, k, value):
        fresh_ref[c * BLOCK + k * SUB : c * BLOCK + (k + 1) * SUB, :] = value

    near = gathered(thirds(velocity_ref[...]), cells >> 5, (cells & (CY - 1)) + CY)
    load = lambda c, k: rows_at(kept_ref, c, k, BLOCK)
    move_points(load, store, BLOCK // SUB, node_getter(near), materials, tables_ref)
    emit_movers(fresh_ref[...].T, materials, lists_ref[3:6, :], far_message_ref, near_message_ref)
    kept, _ = departures(cells, materials, lists_ref[3:6, :])
    old_meta_ref[...] = kept


def settle(
    fresh_ref, old_meta_ref, velocity_ref, turned_ref, new_meta_ref, tables_ref, slots_ref, yo_ref, yi_ref,
    points_ref, tail_ref,
    old_ref, wide_ref, new_ref, cross_ref, middle_ref, out_ref, small_ref, last_ref, sems,
):
    alive = jnp.broadcast_to(old_meta_ref[1:2, :], fresh_ref.shape) >= 0
    old_ref[...] = jnp.where(alive, fresh_ref[...], 0.0).T
    old = LANES
    copies = [pltpu.make_async_copy(old_ref, points_ref.at[0:old], sems.at[0])]
    copies[0].start()
    parts = thirds(velocity_ref[...])

    stride = turned_ref.shape[0] // 8
    cells, materials = (new_meta_ref[0:1, :], new_meta_ref[1:2, :])

    def store_small(c, k, value):
        small_ref[c * stride + k * SUB : c * stride + (k + 1) * SUB, :] = value

    load = lambda c, k: rows_at(turned_ref, c, k, stride)
    near = gathered(parts, cells >> 5, (cells & (CY - 1)) + CY)
    move_points(load, store_small, stride // SUB, node_getter(near), materials, tables_ref)
    new_ref[...] = unpacked_blocks(small_ref, 2 * MCAP, wide_ref)
    copies.append(pltpu.make_async_copy(new_ref, points_ref.at[old : old + 2 * MCAP], sems.at[1]))
    copies[1].start()

    gy = lax.axis_index("gy")
    odd = parity("gy")
    low, high = by_side(yi_ref[...], yo_ref[...], odd)
    lane = iota((SUB, LANES), 1)
    tags = low[0:SUB, LANES : 2 * LANES] + pltpu.roll(high[0:SUB, LANES : 2 * LANES], 2 * MCAP, 1)
    tail = jnp.zeros((SUB, LANES), F32)
    for start, shift in ((32, 32), (48, 16), (96, 80), (112, 64)):
        tail = jnp.where((lane >= start) & (lane < start + MCAP), pltpu.roll(tags, shift, 1), tail)
    materials_row = (iota((SUB, LANES), 0) == 1).astype(jnp.int32)
    tail = tail.astype(jnp.int32) - materials_row
    tail_ref[...] = jnp.where(lane < 2 * MCAP, new_meta_ref[...], tail)
    tags = repeated(tags, 4 * MCAP).astype(jnp.int32) - materials_row

    last = slots_ref.shape[0] - 1
    below = slots_ref[jnp.maximum(gy - 1, 0), PACK:SLOT, :]
    above = slots_ref[jnp.minimum(gy + 1, last), PACK:SLOT, :]
    below = jnp.where(odd, below, pltpu.roll(below, LANES - 2 * MCAP, 1))
    above = jnp.where(odd, above, pltpu.roll(above, 2 * MCAP, 1))
    many = iota((NEAR, LANES), 1)
    nodes = jnp.where((many & (4 * MCAP - 1)) < 2 * MCAP, below, above)
    turned_nodes = pltpu.roll(nodes, LANES // 2, 1)
    halves = (jnp.where(many < LANES // 2, nodes, turned_nodes), jnp.where(many < LANES // 2, turned_nodes, nodes))

    def node_of(a, b, component):
        row = 2 * (4 * a + b) + component
        return halves[row // NEAR][row % NEAR : row % NEAR + 1]

    packed_blocks(jnp.concatenate([low[SUB:], high[SUB:]], axis=0), wide_ref, cross_ref)
    half = cross_ref.shape[0] // 8
    kinds = tags[1:2]

    def store_middle(c, k, value):
        middle_ref[c * half + k * SUB : c * half + (k + 1) * SUB, :] = value

    move_points(lambda c, k: rows_at(cross_ref, c, k, half), store_middle, half // SUB, node_of, kinds, tables_ref)
    row_lane = lane[0:1]
    second = (row_lane & MCAP) != 0
    cell = jnp.where(second, tags[2:3], tags[0:1])
    side = jnp.where((row_lane & (2 * MCAP)) != 0, 2 * CY, 0)
    near = gathered(parts, cell >> 5, (cell & (CY - 1)) + jnp.where(second, side, CY))

    def store_out(c, k, value):
        out_ref[c * half + k * SUB : c * half + (k + 1) * SUB, :] = value

    move_points(
        lambda c, k: rows_at(middle_ref, c, k, half), store_out, half // SUB, node_getter(near), kinds, tables_ref
    )
    last_ref[...] = unpacked_blocks(out_ref, 4 * MCAP, wide_ref)
    region = lambda index: points_ref.at[old + index * MCAP : old + (index + 1) * MCAP]
    for group, index in enumerate((2, 6, 3, 7)):
        source = last_ref.at[group * MCAP : (group + 1) * MCAP]
        copies.append(pltpu.make_async_copy(source, region(index), sems.at[2 + group]))
        copies[-1].start()
    for copy in copies:
        copy.wait()


def assemble(
    part_ref, old_meta_ref, tail_ref, xo_ref, xi_ref,
    points_ref, cells_ref, mats_ref,
    tags_ref, sems,
):
    del part_ref
    base = points_ref.shape[0] - 4 * MCAP
    odd = lax.axis_index("gx") & 1
    copies = []
    for index, (ref, region) in enumerate(((xo_ref, odd), (xi_ref, 1 - odd))):
        start = pl.multiple_of(base + region * MCAP, MCAP)
        copies.append(
            pltpu.make_async_copy(ref.at[0:MCAP, :], points_ref.at[pl.ds(start, MCAP), :], sems.at[index])
        )
        copies[-1].start()
    arrived = arrived_tags(xi_ref[MCAP:MSG, 0:LANES], xo_ref[MCAP:MSG, 0:LANES])
    lane = iota((1, LANES), 1)
    here = (lane >= 4 * MCAP) & (lane < 6 * MCAP)
    for row, ref in ((0, cells_ref), (1, mats_ref)):
        tags_ref[row, 0:1, :] = old_meta_ref[row : row + 1, :]
        tags_ref[row, 1:2, :] = jnp.where(here, arrived[row : row + 1], tail_ref[row : row + 1, :])
        copies.append(pltpu.make_async_copy(tags_ref.at[row], ref, sems.at[2 + row]))
        copies[-1].start()
    for copy in copies:
        copy.wait()


def shards(
    points,
    block_cell,
    block_mat,
    density,
    shear_modulus,
    lame_modulus,
    mig_slot_a,
    mig_dest_a,
    mig_cell_a,
    mig_slot_b,
    mig_dest_b,
    mig_cell_b,
):
    wide = 8 * BLOCK
    I32 = jnp.int32
    row = lambda value: value.reshape(1, -1)
    cells, mats = (row(block_cell), row(block_mat))
    list_a = (row(mig_slot_a), row(mig_dest_a), row(mig_cell_a))
    list_b = (row(mig_slot_b), row(mig_dest_b), row(mig_cell_b))

    halo = ((HALO, LANES), F32)
    tile = ((SUB, LANES), F32)
    tags = ((SUB, LANES), I32)
    grid = ((ROWS, LANES), F32)
    message = ((MSG, wide), F32)
    cross_message = ((CROSS_MSG, wide), F32)
    turned_form = ((wide, LANES), F32)
    half_form = ((wide // 2, LANES), F32)
    quarter_form = ((wide // 4, LANES), F32)
    near_form = ((NEAR, LANES), F32)
    slots_form = ((lax.axis_size("gy"), SLOT, LANES), F32)
    scratch = lambda form: pltpu.VMEM(*form)
    left = pltpu.VMEM((ROWS, 4 * LANES), F32)

    def along_depth(far, near):
        return (swap(far, "gx", 1), swap(near, "gx", 0))

    (lists,) = call(join_lists, (tags,), (), (IN_VMEM,) * 6, *list_a, *list_b)
    (turned,) = call(turn, (turned_form,), (), (IN_VMEM,), points)
    sums, inner, outer, tables, meta = call(
        sums_one,
        (grid, halo, halo, ((3 * NMAT, LANES), F32), tags),
        (left,),
        (IN_VMEM,) * 6,
        turned, cells, mats, row(density), row(shear_modulus), row(lame_modulus),
    )
    picked, picked_tags, chosen = call(
        pick_cross,
        (((4 * MCAP, wide), F32), tile, ((LANES, LANES), F32)),
        (),
        (IN_VMEM,) * 3,
        points, meta, lists,
    )
    merged, inner, outer = call(
        merge_one,
        (grid, cross_message, cross_message),
        (),
        (IN_VMEM,) * 5,
        sums, *along_depth(outer, inner), picked, picked_tags,
    )
    cross_far, cross_near = (swap(outer, "gy", 1), swap(inner, "gy", 0))
    fresh, kept_meta, target, near_nodes, far, near = call(
        advance_one,
        (turned_form, tags, tags, near_form, message, message),
        (scratch(grid), pltpu.VMEM((2 * NEAR, LANES), F32)),
        (IN_VMEM,) * 8,
        turned, meta, lists, merged, cross_far, cross_near, tables, chosen,
    )
    arrived = along_depth(far, near)
    (kept_sums,) = call(sums_kept, (grid,), (left,), (IN_VMEM,) * 3, fresh, target, tables)
    sums, inner, outer, turned, new_meta = call(
        sums_two,
        (grid, halo, halo, quarter_form, tags),
        (left, scratch(turned_form)),
        (IN_VMEM,) * 4,
        kept_sums, *arrived, tables,
    )
    (slots,) = call(
        merge_two,
        (slots_form,),
        (scratch(grid), pltpu.VMEM((SLOT, LANES), F32)),
        (IN_VMEM,) * 4,
        sums, *along_depth(outer, inner), near_nodes,
    )
    slots = lax.all_to_all(slots, "gy", 0, 0)
    fresh, old_meta, velocity, far, near = call(
        advance_two,
        (turned_form, tags, grid, message, message),
        (pltpu.VMEM((PACK + SUB, LANES), F32),),
        (IN_VMEM,) * 5,
        fresh, kept_meta, lists, slots, tables,
    )
    arrived = along_depth(far, near)
    final_form = ((2 * LANES, wide), F32)
    part, tail = call(
        settle,
        (final_form, tags),
        (
            pltpu.VMEM((LANES, wide), F32),
            scratch(turned_form),
            pltpu.VMEM((2 * MCAP, wide), F32),
            scratch(half_form),
            scratch(half_form),
            scratch(half_form),
            scratch(quarter_form),
            pltpu.VMEM((4 * MCAP, wide), F32),
            pltpu.SemaphoreType.DMA((6,)),
        ),
        (IN_VMEM,) * 9,
        fresh, old_meta, velocity, turned, new_meta, tables, slots, cross_far, cross_near,
        out_specs=(IN_HBM, IN_VMEM),
    )
    final_points, final_cells, final_mats = call(
        assemble,
        (final_form, ((2, LANES), I32), ((2, LANES), I32)),
        (pltpu.VMEM((2, 2, LANES), I32), pltpu.SemaphoreType.DMA((4,))),
        (IN_HBM,) + (IN_VMEM,) * 4,
        part, old_meta, tail, *arrived,
        out_specs=(IN_HBM,) * 3,
        aliases={0: 0},
    )
    return (final_points, final_cells.reshape(-1), final_mats.reshape(-1))


def solution(mesh):
    split = P(("gx", "gy"))
    rows = P(("gx", "gy"), None)
    return jax.shard_map(
        shards,
        mesh=mesh,
        in_specs=(rows, split, split, P(), P(), P()) + (split,) * 6,
        out_specs=(rows, split, split),
        check_vma=False,
    )
```

time: 70.4 us -> 66.1 us (0.939)
  the two profiles are of different devices: /device:TPU:389 before, /device:TPU:225 now
where the time goes in v2:
time: 66.1 us; the launch traced here: 65.7 us
  starting transfers between devices  38.6 us (58%)
  blocking collectives  13.3 us (20%)
  Pallas kernels  7.38 us (11%)
  waiting for transfers between devices  3.41 us (5%)
  local copies, waits for them, and re-layouts  2.2 us (3%)
  between operations  0.9 us (1%)
    ppermute x10, starting transfers between devices, swap(): return lax.ppermute(value, axis, pairs)  38.6 us
    all_to_all x1, blocking collectives, shards(): slots = lax.all_to_all(slots, 'gy', 0, 0)  13.3 us
    pallas_call x12, Pallas kernels, call(): pl.pallas_call(kernel, out_shape=tuple((jax.ShapeDtypeStruct(shape, dtype...  7.38 us
    ppermute x10, waiting for transfers between devices, swap(): return lax.ppermute(value, axis, pairs)  3.41 us
    unnamed x26, local copies, waits for them, and re-layouts  2.2 us
  transfers between devices with their start and end apart: 10, of which 3 were waited for; matrix products, arithmetic and copies ran while one was open for 0% of the time, Pallas kernels for 4%

profile of v2, /device:TPU:225, one launch (start us, length us, event | category | flops | bytes accessed | tf_op | source)
XLA Modules:
  0.0 65.7 jit_solution(13844890688590710580)
XLA Ops:
  0.6 0.9 %copy-done = f32[128,512]{1,0:T(8,128)S(1)} copy-done((f32[128,512]{1,0:T(8,128)S(1)}, f32[128,512]{1,0:T(8,128)}, u32[]{:S(2)}) %copy-start) | copy-done | bytes 262168
  1.6 0.1 shard_map.139.turned_ref
  1.7 0.5 copy-done.2
  2.2 0.0 copy-done.3
  2.3 0.0 copy-done.4
  2.3 0.0 copy-done.5
  2.3 0.7 %shard_map.140 = (f32[160,128]{1,0:T(8,128)S(1)}, f32[24,128]{1,0:T(8,128)S(1)}, f32[24,128]{1,0:T(8,128)S(1)}, f32[24,128]{1,0:T(8,128)S(1)}, s32[8,128]{1,0:T(8,128)S(1)}) custom-call(f32[512,128]{1,0:T(8,128)S(1)} %shard_map.139.turned_ref, s32[1,128]{1,0:T(1,128)S(1)} %bitcast.13, s32[1,128]{1,0:T(1,128)S(1)} %bitcast.14, f32[1,8]{1,0:T(1,128)S(1)} %bitcast.15, ...), custom_call_target="tpu_custom_call" | custom-call | flops 4194304 | bytes 524288 | tf_op jit(solution)/shard_map/pallas_call | solution.py:40
  3.1 5.4 %collective-permute-start = (f32[24,128]{1,0:T(8,128)S(1)}, f32[24,128]{1,0:T(8,128)S(1)}, u32[]{:S(2)}, u32[]{:S(2)}) collective-permute-start(f32[24,128]{1,0:T(8,128)S(1)} %get-tuple-element.37), channel_id=1, source_target_pairs={{8,16},{16,8},{24,32},{32,24},{40,48},{48,40},{56,64},{64,56},{72,... | collective-permute-start | bytes 36872 | tf_op jit(solution)/shard_map/ppermute | solution.py:57
  8.4 1.9 %collective-permute-start.1 = (f32[24,128]{1,0:T(8,128)S(1)}, f32[24,128]{1,0:T(8,128)S(1)}, u32[]{:S(2)}, u32[]{:S(2)}) collective-permute-start(f32[24,128]{1,0:T(8,128)S(1)} %get-tuple-element.38), channel_id=1, source_target_pairs={{0,8},{8,0},{16,24},{24,16},{32,40},{40,32},{48,56},{56,48},{64,72... | collective-permute-start | bytes 36872 | tf_op jit(solution)/shard_map/ppermute | solution.py:57
  10.4 0.6 copy-done.10
  11.1 0.5 shard_map.142
  11.7 0.1 shard_map.143
  11.8 0.7 %collective-permute-start.2 = (f32[40,512]{1,0:T(8,128)S(1)}, f32[40,512]{1,0:T(8,128)S(1)}, u32[]{:S(2)}, u32[]{:S(2)}) collective-permute-start(f32[40,512]{1,0:T(8,128)S(1)} %get-tuple-element.42), channel_id=1, source_target_pairs={{1,2},{2,1},{3,4},{4,3},{5,6},{6,5},{9,10},{10,9},{11,12},{12,11},... | collective-permute-start | bytes 245768 | tf_op jit(solution)/shard_map/ppermute | solution.py:57
  12.4 5.5 %collective-permute-start.3 = (f32[40,512]{1,0:T(8,128)S(1)}, f32[40,512]{1,0:T(8,128)S(1)}, u32[]{:S(2)}, u32[]{:S(2)}) collective-permute-start(f32[40,512]{1,0:T(8,128)S(1)} %get-tuple-element.43), channel_id=1, source_target_pairs={{0,1},{1,0},{2,3},{3,2},{4,5},{5,4},{6,7},{7,6},{8,9},{9,8},{10,11... | collective-permute-start | bytes 245768 | tf_op jit(solution)/shard_map/ppermute | solution.py:57
  18.0 1.8 %collective-permute-done.3.yi_ref = f32[40,512]{1,0:T(8,128)S(1)} collective-permute-done((f32[40,512]{1,0:T(8,128)S(1)}, f32[40,512]{1,0:T(8,128)S(1)}, u32[]{:S(2)}, u32[]{:S(2)}) %collective-permute-start.3) | collective-permute-done | bytes 81952 | tf_op jit(solution)/shard_map/ppermute | solution.py:57
  19.8 0.9 %shard_map.144 = (f32[512,128]{1,0:T(8,128)S(1)}, s32[8,128]{1,0:T(8,128)S(1)}, s32[8,128]{1,0:T(8,128)S(1)}, f32[16,128]{1,0:T(8,128)S(1)}, f32[24,512]{1,0:T(8,128)S(1)}, /*index=5*/f32[24,512]{1,0:T(8,128)S(1)}) custom-call(f32[512,128]{1,0:T(8,128)S(1)} %shard_map.139.turned_ref, s32[8,128]{1,0:T(8,128)S(1)} %get-tuple-element.35.meta_ref, ...), custom_call_target="tpu_custom_call" | custom-call | flops 4194304 | bytes 524288 | tf_op jit(solution)/shard_map/pallas_call | solution.py:40
  20.7 6.3 %collective-permute-start.4 = (f32[24,512]{1,0:T(8,128)S(1)}, f32[24,512]{1,0:T(8,128)S(1)}, u32[]{:S(2)}, u32[]{:S(2)}) collective-permute-start(f32[24,512]{1,0:T(8,128)S(1)} %get-tuple-element.49), channel_id=1, source_target_pairs={{8,16},{16,8},{24,32},{32,24},{40,48},{48,40},{56,64},{64,56},{72,... | collective-permute-start | bytes 147464 | tf_op jit(solution)/shard_map/ppermute | solution.py:57
  27.1 1.9 %collective-permute-start.5 = (f32[24,512]{1,0:T(8,128)S(1)}, f32[24,512]{1,0:T(8,128)S(1)}, u32[]{:S(2)}, u32[]{:S(2)}) collective-permute-start(f32[24,512]{1,0:T(8,128)S(1)} %get-tuple-element.50), channel_id=1, source_target_pairs={{0,8},{8,0},{16,24},{24,16},{32,40},{40,32},{48,56},{56,48},{64,72... | collective-permute-start | bytes 147464 | tf_op jit(solution)/shard_map/ppermute | solution.py:57
  29.0 0.7 %shard_map.145.kept_sums_ref = f32[160,128]{1,0:T(8,128)S(1)} custom-call(f32[512,128]{1,0:T(8,128)S(1)} %get-tuple-element.46.fresh_ref.kept_ref, s32[8,128]{1,0:T(8,128)S(1)} %get-tuple-element.48.target_ref, f32[24,128]{1,0:T(8,128)S(1)} %get-tuple-element.44.tables_ref), custom_call_target="tpu_custom_call" | custom-call | flops 4194304 | bytes 524288 | tf_op jit(solution)/shard_map/pallas_call | solution.py:40
  29.7 0.4 collective-permute-done.5.xi_ref
  30.2 0.8 %shard_map.146 = (f32[160,128]{1,0:T(8,128)S(1)}, f32[24,128]{1,0:T(8,128)S(1)}, f32[24,128]{1,0:T(8,128)S(1)}, f32[128,128]{1,0:T(8,128)S(1)}, s32[8,128]{1,0:T(8,128)S(1)}) custom-call(f32[160,128]{1,0:T(8,128)S(1)} %shard_map.145.kept_sums_ref, f32[24,512]{1,0:T(8,128)S(1)} %collective-permute-done.4.xo_ref, f32[24,512]{1,0:T(8,128)S(1)} %collective-permute-done.5.xi_ref, ...), custom_call_target="tpu_custom_call" | custom-call | flops 4194304 | bytes 524288 | tf_op jit(solution)/shard_map/pallas_call | solution.py:40
  31.0 4.8 %collective-permute-start.6 = (f32[24,128]{1,0:T(8,128)S(1)}, f32[24,128]{1,0:T(8,128)S(1)}, u32[]{:S(2)}, u32[]{:S(2)}) collective-permute-start(f32[24,128]{1,0:T(8,128)S(1)} %get-tuple-element.52), channel_id=1, source_target_pairs={{8,16},{16,8},{24,32},{32,24},{40,48},{48,40},{56,64},{64,56},{72,... | collective-permute-start | bytes 36872 | tf_op jit(solution)/shard_map/ppermute | solution.py:57
  35.8 1.9 %collective-permute-start.7 = (f32[24,128]{1,0:T(8,128)S(1)}, f32[24,128]{1,0:T(8,128)S(1)}, u32[]{:S(2)}, u32[]{:S(2)}) collective-permute-start(f32[24,128]{1,0:T(8,128)S(1)} %get-tuple-element.53), channel_id=1, source_target_pairs={{0,8},{8,0},{16,24},{24,16},{32,40},{40,32},{48,56},{56,48},{64,72... | collective-permute-start | bytes 36872 | tf_op jit(solution)/shard_map/ppermute | solution.py:57
  37.8 0.0 collective-permute-done.6.from_outer_ref
  37.8 1.1 %collective-permute-done.7.from_inner_ref = f32[24,128]{1,0:T(8,128)S(1)} collective-permute-done((f32[24,128]{1,0:T(8,128)S(1)}, f32[24,128]{1,0:T(8,128)S(1)}, u32[]{:S(2)}, u32[]{:S(2)}) %collective-permute-start.7) | collective-permute-done | bytes 12320 | tf_op jit(solution)/shard_map/ppermute | solution.py:57
  38.9 0.1 shard_map.147
  39.0 13.3 %all_to_all.5.slots_ref = f32[8,112,128]{2,1,0:T(8,128)S(1)} all-to-all(f32[8,112,128]{2,1,0:T(8,128)S(1)} %shard_map.147), channel_id=1, replica_groups=mesh['gx'=64,'gy'=8] {'gy'}, dimensions={0} | all-to-all | bytes 917504 | tf_op jit(solution)/shard_map/all_to_all | solution.py:792
  52.2 1.0 %shard_map.148 = (f32[512,128]{1,0:T(8,128)S(1)}, s32[8,128]{1,0:T(8,128)S(1)}, f32[160,128]{1,0:T(8,128)S(1)}, f32[24,512]{1,0:T(8,128)S(1)}, f32[24,512]{1,0:T(8,128)S(1)}) custom-call(f32[512,128]{1,0:T(8,128)S(1)} %get-tuple-element.46.fresh_ref.kept_ref, s32[8,128]{1,0:T(8,128)S(1)} %get-tuple-element.47.meta_ref, s32[8,128]{1,0:T(8,128)S(1)} %shard_map.141.lists_ref, ...), custom_call_target="tpu_custom_call" | custom-call | flops 4194304 | bytes 524288 | tf_op jit(solution)/shard_map/pallas_call | solution.py:40
  53.2 8.1 %collective-permute-start.8 = (f32[24,512]{1,0:T(8,128)S(1)}, f32[24,512]{1,0:T(8,128)S(1)}, u32[]{:S(2)}, u32[]{:S(2)}) collective-permute-start(f32[24,512]{1,0:T(8,128)S(1)} %get-tuple-element.62), channel_id=1, source_target_pairs={{8,16},{16,8},{24,32},{32,24},{40,48},{48,40},{56,64},{64,56},{72,... | collective-permute-start | bytes 147464 | tf_op jit(solution)/shard_map/ppermute | solution.py:57
  61.3 1.9 %collective-permute-start.9 = (f32[24,512]{1,0:T(8,128)S(1)}, f32[24,512]{1,0:T(8,128)S(1)}, u32[]{:S(2)}, u32[]{:S(2)}) collective-permute-start(f32[24,512]{1,0:T(8,128)S(1)} %get-tuple-element.63), channel_id=1, source_target_pairs={{0,8},{8,0},{16,24},{24,16},{32,40},{40,32},{48,56},{56,48},{64,72... | collective-permute-start | bytes 147464 | tf_op jit(solution)/shard_map/ppermute | solution.py:57
  63.3 1.6 %shard_map.149 = (f32[256,512]{1,0:T(8,128)}, s32[8,128]{1,0:T(8,128)S(1)}) custom-call(f32[512,128]{1,0:T(8,128)S(1)} %get-tuple-element.55.fresh_ref, s32[8,128]{1,0:T(8,128)S(1)} %get-tuple-element.56.old_meta_ref, f32[160,128]{1,0:T(8,128)S(1)} %get-tuple-element.57.velocity_ref, f32[128,128]{1,0:T(8,128)S(1)} %get-tuple-element.58.turned_ref, ...), custom_call_target="tpu_custom_call" | custom-call | flops 4194304 | bytes 524288 | tf_op jit(solution)/shard_map/pallas_call | solution.py:40
  64.9 0.8 %shard_map.150 = (f32[256,512]{1,0:T(8,128)}, s32[2,128]{1,0:T(2,128)}, s32[2,128]{1,0:T(2,128)}) custom-call(f32[256,512]{1,0:T(8,128)} %get-tuple-element.60.part_ref, s32[8,128]{1,0:T(8,128)S(1)} %get-tuple-element.56.old_meta_ref, s32[8,128]{1,0:T(8,128)S(1)} %get-tuple-element.61.tail_ref, ...), custom_call_target="tpu_custom_call", output_to_operand_aliasing={{0}: (0, {})} | custom-call | flops 4194304 | bytes 524288 | tf_op jit(solution)/shard_map/pallas_call | solution.py:40
  (27 shorter events, 0.2 us)
Async XLA Ops:
  0.6 1.0 %copy-start = (f32[128,512]{1,0:T(8,128)S(1)}, f32[128,512]{1,0:T(8,128)}, u32[]{:S(2)}) copy-start(f32[128,512]{1,0:T(8,128)} %points_ref.3) | copy-start | bytes 786436
  1.6 0.7 copy-start.2
  1.6 0.7 %copy-start.3 = (s32[128]{0:T(128)S(1)}, s32[128]{0:T(128)}, u32[]{:S(2)}) copy-start(s32[128]{0:T(128)} %param.14) | copy-start | bytes 1540
  1.6 0.7 %copy-start.4 = (f32[8]{0:T(128)S(1)}, f32[8]{0:T(128)}, u32[]{:S(2)}) copy-start(f32[8]{0:T(128)} %param.15) | copy-start | bytes 100
  1.6 0.7 %copy-start.5 = (f32[8]{0:T(128)S(1)}, f32[8]{0:T(128)}, u32[]{:S(2)}) copy-start(f32[8]{0:T(128)} %param.16) | copy-start | bytes 100
  1.6 0.7 %copy-start.6 = (f32[8]{0:T(128)S(1)}, f32[8]{0:T(128)}, u32[]{:S(2)}) copy-start(f32[8]{0:T(128)} %param.17) | copy-start | bytes 100
  1.7 9.4 %copy-start.1 = (f32[128,512]{1,0:T(8,128)S(1)}, f32[128,512]{1,0:T(8,128)}, u32[]{:S(2)}) copy-start(f32[128,512]{1,0:T(8,128)} %points_ref.3) | copy-start | bytes 786436
  3.1 8.6 %collective-permute-start = (f32[24,128]{1,0:T(8,128)S(1)}, f32[24,128]{1,0:T(8,128)S(1)}, u32[]{:S(2)}, u32[]{:S(2)}) collective-permute-start(f32[24,128]{1,0:T(8,128)S(1)} %get-tuple-element.37), channel_id=1, source_target_pairs={{8,16},{16,8},{24,32},{32,24},{40,48},{48,40},{56,64},{64,56},{72,... | collective-permute-start | bytes 36872 | tf_op jit(solution)/shard_map/ppermute | solution.py:57
  8.4 3.2 %collective-permute-start.1 = (f32[24,128]{1,0:T(8,128)S(1)}, f32[24,128]{1,0:T(8,128)S(1)}, u32[]{:S(2)}, u32[]{:S(2)}) collective-permute-start(f32[24,128]{1,0:T(8,128)S(1)} %get-tuple-element.38), channel_id=1, source_target_pairs={{0,8},{8,0},{16,24},{24,16},{32,40},{40,32},{48,56},{56,48},{64,72... | collective-permute-start | bytes 36872 | tf_op jit(solution)/shard_map/ppermute | solution.py:57
  10.4 0.7 %copy-start.10 = (s32[64]{0:T(128)S(1)}, s32[64]{0:T(128)}, u32[]{:S(2)}) copy-start(s32[64]{0:T(128)} %param.21) | copy-start | bytes 772
  10.4 0.7 %copy-start.11 = (s32[64]{0:T(128)S(1)}, s32[64]{0:T(128)}, u32[]{:S(2)}) copy-start(s32[64]{0:T(128)} %param.22) | copy-start | bytes 772
  10.4 0.7 %copy-start.12 = (s32[64]{0:T(128)S(1)}, s32[64]{0:T(128)}, u32[]{:S(2)}) copy-start(s32[64]{0:T(128)} %param.23) | copy-start | bytes 772
  10.4 0.7 %copy-start.7 = (s32[64]{0:T(128)S(1)}, s32[64]{0:T(128)}, u32[]{:S(2)}) copy-start(s32[64]{0:T(128)} %param.18) | copy-start | bytes 772
  10.4 0.7 %copy-start.8 = (s32[64]{0:T(128)S(1)}, s32[64]{0:T(128)}, u32[]{:S(2)}) copy-start(s32[64]{0:T(128)} %param.19) | copy-start | bytes 772
  10.4 0.7 %copy-start.9 = (s32[64]{0:T(128)S(1)}, s32[64]{0:T(128)}, u32[]{:S(2)}) copy-start(s32[64]{0:T(128)} %param.20) | copy-start | bytes 772
  11.8 6.2 %collective-permute-start.2 = (f32[40,512]{1,0:T(8,128)S(1)}, f32[40,512]{1,0:T(8,128)S(1)}, u32[]{:S(2)}, u32[]{:S(2)}) collective-permute-start(f32[40,512]{1,0:T(8,128)S(1)} %get-tuple-element.42), channel_id=1, source_target_pairs={{1,2},{2,1},{3,4},{4,3},{5,6},{6,5},{9,10},{10,9},{11,12},{12,11},... | collective-permute-start | bytes 245768 | tf_op jit(solution)/shard_map/ppermute | solution.py:57
  12.4 7.4 %collective-permute-start.3 = (f32[40,512]{1,0:T(8,128)S(1)}, f32[40,512]{1,0:T(8,128)S(1)}, u32[]{:S(2)}, u32[]{:S(2)}) collective-permute-start(f32[40,512]{1,0:T(8,128)S(1)} %get-tuple-element.43), channel_id=1, source_target_pairs={{0,1},{1,0},{2,3},{3,2},{4,5},{5,4},{6,7},{7,6},{8,9},{9,8},{10,11... | collective-permute-start | bytes 245768 | tf_op jit(solution)/shard_map/ppermute | solution.py:57
  20.7 9.0 %collective-permute-start.4 = (f32[24,512]{1,0:T(8,128)S(1)}, f32[24,512]{1,0:T(8,128)S(1)}, u32[]{:S(2)}, u32[]{:S(2)}) collective-permute-start(f32[24,512]{1,0:T(8,128)S(1)} %get-tuple-element.49), channel_id=1, source_target_pairs={{8,16},{16,8},{24,32},{32,24},{40,48},{48,40},{56,64},{64,56},{72,... | collective-permute-start | bytes 147464 | tf_op jit(solution)/shard_map/ppermute | solution.py:57
  27.1 3.1 %collective-permute-start.5 = (f32[24,512]{1,0:T(8,128)S(1)}, f32[24,512]{1,0:T(8,128)S(1)}, u32[]{:S(2)}, u32[]{:S(2)}) collective-permute-start(f32[24,512]{1,0:T(8,128)S(1)} %get-tuple-element.50), channel_id=1, source_target_pairs={{0,8},{8,0},{16,24},{24,16},{32,40},{40,32},{48,56},{56,48},{64,72... | collective-permute-start | bytes 147464 | tf_op jit(solution)/shard_map/ppermute | solution.py:57
  31.0 6.8 %collective-permute-start.6 = (f32[24,128]{1,0:T(8,128)S(1)}, f32[24,128]{1,0:T(8,128)S(1)}, u32[]{:S(2)}, u32[]{:S(2)}) collective-permute-start(f32[24,128]{1,0:T(8,128)S(1)} %get-tuple-element.52), channel_id=1, source_target_pairs={{8,16},{16,8},{24,32},{32,24},{40,48},{48,40},{56,64},{64,56},{72,... | collective-permute-start | bytes 36872 | tf_op jit(solution)/shard_map/ppermute | solution.py:57
  35.8 3.1 %collective-permute-start.7 = (f32[24,128]{1,0:T(8,128)S(1)}, f32[24,128]{1,0:T(8,128)S(1)}, u32[]{:S(2)}, u32[]{:S(2)}) collective-permute-start(f32[24,128]{1,0:T(8,128)S(1)} %get-tuple-element.53), channel_id=1, source_target_pairs={{0,8},{8,0},{16,24},{24,16},{32,40},{40,32},{48,56},{56,48},{64,72... | collective-permute-start | bytes 36872 | tf_op jit(solution)/shard_map/ppermute | solution.py:57
  53.2 11.7 %collective-permute-start.8 = (f32[24,512]{1,0:T(8,128)S(1)}, f32[24,512]{1,0:T(8,128)S(1)}, u32[]{:S(2)}, u32[]{:S(2)}) collective-permute-start(f32[24,512]{1,0:T(8,128)S(1)} %get-tuple-element.62), channel_id=1, source_target_pairs={{8,16},{16,8},{24,32},{32,24},{40,48},{48,40},{56,64},{64,56},{72,... | collective-permute-start | bytes 147464 | tf_op jit(solution)/shard_map/ppermute | solution.py:57
  61.3 3.5 %collective-permute-start.9 = (f32[24,512]{1,0:T(8,128)S(1)}, f32[24,512]{1,0:T(8,128)S(1)}, u32[]{:S(2)}, u32[]{:S(2)}) collective-permute-start(f32[24,512]{1,0:T(8,128)S(1)} %get-tuple-element.63), channel_id=1, source_target_pairs={{0,8},{8,0},{16,24},{24,16},{32,40},{40,32},{48,56},{56,48},{64,72... | collective-permute-start | bytes 147464 | tf_op jit(solution)/shard_map/ppermute | solution.py:57

commit v3 on v2

--- a/solution.py
+++ b/solution.py
@@ -15,12 +15,13 @@
 ROWS = 160
 HALO = 24
 TOP = CX * SUB
-MSG = MCAP + SUB
+PIECES = 8 * BLOCK // LANES
+MSG = PIECES * MCAP + SUB
 DEPTHS = CX + 3
 PACK = 96
-NEAR = 16
-SLOT = PACK + NEAR
-CROSS_MSG = SUB + 2 * MCAP
+NEAR = 32
+SHARE = 22
+CROSS_MSG = 2 * SUB + PIECES * 2 * MCAP
 SPAN = 3 * CY + 3
 
 TIME_STEP = 0.2
@@ -36,16 +37,15 @@
 NT = (((1,), (1,)), ((), ()))
 
 
-def call(kernel, outs, scratch, in_specs, *operands, out_specs=None, aliases=None):
+def call(kernel, outs, scratch, in_specs, *operands, out_specs=None, flops=1 << 22, bytes_accessed=1 << 19):
     return pl.pallas_call(
         kernel,
         out_shape=tuple(jax.ShapeDtypeStruct(shape, dtype) for shape, dtype in outs),
         in_specs=in_specs,
         out_specs=out_specs or tuple(IN_VMEM for _ in outs),
         scratch_shapes=scratch,
-        input_output_aliases=aliases or {},
         compiler_params=pltpu.CompilerParams(vmem_limit_bytes=VMEM_LIMIT),
-        cost_estimate=pl.CostEstimate(flops=1 << 22, bytes_accessed=1 << 19, transcendentals=0),
+        cost_estimate=pl.CostEstimate(flops=flops, bytes_accessed=bytes_accessed, transcendentals=0),
     )(*operands)
 
 
@@ -61,20 +61,24 @@
     return lax.broadcasted_iota(jnp.int32, shape, dim)
 
 
-def thirds(value):
+def halves(value):
     high = value.astype(BF16)
-    rest = value - high.astype(F32)
-    middle = rest.astype(BF16)
-    low = (rest - middle.astype(F32)).astype(BF16)
-    return (high, middle, low)
+    return (high, (value - high.astype(F32)).astype(BF16))
 
 
 def product(parts, onehot, dims):
-    total = None
-    for part in parts:
-        term = lax.dot_general(part, onehot, dims, preferred_element_type=F32)
-        total = term if total is None else total + term
+    rows = parts[0].shape[0]
+    stacked = lax.dot_general(jnp.concatenate(parts, axis=0), onehot, dims, preferred_element_type=F32)
+    total = stacked[0:rows]
+    for index in range(1, len(parts)):
+        total = total + stacked[index * rows : (index + 1) * rows]
     return total
+
+
+def select_rows(onehot, rows):
+    high, low = halves(rows)
+    twice = jnp.concatenate([onehot, onehot], axis=1)
+    return lax.dot_general(twice, jnp.concatenate([high, low], axis=0), NN, preferred_element_type=F32)
 
 
 def stencil(u):
@@ -106,10 +110,16 @@
     return [depth == index for index in range(CX)]
 
 
-def node_terms(load, chunks, rho, alive):
+def scaled(terms, materials, tables_ref):
     sub = iota((SUB, LANES), 0)
-    scale = jnp.where(sub < 3, jnp.broadcast_to(rho * VOLUME, (SUB, LANES)), -VOLUME)
-    scale = jnp.where((sub < 5) & jnp.broadcast_to(alive, (SUB, LANES)), scale, 0.0)
+    wide = lambda row: jnp.broadcast_to(row, (SUB, LANES))
+    scale = jnp.where(sub < 3, wide(by_material(materials, tables_ref, 0) * VOLUME), -VOLUME)
+    scale = jnp.where((sub < 5) & (wide(materials) >= 0), scale, 0.0)
+    return [[term * scale for term in row] for row in terms]
+
+
+def node_terms(load, chunks):
+    sub = iota((SUB, LANES), 0)
     stencils = [(stencil(load(0, k)), stencil(load(1, k))) for k in range(chunks)]
     terms = [[None] * 4 for _ in range(4)]
     for b in range(4):
@@ -133,7 +143,7 @@
             for q in range(5):
                 total = jnp.sum(acc[a][q], axis=0, keepdims=True)
                 packed = jnp.where(sub == q, jnp.broadcast_to(total, (SUB, LANES)), packed)
-            terms[a][b] = packed * scale
+            terms[a][b] = packed
     return terms
 
 
@@ -153,7 +163,7 @@
 
 
 def emit_sums(left_ref, onehots, more_ref, sums_ref, inner_ref, outer_ref):
-    sums = product(thirds(left_ref[...]), jnp.concatenate(onehots, axis=1), NT)
+    sums = product(halves(left_ref[...]), jnp.concatenate(onehots, axis=1), NT)
     if more_ref is not None:
         sums = sums + more_ref[...]
     sums_ref[...] = sums
@@ -163,32 +173,42 @@
     outer_ref[...] = jnp.where(odd, top, bottom)
 
 
-def turn(points_ref, turned_ref):
+def spread_table(table_ref, rows_ref, first):
+    table = table_ref[...]
+    for index in range(NMAT):
+        row = first + index
+        rows_ref[row : row + 1, :] = jnp.broadcast_to(table[:, index : index + 1], (1, LANES))
+
+
+def terms_one(points_ref, turned_ref, terms_ref):
     turned_ref[...] = points_ref[...].T
+    load = lambda c, k: rows_at(turned_ref, c, k, BLOCK)
+    terms = node_terms(load, BLOCK // SUB)
+    for a in range(4):
+        for b in range(4):
+            row = (4 * a + b) * SUB
+            terms_ref[row : row + SUB, :] = terms[a][b]
 
 
 def sums_one(
-    turned_ref, cells_ref, mats_ref, density_ref, shear_ref, lame_ref,
-    sums_ref, inner_ref, outer_ref, tables_ref, meta_ref,
-    left_ref,
+    terms_ref, cells_ref, mats_ref, density_ref,
+    sums_ref, inner_ref, outer_ref, meta_ref,
+    left_ref, density_rows_ref,
 ):
-    for which, table_ref in enumerate((density_ref, shear_ref, lame_ref)):
-        table = table_ref[...]
-        for index in range(NMAT):
-            row = which * NMAT + index
-            tables_ref[row : row + 1, :] = jnp.broadcast_to(table[:, index : index + 1], (1, LANES))
+    spread_table(density_ref, density_rows_ref, 0)
     cells, materials = (cells_ref[...], mats_ref[...])
     meta_ref[0:1, :] = cells
     meta_ref[1:2, :] = materials
-    rho = by_material(materials, tables_ref, 0)
-    load = lambda c, k: turned_ref[c * BLOCK + k * SUB : c * BLOCK + (k + 1) * SUB, :]
-    terms = node_terms(load, BLOCK // SUB, rho, materials >= 0)
+    terms = [[terms_ref[(4 * a + b) * SUB : (4 * a + b + 1) * SUB, :] for b in range(4)] for a in range(4)]
+    terms = scaled(terms, materials, density_rows_ref)
     spread_rows(terms, row_masks(cells >> 5), left_ref)
     emit_sums(left_ref, column_onehot(cells & (CY - 1)), None, sums_ref, inner_ref, outer_ref)
 
 
 def join_lists(*refs):
-    *list_refs, lists_ref = refs
+    *list_refs, density_ref, shear_ref, lame_ref, lists_ref, tables_ref = refs
+    for which, table_ref in enumerate((density_ref, shear_ref, lame_ref)):
+        spread_table(table_ref, tables_ref, which * NMAT)
     for index, ref in enumerate(list_refs):
         row = ref[...]
         rest = jnp.full((1, LANES - row.shape[1]), -1, jnp.int32)
@@ -197,6 +217,18 @@
 
 def by_side(inner, outer, odd):
     return (jnp.where(odd, inner, outer), jnp.where(odd, outer, inner))
+
+
+def put_pieces(ref, first, rows):
+    count = rows.shape[0]
+    for piece in range(PIECES):
+        start = first + piece * count
+        ref[start : start + count, :] = rows[:, piece * LANES : (piece + 1) * LANES]
+
+
+def joined(pieces):
+    count = pieces.shape[0] // PIECES
+    return jnp.concatenate([pieces[piece * count : (piece + 1) * count] for piece in range(PIECES)], axis=1)
 
 
 def matches(dests, targets):
@@ -274,11 +306,7 @@
     tags_ref[...] = tag_tile(
         places[0:1] * float(CY) + places[1:2], found[0:1], found[1:2] * float(CY) + found[2:3]
     )
-    total = None
-    for part in thirds(points_ref[...]):
-        term = lax.dot_general(onehot[0 : 4 * MCAP], part, NN, preferred_element_type=F32)
-        total = term if total is None else total + term
-    rows_ref[...] = total
+    rows_ref[...] = select_rows(onehot[0 : 4 * MCAP], points_ref[...])
 
 
 def merge_rows(sums_ref, from_outer_ref, from_inner_ref, merged_ref):
@@ -309,10 +337,9 @@
         (inner_ref, to_inner, tags, 0),
         (outer_ref, to_outer, pltpu.roll(tags, LANES - movers, 1), movers),
     ):
-        ref[0:SUB, 0:LANES] = halo
-        ref[0:SUB, LANES : 2 * LANES] = jnp.where(lane < movers, tag, 0.0)
-        ref[0:SUB, 2 * LANES :] = jnp.zeros((SUB, 8 * BLOCK - 2 * LANES), F32)
-        ref[SUB:CROSS_MSG, :] = rows_ref[first : first + movers, :]
+        ref[0:SUB, :] = halo
+        ref[SUB : 2 * SUB, :] = jnp.where(lane < movers, tag, 0.0)
+        put_pieces(ref, 2 * SUB, rows_ref[first : first + movers, :])
 
 
 def merge_two(sums_ref, from_outer_ref, from_inner_ref, near_ref, slots_ref, merged_ref, slot_ref):
@@ -320,7 +347,13 @@
     slot_ref[PACK - SUB : PACK, :] = jnp.zeros((SUB, LANES), F32)
     for x in range(DEPTHS):
         slot_ref[5 * x : 5 * x + 5, :] = merged_ref[x * SUB : x * SUB + 5, :]
-    slot_ref[PACK:SLOT, :] = near_ref[...]
+    lane = iota((NEAR, LANES), 1)
+    near = near_ref[...]
+    for third in range(PACK // NEAR):
+        start = third * NEAR
+        moved = pltpu.roll(near, SPAN - SHARE * third, 1)
+        here = (lane >= SPAN) & (lane < SPAN + SHARE)
+        slot_ref[start : start + NEAR, :] = jnp.where(here, moved, slot_ref[start : start + NEAR, :])
     value = slot_ref[...]
     for index in range(slots_ref.shape[0]):
         slots_ref[index] = value
@@ -370,8 +403,9 @@
 def gathered(velocity_parts, depth_of, column_of):
     masks = row_masks(depth_of)
     near = [[None] * 4 for _ in range(4)]
-    for b, onehot in enumerate(column_onehot(column_of)):
-        column = product(velocity_parts, onehot, NN)
+    columns = product(velocity_parts, jnp.concatenate(column_onehot(column_of), axis=1), NN)
+    for b in range(4):
+        column = columns[:, b * LANES : (b + 1) * LANES]
         for a in range(4):
             total = jnp.zeros((SUB, LANES), F32)
             for x in range(CX):
@@ -431,25 +465,14 @@
     return lambda a, b, component: near[a][b][component + 1 : component + 2]
 
 
-def emit_movers(fresh, materials, lists, far_ref, near_ref):
-    home, step_x, _ = home_and_steps()
-    slots, dests, cell = (lists[0:1], lists[1:2], lists[2:3])
-    matched, rank = matches(dests, (home - step_x, home + step_x))
-    placing = placing_rows(matched, rank, (0, 1))
-    chosen = turned_to(placing, holding(slots)).astype(BF16)
-    places = turned_to(small_rows(cell >> 5, cell & (CY - 1)), placing)
-    kinds = turned_to(small_rows(materials + 1), chosen)
-    tags = tag_tile(places[0:1] * float(CY) + places[1:2], kinds[0:1])
-    total = None
-    for part in thirds(fresh):
-        term = lax.dot_general(chosen[0 : 2 * MCAP], part, NN, preferred_element_type=F32)
-        total = term if total is None else total + term
+def emit_movers(fresh, chosen_ref, tags_ref, far_ref, near_ref):
+    rows = select_rows(chosen_ref[...].astype(BF16), fresh.T)
+    tags = tags_ref[...]
     lane = iota((SUB, LANES), 1)
     for o, ref in enumerate((far_ref, near_ref)):
-        ref[0:MCAP, :] = total[o * MCAP : (o + 1) * MCAP]
+        put_pieces(ref, 0, rows[o * MCAP : (o + 1) * MCAP])
         tag = pltpu.roll(tags, LANES - o * MCAP, 1) if o else tags
-        ref[MCAP:MSG, 0:LANES] = jnp.where(lane < MCAP, tag, 0.0)
-        ref[MCAP:MSG, LANES:] = jnp.zeros((SUB, 8 * BLOCK - LANES), F32)
+        ref[MSG - SUB : MSG, :] = jnp.where(lane < MCAP, tag, 0.0)
 
 
 def departures(cells, materials, lists):
@@ -481,43 +504,60 @@
     return (kept, target)
 
 
+def plan_depth(
+    meta_ref, lists_ref,
+    chosen_a_ref, chosen_b_ref, tags_a_ref, tags_b_ref, kept_a_ref, kept_b_ref, target_ref,
+):
+    home, step_x, _ = home_and_steps()
+    cells, materials = (meta_ref[0:1, :], meta_ref[1:2, :])
+    for first, chosen_ref, tags_ref in ((0, chosen_a_ref, tags_a_ref), (3, chosen_b_ref, tags_b_ref)):
+        matched, rank = matches(lists_ref[first + 1 : first + 2, :], (home - step_x, home + step_x))
+        placing = placing_rows(matched, rank, (0, 1))
+        chosen = turned_to(placing, holding(lists_ref[first : first + 1, :]))
+        chosen_ref[...] = chosen[0 : 2 * MCAP]
+        cell = lists_ref[first + 2 : first + 3, :]
+        places = turned_to(small_rows(cell >> 5, cell & (CY - 1)), placing)
+        kinds = turned_to(small_rows(materials + 1), chosen.astype(BF16))
+        tags_ref[...] = tag_tile(places[0:1] * float(CY) + places[1:2], kinds[0:1])
+    kept, target = departures(cells, materials, lists_ref[0:3, :])
+    kept_a_ref[...] = kept
+    target_ref[...] = target
+    kept, _ = departures(kept[0:1], kept[1:2], lists_ref[3:6, :])
+    kept_b_ref[...] = kept
+
+
 def rows_at(ref, c, k, stride):
     return ref[c * stride + k * SUB : c * stride + (k + 1) * SUB, :]
 
 
 def advance_one(
-    turned_ref, meta_ref, lists_ref, merged_ref, yo_ref, yi_ref, tables_ref, chosen_ref,
-    fresh_ref, kept_meta_ref, target_ref, near_ref, far_message_ref, near_message_ref,
-    velocity_ref, nodes_ref,
+    turned_ref, meta_ref, merged_ref, yo_ref, yi_ref, tables_ref, chosen_ref, tags_ref,
+    fresh_ref, nodes_ref, far_message_ref, near_message_ref,
+    velocity_ref,
 ):
-    velocity_one(merged_ref, yi_ref[0:SUB, 0:LANES], yo_ref[0:SUB, 0:LANES], velocity_ref)
+    velocity_one(merged_ref, yi_ref[0:SUB, :], yo_ref[0:SUB, :], velocity_ref)
     cells, materials = (meta_ref[0:1, :], meta_ref[1:2, :])
 
     def store(c, k, value):
         fresh_ref[c * BLOCK + k * SUB : c * BLOCK + (k + 1) * SUB, :] = value
 
-    near = gathered(thirds(velocity_ref[...]), cells >> 5, cells & (CY - 1))
+    near = gathered(halves(velocity_ref[...]), cells >> 5, cells & (CY - 1))
     load = lambda c, k: rows_at(turned_ref, c, k, BLOCK)
     move_points(load, store, BLOCK // SUB, node_getter(near), materials, tables_ref)
-    emit_movers(fresh_ref[...].T, materials, lists_ref[0:3, :], far_message_ref, near_message_ref)
-    kept, target = departures(cells, materials, lists_ref[0:3, :])
-    kept_meta_ref[...] = kept
-    target_ref[...] = target
+    emit_movers(fresh_ref[...], chosen_ref, tags_ref, far_message_ref, near_message_ref)
     for a in range(4):
         for b in range(4):
             row = 2 * (4 * a + b)
             nodes_ref[row : row + 2, :] = near[a][b][1:3]
-    nodes = product(thirds(nodes_ref[...]), chosen_ref[...].astype(BF16), NT)
-    near_ref[...] = nodes[0:NEAR] + pltpu.roll(nodes[NEAR:], LANES // 2, 1)
-
-
-def sums_kept(fresh_ref, target_ref, tables_ref, sums_ref, left_ref):
+
+
+def sums_kept(fresh_ref, target_ref, tables_ref, nodes_ref, chosen_ref, sums_ref, near_ref, left_ref):
     depth, column, materials = (target_ref[0:1, :], target_ref[1:2, :], target_ref[2:3, :])
     load = lambda c, k: rows_at(fresh_ref, c, k, BLOCK)
-    rho = by_material(materials, tables_ref, 0)
-    terms = node_terms(load, BLOCK // SUB, rho, materials >= 0)
+    terms = scaled(node_terms(load, BLOCK // SUB), materials, tables_ref)
     spread_rows(terms, row_masks(depth), left_ref)
-    sums_ref[...] = product(thirds(left_ref[...]), jnp.concatenate(column_onehot(column), axis=1), NT)
+    sums_ref[...] = product(halves(left_ref[...]), jnp.concatenate(column_onehot(column), axis=1), NT)
+    near_ref[...] = product(halves(nodes_ref[...]), chosen_ref[...].astype(BF16), NT)
 
 
 def packed_blocks(rows, wide_ref, turned_ref):
@@ -562,23 +602,22 @@
     sums_ref, inner_ref, outer_ref, turned_ref, new_meta_ref,
     left_ref, wide_ref,
 ):
-    new_meta = arrived_tags(xi_ref[MCAP:MSG, 0:LANES], xo_ref[MCAP:MSG, 0:LANES])
+    new_meta = arrived_tags(xi_ref[MSG - SUB : MSG, :], xo_ref[MSG - SUB : MSG, :])
     new_meta_ref[...] = new_meta
-    low, high = by_side(xi_ref[0:MCAP, :], xo_ref[0:MCAP, :], parity("gx"))
-    packed_blocks(jnp.concatenate([low, high], axis=0), wide_ref, turned_ref)
+    low, high = by_side(xi_ref[0 : MSG - SUB, :], xo_ref[0 : MSG - SUB, :], parity("gx"))
+    packed_blocks(jnp.concatenate([joined(low), joined(high)], axis=0), wide_ref, turned_ref)
     cells, materials = (new_meta[0:1], new_meta[1:2])
     stride = turned_ref.shape[0] // 8
     load = lambda c, k: rows_at(turned_ref, c, k, stride)
-    rho = by_material(materials, tables_ref, 0)
-    terms = node_terms(load, stride // SUB, rho, materials >= 0)
+    terms = scaled(node_terms(load, stride // SUB), materials, tables_ref)
     spread_rows(terms, row_masks(cells >> 5), left_ref)
     onehots = column_onehot((cells & (CY - 1)) + CY)
     emit_sums(left_ref, onehots, kept_sums_ref, sums_ref, inner_ref, outer_ref)
 
 
 def advance_two(
-    kept_ref, meta_ref, lists_ref, slots_ref, tables_ref,
-    fresh_ref, old_meta_ref, velocity_ref, far_message_ref, near_message_ref,
+    kept_ref, meta_ref, slots_ref, tables_ref, chosen_ref, tags_ref,
+    fresh_ref, velocity_ref, far_message_ref, near_message_ref,
     packed_ref,
 ):
     velocity_two(slots_ref, packed_ref, velocity_ref)
@@ -587,25 +626,31 @@
     def store(c, k, value):
         fresh_ref[c * BLOCK + k * SUB : c * BLOCK + (k + 1) * SUB, :] = value
 
-    near = gathered(thirds(velocity_ref[...]), cells >> 5, (cells & (CY - 1)) + CY)
+    near = gathered(halves(velocity_ref[...]), cells >> 5, (cells & (CY - 1)) + CY)
     load = lambda c, k: rows_at(kept_ref, c, k, BLOCK)
     move_points(load, store, BLOCK // SUB, node_getter(near), materials, tables_ref)
-    emit_movers(fresh_ref[...].T, materials, lists_ref[3:6, :], far_message_ref, near_message_ref)
-    kept, _ = departures(cells, materials, lists_ref[3:6, :])
-    old_meta_ref[...] = kept
+    emit_movers(fresh_ref[...], chosen_ref, tags_ref, far_message_ref, near_message_ref)
+
+
+def near_movers(slots_ref, index):
+    lane = iota((NEAR, LANES), 1)
+    nodes = jnp.zeros((NEAR, LANES), F32)
+    for third in range(PACK // NEAR):
+        first = SHARE * third
+        part = slots_ref[index, third * NEAR : (third + 1) * NEAR, :]
+        part = pltpu.roll(part, LANES - SPAN + first, 1)
+        nodes = jnp.where((lane >= first) & (lane < first + SHARE), part, nodes)
+    return nodes
 
 
 def settle(
     fresh_ref, old_meta_ref, velocity_ref, turned_ref, new_meta_ref, tables_ref, slots_ref, yo_ref, yi_ref,
-    points_ref, tail_ref,
-    old_ref, wide_ref, new_ref, cross_ref, middle_ref, out_ref, small_ref, last_ref, sems,
+    rows_ref, tail_ref,
+    wide_ref, cross_ref, middle_ref, out_ref, small_ref,
 ):
     alive = jnp.broadcast_to(old_meta_ref[1:2, :], fresh_ref.shape) >= 0
-    old_ref[...] = jnp.where(alive, fresh_ref[...], 0.0).T
-    old = LANES
-    copies = [pltpu.make_async_copy(old_ref, points_ref.at[0:old], sems.at[0])]
-    copies[0].start()
-    parts = thirds(velocity_ref[...])
+    rows_ref[0:LANES, :] = jnp.where(alive, fresh_ref[...], 0.0).T
+    parts = halves(velocity_ref[...])
 
     stride = turned_ref.shape[0] // 8
     cells, materials = (new_meta_ref[0:1, :], new_meta_ref[1:2, :])
@@ -616,15 +661,13 @@
     load = lambda c, k: rows_at(turned_ref, c, k, stride)
     near = gathered(parts, cells >> 5, (cells & (CY - 1)) + CY)
     move_points(load, store_small, stride // SUB, node_getter(near), materials, tables_ref)
-    new_ref[...] = unpacked_blocks(small_ref, 2 * MCAP, wide_ref)
-    copies.append(pltpu.make_async_copy(new_ref, points_ref.at[old : old + 2 * MCAP], sems.at[1]))
-    copies[1].start()
+    rows_ref[LANES : LANES + 2 * MCAP, :] = unpacked_blocks(small_ref, 2 * MCAP, wide_ref)
 
     gy = lax.axis_index("gy")
     odd = parity("gy")
     low, high = by_side(yi_ref[...], yo_ref[...], odd)
     lane = iota((SUB, LANES), 1)
-    tags = low[0:SUB, LANES : 2 * LANES] + pltpu.roll(high[0:SUB, LANES : 2 * LANES], 2 * MCAP, 1)
+    tags = low[SUB : 2 * SUB] + pltpu.roll(high[SUB : 2 * SUB], 2 * MCAP, 1)
     tail = jnp.zeros((SUB, LANES), F32)
     for start, shift in ((32, 32), (48, 16), (96, 80), (112, 64)):
         tail = jnp.where((lane >= start) & (lane < start + MCAP), pltpu.roll(tags, shift, 1), tail)
@@ -634,20 +677,20 @@
     tags = repeated(tags, 4 * MCAP).astype(jnp.int32) - materials_row
 
     last = slots_ref.shape[0] - 1
-    below = slots_ref[jnp.maximum(gy - 1, 0), PACK:SLOT, :]
-    above = slots_ref[jnp.minimum(gy + 1, last), PACK:SLOT, :]
+    below = near_movers(slots_ref, jnp.maximum(gy - 1, 0))
+    above = near_movers(slots_ref, jnp.minimum(gy + 1, last))
     below = jnp.where(odd, below, pltpu.roll(below, LANES - 2 * MCAP, 1))
     above = jnp.where(odd, above, pltpu.roll(above, 2 * MCAP, 1))
     many = iota((NEAR, LANES), 1)
-    nodes = jnp.where((many & (4 * MCAP - 1)) < 2 * MCAP, below, above)
-    turned_nodes = pltpu.roll(nodes, LANES // 2, 1)
-    halves = (jnp.where(many < LANES // 2, nodes, turned_nodes), jnp.where(many < LANES // 2, turned_nodes, nodes))
+    nodes = jnp.where(many < 2 * MCAP, below, jnp.where(many < 4 * MCAP, above, 0.0))
+    nodes = nodes + pltpu.roll(nodes, 4 * MCAP, 1)
 
     def node_of(a, b, component):
         row = 2 * (4 * a + b) + component
-        return halves[row // NEAR][row % NEAR : row % NEAR + 1]
-
-    packed_blocks(jnp.concatenate([low[SUB:], high[SUB:]], axis=0), wide_ref, cross_ref)
+        return nodes[row : row + 1]
+
+    rows = jnp.concatenate([joined(low[2 * SUB :]), joined(high[2 * SUB :])], axis=0)
+    packed_blocks(rows, wide_ref, cross_ref)
     half = cross_ref.shape[0] // 8
     kinds = tags[1:2]
 
@@ -667,38 +710,37 @@
     move_points(
         lambda c, k: rows_at(middle_ref, c, k, half), store_out, half // SUB, node_getter(near), kinds, tables_ref
     )
-    last_ref[...] = unpacked_blocks(out_ref, 4 * MCAP, wide_ref)
-    region = lambda index: points_ref.at[old + index * MCAP : old + (index + 1) * MCAP]
+    last = unpacked_blocks(out_ref, 4 * MCAP, wide_ref)
     for group, index in enumerate((2, 6, 3, 7)):
-        source = last_ref.at[group * MCAP : (group + 1) * MCAP]
-        copies.append(pltpu.make_async_copy(source, region(index), sems.at[2 + group]))
-        copies[-1].start()
-    for copy in copies:
-        copy.wait()
+        start = LANES + index * MCAP
+        rows_ref[start : start + MCAP, :] = last[group * MCAP : (group + 1) * MCAP]
 
 
 def assemble(
     part_ref, old_meta_ref, tail_ref, xo_ref, xi_ref,
     points_ref, cells_ref, mats_ref,
-    tags_ref, sems,
+    tags_ref, rows_ref, sems,
 ):
-    del part_ref
     base = points_ref.shape[0] - 4 * MCAP
     odd = lax.axis_index("gx") & 1
     copies = []
+    for index, (first, last) in enumerate(((0, base), (base + 2 * MCAP, base + 4 * MCAP))):
+        copies.append(pltpu.make_async_copy(part_ref.at[first:last], points_ref.at[first:last], sems.at[index]))
+        copies[-1].start()
     for index, (ref, region) in enumerate(((xo_ref, odd), (xi_ref, 1 - odd))):
         start = pl.multiple_of(base + region * MCAP, MCAP)
+        rows_ref[index] = joined(ref[0 : MSG - SUB, :])
         copies.append(
-            pltpu.make_async_copy(ref.at[0:MCAP, :], points_ref.at[pl.ds(start, MCAP), :], sems.at[index])
+            pltpu.make_async_copy(rows_ref.at[index], points_ref.at[pl.ds(start, MCAP), :], sems.at[2 + index])
         )
         copies[-1].start()
-    arrived = arrived_tags(xi_ref[MCAP:MSG, 0:LANES], xo_ref[MCAP:MSG, 0:LANES])
+    arrived = arrived_tags(xi_ref[MSG - SUB : MSG, :], xo_ref[MSG - SUB : MSG, :])
     lane = iota((1, LANES), 1)
     here = (lane >= 4 * MCAP) & (lane < 6 * MCAP)
     for row, ref in ((0, cells_ref), (1, mats_ref)):
         tags_ref[row, 0:1, :] = old_meta_ref[row : row + 1, :]
         tags_ref[row, 1:2, :] = jnp.where(here, arrived[row : row + 1], tail_ref[row : row + 1, :])
-        copies.append(pltpu.make_async_copy(tags_ref.at[row], ref, sems.at[2 + row]))
+        copies.append(pltpu.make_async_copy(tags_ref.at[row], ref, sems.at[4 + row]))
         copies[-1].start()
     for copy in copies:
         copy.wait()
@@ -729,27 +771,32 @@
     tile = ((SUB, LANES), F32)
     tags = ((SUB, LANES), I32)
     grid = ((ROWS, LANES), F32)
-    message = ((MSG, wide), F32)
-    cross_message = ((CROSS_MSG, wide), F32)
+    message = ((MSG, LANES), F32)
+    cross_message = ((CROSS_MSG, LANES), F32)
     turned_form = ((wide, LANES), F32)
     half_form = ((wide // 2, LANES), F32)
     quarter_form = ((wide // 4, LANES), F32)
     near_form = ((NEAR, LANES), F32)
-    slots_form = ((lax.axis_size("gy"), SLOT, LANES), F32)
+    slots_form = ((lax.axis_size("gy"), PACK, LANES), F32)
     scratch = lambda form: pltpu.VMEM(*form)
     left = pltpu.VMEM((ROWS, 4 * LANES), F32)
 
     def along_depth(far, near):
         return (swap(far, "gx", 1), swap(near, "gx", 0))
 
-    (lists,) = call(join_lists, (tags,), (), (IN_VMEM,) * 6, *list_a, *list_b)
-    (turned,) = call(turn, (turned_form,), (), (IN_VMEM,), points)
-    sums, inner, outer, tables, meta = call(
+    small = (row(density), row(shear_modulus), row(lame_modulus))
+    lists, tables = call(
+        join_lists, (tags, ((3 * NMAT, LANES), F32)), (), (IN_VMEM,) * 9, *list_a, *list_b, *small
+    )
+    turned, terms = call(
+        terms_one, (turned_form, ((16 * SUB, LANES), F32)), (), (IN_VMEM,), points
+    )
+    sums, inner, outer, meta = call(
         sums_one,
-        (grid, halo, halo, ((3 * NMAT, LANES), F32), tags),
-        (left,),
-        (IN_VMEM,) * 6,
-        turned, cells, mats, row(density), row(shear_modulus), row(lame_modulus),
+        (grid, halo, halo, tags),
+        (left, pltpu.VMEM((NMAT, LANES), F32)),
+        (IN_VMEM,) * 4,
+        terms, cells, mats, small[0],
     )
     picked, picked_tags, chosen = call(
         pick_cross,
@@ -766,15 +813,25 @@
         sums, *along_depth(outer, inner), picked, picked_tags,
     )
     cross_far, cross_near = (swap(outer, "gy", 1), swap(inner, "gy", 0))
-    fresh, kept_meta, target, near_nodes, far, near = call(
+    chosen_form = ((2 * MCAP, LANES), F32)
+    chosen_a, chosen_b, tags_a, tags_b, kept_a, kept_b, target = call(
+        plan_depth,
+        (chosen_form, chosen_form, tile, tile, tags, tags, tags),
+        (),
+        (IN_VMEM,) * 2,
+        meta, lists,
+    )
+    fresh, nodes, far, near = call(
         advance_one,
-        (turned_form, tags, tags, near_form, message, message),
-        (scratch(grid), pltpu.VMEM((2 * NEAR, LANES), F32)),
+        (turned_form, near_form, message, message),
+        (scratch(grid),),
         (IN_VMEM,) * 8,
-        turned, meta, lists, merged, cross_far, cross_near, tables, chosen,
+        turned, meta, merged, cross_far, cross_near, tables, chosen_a, tags_a,
     )
     arrived = along_depth(far, near)
-    (kept_sums,) = call(sums_kept, (grid,), (left,), (IN_VMEM,) * 3, fresh, target, tables)
+    kept_sums, near_nodes = call(
+        sums_kept, (grid, near_form), (left,), (IN_VMEM,) * 5, fresh, target, tables, nodes, chosen
+    )
     sums, inner, outer, turned, new_meta = call(
         sums_two,
         (grid, halo, halo, quarter_form, tags),
@@ -785,17 +842,17 @@
     (slots,) = call(
         merge_two,
         (slots_form,),
-        (scratch(grid), pltpu.VMEM((SLOT, LANES), F32)),
+        (scratch(grid), pltpu.VMEM((PACK, LANES), F32)),
         (IN_VMEM,) * 4,
         sums, *along_depth(outer, inner), near_nodes,
     )
     slots = lax.all_to_all(slots, "gy", 0, 0)
-    fresh, old_meta, velocity, far, near = call(
+    fresh, velocity, far, near = call(
         advance_two,
-        (turned_form, tags, grid, message, message),
+        (turned_form, grid, message, message),
         (pltpu.VMEM((PACK + SUB, LANES), F32),),
-        (IN_VMEM,) * 5,
-        fresh, kept_meta, lists, slots, tables,
+        (IN_VMEM,) * 6,
+        fresh, kept_a, slots, tables, chosen_b, tags_b,
     )
     arrived = along_depth(far, near)
     final_form = ((2 * LANES, wide), F32)
@@ -803,28 +860,22 @@
         settle,
         (final_form, tags),
         (
-            pltpu.VMEM((LANES, wide), F32),
             scratch(turned_form),
-            pltpu.VMEM((2 * MCAP, wide), F32),
             scratch(half_form),
             scratch(half_form),
             scratch(half_form),
             scratch(quarter_form),
-            pltpu.VMEM((4 * MCAP, wide), F32),
-            pltpu.SemaphoreType.DMA((6,)),
         ),
         (IN_VMEM,) * 9,
-        fresh, old_meta, velocity, turned, new_meta, tables, slots, cross_far, cross_near,
-        out_specs=(IN_HBM, IN_VMEM),
+        fresh, kept_b, velocity, turned, new_meta, tables, slots, cross_far, cross_near,
     )
     final_points, final_cells, final_mats = call(
         assemble,
         (final_form, ((2, LANES), I32), ((2, LANES), I32)),
-        (pltpu.VMEM((2, 2, LANES), I32), pltpu.SemaphoreType.DMA((4,))),
-        (IN_HBM,) + (IN_VMEM,) * 4,
-        part, old_meta, tail, *arrived,
+        (pltpu.VMEM((2, 2, LANES), I32), pltpu.VMEM((2, MCAP, wide), F32), pltpu.SemaphoreType.DMA((6,))),
+        (IN_VMEM,) * 5,
+        part, kept_b, tail, *arrived,
         out_specs=(IN_HBM,) * 3,
-        aliases={0: 0},
     )
     return (final_points, final_cells.reshape(-1), final_mats.reshape(-1))
 

time: 66.1 us -> 65.2 us (0.986)
  the two profiles are of different devices: /device:TPU:225 before, /device:TPU:384 now
where the time goes in v3:
time: 65.2 us; the launch traced here: 64.8 us
  starting transfers between devices  32.3 us (50%)
  blocking collectives  12.8 us (20%)
  waiting for transfers between devices  9.28 us (14%)
  Pallas kernels  7.19 us (11%)
  local copies, waits for them, and re-layouts  2.31 us (4%)
  between operations  0.91 us (1%)
    ppermute x10, starting transfers between devices, swap(): return lax.ppermute(value, axis, pairs)  32.3 us
    all_to_all x1, blocking collectives, shards(): slots = lax.all_to_all(slots, 'gy', 0, 0)  12.8 us
    ppermute x10, waiting for transfers between devices, swap(): return lax.ppermute(value, axis, pairs)  9.28 us
    pallas_call x13, Pallas kernels, call(): pl.pallas_call(kernel, out_shape=tuple((jax.ShapeDtypeStruct(shape, dtype...  7.19 us
    unnamed x26, local copies, waits for them, and re-layouts  2.31 us
  transfers between devices with their start and end apart: 10, of which 4 were waited for; matrix products, arithmetic and copies ran while one was open for 0% of the time, Pallas kernels for 4%

profile of v3, /device:TPU:384, one launch (start us, length us, event | category | flops | bytes accessed | tf_op | source)
XLA Modules:
  0.0 64.8 jit_solution(15249691144425479226)
XLA Ops:
  0.6 0.9 %copy-done = f32[128,512]{1,0:T(8,128)S(1)} copy-done((f32[128,512]{1,0:T(8,128)S(1)}, f32[128,512]{1,0:T(8,128)}, u32[]{:S(2)}) %copy-start) | copy-done | bytes 262168
  1.6 0.5 shard_map.139
  2.1 0.6 copy-done.2
  2.7 0.0 copy-done.3
  2.8 0.3 shard_map.140
  3.1 6.2 %collective-permute-start = (f32[24,128]{1,0:T(8,128)S(1)}, f32[24,128]{1,0:T(8,128)S(1)}, u32[]{:S(2)}, u32[]{:S(2)}) collective-permute-start(f32[24,128]{1,0:T(8,128)S(1)} %get-tuple-element.48), channel_id=1, source_target_pairs={{8,16},{16,8},{24,32},{32,24},{40,48},{48,40},{56,64},{64,56},{72,... | collective-permute-start | bytes 36872 | tf_op jit(solution)/shard_map/ppermute | solution.py:57
  9.3 1.9 %collective-permute-start.1 = (f32[24,128]{1,0:T(8,128)S(1)}, f32[24,128]{1,0:T(8,128)S(1)}, u32[]{:S(2)}, u32[]{:S(2)}) collective-permute-start(f32[24,128]{1,0:T(8,128)S(1)} %get-tuple-element.49), channel_id=1, source_target_pairs={{0,8},{8,0},{16,24},{24,16},{32,40},{40,32},{48,56},{56,48},{64,72... | collective-permute-start | bytes 36872 | tf_op jit(solution)/shard_map/ppermute | solution.py:57
  11.3 0.6 copy-done.8
  12.0 0.1 shard_map.141
  12.1 0.5 shard_map.142
  12.6 0.1 shard_map.143
  12.7 0.7 %collective-permute-start.2 = (f32[144,128]{1,0:T(8,128)S(1)}, f32[144,128]{1,0:T(8,128)S(1)}, u32[]{:S(2)}, u32[]{:S(2)}) collective-permute-start(f32[144,128]{1,0:T(8,128)S(1)} %get-tuple-element.54), channel_id=1, source_target_pairs={{1,2},{2,1},{3,4},{4,3},{5,6},{6,5},{9,10},{10,9},{11,12},{12,11},... | collective-permute-start | bytes 221192 | tf_op jit(solution)/shard_map/ppermute | solution.py:57
  13.4 6.1 %collective-permute-start.3 = (f32[144,128]{1,0:T(8,128)S(1)}, f32[144,128]{1,0:T(8,128)S(1)}, u32[]{:S(2)}, u32[]{:S(2)}) collective-permute-start(f32[144,128]{1,0:T(8,128)S(1)} %get-tuple-element.55), channel_id=1, source_target_pairs={{0,1},{1,0},{2,3},{3,2},{4,5},{5,4},{6,7},{7,6},{8,9},{9,8},{10,11... | collective-permute-start | bytes 221192 | tf_op jit(solution)/shard_map/ppermute | solution.py:57
  19.5 0.6 shard_map.144
  20.1 2.1 %collective-permute-done.3.yi_ref = f32[144,128]{1,0:T(8,128)S(1)} collective-permute-done((f32[144,128]{1,0:T(8,128)S(1)}, f32[144,128]{1,0:T(8,128)S(1)}, u32[]{:S(2)}, u32[]{:S(2)}) %collective-permute-start.3) | collective-permute-done | bytes 73760 | tf_op jit(solution)/shard_map/ppermute | solution.py:57
  22.2 0.8 %shard_map.145 = (f32[512,128]{1,0:T(8,128)S(1)}, f32[32,128]{1,0:T(8,128)S(1)}, f32[72,128]{1,0:T(8,128)S(1)}, f32[72,128]{1,0:T(8,128)S(1)}) custom-call(f32[512,128]{1,0:T(8,128)S(1)} %get-tuple-element.44.turned_ref, s32[8,128]{1,0:T(8,128)S(1)} %get-tuple-element.46.meta_ref, f32[160,128]{1,0:T(8,128)S(1)} %get-tuple-element.53.merged_ref, ...), custom_call_target="tpu_custom_call" | custom-call | flops 4194304 | bytes 524288 | tf_op jit(solution)/shard_map/pallas_call | solution.py:41
  23.0 3.8 %collective-permute-start.4 = (f32[72,128]{1,0:T(8,128)S(1)}, f32[72,128]{1,0:T(8,128)S(1)}, u32[]{:S(2)}, u32[]{:S(2)}) collective-permute-start(f32[72,128]{1,0:T(8,128)S(1)} %get-tuple-element.65), channel_id=1, source_target_pairs={{8,16},{16,8},{24,32},{32,24},{40,48},{48,40},{56,64},{64,56},{72,... | collective-permute-start | bytes 110600 | tf_op jit(solution)/shard_map/ppermute | solution.py:57
  26.8 1.9 %collective-permute-start.5 = (f32[72,128]{1,0:T(8,128)S(1)}, f32[72,128]{1,0:T(8,128)S(1)}, u32[]{:S(2)}, u32[]{:S(2)}) collective-permute-start(f32[72,128]{1,0:T(8,128)S(1)} %get-tuple-element.66), channel_id=1, source_target_pairs={{0,8},{8,0},{16,24},{24,16},{32,40},{40,32},{48,56},{56,48},{64,72... | collective-permute-start | bytes 110600 | tf_op jit(solution)/shard_map/ppermute | solution.py:57
  28.8 0.7 %shard_map.146 = (f32[160,128]{1,0:T(8,128)S(1)}, f32[32,128]{1,0:T(8,128)S(1)}) custom-call(f32[512,128]{1,0:T(8,128)S(1)} %get-tuple-element.59.fresh_ref.kept_ref, s32[8,128]{1,0:T(8,128)S(1)} %get-tuple-element.61.target_ref, f32[24,128]{1,0:T(8,128)S(1)} %get-tuple-element.56.tables_ref, f32[32,128]{1,0:T(8,128)S(1)} %get-tuple-element.62.nodes_ref, ...), custom_call_target="tpu_custom_call" | custom-call | flops 4194304 | bytes 524288 | tf_op jit(solution)/shard_map/pallas_call | solution.py:41
  29.4 2.4 %collective-permute-done.4.xo_ref = f32[72,128]{1,0:T(8,128)S(1)} collective-permute-done((f32[72,128]{1,0:T(8,128)S(1)}, f32[72,128]{1,0:T(8,128)S(1)}, u32[]{:S(2)}, u32[]{:S(2)}) %collective-permute-start.4) | collective-permute-done | bytes 36896 | tf_op jit(solution)/shard_map/ppermute | solution.py:57
  31.9 0.7 %shard_map.147 = (f32[160,128]{1,0:T(8,128)S(1)}, f32[24,128]{1,0:T(8,128)S(1)}, f32[24,128]{1,0:T(8,128)S(1)}, f32[128,128]{1,0:T(8,128)S(1)}, s32[8,128]{1,0:T(8,128)S(1)}) custom-call(f32[160,128]{1,0:T(8,128)S(1)} %get-tuple-element.64.kept_sums_ref, f32[72,128]{1,0:T(8,128)S(1)} %collective-permute-done.4.xo_ref, ...), custom_call_target="tpu_custom_call" | custom-call | flops 4194304 | bytes 524288 | tf_op jit(solution)/shard_map/pallas_call | solution.py:41
  32.6 3.8 %collective-permute-start.6 = (f32[24,128]{1,0:T(8,128)S(1)}, f32[24,128]{1,0:T(8,128)S(1)}, u32[]{:S(2)}, u32[]{:S(2)}) collective-permute-start(f32[24,128]{1,0:T(8,128)S(1)} %get-tuple-element.68), channel_id=1, source_target_pairs={{8,16},{16,8},{24,32},{32,24},{40,48},{48,40},{56,64},{64,56},{72,... | collective-permute-start | bytes 36872 | tf_op jit(solution)/shard_map/ppermute | solution.py:57
  36.4 1.9 %collective-permute-start.7 = (f32[24,128]{1,0:T(8,128)S(1)}, f32[24,128]{1,0:T(8,128)S(1)}, u32[]{:S(2)}, u32[]{:S(2)}) collective-permute-start(f32[24,128]{1,0:T(8,128)S(1)} %get-tuple-element.69), channel_id=1, source_target_pairs={{0,8},{8,0},{16,24},{24,16},{32,40},{40,32},{48,56},{56,48},{64,72... | collective-permute-start | bytes 36872 | tf_op jit(solution)/shard_map/ppermute | solution.py:57
  38.4 2.9 %collective-permute-done.6.from_outer_ref = f32[24,128]{1,0:T(8,128)S(1)} collective-permute-done((f32[24,128]{1,0:T(8,128)S(1)}, f32[24,128]{1,0:T(8,128)S(1)}, u32[]{:S(2)}, u32[]{:S(2)}) %collective-permute-start.6) | collective-permute-done | bytes 12320 | tf_op jit(solution)/shard_map/ppermute | solution.py:57
  41.2 0.1 shard_map.148
  41.3 12.8 %all_to_all.5.slots_ref = f32[8,96,128]{2,1,0:T(8,128)S(1)} all-to-all(f32[8,96,128]{2,1,0:T(8,128)S(1)} %shard_map.148), channel_id=1, replica_groups=mesh['gx'=64,'gy'=8] {'gy'}, dimensions={0} | all-to-all | bytes 786432 | tf_op jit(solution)/shard_map/all_to_all | solution.py:849
  54.1 0.9 %shard_map.149 = (f32[512,128]{1,0:T(8,128)S(1)}, f32[160,128]{1,0:T(8,128)S(1)}, f32[72,128]{1,0:T(8,128)S(1)}, f32[72,128]{1,0:T(8,128)S(1)}) custom-call(f32[512,128]{1,0:T(8,128)S(1)} %get-tuple-element.59.fresh_ref.kept_ref, s32[8,128]{1,0:T(8,128)S(1)} %get-tuple-element.60.meta_ref, f32[8,96,128]{2,1,0:T(8,128)S(1)} %all_to_all.5.slots_ref, ...), custom_call_target="tpu_custom_call" | custom-call | flops 4194304 | bytes 524288 | tf_op jit(solution)/shard_map/pallas_call | solution.py:41
  55.0 4.0 %collective-permute-start.8 = (f32[72,128]{1,0:T(8,128)S(1)}, f32[72,128]{1,0:T(8,128)S(1)}, u32[]{:S(2)}, u32[]{:S(2)}) collective-permute-start(f32[72,128]{1,0:T(8,128)S(1)} %get-tuple-element.80), channel_id=1, source_target_pairs={{8,16},{16,8},{24,32},{32,24},{40,48},{48,40},{56,64},{64,56},{72,... | collective-permute-start | bytes 110600 | tf_op jit(solution)/shard_map/ppermute | solution.py:57
  59.0 1.9 %collective-permute-start.9 = (f32[72,128]{1,0:T(8,128)S(1)}, f32[72,128]{1,0:T(8,128)S(1)}, u32[]{:S(2)}, u32[]{:S(2)}) collective-permute-start(f32[72,128]{1,0:T(8,128)S(1)} %get-tuple-element.81), channel_id=1, source_target_pairs={{0,8},{8,0},{16,24},{24,16},{32,40},{40,32},{48,56},{56,48},{64,72... | collective-permute-start | bytes 110600 | tf_op jit(solution)/shard_map/ppermute | solution.py:57
  60.9 1.1 %shard_map.150 = (f32[256,512]{1,0:T(8,128)S(1)}, s32[8,128]{1,0:T(8,128)S(1)}) custom-call(f32[512,128]{1,0:T(8,128)S(1)} %get-tuple-element.73.fresh_ref, s32[8,128]{1,0:T(8,128)S(1)} %get-tuple-element.74.old_meta_ref, f32[160,128]{1,0:T(8,128)S(1)} %get-tuple-element.75.velocity_ref, f32[128,128]{1,0:T(8,128)S(1)} %get-tuple-element.76.turned_ref, ...), custom_call_target="tpu_custom_call" | custom-call | flops 4194304 | bytes 524288 | tf_op jit(solution)/shard_map/pallas_call | solution.py:41
  62.0 1.9 %collective-permute-done.8.xo_ref = f32[72,128]{1,0:T(8,128)S(1)} collective-permute-done((f32[72,128]{1,0:T(8,128)S(1)}, f32[72,128]{1,0:T(8,128)S(1)}, u32[]{:S(2)}, u32[]{:S(2)}) %collective-permute-start.8) | collective-permute-done | bytes 36896 | tf_op jit(solution)/shard_map/ppermute | solution.py:57
  63.9 0.8 %shard_map.151 = (f32[256,512]{1,0:T(8,128)}, s32[2,128]{1,0:T(2,128)}, s32[2,128]{1,0:T(2,128)}) custom-call(f32[256,512]{1,0:T(8,128)S(1)} %get-tuple-element.78.part_ref, s32[8,128]{1,0:T(8,128)S(1)} %get-tuple-element.74.old_meta_ref, s32[8,128]{1,0:T(8,128)S(1)} %get-tuple-element.79.tail_ref, f32[72,128]{1,0:T(8,128)S(1)} %collective-permute-done.8.xo_ref, ...), custom_call_target="tpu_custom_call" | custom-call | flops 4194304 | bytes 524288 | tf_op jit(solution)/shard_map/pallas_call | solution.py:41
  (28 shorter events, 0.2 us)
Async XLA Ops:
  0.6 1.0 %copy-start = (f32[128,512]{1,0:T(8,128)S(1)}, f32[128,512]{1,0:T(8,128)}, u32[]{:S(2)}) copy-start(f32[128,512]{1,0:T(8,128)} %points_ref.3) | copy-start | bytes 786436
  1.6 10.5 %copy-start.1 = (f32[128,512]{1,0:T(8,128)S(1)}, f32[128,512]{1,0:T(8,128)}, u32[]{:S(2)}) copy-start(f32[128,512]{1,0:T(8,128)} %points_ref.3) | copy-start | bytes 786436
  2.1 0.7 %copy-start.2 = (s32[128]{0:T(128)S(1)}, s32[128]{0:T(128)}, u32[]{:S(2)}) copy-start(s32[128]{0:T(128)} %param.13) | copy-start | bytes 1540
  2.1 0.7 %copy-start.3 = (s32[128]{0:T(128)S(1)}, s32[128]{0:T(128)}, u32[]{:S(2)}) copy-start(s32[128]{0:T(128)} %param.14) | copy-start | bytes 1540
  2.1 0.7 %copy-start.4 = (f32[8]{0:T(128)S(1)}, f32[8]{0:T(128)}, u32[]{:S(2)}) copy-start(f32[8]{0:T(128)} %param.15) | copy-start | bytes 100
  3.1 9.5 %collective-permute-start = (f32[24,128]{1,0:T(8,128)S(1)}, f32[24,128]{1,0:T(8,128)S(1)}, u32[]{:S(2)}, u32[]{:S(2)}) collective-permute-start(f32[24,128]{1,0:T(8,128)S(1)} %get-tuple-element.48), channel_id=1, source_target_pairs={{8,16},{16,8},{24,32},{32,24},{40,48},{48,40},{56,64},{64,56},{72,... | collective-permute-start | bytes 36872 | tf_op jit(solution)/shard_map/ppermute | solution.py:57
  9.3 3.3 %collective-permute-start.1 = (f32[24,128]{1,0:T(8,128)S(1)}, f32[24,128]{1,0:T(8,128)S(1)}, u32[]{:S(2)}, u32[]{:S(2)}) collective-permute-start(f32[24,128]{1,0:T(8,128)S(1)} %get-tuple-element.49), channel_id=1, source_target_pairs={{0,8},{8,0},{16,24},{24,16},{32,40},{40,32},{48,56},{56,48},{64,72... | collective-permute-start | bytes 36872 | tf_op jit(solution)/shard_map/ppermute | solution.py:57
  11.2 0.7 %copy-start.8 = (s32[64]{0:T(128)S(1)}, s32[64]{0:T(128)}, u32[]{:S(2)}) copy-start(s32[64]{0:T(128)} %param.21) | copy-start | bytes 772
  11.3 0.7 %copy-start.9 = (s32[64]{0:T(128)S(1)}, s32[64]{0:T(128)}, u32[]{:S(2)}) copy-start(s32[64]{0:T(128)} %param.22) | copy-start | bytes 772
  11.3 0.7 %copy-start.10 = (s32[64]{0:T(128)S(1)}, s32[64]{0:T(128)}, u32[]{:S(2)}) copy-start(s32[64]{0:T(128)} %param.23) | copy-start | bytes 772
  11.3 0.7 %copy-start.11 = (f32[8]{0:T(128)S(1)}, f32[8]{0:T(128)}, u32[]{:S(2)}) copy-start(f32[8]{0:T(128)} %param.16) | copy-start | bytes 100
  11.3 0.7 %copy-start.12 = (f32[8]{0:T(128)S(1)}, f32[8]{0:T(128)}, u32[]{:S(2)}) copy-start(f32[8]{0:T(128)} %param.17) | copy-start | bytes 100
  11.3 0.7 %copy-start.5 = (s32[64]{0:T(128)S(1)}, s32[64]{0:T(128)}, u32[]{:S(2)}) copy-start(s32[64]{0:T(128)} %param.18) | copy-start | bytes 772
  11.3 0.7 %copy-start.6 = (s32[64]{0:T(128)S(1)}, s32[64]{0:T(128)}, u32[]{:S(2)}) copy-start(s32[64]{0:T(128)} %param.19) | copy-start | bytes 772
  11.3 0.7 %copy-start.7 = (s32[64]{0:T(128)S(1)}, s32[64]{0:T(128)}, u32[]{:S(2)}) copy-start(s32[64]{0:T(128)} %param.20) | copy-start | bytes 772
  12.7 7.4 %collective-permute-start.2 = (f32[144,128]{1,0:T(8,128)S(1)}, f32[144,128]{1,0:T(8,128)S(1)}, u32[]{:S(2)}, u32[]{:S(2)}) collective-permute-start(f32[144,128]{1,0:T(8,128)S(1)} %get-tuple-element.54), channel_id=1, source_target_pairs={{1,2},{2,1},{3,4},{4,3},{5,6},{6,5},{9,10},{10,9},{11,12},{12,11},... | collective-permute-start | bytes 221192 | tf_op jit(solution)/shard_map/ppermute | solution.py:57
  13.4 8.7 %collective-permute-start.3 = (f32[144,128]{1,0:T(8,128)S(1)}, f32[144,128]{1,0:T(8,128)S(1)}, u32[]{:S(2)}, u32[]{:S(2)}) collective-permute-start(f32[144,128]{1,0:T(8,128)S(1)} %get-tuple-element.55), channel_id=1, source_target_pairs={{0,1},{1,0},{2,3},{3,2},{4,5},{5,4},{6,7},{7,6},{8,9},{9,8},{10,11... | collective-permute-start | bytes 221192 | tf_op jit(solution)/shard_map/ppermute | solution.py:57
  23.0 8.9 %collective-permute-start.4 = (f32[72,128]{1,0:T(8,128)S(1)}, f32[72,128]{1,0:T(8,128)S(1)}, u32[]{:S(2)}, u32[]{:S(2)}) collective-permute-start(f32[72,128]{1,0:T(8,128)S(1)} %get-tuple-element.65), channel_id=1, source_target_pairs={{8,16},{16,8},{24,32},{32,24},{40,48},{48,40},{56,64},{64,56},{72,... | collective-permute-start | bytes 110600 | tf_op jit(solution)/shard_map/ppermute | solution.py:57
  26.8 5.0 %collective-permute-start.5 = (f32[72,128]{1,0:T(8,128)S(1)}, f32[72,128]{1,0:T(8,128)S(1)}, u32[]{:S(2)}, u32[]{:S(2)}) collective-permute-start(f32[72,128]{1,0:T(8,128)S(1)} %get-tuple-element.66), channel_id=1, source_target_pairs={{0,8},{8,0},{16,24},{24,16},{32,40},{40,32},{48,56},{56,48},{64,72... | collective-permute-start | bytes 110600 | tf_op jit(solution)/shard_map/ppermute | solution.py:57
  32.6 8.6 %collective-permute-start.6 = (f32[24,128]{1,0:T(8,128)S(1)}, f32[24,128]{1,0:T(8,128)S(1)}, u32[]{:S(2)}, u32[]{:S(2)}) collective-permute-start(f32[24,128]{1,0:T(8,128)S(1)} %get-tuple-element.68), channel_id=1, source_target_pairs={{8,16},{16,8},{24,32},{32,24},{40,48},{48,40},{56,64},{64,56},{72,... | collective-permute-start | bytes 36872 | tf_op jit(solution)/shard_map/ppermute | solution.py:57
  36.4 4.8 %collective-permute-start.7 = (f32[24,128]{1,0:T(8,128)S(1)}, f32[24,128]{1,0:T(8,128)S(1)}, u32[]{:S(2)}, u32[]{:S(2)}) collective-permute-start(f32[24,128]{1,0:T(8,128)S(1)} %get-tuple-element.69), channel_id=1, source_target_pairs={{0,8},{8,0},{16,24},{24,16},{32,40},{40,32},{48,56},{56,48},{64,72... | collective-permute-start | bytes 36872 | tf_op jit(solution)/shard_map/ppermute | solution.py:57
  55.0 8.9 %collective-permute-start.8 = (f32[72,128]{1,0:T(8,128)S(1)}, f32[72,128]{1,0:T(8,128)S(1)}, u32[]{:S(2)}, u32[]{:S(2)}) collective-permute-start(f32[72,128]{1,0:T(8,128)S(1)} %get-tuple-element.80), channel_id=1, source_target_pairs={{8,16},{16,8},{24,32},{32,24},{40,48},{48,40},{56,64},{64,56},{72,... | collective-permute-start | bytes 110600 | tf_op jit(solution)/shard_map/ppermute | solution.py:57
  59.0 4.9 %collective-permute-start.9 = (f32[72,128]{1,0:T(8,128)S(1)}, f32[72,128]{1,0:T(8,128)S(1)}, u32[]{:S(2)}, u32[]{:S(2)}) collective-permute-start(f32[72,128]{1,0:T(8,128)S(1)} %get-tuple-element.81), channel_id=1, source_target_pairs={{0,8},{8,0},{16,24},{24,16},{32,40},{40,32},{48,56},{56,48},{64,72... | collective-permute-start | bytes 110600 | tf_op jit(solution)/shard_map/ppermute | solution.py:57

commit v4 on v3

--- a/solution.py
+++ b/solution.py
@@ -18,6 +18,8 @@
 PIECES = 8 * BLOCK // LANES
 MSG = PIECES * MCAP + SUB
 DEPTHS = CX + 3
+BRICK = DEPTHS * SUB
+PAIR = (2 * CX + 4) * SUB
 PACK = 96
 NEAR = 32
 SHARE = 22
@@ -105,9 +107,9 @@
     return [(column == first + b).astype(F32).astype(BF16) for b in range(4)]
 
 
-def row_masks(depth_of):
+def row_masks(depth_of, count=CX):
     depth = jnp.broadcast_to(depth_of, (SUB, LANES))
-    return [depth == index for index in range(CX)]
+    return [depth == index for index in range(count)]
 
 
 def scaled(terms, materials, tables_ref):
@@ -150,27 +152,16 @@
 def spread_rows(terms, masks, left_ref):
     zero = jnp.zeros((SUB, LANES), F32)
     for b in range(4):
-        for x in range(ROWS // SUB):
+        for x in range(left_ref.shape[0] // SUB):
             total = zero
             for a in range(4):
-                if 0 <= x - a < CX:
+                if 0 <= x - a < len(masks):
                     total = total + jnp.where(masks[x - a], terms[a][b], zero)
             left_ref[x * SUB : (x + 1) * SUB, b * LANES : (b + 1) * LANES] = total
 
 
 def parity(axis):
     return (lax.axis_index(axis) & 1) == 1
-
-
-def emit_sums(left_ref, onehots, more_ref, sums_ref, inner_ref, outer_ref):
-    sums = product(halves(left_ref[...]), jnp.concatenate(onehots, axis=1), NT)
-    if more_ref is not None:
-        sums = sums + more_ref[...]
-    sums_ref[...] = sums
-    odd = parity("gx")
-    bottom, top = (sums[0:HALO], sums[TOP : TOP + HALO])
-    inner_ref[...] = jnp.where(odd, bottom, top)
-    outer_ref[...] = jnp.where(odd, top, bottom)
 
 
 def spread_table(table_ref, rows_ref, first):
@@ -202,7 +193,11 @@
     terms = [[terms_ref[(4 * a + b) * SUB : (4 * a + b + 1) * SUB, :] for b in range(4)] for a in range(4)]
     terms = scaled(terms, materials, density_rows_ref)
     spread_rows(terms, row_masks(cells >> 5), left_ref)
-    emit_sums(left_ref, column_onehot(cells & (CY - 1)), None, sums_ref, inner_ref, outer_ref)
+    sums = product(halves(left_ref[...]), jnp.concatenate(column_onehot(cells & (CY - 1)), axis=1), NT)
+    sums_ref[...] = sums
+    to_inner, to_outer = by_side(sums[0:HALO], sums[TOP : TOP + HALO], parity("gx"))
+    inner_ref[...] = to_inner
+    outer_ref[...] = to_outer
 
 
 def join_lists(*refs):
@@ -342,11 +337,22 @@
         put_pieces(ref, 2 * SUB, rows_ref[first : first + movers, :])
 
 
-def merge_two(sums_ref, from_outer_ref, from_inner_ref, near_ref, slots_ref, merged_ref, slot_ref):
-    merge_rows(sums_ref, from_outer_ref, from_inner_ref, merged_ref)
-    slot_ref[PACK - SUB : PACK, :] = jnp.zeros((SUB, LANES), F32)
-    for x in range(DEPTHS):
-        slot_ref[5 * x : 5 * x + 5, :] = merged_ref[x * SUB : x * SUB + 5, :]
+def merge_far(own_ref, from_far_ref, near_nodes_ref, cross_tags_ref, merged_ref, halo_ref):
+    del near_nodes_ref, cross_tags_ref
+    merged = own_ref[...] + from_far_ref[0:PACK, :]
+    merged_ref[...] = merged
+    low = jnp.where(iota((2 * SUB, LANES), 0) < 15, merged[0 : 2 * SUB], 0.0)
+    halo_ref[...] = jnp.where(parity("gx"), low, merged[PACK - 2 * SUB : PACK])
+
+
+def merge_two(sums_ref, from_near_ref, near_ref, new_meta_ref, slots_ref, slot_ref):
+    del new_meta_ref
+    odd = parity("gx")
+    from_near = from_near_ref[...]
+    slot_ref[...] = sums_ref[...]
+    last = PACK - 2 * SUB
+    slot_ref[0 : 2 * SUB] = sums_ref[0 : 2 * SUB] + jnp.where(odd, from_near, 0.0)
+    slot_ref[last:PACK] = sums_ref[last:PACK] + jnp.where(odd, 0.0, from_near)
     lane = iota((NEAR, LANES), 1)
     near = near_ref[...]
     for third in range(PACK // NEAR):
@@ -475,14 +481,21 @@
         ref[MSG - SUB : MSG, :] = jnp.where(lane < MCAP, tag, 0.0)
 
 
+def own_and_far_depth():
+    odd = lax.axis_index("gx") & 1
+    return (CX - CX * odd, CX * odd)
+
+
 def departures(cells, materials, lists):
-    home, _, _ = home_and_steps()
+    home, step_x, _ = home_and_steps()
     slots, dests, cell = (lists[0:1], lists[1:2], lists[2:3])
     moving = (dests >= 0) & (dests != home)
-    low, high = (dests == home - 1, dests == home + 1)
-    cross = jnp.where(low | high, 1, 0)
-    column = (cell & (CY - 1)) + jnp.where(high, 2 * CY, 0)
-    entries = small_rows(jnp.where(moving, 1, 0), cross, cross * (cell >> 5), cross * column)
+    low, high, far = (dests == home - 1, dests == home + 1, dests == home - step_x)
+    carried = jnp.where(low | high | far, 1, 0)
+    own, other = own_and_far_depth()
+    depth = (cell >> 5) + jnp.where(far, other, own)
+    column = (cell & (CY - 1)) + jnp.where(high, 2 * CY, jnp.where(far, CY, 0))
+    entries = small_rows(jnp.where(moving, 1, 0), carried, carried * depth, carried * column)
     found = turned_to(entries, holding(slots)).astype(jnp.int32)
     gone, across = (found[0:1] > 0, found[1:2] > 0)
     sub = iota((SUB, LANES), 0)
@@ -494,7 +507,7 @@
     )
     target = jnp.where(
         sub == 0,
-        wide(jnp.where(across, found[2:3], cells >> 5)),
+        wide(jnp.where(across, found[2:3], (cells >> 5) + own)),
         jnp.where(
             sub == 1,
             wide(jnp.where(across, found[3:4], (cells & (CY - 1)) + CY)),
@@ -551,12 +564,15 @@
             nodes_ref[row : row + 2, :] = near[a][b][1:3]
 
 
-def sums_kept(fresh_ref, target_ref, tables_ref, nodes_ref, chosen_ref, sums_ref, near_ref, left_ref):
+def sums_kept(fresh_ref, target_ref, tables_ref, sums_ref, left_ref):
     depth, column, materials = (target_ref[0:1, :], target_ref[1:2, :], target_ref[2:3, :])
     load = lambda c, k: rows_at(fresh_ref, c, k, BLOCK)
     terms = scaled(node_terms(load, BLOCK // SUB), materials, tables_ref)
-    spread_rows(terms, row_masks(depth), left_ref)
+    spread_rows(terms, row_masks(depth, 2 * CX), left_ref)
     sums_ref[...] = product(halves(left_ref[...]), jnp.concatenate(column_onehot(column), axis=1), NT)
+
+
+def near_cross(nodes_ref, chosen_ref, near_ref):
     near_ref[...] = product(halves(nodes_ref[...]), chosen_ref[...].astype(BF16), NT)
 
 
@@ -597,22 +613,47 @@
     return packed.astype(jnp.int32) - (iota((SUB, LANES), 0) == 1).astype(jnp.int32)
 
 
+def put_packed(ref, sums):
+    ref[PACK - SUB : PACK, :] = jnp.zeros((SUB, LANES), F32)
+    for x in range(DEPTHS):
+        ref[5 * x : 5 * x + 5, :] = sums[x * SUB : x * SUB + 5]
+
+
 def sums_two(
-    kept_sums_ref, xo_ref, xi_ref, tables_ref,
-    sums_ref, inner_ref, outer_ref, turned_ref, new_meta_ref,
-    left_ref, wide_ref,
+    kept_sums_ref, from_near_ref, to_far_ref, tables_ref,
+    own_ref, message_ref,
+    left_ref, wide_ref, turned_ref,
 ):
-    new_meta = arrived_tags(xi_ref[MSG - SUB : MSG, :], xo_ref[MSG - SUB : MSG, :])
-    new_meta_ref[...] = new_meta
-    low, high = by_side(xi_ref[0 : MSG - SUB, :], xo_ref[0 : MSG - SUB, :], parity("gx"))
-    packed_blocks(jnp.concatenate([joined(low), joined(high)], axis=0), wide_ref, turned_ref)
-    cells, materials = (new_meta[0:1], new_meta[1:2])
+    tags = repeated(from_near_ref[MSG - SUB : MSG, :], MCAP).astype(jnp.int32)
+    cells, materials = (tags[0:1], tags[1:2] - 1)
+    packed_blocks(joined(from_near_ref[0 : MSG - SUB, :]), wide_ref, turned_ref)
     stride = turned_ref.shape[0] // 8
     load = lambda c, k: rows_at(turned_ref, c, k, stride)
     terms = scaled(node_terms(load, stride // SUB), materials, tables_ref)
-    spread_rows(terms, row_masks(cells >> 5), left_ref)
-    onehots = column_onehot((cells & (CY - 1)) + CY)
-    emit_sums(left_ref, onehots, kept_sums_ref, sums_ref, inner_ref, outer_ref)
+    own, _ = own_and_far_depth()
+    spread_rows(terms, row_masks((cells >> 5) + own, 2 * CX), left_ref)
+    onehots = jnp.concatenate(column_onehot((cells & (CY - 1)) + CY), axis=1)
+    sums = product(halves(left_ref[...]), onehots, NT) + kept_sums_ref[...]
+    odd = parity("gx")
+    first, second = (sums[0:BRICK], sums[CX * SUB : CX * SUB + BRICK])
+    put_packed(own_ref, jnp.where(odd, first, second))
+    put_packed(message_ref, jnp.where(odd, second, first))
+    message_ref[PACK : PACK + MSG, :] = to_far_ref[...]
+
+
+def arrange_depth(from_near_ref, from_far_ref, turned_ref, new_meta_ref, wide_ref):
+    rows, tags = (slice(0, MSG - SUB), slice(MSG - SUB, MSG))
+    far = from_far_ref[PACK : PACK + MSG, :]
+    new_meta_ref[...] = arrived_tags(from_near_ref[tags, :], far[tags])
+    low, high = by_side(from_near_ref[rows, :], far[rows], parity("gx"))
+    packed_blocks(jnp.concatenate([joined(low), joined(high)], axis=0), wide_ref, turned_ref)
+
+
+def arrange_cross(yo_ref, yi_ref, cross_ref, tags_ref, wide_ref):
+    low, high = by_side(yi_ref[...], yo_ref[...], parity("gy"))
+    tags_ref[...] = low[SUB : 2 * SUB] + pltpu.roll(high[SUB : 2 * SUB], 2 * MCAP, 1)
+    rows = jnp.concatenate([joined(low[2 * SUB :]), joined(high[2 * SUB :])], axis=0)
+    packed_blocks(rows, wide_ref, cross_ref)
 
 
 def advance_two(
@@ -644,9 +685,9 @@
 
 
 def settle(
-    fresh_ref, old_meta_ref, velocity_ref, turned_ref, new_meta_ref, tables_ref, slots_ref, yo_ref, yi_ref,
+    fresh_ref, old_meta_ref, velocity_ref, turned_ref, new_meta_ref, tables_ref, slots_ref, cross_ref, tags_ref,
     rows_ref, tail_ref,
-    wide_ref, cross_ref, middle_ref, out_ref, small_ref,
+    wide_ref, middle_ref, out_ref, small_ref,
 ):
     alive = jnp.broadcast_to(old_meta_ref[1:2, :], fresh_ref.shape) >= 0
     rows_ref[0:LANES, :] = jnp.where(alive, fresh_ref[...], 0.0).T
@@ -665,9 +706,8 @@
 
     gy = lax.axis_index("gy")
     odd = parity("gy")
-    low, high = by_side(yi_ref[...], yo_ref[...], odd)
     lane = iota((SUB, LANES), 1)
-    tags = low[SUB : 2 * SUB] + pltpu.roll(high[SUB : 2 * SUB], 2 * MCAP, 1)
+    tags = tags_ref[...]
     tail = jnp.zeros((SUB, LANES), F32)
     for start, shift in ((32, 32), (48, 16), (96, 80), (112, 64)):
         tail = jnp.where((lane >= start) & (lane < start + MCAP), pltpu.roll(tags, shift, 1), tail)
@@ -689,8 +729,6 @@
         row = 2 * (4 * a + b) + component
         return nodes[row : row + 1]
 
-    rows = jnp.concatenate([joined(low[2 * SUB :]), joined(high[2 * SUB :])], axis=0)
-    packed_blocks(rows, wide_ref, cross_ref)
     half = cross_ref.shape[0] // 8
     kinds = tags[1:2]
 
@@ -828,23 +866,39 @@
         (IN_VMEM,) * 8,
         turned, meta, merged, cross_far, cross_near, tables, chosen_a, tags_a,
     )
-    arrived = along_depth(far, near)
-    kept_sums, near_nodes = call(
-        sums_kept, (grid, near_form), (left,), (IN_VMEM,) * 5, fresh, target, tables, nodes, chosen
-    )
-    sums, inner, outer, turned, new_meta = call(
+    from_near = swap(near, "gx", 0)
+    pair_form = ((PAIR, LANES), F32)
+    pair_left = pltpu.VMEM((PAIR, 4 * LANES), F32)
+    (kept_sums,) = call(sums_kept, (pair_form,), (pair_left,), (IN_VMEM,) * 3, fresh, target, tables)
+    (near_nodes,) = call(near_cross, (near_form,), (), (IN_VMEM,) * 2, nodes, chosen)
+    packed_form = ((PACK, LANES), F32)
+    own, far_message = call(
         sums_two,
-        (grid, halo, halo, quarter_form, tags),
-        (left, scratch(turned_form)),
+        (packed_form, ((PACK + MSG, LANES), F32)),
+        (pair_left, scratch(turned_form), pltpu.VMEM((wide // 8, LANES), F32)),
         (IN_VMEM,) * 4,
-        kept_sums, *arrived, tables,
+        kept_sums, from_near, far, tables,
+    )
+    from_far = swap(far_message, "gx", 1)
+    cross, cross_tags = call(
+        arrange_cross, (half_form, tile), (scratch(turned_form),), (IN_VMEM,) * 2, cross_far, cross_near
+    )
+    merged, halo_message = call(
+        merge_far,
+        (packed_form, ((2 * SUB, LANES), F32)),
+        (),
+        (IN_VMEM,) * 4,
+        own, from_far, near_nodes, cross_tags,
+    )
+    turned, new_meta = call(
+        arrange_depth, (quarter_form, tags), (scratch(turned_form),), (IN_VMEM,) * 2, from_near, from_far
     )
     (slots,) = call(
         merge_two,
         (slots_form,),
-        (scratch(grid), pltpu.VMEM((PACK, LANES), F32)),
+        (scratch(packed_form),),
         (IN_VMEM,) * 4,
-        sums, *along_depth(outer, inner), near_nodes,
+        merged, swap(halo_message, "gx", 0), near_nodes, new_meta,
     )
     slots = lax.all_to_all(slots, "gy", 0, 0)
     fresh, velocity, far, near = call(
@@ -863,11 +917,10 @@
             scratch(turned_form),
             scratch(half_form),
             scratch(half_form),
-            scratch(half_form),
             scratch(quarter_form),
         ),
         (IN_VMEM,) * 9,
-        fresh, kept_b, velocity, turned, new_meta, tables, slots, cross_far, cross_near,
+        fresh, kept_b, velocity, turned, new_meta, tables, slots, cross, cross_tags,
     )
     final_points, final_cells, final_mats = call(
         assemble,

time: 65.2 us -> 64.2 us (0.985)
  starting transfers between devices: 32.3 us -> 27.1 us
  waiting for transfers between devices: 9.28 us -> 11.9 us
  blocking collectives: 12.8 us -> 13.8 us
    ppermute x10 -> x9, starting transfers between devices: 32.3 us -> 27.1 us  [swap(): return lax.ppermute(value, axis, pairs)]
    ppermute x10 -> x9, waiting for transfers between devices: 9.28 us -> 11.9 us  [swap(): return lax.ppermute(value, axis, pairs)]
    all_to_all x1, blocking collectives: 12.8 us -> 13.8 us  [shards(): slots = lax.all_to_all(slots, 'gy', 0, 0)]
    pallas_call x13 -> x17, Pallas kernels: 7.19 us -> 7.7 us  [call(): pl.pallas_call(kernel, out_shape=tuple((jax.ShapeDtypeStruct(shape, dtype...]
  transfers between devices with their start and end apart: 10 -> 9, of which waited for: 4 -> 5; matrix products, arithmetic and copies ran while one was open for 0% -> 0% of each run, Pallas kernels for 4% -> 5%
where the time goes in v4:
time: 64.2 us; the launch traced here: 63.8 us
  starting transfers between devices  27.1 us (42%)
  blocking collectives  13.8 us (21%)
  waiting for transfers between devices  11.9 us (19%)
  Pallas kernels  7.7 us (12%)
  local copies, waits for them, and re-layouts  2.31 us (4%)
  between operations  0.91 us (1%)
    ppermute x9, starting transfers between devices, swap(): return lax.ppermute(value, axis, pairs)  27.1 us
    all_to_all x1, blocking collectives, shards(): slots = lax.all_to_all(slots, 'gy', 0, 0)  13.8 us
    ppermute x9, waiting for transfers between devices, swap(): return lax.ppermute(value, axis, pairs)  11.9 us
    pallas_call x17, Pallas kernels, call(): pl.pallas_call(kernel, out_shape=tuple((jax.ShapeDtypeStruct(shape, dtype...  7.7 us
    unnamed x26, local copies, waits for them, and re-layouts  2.31 us
  transfers between devices with their start and end apart: 9, of which 5 were waited for; matrix products, arithmetic and copies ran while one was open for 0% of the time, Pallas kernels for 5%

profile of v4, /device:TPU:384, one launch (start us, length us, event | category | flops | bytes accessed | tf_op | source)
XLA Modules:
  0.0 63.8 jit_solution(3278085232988080645)
XLA Ops:
  0.6 0.9 %copy-done = f32[128,512]{1,0:T(8,128)S(1)} copy-done((f32[128,512]{1,0:T(8,128)S(1)}, f32[128,512]{1,0:T(8,128)}, u32[]{:S(2)}) %copy-start) | copy-done | bytes 262168
  1.6 0.5 shard_map.139
  2.1 0.6 copy-done.2
  2.8 0.3 shard_map.140
  3.1 6.2 %collective-permute-start = (f32[24,128]{1,0:T(8,128)S(1)}, f32[24,128]{1,0:T(8,128)S(1)}, u32[]{:S(2)}, u32[]{:S(2)}) collective-permute-start(f32[24,128]{1,0:T(8,128)S(1)} %get-tuple-element.49), channel_id=1, source_target_pairs={{8,16},{16,8},{24,32},{32,24},{40,48},{48,40},{56,64},{64,56},{72,... | collective-permute-start | bytes 36872 | tf_op jit(solution)/shard_map/ppermute | solution.py:59
  9.3 1.9 %collective-permute-start.1 = (f32[24,128]{1,0:T(8,128)S(1)}, f32[24,128]{1,0:T(8,128)S(1)}, u32[]{:S(2)}, u32[]{:S(2)}) collective-permute-start(f32[24,128]{1,0:T(8,128)S(1)} %get-tuple-element.50), channel_id=1, source_target_pairs={{0,8},{8,0},{16,24},{24,16},{32,40},{40,32},{48,56},{56,48},{64,72... | collective-permute-start | bytes 36872 | tf_op jit(solution)/shard_map/ppermute | solution.py:59
  11.3 0.6 copy-done.8
  12.1 0.5 shard_map.142
  12.6 0.1 shard_map.143
  12.7 0.7 %collective-permute-start.2 = (f32[144,128]{1,0:T(8,128)S(1)}, f32[144,128]{1,0:T(8,128)S(1)}, u32[]{:S(2)}, u32[]{:S(2)}) collective-permute-start(f32[144,128]{1,0:T(8,128)S(1)} %get-tuple-element.55), channel_id=1, source_target_pairs={{1,2},{2,1},{3,4},{4,3},{5,6},{6,5},{9,10},{10,9},{11,12},{12,11},... | collective-permute-start | bytes 221192 | tf_op jit(solution)/shard_map/ppermute | solution.py:59
  13.4 6.1 %collective-permute-start.3 = (f32[144,128]{1,0:T(8,128)S(1)}, f32[144,128]{1,0:T(8,128)S(1)}, u32[]{:S(2)}, u32[]{:S(2)}) collective-permute-start(f32[144,128]{1,0:T(8,128)S(1)} %get-tuple-element.56), channel_id=1, source_target_pairs={{0,1},{1,0},{2,3},{3,2},{4,5},{5,4},{6,7},{7,6},{8,9},{9,8},{10,11... | collective-permute-start | bytes 221192 | tf_op jit(solution)/shard_map/ppermute | solution.py:59
  19.5 0.6 shard_map.144
  20.1 2.1 %collective-permute-done.3.yi_ref = f32[144,128]{1,0:T(8,128)S(1)} collective-permute-done((f32[144,128]{1,0:T(8,128)S(1)}, f32[144,128]{1,0:T(8,128)S(1)}, u32[]{:S(2)}, u32[]{:S(2)}) %collective-permute-start.3) | collective-permute-done | bytes 73760 | tf_op jit(solution)/shard_map/ppermute | solution.py:59
  22.2 0.8 %shard_map.145 = (f32[512,128]{1,0:T(8,128)S(1)}, f32[32,128]{1,0:T(8,128)S(1)}, f32[72,128]{1,0:T(8,128)S(1)}, f32[72,128]{1,0:T(8,128)S(1)}) custom-call(f32[512,128]{1,0:T(8,128)S(1)} %get-tuple-element.45.turned_ref, s32[8,128]{1,0:T(8,128)S(1)} %get-tuple-element.47.meta_ref, f32[160,128]{1,0:T(8,128)S(1)} %get-tuple-element.54.merged_ref, ...), custom_call_target="tpu_custom_call" | custom-call | flops 4194304 | bytes 524288 | tf_op jit(solution)/shard_map/pallas_call | solution.py:43
  23.0 1.9 %collective-permute-start.4 = (f32[72,128]{1,0:T(8,128)S(1)}, f32[72,128]{1,0:T(8,128)S(1)}, u32[]{:S(2)}, u32[]{:S(2)}) collective-permute-start(f32[72,128]{1,0:T(8,128)S(1)} %get-tuple-element.63), channel_id=1, source_target_pairs={{0,8},{8,0},{16,24},{24,16},{32,40},{40,32},{48,56},{56,48},{64,72... | collective-permute-start | bytes 110600 | tf_op jit(solution)/shard_map/ppermute | solution.py:59
  24.9 0.8 %shard_map.146.kept_sums_ref = f32[288,128]{1,0:T(8,128)S(1)} custom-call(f32[512,128]{1,0:T(8,128)S(1)} %get-tuple-element.60.fresh_ref.kept_ref, s32[8,128]{1,0:T(8,128)S(1)} %get-tuple-element.62.target_ref, f32[24,128]{1,0:T(8,128)S(1)} %get-tuple-element.57.tables_ref), custom_call_target="tpu_custom_call" | custom-call | flops 4194304 | bytes 524288 | tf_op jit(solution)/shard_map/pallas_call | solution.py:43
  25.7 0.4 collective-permute-done.4.from_near_ref
  26.1 0.7 %shard_map.147 = (f32[96,128]{1,0:T(8,128)S(1)}, f32[168,128]{1,0:T(8,128)S(1)}) custom-call(f32[288,128]{1,0:T(8,128)S(1)} %shard_map.146.kept_sums_ref, f32[72,128]{1,0:T(8,128)S(1)} %collective-permute-done.4.from_near_ref, f32[72,128]{1,0:T(8,128)S(1)} %get-tuple-element.64.to_far_ref, f32[24,128]{1,0:T(8,128)S(1)} %get-tuple-element.57.tables_ref), custom_call_target="tpu_custom_call" | custom-call | flops 4194304 | bytes 524288 | tf_op jit(solution)/shard_map/pallas_call | solution.py:43
  26.8 3.8 %collective-permute-start.5 = (f32[168,128]{1,0:T(8,128)S(1)}, f32[168,128]{1,0:T(8,128)S(1)}, u32[]{:S(2)}, u32[]{:S(2)}) collective-permute-start(f32[168,128]{1,0:T(8,128)S(1)} %get-tuple-element.66), channel_id=1, source_target_pairs={{8,16},{16,8},{24,32},{32,24},{40,48},{48,40},{56,64},{64,56},{72,... | collective-permute-start | bytes 258056 | tf_op jit(solution)/shard_map/ppermute | solution.py:59
  30.6 0.1 shard_map.148.near_nodes_ref.near_ref
  30.7 0.2 shard_map.149
  31.0 5.2 %collective-permute-done.5.from_far_ref = f32[168,128]{1,0:T(8,128)S(1)} collective-permute-done((f32[168,128]{1,0:T(8,128)S(1)}, f32[168,128]{1,0:T(8,128)S(1)}, u32[]{:S(2)}, u32[]{:S(2)}) %collective-permute-start.5) | collective-permute-done | bytes 86048 | tf_op jit(solution)/shard_map/ppermute | solution.py:59
  36.2 1.9 %collective-permute-start.6 = (f32[16,128]{1,0:T(8,128)S(1)}, f32[16,128]{1,0:T(8,128)S(1)}, u32[]{:S(2)}, u32[]{:S(2)}) collective-permute-start(f32[16,128]{1,0:T(8,128)S(1)} %get-tuple-element.71), channel_id=1, source_target_pairs={{0,8},{8,0},{16,24},{24,16},{32,40},{40,32},{48,56},{56,48},{64,72... | collective-permute-start | bytes 24584 | tf_op jit(solution)/shard_map/ppermute | solution.py:59
  38.1 0.3 shard_map.151
  38.4 0.9 %collective-permute-done.6.from_near_ref = f32[16,128]{1,0:T(8,128)S(1)} collective-permute-done((f32[16,128]{1,0:T(8,128)S(1)}, f32[16,128]{1,0:T(8,128)S(1)}, u32[]{:S(2)}, u32[]{:S(2)}) %collective-permute-start.6) | collective-permute-done | bytes 8224 | tf_op jit(solution)/shard_map/ppermute | solution.py:59
  39.4 13.8 %all_to_all.5.slots_ref = f32[8,96,128]{2,1,0:T(8,128)S(1)} all-to-all(f32[8,96,128]{2,1,0:T(8,128)S(1)} %shard_map.152), channel_id=1, replica_groups=mesh['gx'=64,'gy'=8] {'gy'}, dimensions={0} | all-to-all | bytes 786432 | tf_op jit(solution)/shard_map/all_to_all | solution.py:903
  53.2 0.9 %shard_map.153 = (f32[512,128]{1,0:T(8,128)S(1)}, f32[160,128]{1,0:T(8,128)S(1)}, f32[72,128]{1,0:T(8,128)S(1)}, f32[72,128]{1,0:T(8,128)S(1)}) custom-call(f32[512,128]{1,0:T(8,128)S(1)} %get-tuple-element.60.fresh_ref.kept_ref, s32[8,128]{1,0:T(8,128)S(1)} %get-tuple-element.61.meta_ref, f32[8,96,128]{2,1,0:T(8,128)S(1)} %all_to_all.5.slots_ref, ...), custom_call_target="tpu_custom_call" | custom-call | flops 4194304 | bytes 524288 | tf_op jit(solution)/shard_map/pallas_call | solution.py:43
  54.1 2.6 %collective-permute-start.7 = (f32[72,128]{1,0:T(8,128)S(1)}, f32[72,128]{1,0:T(8,128)S(1)}, u32[]{:S(2)}, u32[]{:S(2)}) collective-permute-start(f32[72,128]{1,0:T(8,128)S(1)} %get-tuple-element.82), channel_id=1, source_target_pairs={{8,16},{16,8},{24,32},{32,24},{40,48},{48,40},{56,64},{64,56},{72,... | collective-permute-start | bytes 110600 | tf_op jit(solution)/shard_map/ppermute | solution.py:59
  56.7 1.9 %collective-permute-start.8 = (f32[72,128]{1,0:T(8,128)S(1)}, f32[72,128]{1,0:T(8,128)S(1)}, u32[]{:S(2)}, u32[]{:S(2)}) collective-permute-start(f32[72,128]{1,0:T(8,128)S(1)} %get-tuple-element.83), channel_id=1, source_target_pairs={{0,8},{8,0},{16,24},{24,16},{32,40},{40,32},{48,56},{56,48},{64,72... | collective-permute-start | bytes 110600 | tf_op jit(solution)/shard_map/ppermute | solution.py:59
  58.6 0.9 %shard_map.154 = (f32[256,512]{1,0:T(8,128)S(1)}, s32[8,128]{1,0:T(8,128)S(1)}) custom-call(f32[512,128]{1,0:T(8,128)S(1)} %get-tuple-element.75.fresh_ref, s32[8,128]{1,0:T(8,128)S(1)} %get-tuple-element.76.old_meta_ref, f32[160,128]{1,0:T(8,128)S(1)} %get-tuple-element.77.velocity_ref, f32[128,128]{1,0:T(8,128)S(1)} %get-tuple-element.78.turned_ref, ...), custom_call_target="tpu_custom_call" | custom-call | flops 4194304 | bytes 524288 | tf_op jit(solution)/shard_map/pallas_call | solution.py:43
  59.6 3.4 %collective-permute-done.7.xo_ref = f32[72,128]{1,0:T(8,128)S(1)} collective-permute-done((f32[72,128]{1,0:T(8,128)S(1)}, f32[72,128]{1,0:T(8,128)S(1)}, u32[]{:S(2)}, u32[]{:S(2)}) %collective-permute-start.7) | collective-permute-done | bytes 36896 | tf_op jit(solution)/shard_map/ppermute | solution.py:59
  63.0 0.8 %shard_map.155 = (f32[256,512]{1,0:T(8,128)}, s32[2,128]{1,0:T(2,128)}, s32[2,128]{1,0:T(2,128)}) custom-call(f32[256,512]{1,0:T(8,128)S(1)} %get-tuple-element.80.part_ref, s32[8,128]{1,0:T(8,128)S(1)} %get-tuple-element.76.old_meta_ref, s32[8,128]{1,0:T(8,128)S(1)} %get-tuple-element.81.tail_ref, f32[72,128]{1,0:T(8,128)S(1)} %collective-permute-done.7.xo_ref, ...), custom_call_target="tpu_custom_call" | custom-call | flops 4194304 | bytes 524288 | tf_op jit(solution)/shard_map/pallas_call | solution.py:43
  (30 shorter events, 0.4 us)
Async XLA Ops:
  0.6 1.0 %copy-start = (f32[128,512]{1,0:T(8,128)S(1)}, f32[128,512]{1,0:T(8,128)}, u32[]{:S(2)}) copy-start(f32[128,512]{1,0:T(8,128)} %points_ref.3) | copy-start | bytes 786436
  1.6 10.5 %copy-start.1 = (f32[128,512]{1,0:T(8,128)S(1)}, f32[128,512]{1,0:T(8,128)}, u32[]{:S(2)}) copy-start(f32[128,512]{1,0:T(8,128)} %points_ref.3) | copy-start | bytes 786436
  2.1 0.7 %copy-start.2 = (s32[128]{0:T(128)S(1)}, s32[128]{0:T(128)}, u32[]{:S(2)}) copy-start(s32[128]{0:T(128)} %param.13) | copy-start | bytes 1540
  2.1 0.7 %copy-start.3 = (s32[128]{0:T(128)S(1)}, s32[128]{0:T(128)}, u32[]{:S(2)}) copy-start(s32[128]{0:T(128)} %param.14) | copy-start | bytes 1540
  2.1 0.7 %copy-start.4 = (f32[8]{0:T(128)S(1)}, f32[8]{0:T(128)}, u32[]{:S(2)}) copy-start(f32[8]{0:T(128)} %param.15) | copy-start | bytes 100
  3.1 9.5 %collective-permute-start = (f32[24,128]{1,0:T(8,128)S(1)}, f32[24,128]{1,0:T(8,128)S(1)}, u32[]{:S(2)}, u32[]{:S(2)}) collective-permute-start(f32[24,128]{1,0:T(8,128)S(1)} %get-tuple-element.49), channel_id=1, source_target_pairs={{8,16},{16,8},{24,32},{32,24},{40,48},{48,40},{56,64},{64,56},{72,... | collective-permute-start | bytes 36872 | tf_op jit(solution)/shard_map/ppermute | solution.py:59
  9.3 3.3 %collective-permute-start.1 = (f32[24,128]{1,0:T(8,128)S(1)}, f32[24,128]{1,0:T(8,128)S(1)}, u32[]{:S(2)}, u32[]{:S(2)}) collective-permute-start(f32[24,128]{1,0:T(8,128)S(1)} %get-tuple-element.50), channel_id=1, source_target_pairs={{0,8},{8,0},{16,24},{24,16},{32,40},{40,32},{48,56},{56,48},{64,72... | collective-permute-start | bytes 36872 | tf_op jit(solution)/shard_map/ppermute | solution.py:59
  11.2 0.7 %copy-start.8 = (s32[64]{0:T(128)S(1)}, s32[64]{0:T(128)}, u32[]{:S(2)}) copy-start(s32[64]{0:T(128)} %param.21) | copy-start | bytes 772
  11.3 0.7 %copy-start.9 = (s32[64]{0:T(128)S(1)}, s32[64]{0:T(128)}, u32[]{:S(2)}) copy-start(s32[64]{0:T(128)} %param.22) | copy-start | bytes 772
  11.3 0.7 %copy-start.10 = (s32[64]{0:T(128)S(1)}, s32[64]{0:T(128)}, u32[]{:S(2)}) copy-start(s32[64]{0:T(128)} %param.23) | copy-start | bytes 772
  11.3 0.7 %copy-start.11 = (f32[8]{0:T(128)S(1)}, f32[8]{0:T(128)}, u32[]{:S(2)}) copy-start(f32[8]{0:T(128)} %param.16) | copy-start | bytes 100
  11.3 0.7 %copy-start.12 = (f32[8]{0:T(128)S(1)}, f32[8]{0:T(128)}, u32[]{:S(2)}) copy-start(f32[8]{0:T(128)} %param.17) | copy-start | bytes 100
  11.3 0.7 %copy-start.5 = (s32[64]{0:T(128)S(1)}, s32[64]{0:T(128)}, u32[]{:S(2)}) copy-start(s32[64]{0:T(128)} %param.18) | copy-start | bytes 772
  11.3 0.7 %copy-start.6 = (s32[64]{0:T(128)S(1)}, s32[64]{0:T(128)}, u32[]{:S(2)}) copy-start(s32[64]{0:T(128)} %param.19) | copy-start | bytes 772
  11.3 0.7 %copy-start.7 = (s32[64]{0:T(128)S(1)}, s32[64]{0:T(128)}, u32[]{:S(2)}) copy-start(s32[64]{0:T(128)} %param.20) | copy-start | bytes 772
  12.7 7.4 %collective-permute-start.2 = (f32[144,128]{1,0:T(8,128)S(1)}, f32[144,128]{1,0:T(8,128)S(1)}, u32[]{:S(2)}, u32[]{:S(2)}) collective-permute-start(f32[144,128]{1,0:T(8,128)S(1)} %get-tuple-element.55), channel_id=1, source_target_pairs={{1,2},{2,1},{3,4},{4,3},{5,6},{6,5},{9,10},{10,9},{11,12},{12,11},... | collective-permute-start | bytes 221192 | tf_op jit(solution)/shard_map/ppermute | solution.py:59
  13.4 8.7 %collective-permute-start.3 = (f32[144,128]{1,0:T(8,128)S(1)}, f32[144,128]{1,0:T(8,128)S(1)}, u32[]{:S(2)}, u32[]{:S(2)}) collective-permute-start(f32[144,128]{1,0:T(8,128)S(1)} %get-tuple-element.56), channel_id=1, source_target_pairs={{0,1},{1,0},{2,3},{3,2},{4,5},{5,4},{6,7},{7,6},{8,9},{9,8},{10,11... | collective-permute-start | bytes 221192 | tf_op jit(solution)/shard_map/ppermute | solution.py:59
  23.0 3.1 %collective-permute-start.4 = (f32[72,128]{1,0:T(8,128)S(1)}, f32[72,128]{1,0:T(8,128)S(1)}, u32[]{:S(2)}, u32[]{:S(2)}) collective-permute-start(f32[72,128]{1,0:T(8,128)S(1)} %get-tuple-element.63), channel_id=1, source_target_pairs={{0,8},{8,0},{16,24},{24,16},{32,40},{40,32},{48,56},{56,48},{64,72... | collective-permute-start | bytes 110600 | tf_op jit(solution)/shard_map/ppermute | solution.py:59
  26.8 9.4 %collective-permute-start.5 = (f32[168,128]{1,0:T(8,128)S(1)}, f32[168,128]{1,0:T(8,128)S(1)}, u32[]{:S(2)}, u32[]{:S(2)}) collective-permute-start(f32[168,128]{1,0:T(8,128)S(1)} %get-tuple-element.66), channel_id=1, source_target_pairs={{8,16},{16,8},{24,32},{32,24},{40,48},{48,40},{56,64},{64,56},{72,... | collective-permute-start | bytes 258056 | tf_op jit(solution)/shard_map/ppermute | solution.py:59
  36.2 3.1 %collective-permute-start.6 = (f32[16,128]{1,0:T(8,128)S(1)}, f32[16,128]{1,0:T(8,128)S(1)}, u32[]{:S(2)}, u32[]{:S(2)}) collective-permute-start(f32[16,128]{1,0:T(8,128)S(1)} %get-tuple-element.71), channel_id=1, source_target_pairs={{0,8},{8,0},{16,24},{24,16},{32,40},{40,32},{48,56},{56,48},{64,72... | collective-permute-start | bytes 24584 | tf_op jit(solution)/shard_map/ppermute | solution.py:59
  54.1 8.9 %collective-permute-start.7 = (f32[72,128]{1,0:T(8,128)S(1)}, f32[72,128]{1,0:T(8,128)S(1)}, u32[]{:S(2)}, u32[]{:S(2)}) collective-permute-start(f32[72,128]{1,0:T(8,128)S(1)} %get-tuple-element.82), channel_id=1, source_target_pairs={{8,16},{16,8},{24,32},{32,24},{40,48},{48,40},{56,64},{64,56},{72,... | collective-permute-start | bytes 110600 | tf_op jit(solution)/shard_map/ppermute | solution.py:59
  56.7 6.2 %collective-permute-start.8 = (f32[72,128]{1,0:T(8,128)S(1)}, f32[72,128]{1,0:T(8,128)S(1)}, u32[]{:S(2)}, u32[]{:S(2)}) collective-permute-start(f32[72,128]{1,0:T(8,128)S(1)} %get-tuple-element.83), channel_id=1, source_target_pairs={{0,8},{8,0},{16,24},{24,16},{32,40},{40,32},{48,56},{56,48},{64,72... | collective-permute-start | bytes 110600 | tf_op jit(solution)/shard_map/ppermute | solution.py:59

commit v5 on v4

--- a/solution.py
+++ b/solution.py
@@ -20,9 +20,12 @@
 DEPTHS = CX + 3
 BRICK = DEPTHS * SUB
 PAIR = (2 * CX + 4) * SUB
-PACK = 96
+KEPT = 3
+PACK = 64
 NEAR = 32
-SHARE = 22
+SHARE = 29
+REST = 4 * MCAP - 2 * SHARE
+SLOT = PACK + SUB
 CROSS_MSG = 2 * SUB + PIECES * 2 * MCAP
 SPAN = 3 * CY + 3
 
@@ -115,9 +118,42 @@
 def scaled(terms, materials, tables_ref):
     sub = iota((SUB, LANES), 0)
     wide = lambda row: jnp.broadcast_to(row, (SUB, LANES))
-    scale = jnp.where(sub < 3, wide(by_material(materials, tables_ref, 0) * VOLUME), -VOLUME)
-    scale = jnp.where((sub < 5) & (wide(materials) >= 0), scale, 0.0)
-    return [[term * scale for term in row] for row in terms]
+    mass = jnp.where((sub < KEPT) & (wide(materials) >= 0), wide(by_material(materials, tables_ref, 0) * VOLUME), 0.0)
+    push = jnp.where((sub > 0) & (sub < KEPT) & (wide(materials) >= 0), -VOLUME * TIME_STEP, 0.0)
+    return [[term * mass + pltpu.roll(term, SUB - 2, 0) * push for term in row] for row in terms]
+
+
+def weighted_terms(load, chunks, materials, tables_ref):
+    sub = iota((SUB, LANES), 0)
+    wide = lambda row: jnp.broadcast_to(row, (SUB, LANES))
+    rho = wide(by_material(materials, tables_ref, 0))
+    scale = jnp.where(sub == 0, rho * VOLUME, VOLUME)
+    scale = jnp.where((sub < KEPT) & (wide(materials) >= 0), scale, 0.0)
+    stencils = [(stencil(load(0, k)), stencil(load(1, k))) for k in range(chunks)]
+    points = [
+        (rho * load(2, k), rho * load(3, k)) + tuple(-TIME_STEP * load(c, k) for c in (4, 5, 6))
+        for k in range(chunks)
+    ]
+    terms = [[None] * 4 for _ in range(4)]
+    for b in range(4):
+        acc = [[None] * KEPT for _ in range(4)]
+        for k in range(chunks):
+            (weight_x, slope_x), (weight_y, slope_y) = stencils[k]
+            wy, dy = weight_y[b], slope_y[b]
+            px, py, sxx, syy, sxy = points[k]
+            g1, h1 = (wy * px + dy * sxy, wy * sxx)
+            g2, h2 = (wy * py + dy * syy, wy * sxy)
+            for a in range(4):
+                wx, dx = weight_x[a], slope_x[a]
+                new = (wx * wy, wx * g1 + dx * h1, wx * g2 + dx * h2)
+                acc[a] = [n if o is None else o + n for o, n in zip(acc[a], new)]
+        for a in range(4):
+            packed = jnp.zeros((SUB, LANES), F32)
+            for q in range(KEPT):
+                total = jnp.sum(acc[a][q], axis=0, keepdims=True)
+                packed = jnp.where(sub == q, jnp.broadcast_to(total, (SUB, LANES)), packed)
+            terms[a][b] = packed * scale
+    return terms
 
 
 def node_terms(load, chunks):
@@ -182,32 +218,28 @@
 
 
 def sums_one(
-    terms_ref, cells_ref, mats_ref, density_ref,
-    sums_ref, inner_ref, outer_ref, meta_ref,
-    left_ref, density_rows_ref,
+    terms_ref, cells_ref, mats_ref, density_ref, shear_ref, lame_ref,
+    slot_a_ref, dest_a_ref, cell_a_ref, slot_b_ref, dest_b_ref, cell_b_ref,
+    sums_ref, inner_ref, outer_ref, meta_ref, lists_ref, tables_ref,
+    left_ref,
 ):
-    spread_table(density_ref, density_rows_ref, 0)
+    for which, table_ref in enumerate((density_ref, shear_ref, lame_ref)):
+        spread_table(table_ref, tables_ref, which * NMAT)
+    for index, ref in enumerate((slot_a_ref, dest_a_ref, cell_a_ref, slot_b_ref, dest_b_ref, cell_b_ref)):
+        entries = ref[...]
+        rest = jnp.full((1, LANES - entries.shape[1]), -1, jnp.int32)
+        lists_ref[index : index + 1, :] = jnp.concatenate([entries, rest], axis=1)
     cells, materials = (cells_ref[...], mats_ref[...])
     meta_ref[0:1, :] = cells
     meta_ref[1:2, :] = materials
     terms = [[terms_ref[(4 * a + b) * SUB : (4 * a + b + 1) * SUB, :] for b in range(4)] for a in range(4)]
-    terms = scaled(terms, materials, density_rows_ref)
+    terms = scaled(terms, materials, tables_ref)
     spread_rows(terms, row_masks(cells >> 5), left_ref)
     sums = product(halves(left_ref[...]), jnp.concatenate(column_onehot(cells & (CY - 1)), axis=1), NT)
     sums_ref[...] = sums
     to_inner, to_outer = by_side(sums[0:HALO], sums[TOP : TOP + HALO], parity("gx"))
     inner_ref[...] = to_inner
     outer_ref[...] = to_outer
-
-
-def join_lists(*refs):
-    *list_refs, density_ref, shear_ref, lame_ref, lists_ref, tables_ref = refs
-    for which, table_ref in enumerate((density_ref, shear_ref, lame_ref)):
-        spread_table(table_ref, tables_ref, which * NMAT)
-    for index, ref in enumerate(list_refs):
-        row = ref[...]
-        rest = jnp.full((1, LANES - row.shape[1]), -1, jnp.int32)
-        lists_ref[index : index + 1, :] = jnp.concatenate([row, rest], axis=1)
 
 
 def by_side(inner, outer, odd):
@@ -341,7 +373,7 @@
     del near_nodes_ref, cross_tags_ref
     merged = own_ref[...] + from_far_ref[0:PACK, :]
     merged_ref[...] = merged
-    low = jnp.where(iota((2 * SUB, LANES), 0) < 15, merged[0 : 2 * SUB], 0.0)
+    low = jnp.where(iota((2 * SUB, LANES), 0) < 3 * KEPT, merged[0 : 2 * SUB], 0.0)
     halo_ref[...] = jnp.where(parity("gx"), low, merged[PACK - 2 * SUB : PACK])
 
 
@@ -349,17 +381,22 @@
     del new_meta_ref
     odd = parity("gx")
     from_near = from_near_ref[...]
-    slot_ref[...] = sums_ref[...]
+    slot_ref[0:PACK, :] = sums_ref[...]
     last = PACK - 2 * SUB
     slot_ref[0 : 2 * SUB] = sums_ref[0 : 2 * SUB] + jnp.where(odd, from_near, 0.0)
     slot_ref[last:PACK] = sums_ref[last:PACK] + jnp.where(odd, 0.0, from_near)
     lane = iota((NEAR, LANES), 1)
     near = near_ref[...]
-    for third in range(PACK // NEAR):
-        start = third * NEAR
-        moved = pltpu.roll(near, SPAN - SHARE * third, 1)
-        here = (lane >= SPAN) & (lane < SPAN + SHARE)
-        slot_ref[start : start + NEAR, :] = jnp.where(here, moved, slot_ref[start : start + NEAR, :])
+    for half in range(2):
+        start = half * NEAR
+        moved = pltpu.roll(near, SPAN - SHARE * half, 1)
+        slot_ref[start : start + NEAR, :] = jnp.where(lane >= SPAN, moved, slot_ref[start : start + NEAR, :])
+    lane = iota((SUB, LANES), 1)
+    rest = jnp.zeros((SUB, LANES), F32)
+    for part in range(NEAR // SUB):
+        moved = pltpu.roll(near[part * SUB : (part + 1) * SUB], LANES - 2 * SHARE + REST * part, 1)
+        rest = jnp.where((lane >= REST * part) & (lane < REST * (part + 1)), moved, rest)
+    slot_ref[PACK:SLOT, :] = rest
     value = slot_ref[...]
     for index in range(slots_ref.shape[0]):
         slots_ref[index] = value
@@ -370,7 +407,7 @@
     inside_x = (node_x > 0) & (node_x < CX * lax.axis_size("gx") - 1)
     inside_y = (node_y > 0) & (node_y < CY * lax.axis_size("gy") - 1)
     mass = jnp.maximum(jnp.broadcast_to(row[0:1], (SUB, LANES)), MASS_FLOOR)
-    value = (row + TIME_STEP * pltpu.roll(row, SUB - 2, 0)) / mass
+    value = row / mass
     velocity_ref[x * SUB : (x + 1) * SUB, :] = jnp.where(inside_y & inside_x, value, 0.0)
 
 
@@ -398,11 +435,10 @@
         moved = pltpu.roll(slots_ref[index, 0:PACK, :], shift & (LANES - 1), 1)
         valid = (lane >= shift) & (lane < SPAN + shift) & (lane < SPAN)
         total = total + jnp.where(valid, moved, 0.0)
-    packed_ref[0:PACK, :] = total
-    packed_ref[PACK:, :] = jnp.zeros((packed_ref.shape[0] - PACK, LANES), F32)
+    packed_ref[...] = total
     node_y = (gy - 1) * CY - 1 + iota((SUB, LANES), 1)
     for x in range(DEPTHS):
-        put_velocity(packed_ref[5 * x : 5 * x + SUB, :], x, node_y, velocity_ref)
+        put_velocity(packed_ref[KEPT * x : KEPT * x + SUB, :], x, node_y, velocity_ref)
     velocity_ref[DEPTHS * SUB :, :] = jnp.zeros((ROWS - DEPTHS * SUB, LANES), F32)
 
 
@@ -567,7 +603,7 @@
 def sums_kept(fresh_ref, target_ref, tables_ref, sums_ref, left_ref):
     depth, column, materials = (target_ref[0:1, :], target_ref[1:2, :], target_ref[2:3, :])
     load = lambda c, k: rows_at(fresh_ref, c, k, BLOCK)
-    terms = scaled(node_terms(load, BLOCK // SUB), materials, tables_ref)
+    terms = weighted_terms(load, BLOCK // SUB, materials, tables_ref)
     spread_rows(terms, row_masks(depth, 2 * CX), left_ref)
     sums_ref[...] = product(halves(left_ref[...]), jnp.concatenate(column_onehot(column), axis=1), NT)
 
@@ -616,7 +652,7 @@
 def put_packed(ref, sums):
     ref[PACK - SUB : PACK, :] = jnp.zeros((SUB, LANES), F32)
     for x in range(DEPTHS):
-        ref[5 * x : 5 * x + 5, :] = sums[x * SUB : x * SUB + 5]
+        ref[KEPT * x : KEPT * (x + 1), :] = sums[x * SUB : x * SUB + KEPT]
 
 
 def sums_two(
@@ -629,7 +665,7 @@
     packed_blocks(joined(from_near_ref[0 : MSG - SUB, :]), wide_ref, turned_ref)
     stride = turned_ref.shape[0] // 8
     load = lambda c, k: rows_at(turned_ref, c, k, stride)
-    terms = scaled(node_terms(load, stride // SUB), materials, tables_ref)
+    terms = weighted_terms(load, stride // SUB, materials, tables_ref)
     own, _ = own_and_far_depth()
     spread_rows(terms, row_masks((cells >> 5) + own, 2 * CX), left_ref)
     onehots = jnp.concatenate(column_onehot((cells & (CY - 1)) + CY), axis=1)
@@ -675,12 +711,15 @@
 
 def near_movers(slots_ref, index):
     lane = iota((NEAR, LANES), 1)
-    nodes = jnp.zeros((NEAR, LANES), F32)
-    for third in range(PACK // NEAR):
-        first = SHARE * third
-        part = slots_ref[index, third * NEAR : (third + 1) * NEAR, :]
-        part = pltpu.roll(part, LANES - SPAN + first, 1)
-        nodes = jnp.where((lane >= first) & (lane < first + SHARE), part, nodes)
+    rest = slots_ref[index, PACK:SLOT, :]
+    parts = []
+    for part in range(NEAR // SUB):
+        parts.append(pltpu.roll(rest, (2 * SHARE - REST * part) % LANES, 1))
+    nodes = jnp.concatenate(parts, axis=0)
+    for half in range(2):
+        first = SHARE * half
+        moved = pltpu.roll(slots_ref[index, half * NEAR : (half + 1) * NEAR, :], LANES - SPAN + first, 1)
+        nodes = jnp.where((lane >= first) & (lane < first + SHARE), moved, nodes)
     return nodes
 
 
@@ -815,26 +854,22 @@
     half_form = ((wide // 2, LANES), F32)
     quarter_form = ((wide // 4, LANES), F32)
     near_form = ((NEAR, LANES), F32)
-    slots_form = ((lax.axis_size("gy"), PACK, LANES), F32)
+    slots_form = ((lax.axis_size("gy"), SLOT, LANES), F32)
     scratch = lambda form: pltpu.VMEM(*form)
     left = pltpu.VMEM((ROWS, 4 * LANES), F32)
 
     def along_depth(far, near):
         return (swap(far, "gx", 1), swap(near, "gx", 0))
 
-    small = (row(density), row(shear_modulus), row(lame_modulus))
-    lists, tables = call(
-        join_lists, (tags, ((3 * NMAT, LANES), F32)), (), (IN_VMEM,) * 9, *list_a, *list_b, *small
-    )
     turned, terms = call(
         terms_one, (turned_form, ((16 * SUB, LANES), F32)), (), (IN_VMEM,), points
     )
-    sums, inner, outer, meta = call(
+    sums, inner, outer, meta, lists, tables = call(
         sums_one,
-        (grid, halo, halo, tags),
-        (left, pltpu.VMEM((NMAT, LANES), F32)),
-        (IN_VMEM,) * 4,
-        terms, cells, mats, small[0],
+        (grid, halo, halo, tags, tags, ((3 * NMAT, LANES), F32)),
+        (left,),
+        (IN_VMEM,) * 12,
+        terms, cells, mats, row(density), row(shear_modulus), row(lame_modulus), *list_a, *list_b,
     )
     picked, picked_tags, chosen = call(
         pick_cross,
@@ -896,7 +931,7 @@
     (slots,) = call(
         merge_two,
         (slots_form,),
-        (scratch(packed_form),),
+        (pltpu.VMEM((SLOT, LANES), F32),),
         (IN_VMEM,) * 4,
         merged, swap(halo_message, "gx", 0), near_nodes, new_meta,
     )
@@ -904,7 +939,7 @@
     fresh, velocity, far, near = call(
         advance_two,
         (turned_form, grid, message, message),
-        (pltpu.VMEM((PACK + SUB, LANES), F32),),
+        (scratch(packed_form),),
         (IN_VMEM,) * 6,
         fresh, kept_a, slots, tables, chosen_b, tags_b,
     )

time: 64.2 us -> 63.2 us (0.984)
  starting transfers between devices: 27.1 us -> 27.9 us
    ppermute x9, starting transfers between devices: 27.1 us -> 27.9 us  [swap(): return lax.ppermute(value, axis, pairs)]
    unnamed x26, local copies, waits for them, and re-layouts: 2.31 us -> 1.67 us
    pallas_call x17 -> x16, Pallas kernels: 7.7 us -> 7.54 us  [call(): pl.pallas_call(kernel, out_shape=tuple((jax.ShapeDtypeStruct(shape, dtype...]
  transfers between devices with their start and end apart: 9 -> 9, of which waited for: 5 -> 6; matrix products, arithmetic and copies ran while one was open for 0% -> 0% of each run, Pallas kernels for 5% -> 5%
where the time goes in v5:
time: 63.2 us; the launch traced here: 62.8 us
  starting transfers between devices  27.9 us (44%)
  blocking collectives  13.4 us (21%)
  waiting for transfers between devices  11.4 us (18%)
  Pallas kernels  7.54 us (12%)
  local copies, waits for them, and re-layouts  1.67 us (3%)
  between operations  0.91 us (1%)
    ppermute x9, starting transfers between devices, swap(): return lax.ppermute(value, axis, pairs)  27.9 us
    all_to_all x1, blocking collectives, shards(): slots = lax.all_to_all(slots, 'gy', 0, 0)  13.4 us
    ppermute x9, waiting for transfers between devices, swap(): return lax.ppermute(value, axis, pairs)  11.4 us
    pallas_call x16, Pallas kernels, call(): pl.pallas_call(kernel, out_shape=tuple((jax.ShapeDtypeStruct(shape, dtype...  7.54 us
    unnamed x26, local copies, waits for them, and re-layouts  1.67 us
  transfers between devices with their start and end apart: 9, of which 6 were waited for; matrix products, arithmetic and copies ran while one was open for 0% of the time, Pallas kernels for 5%

profile of v5, /device:TPU:384, one launch (start us, length us, event | category | flops | bytes accessed | tf_op | source)
XLA Modules:
  0.0 62.8 jit_solution(10861177097321461574)
XLA Ops:
  0.6 0.9 %copy-done = f32[128,512]{1,0:T(8,128)S(1)} copy-done((f32[128,512]{1,0:T(8,128)S(1)}, f32[128,512]{1,0:T(8,128)}, u32[]{:S(2)}) %copy-start) | copy-done | bytes 262168
  1.6 0.5 shard_map.139
  2.2 0.5 copy-done.5
  2.9 0.3 shard_map.140
  3.2 6.2 %collective-permute-start = (f32[24,128]{1,0:T(8,128)S(1)}, f32[24,128]{1,0:T(8,128)S(1)}, u32[]{:S(2)}, u32[]{:S(2)}) collective-permute-start(f32[24,128]{1,0:T(8,128)S(1)} %get-tuple-element.49), channel_id=1, source_target_pairs={{8,16},{16,8},{24,32},{32,24},{40,48},{48,40},{56,64},{64,56},{72,... | collective-permute-start | bytes 36872 | tf_op jit(solution)/shard_map/ppermute | solution.py:62
  9.4 1.9 %collective-permute-start.1 = (f32[24,128]{1,0:T(8,128)S(1)}, f32[24,128]{1,0:T(8,128)S(1)}, u32[]{:S(2)}, u32[]{:S(2)}) collective-permute-start(f32[24,128]{1,0:T(8,128)S(1)} %get-tuple-element.50), channel_id=1, source_target_pairs={{0,8},{8,0},{16,24},{24,16},{32,40},{40,32},{48,56},{56,48},{64,72... | collective-permute-start | bytes 36872 | tf_op jit(solution)/shard_map/ppermute | solution.py:62
  11.4 0.5 shard_map.141
  11.9 0.6 %collective-permute-done.1.from_inner_ref = f32[24,128]{1,0:T(8,128)S(1)} collective-permute-done((f32[24,128]{1,0:T(8,128)S(1)}, f32[24,128]{1,0:T(8,128)S(1)}, u32[]{:S(2)}, u32[]{:S(2)}) %collective-permute-start.1) | collective-permute-done | bytes 12320 | tf_op jit(solution)/shard_map/ppermute | solution.py:62
  12.5 0.1 shard_map.142
  12.6 0.7 %collective-permute-start.2 = (f32[144,128]{1,0:T(8,128)S(1)}, f32[144,128]{1,0:T(8,128)S(1)}, u32[]{:S(2)}, u32[]{:S(2)}) collective-permute-start(f32[144,128]{1,0:T(8,128)S(1)} %get-tuple-element.55), channel_id=1, source_target_pairs={{1,2},{2,1},{3,4},{4,3},{5,6},{6,5},{9,10},{10,9},{11,12},{12,11},... | collective-permute-start | bytes 221192 | tf_op jit(solution)/shard_map/ppermute | solution.py:62
  13.3 6.1 %collective-permute-start.3 = (f32[144,128]{1,0:T(8,128)S(1)}, f32[144,128]{1,0:T(8,128)S(1)}, u32[]{:S(2)}, u32[]{:S(2)}) collective-permute-start(f32[144,128]{1,0:T(8,128)S(1)} %get-tuple-element.56), channel_id=1, source_target_pairs={{0,1},{1,0},{2,3},{3,2},{4,5},{5,4},{6,7},{7,6},{8,9},{9,8},{10,11... | collective-permute-start | bytes 221192 | tf_op jit(solution)/shard_map/ppermute | solution.py:62
  19.4 0.6 shard_map.143
  20.0 1.7 %collective-permute-done.3.yi_ref = f32[144,128]{1,0:T(8,128)S(1)} collective-permute-done((f32[144,128]{1,0:T(8,128)S(1)}, f32[144,128]{1,0:T(8,128)S(1)}, u32[]{:S(2)}, u32[]{:S(2)}) %collective-permute-start.3) | collective-permute-done | bytes 73760 | tf_op jit(solution)/shard_map/ppermute | solution.py:62
  21.7 0.8 %shard_map.144 = (f32[512,128]{1,0:T(8,128)S(1)}, f32[32,128]{1,0:T(8,128)S(1)}, f32[72,128]{1,0:T(8,128)S(1)}, f32[72,128]{1,0:T(8,128)S(1)}) custom-call(f32[512,128]{1,0:T(8,128)S(1)} %get-tuple-element.45.turned_ref, s32[8,128]{1,0:T(8,128)S(1)} %get-tuple-element.47.meta_ref, f32[160,128]{1,0:T(8,128)S(1)} %get-tuple-element.54.merged_ref, ...), custom_call_target="tpu_custom_call" | custom-call | flops 4194304 | bytes 524288 | tf_op jit(solution)/shard_map/pallas_call | solution.py:46
  22.5 1.9 %collective-permute-start.4 = (f32[72,128]{1,0:T(8,128)S(1)}, f32[72,128]{1,0:T(8,128)S(1)}, u32[]{:S(2)}, u32[]{:S(2)}) collective-permute-start(f32[72,128]{1,0:T(8,128)S(1)} %get-tuple-element.63), channel_id=1, source_target_pairs={{0,8},{8,0},{16,24},{24,16},{32,40},{40,32},{48,56},{56,48},{64,72... | collective-permute-start | bytes 110600 | tf_op jit(solution)/shard_map/ppermute | solution.py:62
  24.5 0.7 %shard_map.145.kept_sums_ref = f32[288,128]{1,0:T(8,128)S(1)} custom-call(f32[512,128]{1,0:T(8,128)S(1)} %get-tuple-element.60.fresh_ref.kept_ref, s32[8,128]{1,0:T(8,128)S(1)} %get-tuple-element.62.target_ref, f32[24,128]{1,0:T(8,128)S(1)} %get-tuple-element.57.tables_ref), custom_call_target="tpu_custom_call" | custom-call | flops 4194304 | bytes 524288 | tf_op jit(solution)/shard_map/pallas_call | solution.py:46
  25.2 0.5 collective-permute-done.4.from_near_ref
  25.7 0.7 %shard_map.146 = (f32[64,128]{1,0:T(8,128)S(1)}, f32[136,128]{1,0:T(8,128)S(1)}) custom-call(f32[288,128]{1,0:T(8,128)S(1)} %shard_map.145.kept_sums_ref, f32[72,128]{1,0:T(8,128)S(1)} %collective-permute-done.4.from_near_ref, f32[72,128]{1,0:T(8,128)S(1)} %get-tuple-element.64.to_far_ref, f32[24,128]{1,0:T(8,128)S(1)} %get-tuple-element.57.tables_ref), custom_call_target="tpu_custom_call" | custom-call | flops 4194304 | bytes 524288 | tf_op jit(solution)/shard_map/pallas_call | solution.py:46
  26.4 4.4 %collective-permute-start.5 = (f32[136,128]{1,0:T(8,128)S(1)}, f32[136,128]{1,0:T(8,128)S(1)}, u32[]{:S(2)}, u32[]{:S(2)}) collective-permute-start(f32[136,128]{1,0:T(8,128)S(1)} %get-tuple-element.66), channel_id=1, source_target_pairs={{8,16},{16,8},{24,32},{32,24},{40,48},{48,40},{56,64},{64,56},{72,... | collective-permute-start | bytes 208904 | tf_op jit(solution)/shard_map/ppermute | solution.py:62
  30.8 0.1 shard_map.147.near_nodes_ref.near_ref
  30.9 0.2 shard_map.148
  31.2 4.5 %collective-permute-done.5.from_far_ref = f32[136,128]{1,0:T(8,128)S(1)} collective-permute-done((f32[136,128]{1,0:T(8,128)S(1)}, f32[136,128]{1,0:T(8,128)S(1)}, u32[]{:S(2)}, u32[]{:S(2)}) %collective-permute-start.5) | collective-permute-done | bytes 69664 | tf_op jit(solution)/shard_map/ppermute | solution.py:62
  35.6 1.9 %collective-permute-start.6 = (f32[16,128]{1,0:T(8,128)S(1)}, f32[16,128]{1,0:T(8,128)S(1)}, u32[]{:S(2)}, u32[]{:S(2)}) collective-permute-start(f32[16,128]{1,0:T(8,128)S(1)} %get-tuple-element.71), channel_id=1, source_target_pairs={{0,8},{8,0},{16,24},{24,16},{32,40},{40,32},{48,56},{56,48},{64,72... | collective-permute-start | bytes 24584 | tf_op jit(solution)/shard_map/ppermute | solution.py:62
  37.6 0.3 shard_map.150
  37.8 0.9 %collective-permute-done.6.from_near_ref = f32[16,128]{1,0:T(8,128)S(1)} collective-permute-done((f32[16,128]{1,0:T(8,128)S(1)}, f32[16,128]{1,0:T(8,128)S(1)}, u32[]{:S(2)}, u32[]{:S(2)}) %collective-permute-start.6) | collective-permute-done | bytes 8224 | tf_op jit(solution)/shard_map/ppermute | solution.py:62
  38.8 13.4 %all_to_all.5.slots_ref = f32[8,72,128]{2,1,0:T(8,128)S(1)} all-to-all(f32[8,72,128]{2,1,0:T(8,128)S(1)} %shard_map.151), channel_id=1, replica_groups=mesh['gx'=64,'gy'=8] {'gy'}, dimensions={0} | all-to-all | bytes 589824 | tf_op jit(solution)/shard_map/all_to_all | solution.py:938
  52.2 0.8 %shard_map.152 = (f32[512,128]{1,0:T(8,128)S(1)}, f32[160,128]{1,0:T(8,128)S(1)}, f32[72,128]{1,0:T(8,128)S(1)}, f32[72,128]{1,0:T(8,128)S(1)}) custom-call(f32[512,128]{1,0:T(8,128)S(1)} %get-tuple-element.60.fresh_ref.kept_ref, s32[8,128]{1,0:T(8,128)S(1)} %get-tuple-element.61.meta_ref, f32[8,72,128]{2,1,0:T(8,128)S(1)} %all_to_all.5.slots_ref, ...), custom_call_target="tpu_custom_call" | custom-call | flops 4194304 | bytes 524288 | tf_op jit(solution)/shard_map/pallas_call | solution.py:46
  53.0 2.8 %collective-permute-start.7 = (f32[72,128]{1,0:T(8,128)S(1)}, f32[72,128]{1,0:T(8,128)S(1)}, u32[]{:S(2)}, u32[]{:S(2)}) collective-permute-start(f32[72,128]{1,0:T(8,128)S(1)} %get-tuple-element.82), channel_id=1, source_target_pairs={{8,16},{16,8},{24,32},{32,24},{40,48},{48,40},{56,64},{64,56},{72,... | collective-permute-start | bytes 110600 | tf_op jit(solution)/shard_map/ppermute | solution.py:62
  55.9 1.9 %collective-permute-start.8 = (f32[72,128]{1,0:T(8,128)S(1)}, f32[72,128]{1,0:T(8,128)S(1)}, u32[]{:S(2)}, u32[]{:S(2)}) collective-permute-start(f32[72,128]{1,0:T(8,128)S(1)} %get-tuple-element.83), channel_id=1, source_target_pairs={{0,8},{8,0},{16,24},{24,16},{32,40},{40,32},{48,56},{56,48},{64,72... | collective-permute-start | bytes 110600 | tf_op jit(solution)/shard_map/ppermute | solution.py:62
  57.8 0.9 %shard_map.153 = (f32[256,512]{1,0:T(8,128)S(1)}, s32[8,128]{1,0:T(8,128)S(1)}) custom-call(f32[512,128]{1,0:T(8,128)S(1)} %get-tuple-element.75.fresh_ref, s32[8,128]{1,0:T(8,128)S(1)} %get-tuple-element.76.old_meta_ref, f32[160,128]{1,0:T(8,128)S(1)} %get-tuple-element.77.velocity_ref, f32[128,128]{1,0:T(8,128)S(1)} %get-tuple-element.78.turned_ref, ...), custom_call_target="tpu_custom_call" | custom-call | flops 4194304 | bytes 524288 | tf_op jit(solution)/shard_map/pallas_call | solution.py:46
  58.7 3.2 %collective-permute-done.7.xo_ref = f32[72,128]{1,0:T(8,128)S(1)} collective-permute-done((f32[72,128]{1,0:T(8,128)S(1)}, f32[72,128]{1,0:T(8,128)S(1)}, u32[]{:S(2)}, u32[]{:S(2)}) %collective-permute-start.7) | collective-permute-done | bytes 36896 | tf_op jit(solution)/shard_map/ppermute | solution.py:62
  61.9 0.8 %shard_map.154 = (f32[256,512]{1,0:T(8,128)}, s32[2,128]{1,0:T(2,128)}, s32[2,128]{1,0:T(2,128)}) custom-call(f32[256,512]{1,0:T(8,128)S(1)} %get-tuple-element.80.part_ref, s32[8,128]{1,0:T(8,128)S(1)} %get-tuple-element.76.old_meta_ref, s32[8,128]{1,0:T(8,128)S(1)} %get-tuple-element.81.tail_ref, f32[72,128]{1,0:T(8,128)S(1)} %collective-permute-done.7.xo_ref, ...), custom_call_target="tpu_custom_call" | custom-call | flops 4194304 | bytes 524288 | tf_op jit(solution)/shard_map/pallas_call | solution.py:46
  (29 shorter events, 0.3 us)
Async XLA Ops:
  0.6 1.0 %copy-start = (f32[128,512]{1,0:T(8,128)S(1)}, f32[128,512]{1,0:T(8,128)}, u32[]{:S(2)}) copy-start(f32[128,512]{1,0:T(8,128)} %points_ref.3) | copy-start | bytes 786436
  1.6 9.8 %copy-start.1 = (f32[128,512]{1,0:T(8,128)S(1)}, f32[128,512]{1,0:T(8,128)}, u32[]{:S(2)}) copy-start(f32[128,512]{1,0:T(8,128)} %points_ref.3) | copy-start | bytes 786436
  2.1 0.7 %copy-start.5 = (f32[8]{0:T(128)S(1)}, f32[8]{0:T(128)}, u32[]{:S(2)}) copy-start(f32[8]{0:T(128)} %param.16) | copy-start | bytes 100
  2.1 0.7 %copy-start.6 = (f32[8]{0:T(128)S(1)}, f32[8]{0:T(128)}, u32[]{:S(2)}) copy-start(f32[8]{0:T(128)} %param.17) | copy-start | bytes 100
  2.1 0.7 %copy-start.7 = (s32[64]{0:T(128)S(1)}, s32[64]{0:T(128)}, u32[]{:S(2)}) copy-start(s32[64]{0:T(128)} %param.18) | copy-start | bytes 772
  2.1 0.7 %copy-start.8 = (s32[64]{0:T(128)S(1)}, s32[64]{0:T(128)}, u32[]{:S(2)}) copy-start(s32[64]{0:T(128)} %param.19) | copy-start | bytes 772
  2.1 0.7 %copy-start.9 = (s32[64]{0:T(128)S(1)}, s32[64]{0:T(128)}, u32[]{:S(2)}) copy-start(s32[64]{0:T(128)} %param.20) | copy-start | bytes 772
  2.1 0.7 %copy-start.10 = (s32[64]{0:T(128)S(1)}, s32[64]{0:T(128)}, u32[]{:S(2)}) copy-start(s32[64]{0:T(128)} %param.21) | copy-start | bytes 772
  2.2 0.7 %copy-start.11 = (s32[64]{0:T(128)S(1)}, s32[64]{0:T(128)}, u32[]{:S(2)}) copy-start(s32[64]{0:T(128)} %param.22) | copy-start | bytes 772
  2.2 0.7 %copy-start.12 = (s32[64]{0:T(128)S(1)}, s32[64]{0:T(128)}, u32[]{:S(2)}) copy-start(s32[64]{0:T(128)} %param.23) | copy-start | bytes 772
  2.2 0.7 %copy-start.2 = (s32[128]{0:T(128)S(1)}, s32[128]{0:T(128)}, u32[]{:S(2)}) copy-start(s32[128]{0:T(128)} %param.13) | copy-start | bytes 1540
  2.2 0.7 %copy-start.3 = (s32[128]{0:T(128)S(1)}, s32[128]{0:T(128)}, u32[]{:S(2)}) copy-start(s32[128]{0:T(128)} %param.14) | copy-start | bytes 1540
  2.2 0.7 %copy-start.4 = (f32[8]{0:T(128)S(1)}, f32[8]{0:T(128)}, u32[]{:S(2)}) copy-start(f32[8]{0:T(128)} %param.15) | copy-start | bytes 100
  3.2 8.6 %collective-permute-start = (f32[24,128]{1,0:T(8,128)S(1)}, f32[24,128]{1,0:T(8,128)S(1)}, u32[]{:S(2)}, u32[]{:S(2)}) collective-permute-start(f32[24,128]{1,0:T(8,128)S(1)} %get-tuple-element.49), channel_id=1, source_target_pairs={{8,16},{16,8},{24,32},{32,24},{40,48},{48,40},{56,64},{64,56},{72,... | collective-permute-start | bytes 36872 | tf_op jit(solution)/shard_map/ppermute | solution.py:62
  9.4 3.1 %collective-permute-start.1 = (f32[24,128]{1,0:T(8,128)S(1)}, f32[24,128]{1,0:T(8,128)S(1)}, u32[]{:S(2)}, u32[]{:S(2)}) collective-permute-start(f32[24,128]{1,0:T(8,128)S(1)} %get-tuple-element.50), channel_id=1, source_target_pairs={{0,8},{8,0},{16,24},{24,16},{32,40},{40,32},{48,56},{56,48},{64,72... | collective-permute-start | bytes 36872 | tf_op jit(solution)/shard_map/ppermute | solution.py:62
  12.6 7.4 %collective-permute-start.2 = (f32[144,128]{1,0:T(8,128)S(1)}, f32[144,128]{1,0:T(8,128)S(1)}, u32[]{:S(2)}, u32[]{:S(2)}) collective-permute-start(f32[144,128]{1,0:T(8,128)S(1)} %get-tuple-element.55), channel_id=1, source_target_pairs={{1,2},{2,1},{3,4},{4,3},{5,6},{6,5},{9,10},{10,9},{11,12},{12,11},... | collective-permute-start | bytes 221192 | tf_op jit(solution)/shard_map/ppermute | solution.py:62
  13.3 8.4 %collective-permute-start.3 = (f32[144,128]{1,0:T(8,128)S(1)}, f32[144,128]{1,0:T(8,128)S(1)}, u32[]{:S(2)}, u32[]{:S(2)}) collective-permute-start(f32[144,128]{1,0:T(8,128)S(1)} %get-tuple-element.56), channel_id=1, source_target_pairs={{0,1},{1,0},{2,3},{3,2},{4,5},{5,4},{6,7},{7,6},{8,9},{9,8},{10,11... | collective-permute-start | bytes 221192 | tf_op jit(solution)/shard_map/ppermute | solution.py:62
  22.5 3.1 %collective-permute-start.4 = (f32[72,128]{1,0:T(8,128)S(1)}, f32[72,128]{1,0:T(8,128)S(1)}, u32[]{:S(2)}, u32[]{:S(2)}) collective-permute-start(f32[72,128]{1,0:T(8,128)S(1)} %get-tuple-element.63), channel_id=1, source_target_pairs={{0,8},{8,0},{16,24},{24,16},{32,40},{40,32},{48,56},{56,48},{64,72... | collective-permute-start | bytes 110600 | tf_op jit(solution)/shard_map/ppermute | solution.py:62
  26.4 9.2 %collective-permute-start.5 = (f32[136,128]{1,0:T(8,128)S(1)}, f32[136,128]{1,0:T(8,128)S(1)}, u32[]{:S(2)}, u32[]{:S(2)}) collective-permute-start(f32[136,128]{1,0:T(8,128)S(1)} %get-tuple-element.66), channel_id=1, source_target_pairs={{8,16},{16,8},{24,32},{32,24},{40,48},{48,40},{56,64},{64,56},{72,... | collective-permute-start | bytes 208904 | tf_op jit(solution)/shard_map/ppermute | solution.py:62
  35.6 3.1 %collective-permute-start.6 = (f32[16,128]{1,0:T(8,128)S(1)}, f32[16,128]{1,0:T(8,128)S(1)}, u32[]{:S(2)}, u32[]{:S(2)}) collective-permute-start(f32[16,128]{1,0:T(8,128)S(1)} %get-tuple-element.71), channel_id=1, source_target_pairs={{0,8},{8,0},{16,24},{24,16},{32,40},{40,32},{48,56},{56,48},{64,72... | collective-permute-start | bytes 24584 | tf_op jit(solution)/shard_map/ppermute | solution.py:62
  53.0 8.9 %collective-permute-start.7 = (f32[72,128]{1,0:T(8,128)S(1)}, f32[72,128]{1,0:T(8,128)S(1)}, u32[]{:S(2)}, u32[]{:S(2)}) collective-permute-start(f32[72,128]{1,0:T(8,128)S(1)} %get-tuple-element.82), channel_id=1, source_target_pairs={{8,16},{16,8},{24,32},{32,24},{40,48},{48,40},{56,64},{64,56},{72,... | collective-permute-start | bytes 110600 | tf_op jit(solution)/shard_map/ppermute | solution.py:62
  55.9 6.0 %collective-permute-start.8 = (f32[72,128]{1,0:T(8,128)S(1)}, f32[72,128]{1,0:T(8,128)S(1)}, u32[]{:S(2)}, u32[]{:S(2)}) collective-permute-start(f32[72,128]{1,0:T(8,128)S(1)} %get-tuple-element.83), channel_id=1, source_target_pairs={{0,8},{8,0},{16,24},{24,16},{32,40},{40,32},{48,56},{56,48},{64,72... | collective-permute-start | bytes 110600 | tf_op jit(solution)/shard_map/ppermute | solution.py:62

commit v6 on v5

--- a/solution.py
+++ b/solution.py
@@ -207,7 +207,8 @@
         rows_ref[row : row + 1, :] = jnp.broadcast_to(table[:, index : index + 1], (1, LANES))
 
 
-def terms_one(points_ref, turned_ref, terms_ref):
+def terms_one(points_ref, meta_ref, turned_ref, terms_ref):
+    del meta_ref
     turned_ref[...] = points_ref[...].T
     load = lambda c, k: rows_at(turned_ref, c, k, BLOCK)
     terms = node_terms(load, BLOCK // SUB)
@@ -217,21 +218,29 @@
             terms_ref[row : row + SUB, :] = terms[a][b]
 
 
-def sums_one(
-    terms_ref, cells_ref, mats_ref, density_ref, shear_ref, lame_ref,
+def blank(blank_ref):
+    blank_ref[...] = jnp.zeros_like(blank_ref)
+
+
+def prepare(
+    blank_ref, cells_ref, mats_ref, density_ref, shear_ref, lame_ref,
     slot_a_ref, dest_a_ref, cell_a_ref, slot_b_ref, dest_b_ref, cell_b_ref,
-    sums_ref, inner_ref, outer_ref, meta_ref, lists_ref, tables_ref,
-    left_ref,
+    meta_ref, lists_ref, tables_ref,
 ):
     for which, table_ref in enumerate((density_ref, shear_ref, lame_ref)):
         spread_table(table_ref, tables_ref, which * NMAT)
+    lists_ref[...] = blank_ref[...]
     for index, ref in enumerate((slot_a_ref, dest_a_ref, cell_a_ref, slot_b_ref, dest_b_ref, cell_b_ref)):
         entries = ref[...]
         rest = jnp.full((1, LANES - entries.shape[1]), -1, jnp.int32)
         lists_ref[index : index + 1, :] = jnp.concatenate([entries, rest], axis=1)
-    cells, materials = (cells_ref[...], mats_ref[...])
-    meta_ref[0:1, :] = cells
-    meta_ref[1:2, :] = materials
+    meta_ref[...] = blank_ref[...]
+    meta_ref[0:1, :] = cells_ref[...]
+    meta_ref[1:2, :] = mats_ref[...]
+
+
+def sums_one(terms_ref, meta_ref, tables_ref, sums_ref, inner_ref, outer_ref, left_ref):
+    cells, materials = (meta_ref[0:1, :], meta_ref[1:2, :])
     terms = [[terms_ref[(4 * a + b) * SUB : (4 * a + b + 1) * SUB, :] for b in range(4)] for a in range(4)]
     terms = scaled(terms, materials, tables_ref)
     spread_rows(terms, row_masks(cells >> 5), left_ref)
@@ -507,8 +516,8 @@
     return lambda a, b, component: near[a][b][component + 1 : component + 2]
 
 
-def emit_movers(fresh, chosen_ref, tags_ref, far_ref, near_ref):
-    rows = select_rows(chosen_ref[...].astype(BF16), fresh.T)
+def emit_movers(advanced, chosen_ref, tags_ref, far_ref, near_ref):
+    rows = select_rows(chosen_ref[...].astype(BF16), advanced)
     tags = tags_ref[...]
     lane = iota((SUB, LANES), 1)
     for o, ref in enumerate((far_ref, near_ref)):
@@ -555,7 +564,7 @@
 
 def plan_depth(
     meta_ref, lists_ref,
-    chosen_a_ref, chosen_b_ref, tags_a_ref, tags_b_ref, kept_a_ref, kept_b_ref, target_ref,
+    chosen_a_ref, chosen_b_ref, tags_a_ref, tags_b_ref, kept_a_ref, kept_b_ref, target_ref, stays_ref,
 ):
     home, step_x, _ = home_and_steps()
     cells, materials = (meta_ref[0:1, :], meta_ref[1:2, :])
@@ -573,6 +582,7 @@
     target_ref[...] = target
     kept, _ = departures(kept[0:1], kept[1:2], lists_ref[3:6, :])
     kept_b_ref[...] = kept
+    stays_ref[...] = jnp.broadcast_to((kept[1:2] >= 0).astype(F32), stays_ref.shape).T
 
 
 def rows_at(ref, c, k, stride):
@@ -593,7 +603,7 @@
     near = gathered(halves(velocity_ref[...]), cells >> 5, cells & (CY - 1))
     load = lambda c, k: rows_at(turned_ref, c, k, BLOCK)
     move_points(load, store, BLOCK // SUB, node_getter(near), materials, tables_ref)
-    emit_movers(fresh_ref[...], chosen_ref, tags_ref, far_message_ref, near_message_ref)
+    emit_movers(fresh_ref[...].T, chosen_ref, tags_ref, far_message_ref, near_message_ref)
     for a in range(4):
         for b in range(4):
             row = 2 * (4 * a + b)
@@ -625,17 +635,6 @@
         turned_ref[c * stride : (c + 1) * stride, :] = total
 
 
-def unpacked_blocks(turned_ref, count, wide_ref):
-    stride = BLOCK * count // LANES
-    for c in range(8):
-        value = turned_ref[c * stride : (c + 1) * stride, :]
-        for group in range(LANES // count):
-            start = c * BLOCK + group * stride
-            shift = (LANES - count * group) % LANES
-            wide_ref[start : start + stride, :] = pltpu.roll(value, shift, 1) if shift else value
-    return wide_ref[...].T[0:count]
-
-
 def repeated(tile, count):
     while count < LANES:
         tile = tile + pltpu.roll(tile, count, 1)
@@ -666,14 +665,16 @@
     stride = turned_ref.shape[0] // 8
     load = lambda c, k: rows_at(turned_ref, c, k, stride)
     terms = weighted_terms(load, stride // SUB, materials, tables_ref)
-    own, _ = own_and_far_depth()
-    spread_rows(terms, row_masks((cells >> 5) + own, 2 * CX), left_ref)
+    spread_rows(terms, row_masks(cells >> 5), left_ref)
     onehots = jnp.concatenate(column_onehot((cells & (CY - 1)) + CY), axis=1)
-    sums = product(halves(left_ref[...]), onehots, NT) + kept_sums_ref[...]
+    part = product(halves(left_ref[...]), onehots, NT)
     odd = parity("gx")
-    first, second = (sums[0:BRICK], sums[CX * SUB : CX * SUB + BRICK])
-    put_packed(own_ref, jnp.where(odd, first, second))
-    put_packed(message_ref, jnp.where(odd, second, first))
+    first, second = (kept_sums_ref[0:BRICK, :], kept_sums_ref[CX * SUB : CX * SUB + BRICK, :])
+    put_packed(own_ref, jnp.where(odd, first, second) + part[0:BRICK])
+    far = jnp.where(odd, second, first)
+    low = far[0:HALO] + jnp.where(odd, part[TOP : TOP + HALO], 0.0)
+    high = far[TOP : TOP + HALO] + jnp.where(odd, 0.0, part[0:HALO])
+    put_packed(message_ref, jnp.concatenate([low, far[HALO:TOP], high], axis=0))
     message_ref[PACK : PACK + MSG, :] = to_far_ref[...]
 
 
@@ -694,8 +695,8 @@
 
 def advance_two(
     kept_ref, meta_ref, slots_ref, tables_ref, chosen_ref, tags_ref,
-    fresh_ref, velocity_ref, far_message_ref, near_message_ref,
-    packed_ref,
+    rows_ref, velocity_ref, far_message_ref, near_message_ref,
+    packed_ref, fresh_ref,
 ):
     velocity_two(slots_ref, packed_ref, velocity_ref)
     cells, materials = (meta_ref[0:1, :], meta_ref[1:2, :])
@@ -706,7 +707,9 @@
     near = gathered(halves(velocity_ref[...]), cells >> 5, (cells & (CY - 1)) + CY)
     load = lambda c, k: rows_at(kept_ref, c, k, BLOCK)
     move_points(load, store, BLOCK // SUB, node_getter(near), materials, tables_ref)
-    emit_movers(fresh_ref[...], chosen_ref, tags_ref, far_message_ref, near_message_ref)
+    advanced = fresh_ref[...].T
+    rows_ref[...] = advanced
+    emit_movers(advanced, chosen_ref, tags_ref, far_message_ref, near_message_ref)
 
 
 def near_movers(slots_ref, index):
@@ -724,12 +727,14 @@
 
 
 def settle(
-    fresh_ref, old_meta_ref, velocity_ref, turned_ref, new_meta_ref, tables_ref, slots_ref, cross_ref, tags_ref,
+    advanced_ref, stays_ref, velocity_ref, turned_ref, new_meta_ref, tables_ref, slots_ref, cross_ref, tags_ref,
     rows_ref, tail_ref,
     wide_ref, middle_ref, out_ref, small_ref,
 ):
-    alive = jnp.broadcast_to(old_meta_ref[1:2, :], fresh_ref.shape) >= 0
-    rows_ref[0:LANES, :] = jnp.where(alive, fresh_ref[...], 0.0).T
+    stays = stays_ref[...] > 0.5
+    for piece in range(PIECES):
+        columns = slice(piece * LANES, (piece + 1) * LANES)
+        rows_ref[0:LANES, columns] = jnp.where(stays, advanced_ref[:, columns], 0.0)
     parts = halves(velocity_ref[...])
 
     stride = turned_ref.shape[0] // 8
@@ -741,7 +746,6 @@
     load = lambda c, k: rows_at(turned_ref, c, k, stride)
     near = gathered(parts, cells >> 5, (cells & (CY - 1)) + CY)
     move_points(load, store_small, stride // SUB, node_getter(near), materials, tables_ref)
-    rows_ref[LANES : LANES + 2 * MCAP, :] = unpacked_blocks(small_ref, 2 * MCAP, wide_ref)
 
     gy = lax.axis_index("gy")
     odd = parity("gy")
@@ -787,7 +791,18 @@
     move_points(
         lambda c, k: rows_at(middle_ref, c, k, half), store_out, half // SUB, node_getter(near), kinds, tables_ref
     )
-    last = unpacked_blocks(out_ref, 4 * MCAP, wide_ref)
+    crossed = lane < 4 * MCAP
+    for c in range(8):
+        for k in range(BLOCK // SUB):
+            group, rest = divmod(k * SUB, half)
+            first = out_ref[c * half + rest : c * half + rest + SUB, :]
+            first = pltpu.roll(first, LANES - 4 * MCAP * group, 1) if group else first
+            group, rest = divmod(k * SUB, stride)
+            second = small_ref[c * stride + rest : c * stride + rest + SUB, :]
+            second = pltpu.roll(second, (4 * MCAP - 2 * MCAP * group) % LANES, 1)
+            wide_ref[c * BLOCK + k * SUB : c * BLOCK + (k + 1) * SUB, :] = jnp.where(crossed, first, second)
+    last = wide_ref[...].T
+    rows_ref[LANES : LANES + 2 * MCAP, :] = last[4 * MCAP : 6 * MCAP]
     for group, index in enumerate((2, 6, 3, 7)):
         start = LANES + index * MCAP
         rows_ref[start : start + MCAP, :] = last[group * MCAP : (group + 1) * MCAP]
@@ -861,16 +876,18 @@
     def along_depth(far, near):
         return (swap(far, "gx", 1), swap(near, "gx", 0))
 
+    (nothing,) = call(blank, (tags,), (), (), flops=1 << 28, bytes_accessed=1 << 10)
+    meta, lists, tables = call(
+        prepare,
+        (tags, tags, ((3 * NMAT, LANES), F32)),
+        (),
+        (IN_VMEM,) * 12,
+        nothing, cells, mats, row(density), row(shear_modulus), row(lame_modulus), *list_a, *list_b,
+    )
     turned, terms = call(
-        terms_one, (turned_form, ((16 * SUB, LANES), F32)), (), (IN_VMEM,), points
-    )
-    sums, inner, outer, meta, lists, tables = call(
-        sums_one,
-        (grid, halo, halo, tags, tags, ((3 * NMAT, LANES), F32)),
-        (left,),
-        (IN_VMEM,) * 12,
-        terms, cells, mats, row(density), row(shear_modulus), row(lame_modulus), *list_a, *list_b,
-    )
+        terms_one, (turned_form, ((16 * SUB, LANES), F32)), (), (IN_VMEM,) * 2, points, meta
+    )
+    sums, inner, outer = call(sums_one, (grid, halo, halo), (left,), (IN_VMEM,) * 3, terms, meta, tables)
     picked, picked_tags, chosen = call(
         pick_cross,
         (((4 * MCAP, wide), F32), tile, ((LANES, LANES), F32)),
@@ -887,9 +904,9 @@
     )
     cross_far, cross_near = (swap(outer, "gy", 1), swap(inner, "gy", 0))
     chosen_form = ((2 * MCAP, LANES), F32)
-    chosen_a, chosen_b, tags_a, tags_b, kept_a, kept_b, target = call(
+    chosen_a, chosen_b, tags_a, tags_b, kept_a, kept_b, target, stays = call(
         plan_depth,
-        (chosen_form, chosen_form, tile, tile, tags, tags, tags),
+        (chosen_form, chosen_form, tile, tile, tags, tags, tags, ((LANES, LANES), F32)),
         (),
         (IN_VMEM,) * 2,
         meta, lists,
@@ -910,7 +927,7 @@
     own, far_message = call(
         sums_two,
         (packed_form, ((PACK + MSG, LANES), F32)),
-        (pair_left, scratch(turned_form), pltpu.VMEM((wide // 8, LANES), F32)),
+        (left, scratch(turned_form), pltpu.VMEM((wide // 8, LANES), F32)),
         (IN_VMEM,) * 4,
         kept_sums, from_near, far, tables,
     )
@@ -936,10 +953,10 @@
         merged, swap(halo_message, "gx", 0), near_nodes, new_meta,
     )
     slots = lax.all_to_all(slots, "gy", 0, 0)
-    fresh, velocity, far, near = call(
+    advanced, velocity, far, near = call(
         advance_two,
-        (turned_form, grid, message, message),
-        (scratch(packed_form),),
+        (((LANES, wide), F32), grid, message, message),
+        (scratch(packed_form), scratch(turned_form)),
         (IN_VMEM,) * 6,
         fresh, kept_a, slots, tables, chosen_b, tags_b,
     )
@@ -955,7 +972,7 @@
             scratch(quarter_form),
         ),
         (IN_VMEM,) * 9,
-        fresh, kept_b, velocity, turned, new_meta, tables, slots, cross, cross_tags,
+        advanced, stays, velocity, turned, new_meta, tables, slots, cross, cross_tags,
     )
     final_points, final_cells, final_mats = call(
         assemble,

time: 63.2 us -> 62.3 us (0.986)
  local copies, waits for them, and re-layouts: 1.67 us -> 0.91 us
    unnamed x26 -> x24, local copies, waits for them, and re-layouts: 1.67 us -> 0.91 us
    pallas_call x16 -> x18, Pallas kernels: 7.54 us -> 7.47 us  [call(): pl.pallas_call(kernel, out_shape=tuple((jax.ShapeDtypeStruct(shape, dtype...]
where the time goes in v6:
time: 62.3 us; the launch traced here: 62 us
  starting transfers between devices  27.9 us (45%)
  blocking collectives  13.4 us (22%)
  waiting for transfers between devices  11.4 us (18%)
  Pallas kernels  7.47 us (12%)
  between operations  0.92 us (1%)
  local copies, waits for them, and re-layouts  0.91 us (1%)
    ppermute x9, starting transfers between devices, swap(): return lax.ppermute(value, axis, pairs)  27.9 us
    all_to_all x1, blocking collectives, shards(): slots = lax.all_to_all(slots, 'gy', 0, 0)  13.4 us
    ppermute x9, waiting for transfers between devices, swap(): return lax.ppermute(value, axis, pairs)  11.4 us
    pallas_call x18, Pallas kernels, call(): pl.pallas_call(kernel, out_shape=tuple((jax.ShapeDtypeStruct(shape, dtype...  7.47 us
  transfers between devices with their start and end apart: 9, of which 6 were waited for; matrix products, arithmetic and copies ran while one was open for 0% of the time, Pallas kernels for 5%

profile of v6, /device:TPU:384, one launch (start us, length us, event | category | flops | bytes accessed | tf_op | source)
XLA Modules:
  0.0 62.0 jit_solution(12073505229434242486)
XLA Ops:
  0.8 0.6 copy-done.4
  1.6 0.1 copy-done
  1.8 0.5 shard_map.141
  2.3 0.3 shard_map.142
  2.5 6.2 %collective-permute-start = (f32[24,128]{1,0:T(8,128)S(1)}, f32[24,128]{1,0:T(8,128)S(1)}, u32[]{:S(2)}, u32[]{:S(2)}) collective-permute-start(f32[24,128]{1,0:T(8,128)S(1)} %get-tuple-element.51), channel_id=1, source_target_pairs={{8,16},{16,8},{24,32},{32,24},{40,48},{48,40},{56,64},{64,56},{72,... | collective-permute-start | bytes 36872 | tf_op jit(solution)/shard_map/ppermute | solution.py:62
  8.7 1.9 %collective-permute-start.1 = (f32[24,128]{1,0:T(8,128)S(1)}, f32[24,128]{1,0:T(8,128)S(1)}, u32[]{:S(2)}, u32[]{:S(2)}) collective-permute-start(f32[24,128]{1,0:T(8,128)S(1)} %get-tuple-element.52), channel_id=1, source_target_pairs={{0,8},{8,0},{16,24},{24,16},{32,40},{40,32},{48,56},{56,48},{64,72... | collective-permute-start | bytes 36872 | tf_op jit(solution)/shard_map/ppermute | solution.py:62
  10.7 0.5 shard_map.143
  11.2 0.6 %collective-permute-done.1.from_inner_ref = f32[24,128]{1,0:T(8,128)S(1)} collective-permute-done((f32[24,128]{1,0:T(8,128)S(1)}, f32[24,128]{1,0:T(8,128)S(1)}, u32[]{:S(2)}, u32[]{:S(2)}) %collective-permute-start.1) | collective-permute-done | bytes 12320 | tf_op jit(solution)/shard_map/ppermute | solution.py:62
  11.8 0.1 shard_map.144
  11.9 0.7 %collective-permute-start.2 = (f32[144,128]{1,0:T(8,128)S(1)}, f32[144,128]{1,0:T(8,128)S(1)}, u32[]{:S(2)}, u32[]{:S(2)}) collective-permute-start(f32[144,128]{1,0:T(8,128)S(1)} %get-tuple-element.57), channel_id=1, source_target_pairs={{1,2},{2,1},{3,4},{4,3},{5,6},{6,5},{9,10},{10,9},{11,12},{12,11},... | collective-permute-start | bytes 221192 | tf_op jit(solution)/shard_map/ppermute | solution.py:62
  12.6 6.1 %collective-permute-start.3 = (f32[144,128]{1,0:T(8,128)S(1)}, f32[144,128]{1,0:T(8,128)S(1)}, u32[]{:S(2)}, u32[]{:S(2)}) collective-permute-start(f32[144,128]{1,0:T(8,128)S(1)} %get-tuple-element.58), channel_id=1, source_target_pairs={{0,1},{1,0},{2,3},{3,2},{4,5},{5,4},{6,7},{7,6},{8,9},{9,8},{10,11... | collective-permute-start | bytes 221192 | tf_op jit(solution)/shard_map/ppermute | solution.py:62
  18.7 0.7 %shard_map.145 = (f32[32,128]{1,0:T(8,128)S(1)}, f32[32,128]{1,0:T(8,128)S(1)}, f32[8,128]{1,0:T(8,128)S(1)}, f32[8,128]{1,0:T(8,128)S(1)}, s32[8,128]{1,0:T(8,1...) custom-call(s32[8,128]{1,0:T(8,128)S(1)} %get-tuple-element.46.meta_ref, ...), custom_call_target="tpu_custom_call" | custom-call | flops 4194304 | bytes 524288 | tf_op jit(solution)/shard_map/pallas_call | solution.py:46
  19.4 1.6 %collective-permute-done.3.yi_ref = f32[144,128]{1,0:T(8,128)S(1)} collective-permute-done((f32[144,128]{1,0:T(8,128)S(1)}, f32[144,128]{1,0:T(8,128)S(1)}, u32[]{:S(2)}, u32[]{:S(2)}) %collective-permute-start.3) | collective-permute-done | bytes 73760 | tf_op jit(solution)/shard_map/ppermute | solution.py:62
  21.0 0.8 %shard_map.146 = (f32[512,128]{1,0:T(8,128)S(1)}, f32[32,128]{1,0:T(8,128)S(1)}, f32[72,128]{1,0:T(8,128)S(1)}, f32[72,128]{1,0:T(8,128)S(1)}) custom-call(f32[512,128]{1,0:T(8,128)S(1)} %get-tuple-element.47.turned_ref, s32[8,128]{1,0:T(8,128)S(1)} %get-tuple-element.46.meta_ref, f32[160,128]{1,0:T(8,128)S(1)} %get-tuple-element.56.merged_ref, ...), custom_call_target="tpu_custom_call" | custom-call | flops 4194304 | bytes 524288 | tf_op jit(solution)/shard_map/pallas_call | solution.py:46
  21.9 1.9 %collective-permute-start.4 = (f32[72,128]{1,0:T(8,128)S(1)}, f32[72,128]{1,0:T(8,128)S(1)}, u32[]{:S(2)}, u32[]{:S(2)}) collective-permute-start(f32[72,128]{1,0:T(8,128)S(1)} %get-tuple-element.64), channel_id=1, source_target_pairs={{0,8},{8,0},{16,24},{24,16},{32,40},{40,32},{48,56},{56,48},{64,72... | collective-permute-start | bytes 110600 | tf_op jit(solution)/shard_map/ppermute | solution.py:62
  23.8 0.7 %shard_map.147.kept_sums_ref = f32[288,128]{1,0:T(8,128)S(1)} custom-call(f32[512,128]{1,0:T(8,128)S(1)} %get-tuple-element.61.fresh_ref.kept_ref, s32[8,128]{1,0:T(8,128)S(1)} %get-tuple-element.63.target_ref, f32[24,128]{1,0:T(8,128)S(1)} %get-tuple-element.49.tables_ref), custom_call_target="tpu_custom_call" | custom-call | flops 4194304 | bytes 524288 | tf_op jit(solution)/shard_map/pallas_call | solution.py:46
  24.5 0.5 collective-permute-done.4.from_near_ref
  25.0 0.6 %shard_map.148 = (f32[64,128]{1,0:T(8,128)S(1)}, f32[136,128]{1,0:T(8,128)S(1)}) custom-call(f32[288,128]{1,0:T(8,128)S(1)} %shard_map.147.kept_sums_ref, f32[72,128]{1,0:T(8,128)S(1)} %collective-permute-done.4.from_near_ref, f32[72,128]{1,0:T(8,128)S(1)} %get-tuple-element.65.to_far_ref, f32[24,128]{1,0:T(8,128)S(1)} %get-tuple-element.49.tables_ref), custom_call_target="tpu_custom_call" | custom-call | flops 4194304 | bytes 524288 | tf_op jit(solution)/shard_map/pallas_call | solution.py:46
  25.6 4.4 %collective-permute-start.5 = (f32[136,128]{1,0:T(8,128)S(1)}, f32[136,128]{1,0:T(8,128)S(1)}, u32[]{:S(2)}, u32[]{:S(2)}) collective-permute-start(f32[136,128]{1,0:T(8,128)S(1)} %get-tuple-element.67), channel_id=1, source_target_pairs={{8,16},{16,8},{24,32},{32,24},{40,48},{48,40},{56,64},{64,56},{72,... | collective-permute-start | bytes 208904 | tf_op jit(solution)/shard_map/ppermute | solution.py:62
  30.0 0.1 shard_map.149.near_nodes_ref.near_ref
  30.1 0.2 shard_map.150
  30.4 4.5 %collective-permute-done.5.from_far_ref = f32[136,128]{1,0:T(8,128)S(1)} collective-permute-done((f32[136,128]{1,0:T(8,128)S(1)}, f32[136,128]{1,0:T(8,128)S(1)}, u32[]{:S(2)}, u32[]{:S(2)}) %collective-permute-start.5) | collective-permute-done | bytes 69664 | tf_op jit(solution)/shard_map/ppermute | solution.py:62
  34.9 1.9 %collective-permute-start.6 = (f32[16,128]{1,0:T(8,128)S(1)}, f32[16,128]{1,0:T(8,128)S(1)}, u32[]{:S(2)}, u32[]{:S(2)}) collective-permute-start(f32[16,128]{1,0:T(8,128)S(1)} %get-tuple-element.72), channel_id=1, source_target_pairs={{0,8},{8,0},{16,24},{24,16},{32,40},{40,32},{48,56},{56,48},{64,72... | collective-permute-start | bytes 24584 | tf_op jit(solution)/shard_map/ppermute | solution.py:62
  36.8 0.3 shard_map.152
  37.0 0.9 %collective-permute-done.6.from_near_ref = f32[16,128]{1,0:T(8,128)S(1)} collective-permute-done((f32[16,128]{1,0:T(8,128)S(1)}, f32[16,128]{1,0:T(8,128)S(1)}, u32[]{:S(2)}, u32[]{:S(2)}) %collective-permute-start.6) | collective-permute-done | bytes 8224 | tf_op jit(solution)/shard_map/ppermute | solution.py:62
  38.0 13.4 %all_to_all.5.slots_ref = f32[8,72,128]{2,1,0:T(8,128)S(1)} all-to-all(f32[8,72,128]{2,1,0:T(8,128)S(1)} %shard_map.153), channel_id=1, replica_groups=mesh['gx'=64,'gy'=8] {'gy'}, dimensions={0} | all-to-all | bytes 589824 | tf_op jit(solution)/shard_map/all_to_all | solution.py:955
  51.4 0.8 %shard_map.154 = (f32[128,512]{1,0:T(8,128)S(1)}, f32[160,128]{1,0:T(8,128)S(1)}, f32[72,128]{1,0:T(8,128)S(1)}, f32[72,128]{1,0:T(8,128)S(1)}) custom-call(f32[512,128]{1,0:T(8,128)S(1)} %get-tuple-element.61.fresh_ref.kept_ref, s32[8,128]{1,0:T(8,128)S(1)} %get-tuple-element.62.meta_ref, f32[8,72,128]{2,1,0:T(8,128)S(1)} %all_to_all.5.slots_ref, ...), custom_call_target="tpu_custom_call" | custom-call | flops 4194304 | bytes 524288 | tf_op jit(solution)/shard_map/pallas_call | solution.py:46
  52.2 2.9 %collective-permute-start.7 = (f32[72,128]{1,0:T(8,128)S(1)}, f32[72,128]{1,0:T(8,128)S(1)}, u32[]{:S(2)}, u32[]{:S(2)}) collective-permute-start(f32[72,128]{1,0:T(8,128)S(1)} %get-tuple-element.84), channel_id=1, source_target_pairs={{8,16},{16,8},{24,32},{32,24},{40,48},{48,40},{56,64},{64,56},{72,... | collective-permute-start | bytes 110600 | tf_op jit(solution)/shard_map/ppermute | solution.py:62
  55.1 1.9 %collective-permute-start.8 = (f32[72,128]{1,0:T(8,128)S(1)}, f32[72,128]{1,0:T(8,128)S(1)}, u32[]{:S(2)}, u32[]{:S(2)}) collective-permute-start(f32[72,128]{1,0:T(8,128)S(1)} %get-tuple-element.85), channel_id=1, source_target_pairs={{0,8},{8,0},{16,24},{24,16},{32,40},{40,32},{48,56},{56,48},{64,72... | collective-permute-start | bytes 110600 | tf_op jit(solution)/shard_map/ppermute | solution.py:62
  57.0 0.8 %shard_map.155 = (f32[256,512]{1,0:T(8,128)S(1)}, s32[8,128]{1,0:T(8,128)S(1)}) custom-call(f32[128,512]{1,0:T(8,128)S(1)} %get-tuple-element.76.advanced_ref, f32[128,128]{1,0:T(8,128)S(1)} %get-tuple-element.77.stays_ref, f32[160,128]{1,0:T(8,128)S(1)} %get-tuple-element.78.velocity_ref, f32[128,128]{1,0:T(8,128)S(1)} %get-tuple-element.79.turned_ref, ...), custom_call_target="tpu_custom_call" | custom-call | flops 4194304 | bytes 524288 | tf_op jit(solution)/shard_map/pallas_call | solution.py:46
  57.8 3.3 %collective-permute-done.7.xo_ref = f32[72,128]{1,0:T(8,128)S(1)} collective-permute-done((f32[72,128]{1,0:T(8,128)S(1)}, f32[72,128]{1,0:T(8,128)S(1)}, u32[]{:S(2)}, u32[]{:S(2)}) %collective-permute-start.7) | collective-permute-done | bytes 36896 | tf_op jit(solution)/shard_map/ppermute | solution.py:62
  61.1 0.8 %shard_map.156 = (f32[256,512]{1,0:T(8,128)}, s32[2,128]{1,0:T(2,128)}, s32[2,128]{1,0:T(2,128)}) custom-call(f32[256,512]{1,0:T(8,128)S(1)} %get-tuple-element.81.part_ref, s32[8,128]{1,0:T(8,128)S(1)} %get-tuple-element.82.old_meta_ref, s32[8,128]{1,0:T(8,128)S(1)} %get-tuple-element.83.tail_ref, f32[72,128]{1,0:T(8,128)S(1)} %collective-permute-done.7.xo_ref, ...), custom_call_target="tpu_custom_call" | custom-call | flops 4194304 | bytes 524288 | tf_op jit(solution)/shard_map/pallas_call | solution.py:46
  (29 shorter events, 0.4 us)
Async XLA Ops:
  0.6 1.1 %copy-start = (f32[128,512]{1,0:T(8,128)S(1)}, f32[128,512]{1,0:T(8,128)}, u32[]{:S(2)}) copy-start(f32[128,512]{1,0:T(8,128)} %points_ref.3) | copy-start | bytes 786436
  0.6 0.7 %copy-start.4 = (f32[8]{0:T(128)S(1)}, f32[8]{0:T(128)}, u32[]{:S(2)}) copy-start(f32[8]{0:T(128)} %param.16) | copy-start | bytes 100
  0.7 0.7 %copy-start.5 = (f32[8]{0:T(128)S(1)}, f32[8]{0:T(128)}, u32[]{:S(2)}) copy-start(f32[8]{0:T(128)} %param.17) | copy-start | bytes 100
  0.7 0.7 %copy-start.6 = (s32[64]{0:T(128)S(1)}, s32[64]{0:T(128)}, u32[]{:S(2)}) copy-start(s32[64]{0:T(128)} %param.18) | copy-start | bytes 772
  0.7 0.7 %copy-start.7 = (s32[64]{0:T(128)S(1)}, s32[64]{0:T(128)}, u32[]{:S(2)}) copy-start(s32[64]{0:T(128)} %param.19) | copy-start | bytes 772
  0.7 0.7 %copy-start.8 = (s32[64]{0:T(128)S(1)}, s32[64]{0:T(128)}, u32[]{:S(2)}) copy-start(s32[64]{0:T(128)} %param.20) | copy-start | bytes 772
  0.7 0.7 %copy-start.9 = (s32[64]{0:T(128)S(1)}, s32[64]{0:T(128)}, u32[]{:S(2)}) copy-start(s32[64]{0:T(128)} %param.21) | copy-start | bytes 772
  0.7 0.7 %copy-start.10 = (s32[64]{0:T(128)S(1)}, s32[64]{0:T(128)}, u32[]{:S(2)}) copy-start(s32[64]{0:T(128)} %param.22) | copy-start | bytes 772
  0.7 0.7 %copy-start.11 = (s32[64]{0:T(128)S(1)}, s32[64]{0:T(128)}, u32[]{:S(2)}) copy-start(s32[64]{0:T(128)} %param.23) | copy-start | bytes 772
  0.7 0.7 %copy-start.1 = (s32[128]{0:T(128)S(1)}, s32[128]{0:T(128)}, u32[]{:S(2)}) copy-start(s32[128]{0:T(128)} %param.13) | copy-start | bytes 1540
  0.8 0.7 %copy-start.2 = (s32[128]{0:T(128)S(1)}, s32[128]{0:T(128)}, u32[]{:S(2)}) copy-start(s32[128]{0:T(128)} %param.14) | copy-start | bytes 1540
  0.8 0.7 %copy-start.3 = (f32[8]{0:T(128)S(1)}, f32[8]{0:T(128)}, u32[]{:S(2)}) copy-start(f32[8]{0:T(128)} %param.15) | copy-start | bytes 100
  2.5 8.6 %collective-permute-start = (f32[24,128]{1,0:T(8,128)S(1)}, f32[24,128]{1,0:T(8,128)S(1)}, u32[]{:S(2)}, u32[]{:S(2)}) collective-permute-start(f32[24,128]{1,0:T(8,128)S(1)} %get-tuple-element.51), channel_id=1, source_target_pairs={{8,16},{16,8},{24,32},{32,24},{40,48},{48,40},{56,64},{64,56},{72,... | collective-permute-start | bytes 36872 | tf_op jit(solution)/shard_map/ppermute | solution.py:62
  8.7 3.1 %collective-permute-start.1 = (f32[24,128]{1,0:T(8,128)S(1)}, f32[24,128]{1,0:T(8,128)S(1)}, u32[]{:S(2)}, u32[]{:S(2)}) collective-permute-start(f32[24,128]{1,0:T(8,128)S(1)} %get-tuple-element.52), channel_id=1, source_target_pairs={{0,8},{8,0},{16,24},{24,16},{32,40},{40,32},{48,56},{56,48},{64,72... | collective-permute-start | bytes 36872 | tf_op jit(solution)/shard_map/ppermute | solution.py:62
  11.9 7.5 %collective-permute-start.2 = (f32[144,128]{1,0:T(8,128)S(1)}, f32[144,128]{1,0:T(8,128)S(1)}, u32[]{:S(2)}, u32[]{:S(2)}) collective-permute-start(f32[144,128]{1,0:T(8,128)S(1)} %get-tuple-element.57), channel_id=1, source_target_pairs={{1,2},{2,1},{3,4},{4,3},{5,6},{6,5},{9,10},{10,9},{11,12},{12,11},... | collective-permute-start | bytes 221192 | tf_op jit(solution)/shard_map/ppermute | solution.py:62
  12.6 8.4 %collective-permute-start.3 = (f32[144,128]{1,0:T(8,128)S(1)}, f32[144,128]{1,0:T(8,128)S(1)}, u32[]{:S(2)}, u32[]{:S(2)}) collective-permute-start(f32[144,128]{1,0:T(8,128)S(1)} %get-tuple-element.58), channel_id=1, source_target_pairs={{0,1},{1,0},{2,3},{3,2},{4,5},{5,4},{6,7},{7,6},{8,9},{9,8},{10,11... | collective-permute-start | bytes 221192 | tf_op jit(solution)/shard_map/ppermute | solution.py:62
  21.9 3.1 %collective-permute-start.4 = (f32[72,128]{1,0:T(8,128)S(1)}, f32[72,128]{1,0:T(8,128)S(1)}, u32[]{:S(2)}, u32[]{:S(2)}) collective-permute-start(f32[72,128]{1,0:T(8,128)S(1)} %get-tuple-element.64), channel_id=1, source_target_pairs={{0,8},{8,0},{16,24},{24,16},{32,40},{40,32},{48,56},{56,48},{64,72... | collective-permute-start | bytes 110600 | tf_op jit(solution)/shard_map/ppermute | solution.py:62
  25.6 9.2 %collective-permute-start.5 = (f32[136,128]{1,0:T(8,128)S(1)}, f32[136,128]{1,0:T(8,128)S(1)}, u32[]{:S(2)}, u32[]{:S(2)}) collective-permute-start(f32[136,128]{1,0:T(8,128)S(1)} %get-tuple-element.67), channel_id=1, source_target_pairs={{8,16},{16,8},{24,32},{32,24},{40,48},{48,40},{56,64},{64,56},{72,... | collective-permute-start | bytes 208904 | tf_op jit(solution)/shard_map/ppermute | solution.py:62
  34.9 3.1 %collective-permute-start.6 = (f32[16,128]{1,0:T(8,128)S(1)}, f32[16,128]{1,0:T(8,128)S(1)}, u32[]{:S(2)}, u32[]{:S(2)}) collective-permute-start(f32[16,128]{1,0:T(8,128)S(1)} %get-tuple-element.72), channel_id=1, source_target_pairs={{0,8},{8,0},{16,24},{24,16},{32,40},{40,32},{48,56},{56,48},{64,72... | collective-permute-start | bytes 24584 | tf_op jit(solution)/shard_map/ppermute | solution.py:62
  52.2 8.9 %collective-permute-start.7 = (f32[72,128]{1,0:T(8,128)S(1)}, f32[72,128]{1,0:T(8,128)S(1)}, u32[]{:S(2)}, u32[]{:S(2)}) collective-permute-start(f32[72,128]{1,0:T(8,128)S(1)} %get-tuple-element.84), channel_id=1, source_target_pairs={{8,16},{16,8},{24,32},{32,24},{40,48},{48,40},{56,64},{64,56},{72,... | collective-permute-start | bytes 110600 | tf_op jit(solution)/shard_map/ppermute | solution.py:62
  55.1 6.0 %collective-permute-start.8 = (f32[72,128]{1,0:T(8,128)S(1)}, f32[72,128]{1,0:T(8,128)S(1)}, u32[]{:S(2)}, u32[]{:S(2)}) collective-permute-start(f32[72,128]{1,0:T(8,128)S(1)} %get-tuple-element.85), channel_id=1, source_target_pairs={{0,8},{8,0},{16,24},{24,16},{32,40},{40,32},{48,56},{56,48},{64,72... | collective-permute-start | bytes 110600 | tf_op jit(solution)/shard_map/ppermute | solution.py:62

commit v7 on v6

--- a/solution.py
+++ b/solution.py
@@ -23,9 +23,8 @@
 KEPT = 3
 PACK = 64
 NEAR = 32
-SHARE = 29
-REST = 4 * MCAP - 2 * SHARE
-SLOT = PACK + SUB
+HALF = LANES // 2
+SLOT = PACK // 2 + 2 * SUB
 CROSS_MSG = 2 * SUB + PIECES * 2 * MCAP
 SPAN = 3 * CY + 3
 
@@ -60,6 +59,11 @@
     for low in range(first, count - 1, 2):
         pairs += [(low, low + 1), (low + 1, low)]
     return lax.ppermute(value, axis, pairs)
+
+
+def chip_columns():
+    down, across = (lax.axis_size("gx"), lax.axis_size("gy"))
+    return [list(range(first * across, (first + 2) * across)) for first in range(0, down, 2)]
 
 
 def iota(shape, dim):
@@ -378,37 +382,52 @@
         put_pieces(ref, 2 * SUB, rows_ref[first : first + movers, :])
 
 
-def merge_far(own_ref, from_far_ref, near_nodes_ref, cross_tags_ref, merged_ref, halo_ref):
-    del near_nodes_ref, cross_tags_ref
+def merge_far(own_ref, from_far_ref, near_ref, cross_tags_ref, merged_ref, slots_ref):
+    del cross_tags_ref
     merged = own_ref[...] + from_far_ref[0:PACK, :]
     merged_ref[...] = merged
+    gy = lax.axis_index("gy")
+    mine = lax.axis_index("gx") & 1
     low = jnp.where(iota((2 * SUB, LANES), 0) < 3 * KEPT, merged[0 : 2 * SUB], 0.0)
-    halo_ref[...] = jnp.where(parity("gx"), low, merged[PACK - 2 * SUB : PACK])
-
-
-def merge_two(sums_ref, from_near_ref, near_ref, new_meta_ref, slots_ref, slot_ref):
-    del new_meta_ref
-    odd = parity("gx")
-    from_near = from_near_ref[...]
-    slot_ref[0:PACK, :] = sums_ref[...]
-    last = PACK - 2 * SUB
-    slot_ref[0 : 2 * SUB] = sums_ref[0 : 2 * SUB] + jnp.where(odd, from_near, 0.0)
-    slot_ref[last:PACK] = sums_ref[last:PACK] + jnp.where(odd, 0.0, from_near)
-    lane = iota((NEAR, LANES), 1)
+    halo = jnp.where(parity("gx"), low, merged[PACK - 2 * SUB : PACK])
     near = near_ref[...]
-    for half in range(2):
-        start = half * NEAR
-        moved = pltpu.roll(near, SPAN - SHARE * half, 1)
-        slot_ref[start : start + NEAR, :] = jnp.where(lane >= SPAN, moved, slot_ref[start : start + NEAR, :])
-    lane = iota((SUB, LANES), 1)
-    rest = jnp.zeros((SUB, LANES), F32)
-    for part in range(NEAR // SUB):
-        moved = pltpu.roll(near[part * SUB : (part + 1) * SUB], LANES - 2 * SHARE + REST * part, 1)
-        rest = jnp.where((lane >= REST * part) & (lane < REST * (part + 1)), moved, rest)
-    slot_ref[PACK:SLOT, :] = rest
-    value = slot_ref[...]
-    for index in range(slots_ref.shape[0]):
-        slots_ref[index] = value
+    tile_lane = iota((SUB, LANES), 1)
+    velocities = []
+    for start in (0, HALF // 2):
+        tile = jnp.zeros((SUB, LANES), F32)
+        for part in range(NEAR // SUB):
+            shift = (part * NEAR - start) % LANES
+            rows = near[part * SUB : (part + 1) * SUB]
+            moved = pltpu.roll(rows, shift, 1) if shift else rows
+            tile = jnp.where((tile_lane >= part * NEAR) & (tile_lane < (part + 1) * NEAR), moved, tile)
+        velocities.append(tile)
+    down, up = by_side(velocities[0], velocities[1], parity("gy"))
+    lane = iota((PACK, LANES), 1)
+    half_lane = iota((PACK // 2, LANES), 1)
+    halo_lane = iota((2 * SUB, LANES), 1)
+    across = slots_ref.shape[0] // 2
+    for index in range(across):
+        away = index - gy
+        first = jnp.where(away > 0, 0, CY)
+        shift = CY * away + first
+        source = lane + shift
+        valid = (source >= 0) & (source < SPAN) & (lane + first < SPAN)
+        window = jnp.where(valid, pltpu.roll(merged, (-shift) & (LANES - 1), 1), 0.0)
+        slot = mine * across + index
+        right = pltpu.roll(window[PACK // 2 :], HALF, 1)
+        slots_ref[slot, 0 : PACK // 2, :] = jnp.where(half_lane < HALF, window[0 : PACK // 2], right)
+        rest = jnp.zeros((SUB, LANES), F32)
+        for group in range(PACK // SUB):
+            moved = pltpu.roll(window[group * SUB : (group + 1) * SUB], HALF + 3 * group, 1)
+            rest = jnp.where((tile_lane >= 3 * group) & (tile_lane < 3 * group + 3), moved, rest)
+        slots_ref[slot, PACK // 2 : PACK // 2 + SUB, :] = rest
+        slots_ref[slot, PACK // 2 + SUB : SLOT, :] = jnp.where(away > 0, up, down)
+        shift = CY * away
+        source = halo_lane + shift
+        valid = (source >= 0) & (source < SPAN) & (halo_lane < SPAN)
+        slot = (1 - mine) * across + index
+        slots_ref[slot, 0 : 2 * SUB, :] = jnp.where(valid, pltpu.roll(halo, (-shift) & (LANES - 1), 1), 0.0)
+        slots_ref[slot, 2 * SUB : SLOT, :] = jnp.zeros((SLOT - 2 * SUB, LANES), F32)
 
 
 def put_velocity(row, x, node_y, velocity_ref):
@@ -435,16 +454,37 @@
     velocity_ref[DEPTHS * SUB :, :] = jnp.zeros((ROWS - DEPTHS * SUB, LANES), F32)
 
 
-def velocity_two(slots_ref, packed_ref, velocity_ref):
+def velocity_two(slots_ref, merged_ref, packed_ref, velocity_ref):
     gy = lax.axis_index("gy")
-    lane = iota((PACK, LANES), 1)
-    total = jnp.zeros((PACK, LANES), F32)
-    for index in range(slots_ref.shape[0]):
-        shift = CY * (index - gy)
-        moved = pltpu.roll(slots_ref[index, 0:PACK, :], shift & (LANES - 1), 1)
-        valid = (lane >= shift) & (lane < SPAN + shift) & (lane < SPAN)
-        total = total + jnp.where(valid, moved, 0.0)
+    mine = lax.axis_index("gx") & 1
+    odd = parity("gx")
+    across = slots_ref.shape[0] // 2
+    part = PACK // 2 + SUB
+    from_low = jnp.zeros((part, LANES), F32)
+    from_high = jnp.zeros((part, LANES), F32)
+    halo = jnp.zeros((2 * SUB, LANES), F32)
+    for index in range(across):
+        value = slots_ref[mine * across + index, 0:part, :]
+        from_low = from_low + jnp.where(index < gy, value, 0.0)
+        from_high = from_high + jnp.where(index > gy, value, 0.0)
+        halo = halo + slots_ref[(1 - mine) * across + index, 0 : 2 * SUB, :]
+    half_lane = iota((PACK // 2, LANES), 1)
+    tile_lane = iota((SUB, LANES), 1)
+    total = merged_ref[...]
+    for value, first in ((from_low, 0), (from_high, CY)):
+        body = value[0 : PACK // 2]
+        upper = jnp.where(half_lane < HALF, body, 0.0)
+        lower = jnp.where(half_lane < HALF, pltpu.roll(body, HALF, 1), 0.0)
+        rest = []
+        for group in range(PACK // SUB):
+            moved = pltpu.roll(value[PACK // 2 :], HALF - 3 * group, 1)
+            rest.append(jnp.where((tile_lane >= HALF) & (tile_lane < HALF + 3), moved, 0.0))
+        window = jnp.concatenate([upper, lower], axis=0) + jnp.concatenate(rest, axis=0)
+        total = total + (pltpu.roll(window, first, 1) if first else window)
     packed_ref[...] = total
+    last = PACK - 2 * SUB
+    packed_ref[0 : 2 * SUB, :] = total[0 : 2 * SUB] + jnp.where(odd, halo, 0.0)
+    packed_ref[last:PACK, :] = total[last:PACK] + jnp.where(odd, 0.0, halo)
     node_y = (gy - 1) * CY - 1 + iota((SUB, LANES), 1)
     for x in range(DEPTHS):
         put_velocity(packed_ref[KEPT * x : KEPT * x + SUB, :], x, node_y, velocity_ref)
@@ -694,11 +734,11 @@
 
 
 def advance_two(
-    kept_ref, meta_ref, slots_ref, tables_ref, chosen_ref, tags_ref,
+    kept_ref, meta_ref, slots_ref, merged_ref, tables_ref, chosen_ref, tags_ref,
     rows_ref, velocity_ref, far_message_ref, near_message_ref,
     packed_ref, fresh_ref,
 ):
-    velocity_two(slots_ref, packed_ref, velocity_ref)
+    velocity_two(slots_ref, merged_ref, packed_ref, velocity_ref)
     cells, materials = (meta_ref[0:1, :], meta_ref[1:2, :])
 
     def store(c, k, value):
@@ -713,17 +753,13 @@
 
 
 def near_movers(slots_ref, index):
-    lane = iota((NEAR, LANES), 1)
-    rest = slots_ref[index, PACK:SLOT, :]
+    lane = iota((SUB, LANES), 1)
+    tile = slots_ref[index, PACK // 2 + SUB : SLOT, :]
     parts = []
     for part in range(NEAR // SUB):
-        parts.append(pltpu.roll(rest, (2 * SHARE - REST * part) % LANES, 1))
-    nodes = jnp.concatenate(parts, axis=0)
-    for half in range(2):
-        first = SHARE * half
-        moved = pltpu.roll(slots_ref[index, half * NEAR : (half + 1) * NEAR, :], LANES - SPAN + first, 1)
-        nodes = jnp.where((lane >= first) & (lane < first + SHARE), moved, nodes)
-    return nodes
+        moved = pltpu.roll(tile, LANES - part * NEAR, 1) if part else tile
+        parts.append(jnp.where(lane < 2 * MCAP, moved, 0.0))
+    return jnp.concatenate(parts, axis=0)
 
 
 def settle(
@@ -748,7 +784,6 @@
     move_points(load, store_small, stride // SUB, node_getter(near), materials, tables_ref)
 
     gy = lax.axis_index("gy")
-    odd = parity("gy")
     lane = iota((SUB, LANES), 1)
     tags = tags_ref[...]
     tail = jnp.zeros((SUB, LANES), F32)
@@ -759,13 +794,11 @@
     tail_ref[...] = jnp.where(lane < 2 * MCAP, new_meta_ref[...], tail)
     tags = repeated(tags, 4 * MCAP).astype(jnp.int32) - materials_row
 
-    last = slots_ref.shape[0] - 1
-    below = near_movers(slots_ref, jnp.maximum(gy - 1, 0))
-    above = near_movers(slots_ref, jnp.minimum(gy + 1, last))
-    below = jnp.where(odd, below, pltpu.roll(below, LANES - 2 * MCAP, 1))
-    above = jnp.where(odd, above, pltpu.roll(above, 2 * MCAP, 1))
-    many = iota((NEAR, LANES), 1)
-    nodes = jnp.where(many < 2 * MCAP, below, jnp.where(many < 4 * MCAP, above, 0.0))
+    across = slots_ref.shape[0] // 2
+    column = (lax.axis_index("gx") & 1) * across
+    below = near_movers(slots_ref, column + jnp.maximum(gy - 1, 0))
+    above = near_movers(slots_ref, column + jnp.minimum(gy + 1, across - 1))
+    nodes = below + pltpu.roll(above, 2 * MCAP, 1)
     nodes = nodes + pltpu.roll(nodes, 4 * MCAP, 1)
 
     def node_of(a, b, component):
@@ -869,7 +902,7 @@
     half_form = ((wide // 2, LANES), F32)
     quarter_form = ((wide // 4, LANES), F32)
     near_form = ((NEAR, LANES), F32)
-    slots_form = ((lax.axis_size("gy"), SLOT, LANES), F32)
+    slots_form = ((2 * lax.axis_size("gy"), SLOT, LANES), F32)
     scratch = lambda form: pltpu.VMEM(*form)
     left = pltpu.VMEM((ROWS, 4 * LANES), F32)
 
@@ -935,30 +968,19 @@
     cross, cross_tags = call(
         arrange_cross, (half_form, tile), (scratch(turned_form),), (IN_VMEM,) * 2, cross_far, cross_near
     )
-    merged, halo_message = call(
-        merge_far,
-        (packed_form, ((2 * SUB, LANES), F32)),
-        (),
-        (IN_VMEM,) * 4,
-        own, from_far, near_nodes, cross_tags,
+    merged, slots = call(
+        merge_far, (packed_form, slots_form), (), (IN_VMEM,) * 4, own, from_far, near_nodes, cross_tags
     )
     turned, new_meta = call(
         arrange_depth, (quarter_form, tags), (scratch(turned_form),), (IN_VMEM,) * 2, from_near, from_far
     )
-    (slots,) = call(
-        merge_two,
-        (slots_form,),
-        (pltpu.VMEM((SLOT, LANES), F32),),
-        (IN_VMEM,) * 4,
-        merged, swap(halo_message, "gx", 0), near_nodes, new_meta,
-    )
-    slots = lax.all_to_all(slots, "gy", 0, 0)
+    slots = lax.all_to_all(slots, ("gx", "gy"), 0, 0, axis_index_groups=chip_columns())
     advanced, velocity, far, near = call(
         advance_two,
         (((LANES, wide), F32), grid, message, message),
         (scratch(packed_form), scratch(turned_form)),
-        (IN_VMEM,) * 6,
-        fresh, kept_a, slots, tables, chosen_b, tags_b,
+        (IN_VMEM,) * 7,
+        fresh, kept_a, slots, merged, tables, chosen_b, tags_b,
     )
     arrived = along_depth(far, near)
     final_form = ((2 * LANES, wide), F32)

time: 62.3 us -> 61.1 us (0.981)
  waiting for transfers between devices: 11.4 us -> 9.86 us
  starting transfers between devices: 27.9 us -> 26.4 us
  blocking collectives: 13.4 us -> 14.8 us
    ppermute x9 -> x8, waiting for transfers between devices: 11.4 us -> 9.86 us  [swap(): return lax.ppermute(value, axis, pairs)]
    ppermute x9 -> x8, starting transfers between devices: 27.9 us -> 26.4 us  [swap(): return lax.ppermute(value, axis, pairs)]
    all_to_all x1, blocking collectives: 13.4 us -> 14.8 us  [shards(): lax.all_to_all(slots, ('gx', 'gy'), 0, 0, axis_index_groups=chip_columns())]
    pallas_call x18 -> x17, Pallas kernels: 7.47 us -> 7.88 us  [call(): pl.pallas_call(kernel, out_shape=tuple((jax.ShapeDtypeStruct(shape, dtype...]
  transfers between devices with their start and end apart: 9 -> 8, of which waited for: 6 -> 5; matrix products, arithmetic and copies ran while one was open for 0% -> 0% of each run, Pallas kernels for 5% -> 5%
where the time goes in v7:
time: 61.1 us; the launch traced here: 60.8 us
  starting transfers between devices  26.4 us (43%)
  blocking collectives  14.8 us (24%)
  waiting for transfers between devices  9.86 us (16%)
  Pallas kernels  7.88 us (13%)
  local copies, waits for them, and re-layouts  0.91 us (1%)
  between operations  0.91 us (1%)
    ppermute x8, starting transfers between devices, swap(): return lax.ppermute(value, axis, pairs)  26.4 us
    all_to_all x1, blocking collectives, shards(): lax.all_to_all(slots, ('gx', 'gy'), 0, 0, axis_index_groups=chip_columns())  14.8 us
    ppermute x8, waiting for transfers between devices, swap(): return lax.ppermute(value, axis, pairs)  9.86 us
    pallas_call x17, Pallas kernels, call(): pl.pallas_call(kernel, out_shape=tuple((jax.ShapeDtypeStruct(shape, dtype...  7.88 us
  transfers between devices with their start and end apart: 8, of which 5 were waited for; matrix products, arithmetic and copies ran while one was open for 0% of the time, Pallas kernels for 5%

profile of v7, /device:TPU:384, one launch (start us, length us, event | category | flops | bytes accessed | tf_op | source)
XLA Modules:
  0.0 60.8 jit_solution(3666745645307385401)
XLA Ops:
  0.8 0.6 copy-done.4
  1.5 0.1 shard_map.140
  1.6 0.1 copy-done
  1.8 0.5 shard_map.141
  2.3 0.3 shard_map.142
  2.5 6.2 %collective-permute-start = (f32[24,128]{1,0:T(8,128)S(1)}, f32[24,128]{1,0:T(8,128)S(1)}, u32[]{:S(2)}, u32[]{:S(2)}) collective-permute-start(f32[24,128]{1,0:T(8,128)S(1)} %get-tuple-element.51), channel_id=1, source_target_pairs={{8,16},{16,8},{24,32},{32,24},{40,48},{48,40},{56,64},{64,56},{72,... | collective-permute-start | bytes 36872 | tf_op jit(solution)/shard_map/ppermute | solution.py:61
  8.7 1.9 %collective-permute-start.1 = (f32[24,128]{1,0:T(8,128)S(1)}, f32[24,128]{1,0:T(8,128)S(1)}, u32[]{:S(2)}, u32[]{:S(2)}) collective-permute-start(f32[24,128]{1,0:T(8,128)S(1)} %get-tuple-element.52), channel_id=1, source_target_pairs={{0,8},{8,0},{16,24},{24,16},{32,40},{40,32},{48,56},{56,48},{64,72... | collective-permute-start | bytes 36872 | tf_op jit(solution)/shard_map/ppermute | solution.py:61
  10.7 0.5 shard_map.143
  11.2 0.6 %collective-permute-done.1.from_inner_ref = f32[24,128]{1,0:T(8,128)S(1)} collective-permute-done((f32[24,128]{1,0:T(8,128)S(1)}, f32[24,128]{1,0:T(8,128)S(1)}, u32[]{:S(2)}, u32[]{:S(2)}) %collective-permute-start.1) | collective-permute-done | bytes 12320 | tf_op jit(solution)/shard_map/ppermute | solution.py:61
  11.8 0.1 shard_map.144
  11.9 0.7 %collective-permute-start.2 = (f32[144,128]{1,0:T(8,128)S(1)}, f32[144,128]{1,0:T(8,128)S(1)}, u32[]{:S(2)}, u32[]{:S(2)}) collective-permute-start(f32[144,128]{1,0:T(8,128)S(1)} %get-tuple-element.57), channel_id=1, source_target_pairs={{1,2},{2,1},{3,4},{4,3},{5,6},{6,5},{9,10},{10,9},{11,12},{12,11},... | collective-permute-start | bytes 221192 | tf_op jit(solution)/shard_map/ppermute | solution.py:61
  12.6 6.1 %collective-permute-start.3 = (f32[144,128]{1,0:T(8,128)S(1)}, f32[144,128]{1,0:T(8,128)S(1)}, u32[]{:S(2)}, u32[]{:S(2)}) collective-permute-start(f32[144,128]{1,0:T(8,128)S(1)} %get-tuple-element.58), channel_id=1, source_target_pairs={{0,1},{1,0},{2,3},{3,2},{4,5},{5,4},{6,7},{7,6},{8,9},{9,8},{10,11... | collective-permute-start | bytes 221192 | tf_op jit(solution)/shard_map/ppermute | solution.py:61
  18.7 0.7 %shard_map.145 = (f32[32,128]{1,0:T(8,128)S(1)}, f32[32,128]{1,0:T(8,128)S(1)}, f32[8,128]{1,0:T(8,128)S(1)}, f32[8,128]{1,0:T(8,128)S(1)}, s32[8,128]{1,0:T(8,1...) custom-call(s32[8,128]{1,0:T(8,128)S(1)} %get-tuple-element.46.meta_ref, ...), custom_call_target="tpu_custom_call" | custom-call | flops 4194304 | bytes 524288 | tf_op jit(solution)/shard_map/pallas_call | solution.py:45
  19.4 1.6 %collective-permute-done.3.yi_ref = f32[144,128]{1,0:T(8,128)S(1)} collective-permute-done((f32[144,128]{1,0:T(8,128)S(1)}, f32[144,128]{1,0:T(8,128)S(1)}, u32[]{:S(2)}, u32[]{:S(2)}) %collective-permute-start.3) | collective-permute-done | bytes 73760 | tf_op jit(solution)/shard_map/ppermute | solution.py:61
  21.0 0.8 %shard_map.146 = (f32[512,128]{1,0:T(8,128)S(1)}, f32[32,128]{1,0:T(8,128)S(1)}, f32[72,128]{1,0:T(8,128)S(1)}, f32[72,128]{1,0:T(8,128)S(1)}) custom-call(f32[512,128]{1,0:T(8,128)S(1)} %get-tuple-element.47.turned_ref, s32[8,128]{1,0:T(8,128)S(1)} %get-tuple-element.46.meta_ref, f32[160,128]{1,0:T(8,128)S(1)} %get-tuple-element.56.merged_ref, ...), custom_call_target="tpu_custom_call" | custom-call | flops 4194304 | bytes 524288 | tf_op jit(solution)/shard_map/pallas_call | solution.py:45
  21.9 1.9 %collective-permute-start.4 = (f32[72,128]{1,0:T(8,128)S(1)}, f32[72,128]{1,0:T(8,128)S(1)}, u32[]{:S(2)}, u32[]{:S(2)}) collective-permute-start(f32[72,128]{1,0:T(8,128)S(1)} %get-tuple-element.64), channel_id=1, source_target_pairs={{0,8},{8,0},{16,24},{24,16},{32,40},{40,32},{48,56},{56,48},{64,72... | collective-permute-start | bytes 110600 | tf_op jit(solution)/shard_map/ppermute | solution.py:61
  23.8 0.7 %shard_map.147.kept_sums_ref = f32[288,128]{1,0:T(8,128)S(1)} custom-call(f32[512,128]{1,0:T(8,128)S(1)} %get-tuple-element.61.fresh_ref.kept_ref, s32[8,128]{1,0:T(8,128)S(1)} %get-tuple-element.63.target_ref, f32[24,128]{1,0:T(8,128)S(1)} %get-tuple-element.49.tables_ref), custom_call_target="tpu_custom_call" | custom-call | flops 4194304 | bytes 524288 | tf_op jit(solution)/shard_map/pallas_call | solution.py:45
  24.5 0.5 collective-permute-done.4.from_near_ref
  25.0 0.6 %shard_map.148 = (f32[64,128]{1,0:T(8,128)S(1)}, f32[136,128]{1,0:T(8,128)S(1)}) custom-call(f32[288,128]{1,0:T(8,128)S(1)} %shard_map.147.kept_sums_ref, f32[72,128]{1,0:T(8,128)S(1)} %collective-permute-done.4.from_near_ref, f32[72,128]{1,0:T(8,128)S(1)} %get-tuple-element.65.to_far_ref, f32[24,128]{1,0:T(8,128)S(1)} %get-tuple-element.49.tables_ref), custom_call_target="tpu_custom_call" | custom-call | flops 4194304 | bytes 524288 | tf_op jit(solution)/shard_map/pallas_call | solution.py:45
  25.6 4.4 %collective-permute-start.5 = (f32[136,128]{1,0:T(8,128)S(1)}, f32[136,128]{1,0:T(8,128)S(1)}, u32[]{:S(2)}, u32[]{:S(2)}) collective-permute-start(f32[136,128]{1,0:T(8,128)S(1)} %get-tuple-element.67), channel_id=1, source_target_pairs={{8,16},{16,8},{24,32},{32,24},{40,48},{48,40},{56,64},{64,56},{72,... | collective-permute-start | bytes 208904 | tf_op jit(solution)/shard_map/ppermute | solution.py:61
  30.0 0.1 shard_map.149.near_ref
  30.1 0.2 shard_map.150
  30.4 4.5 %collective-permute-done.5.from_far_ref = f32[136,128]{1,0:T(8,128)S(1)} collective-permute-done((f32[136,128]{1,0:T(8,128)S(1)}, f32[136,128]{1,0:T(8,128)S(1)}, u32[]{:S(2)}, u32[]{:S(2)}) %collective-permute-start.5) | collective-permute-done | bytes 69664 | tf_op jit(solution)/shard_map/ppermute | solution.py:61
  34.8 0.5 shard_map.151
  35.3 14.8 %all_to_all.5.slots_ref = f32[16,48,128]{2,1,0:T(8,128)S(1)} all-to-all(f32[16,48,128]{2,1,0:T(8,128)S(1)} %get-tuple-element.71), channel_id=1, replica_groups={{0,1,2,3,4,5,6,7,8,9,10,11,12,13,14,15},{16,17,18,19,20,21,22,23,24,25,..., dimensions={0} | all-to-all | bytes 786432 | tf_op jit(solution)/shard_map/all_to_all | solution.py:977
  50.2 0.9 %shard_map.152 = (f32[128,512]{1,0:T(8,128)S(1)}, f32[160,128]{1,0:T(8,128)S(1)}, f32[72,128]{1,0:T(8,128)S(1)}, f32[72,128]{1,0:T(8,128)S(1)}) custom-call(f32[512,128]{1,0:T(8,128)S(1)} %get-tuple-element.61.fresh_ref.kept_ref, s32[8,128]{1,0:T(8,128)S(1)} %get-tuple-element.62.meta_ref, f32[16,48,128]{2,1,0:T(8,128)S(1)} %all_to_all.5.slots_ref, ...), custom_call_target="tpu_custom_call" | custom-call | flops 4194304 | bytes 524288 | tf_op jit(solution)/shard_map/pallas_call | solution.py:45
  51.1 3.3 %collective-permute-start.6 = (f32[72,128]{1,0:T(8,128)S(1)}, f32[72,128]{1,0:T(8,128)S(1)}, u32[]{:S(2)}, u32[]{:S(2)}) collective-permute-start(f32[72,128]{1,0:T(8,128)S(1)} %get-tuple-element.84), channel_id=1, source_target_pairs={{8,16},{16,8},{24,32},{32,24},{40,48},{48,40},{56,64},{64,56},{72,... | collective-permute-start | bytes 110600 | tf_op jit(solution)/shard_map/ppermute | solution.py:61
  54.3 1.9 %collective-permute-start.7 = (f32[72,128]{1,0:T(8,128)S(1)}, f32[72,128]{1,0:T(8,128)S(1)}, u32[]{:S(2)}, u32[]{:S(2)}) collective-permute-start(f32[72,128]{1,0:T(8,128)S(1)} %get-tuple-element.85), channel_id=1, source_target_pairs={{0,8},{8,0},{16,24},{24,16},{32,40},{40,32},{48,56},{56,48},{64,72... | collective-permute-start | bytes 110600 | tf_op jit(solution)/shard_map/ppermute | solution.py:61
  56.3 0.3 shard_map.153
  56.5 0.8 %shard_map.154 = (f32[256,512]{1,0:T(8,128)S(1)}, s32[8,128]{1,0:T(8,128)S(1)}) custom-call(f32[128,512]{1,0:T(8,128)S(1)} %get-tuple-element.75.advanced_ref, f32[128,128]{1,0:T(8,128)S(1)} %get-tuple-element.76.stays_ref, f32[160,128]{1,0:T(8,128)S(1)} %get-tuple-element.77.velocity_ref, f32[128,128]{1,0:T(8,128)S(1)} %get-tuple-element.78.turned_ref, ...), custom_call_target="tpu_custom_call" | custom-call | flops 4194304 | bytes 524288 | tf_op jit(solution)/shard_map/pallas_call | solution.py:45
  57.3 2.6 %collective-permute-done.6.xo_ref = f32[72,128]{1,0:T(8,128)S(1)} collective-permute-done((f32[72,128]{1,0:T(8,128)S(1)}, f32[72,128]{1,0:T(8,128)S(1)}, u32[]{:S(2)}, u32[]{:S(2)}) %collective-permute-start.6) | collective-permute-done | bytes 36896 | tf_op jit(solution)/shard_map/ppermute | solution.py:61
  59.9 0.8 %shard_map.155 = (f32[256,512]{1,0:T(8,128)}, s32[2,128]{1,0:T(2,128)}, s32[2,128]{1,0:T(2,128)}) custom-call(f32[256,512]{1,0:T(8,128)S(1)} %get-tuple-element.81.part_ref, s32[8,128]{1,0:T(8,128)S(1)} %get-tuple-element.82.old_meta_ref, s32[8,128]{1,0:T(8,128)S(1)} %get-tuple-element.83.tail_ref, f32[72,128]{1,0:T(8,128)S(1)} %collective-permute-done.6.xo_ref, ...), custom_call_target="tpu_custom_call" | custom-call | flops 4194304 | bytes 524288 | tf_op jit(solution)/shard_map/pallas_call | solution.py:45
  (26 shorter events, 0.2 us)
Async XLA Ops:
  0.6 1.1 %copy-start = (f32[128,512]{1,0:T(8,128)S(1)}, f32[128,512]{1,0:T(8,128)}, u32[]{:S(2)}) copy-start(f32[128,512]{1,0:T(8,128)} %points_ref.3) | copy-start | bytes 786436
  0.6 0.7 %copy-start.4 = (f32[8]{0:T(128)S(1)}, f32[8]{0:T(128)}, u32[]{:S(2)}) copy-start(f32[8]{0:T(128)} %param.16) | copy-start | bytes 100
  0.7 0.7 %copy-start.5 = (f32[8]{0:T(128)S(1)}, f32[8]{0:T(128)}, u32[]{:S(2)}) copy-start(f32[8]{0:T(128)} %param.17) | copy-start | bytes 100
  0.7 0.7 %copy-start.6 = (s32[64]{0:T(128)S(1)}, s32[64]{0:T(128)}, u32[]{:S(2)}) copy-start(s32[64]{0:T(128)} %param.18) | copy-start | bytes 772
  0.7 0.7 %copy-start.7 = (s32[64]{0:T(128)S(1)}, s32[64]{0:T(128)}, u32[]{:S(2)}) copy-start(s32[64]{0:T(128)} %param.19) | copy-start | bytes 772
  0.7 0.7 %copy-start.8 = (s32[64]{0:T(128)S(1)}, s32[64]{0:T(128)}, u32[]{:S(2)}) copy-start(s32[64]{0:T(128)} %param.20) | copy-start | bytes 772
  0.7 0.7 %copy-start.9 = (s32[64]{0:T(128)S(1)}, s32[64]{0:T(128)}, u32[]{:S(2)}) copy-start(s32[64]{0:T(128)} %param.21) | copy-start | bytes 772
  0.7 0.7 %copy-start.10 = (s32[64]{0:T(128)S(1)}, s32[64]{0:T(128)}, u32[]{:S(2)}) copy-start(s32[64]{0:T(128)} %param.22) | copy-start | bytes 772
  0.7 0.7 %copy-start.11 = (s32[64]{0:T(128)S(1)}, s32[64]{0:T(128)}, u32[]{:S(2)}) copy-start(s32[64]{0:T(128)} %param.23) | copy-start | bytes 772
  0.7 0.7 %copy-start.1 = (s32[128]{0:T(128)S(1)}, s32[128]{0:T(128)}, u32[]{:S(2)}) copy-start(s32[128]{0:T(128)} %param.13) | copy-start | bytes 1540
  0.8 0.7 %copy-start.2 = (s32[128]{0:T(128)S(1)}, s32[128]{0:T(128)}, u32[]{:S(2)}) copy-start(s32[128]{0:T(128)} %param.14) | copy-start | bytes 1540
  0.8 0.7 %copy-start.3 = (f32[8]{0:T(128)S(1)}, f32[8]{0:T(128)}, u32[]{:S(2)}) copy-start(f32[8]{0:T(128)} %param.15) | copy-start | bytes 100
  2.5 8.6 %collective-permute-start = (f32[24,128]{1,0:T(8,128)S(1)}, f32[24,128]{1,0:T(8,128)S(1)}, u32[]{:S(2)}, u32[]{:S(2)}) collective-permute-start(f32[24,128]{1,0:T(8,128)S(1)} %get-tuple-element.51), channel_id=1, source_target_pairs={{8,16},{16,8},{24,32},{32,24},{40,48},{48,40},{56,64},{64,56},{72,... | collective-permute-start | bytes 36872 | tf_op jit(solution)/shard_map/ppermute | solution.py:61
  8.7 3.1 %collective-permute-start.1 = (f32[24,128]{1,0:T(8,128)S(1)}, f32[24,128]{1,0:T(8,128)S(1)}, u32[]{:S(2)}, u32[]{:S(2)}) collective-permute-start(f32[24,128]{1,0:T(8,128)S(1)} %get-tuple-element.52), channel_id=1, source_target_pairs={{0,8},{8,0},{16,24},{24,16},{32,40},{40,32},{48,56},{56,48},{64,72... | collective-permute-start | bytes 36872 | tf_op jit(solution)/shard_map/ppermute | solution.py:61
  11.9 7.5 %collective-permute-start.2 = (f32[144,128]{1,0:T(8,128)S(1)}, f32[144,128]{1,0:T(8,128)S(1)}, u32[]{:S(2)}, u32[]{:S(2)}) collective-permute-start(f32[144,128]{1,0:T(8,128)S(1)} %get-tuple-element.57), channel_id=1, source_target_pairs={{1,2},{2,1},{3,4},{4,3},{5,6},{6,5},{9,10},{10,9},{11,12},{12,11},... | collective-permute-start | bytes 221192 | tf_op jit(solution)/shard_map/ppermute | solution.py:61
  12.6 8.4 %collective-permute-start.3 = (f32[144,128]{1,0:T(8,128)S(1)}, f32[144,128]{1,0:T(8,128)S(1)}, u32[]{:S(2)}, u32[]{:S(2)}) collective-permute-start(f32[144,128]{1,0:T(8,128)S(1)} %get-tuple-element.58), channel_id=1, source_target_pairs={{0,1},{1,0},{2,3},{3,2},{4,5},{5,4},{6,7},{7,6},{8,9},{9,8},{10,11... | collective-permute-start | bytes 221192 | tf_op jit(solution)/shard_map/ppermute | solution.py:61
  21.9 3.1 %collective-permute-start.4 = (f32[72,128]{1,0:T(8,128)S(1)}, f32[72,128]{1,0:T(8,128)S(1)}, u32[]{:S(2)}, u32[]{:S(2)}) collective-permute-start(f32[72,128]{1,0:T(8,128)S(1)} %get-tuple-element.64), channel_id=1, source_target_pairs={{0,8},{8,0},{16,24},{24,16},{32,40},{40,32},{48,56},{56,48},{64,72... | collective-permute-start | bytes 110600 | tf_op jit(solution)/shard_map/ppermute | solution.py:61
  25.6 9.2 %collective-permute-start.5 = (f32[136,128]{1,0:T(8,128)S(1)}, f32[136,128]{1,0:T(8,128)S(1)}, u32[]{:S(2)}, u32[]{:S(2)}) collective-permute-start(f32[136,128]{1,0:T(8,128)S(1)} %get-tuple-element.67), channel_id=1, source_target_pairs={{8,16},{16,8},{24,32},{32,24},{40,48},{48,40},{56,64},{64,56},{72,... | collective-permute-start | bytes 208904 | tf_op jit(solution)/shard_map/ppermute | solution.py:61
  51.1 8.9 %collective-permute-start.6 = (f32[72,128]{1,0:T(8,128)S(1)}, f32[72,128]{1,0:T(8,128)S(1)}, u32[]{:S(2)}, u32[]{:S(2)}) collective-permute-start(f32[72,128]{1,0:T(8,128)S(1)} %get-tuple-element.84), channel_id=1, source_target_pairs={{8,16},{16,8},{24,32},{32,24},{40,48},{48,40},{56,64},{64,56},{72,... | collective-permute-start | bytes 110600 | tf_op jit(solution)/shard_map/ppermute | solution.py:61
  54.3 5.6 %collective-permute-start.7 = (f32[72,128]{1,0:T(8,128)S(1)}, f32[72,128]{1,0:T(8,128)S(1)}, u32[]{:S(2)}, u32[]{:S(2)}) collective-permute-start(f32[72,128]{1,0:T(8,128)S(1)} %get-tuple-element.85), channel_id=1, source_target_pairs={{0,8},{8,0},{16,24},{24,16},{32,40},{40,32},{48,56},{56,48},{64,72... | collective-permute-start | bytes 110600 | tf_op jit(solution)/shard_map/ppermute | solution.py:61

commit v8 on v7

--- a/solution.py
+++ b/solution.py
@@ -24,6 +24,7 @@
 PACK = 64
 NEAR = 32
 HALF = LANES // 2
+REACH = range(-3, 4)
 SLOT = PACK // 2 + 2 * SUB
 CROSS_MSG = 2 * SUB + PIECES * 2 * MCAP
 SPAN = 3 * CY + 3
@@ -406,28 +407,34 @@
     half_lane = iota((PACK // 2, LANES), 1)
     halo_lane = iota((2 * SUB, LANES), 1)
     across = slots_ref.shape[0] // 2
-    for index in range(across):
-        away = index - gy
-        first = jnp.where(away > 0, 0, CY)
-        shift = CY * away + first
+    unread = mine * across + gy
+    for away in REACH:
+        index = gy + away
+        there = (index >= 0) & (index < across)
+        shift = CY * away
+        source = halo_lane + shift
+        valid = (source >= 0) & (source < SPAN) & (halo_lane < SPAN)
+        moved = pltpu.roll(halo, (-shift) % LANES, 1) if away else halo
+        slot = jnp.where(there, (1 - mine) * across + index, unread)
+        slots_ref[slot, 0 : 2 * SUB, :] = jnp.where(valid, moved, 0.0)
+        if away == 0:
+            continue
+        slot = jnp.where(there, mine * across + index, unread)
+        first = 0 if away > 0 else CY
+        shift += first
         source = lane + shift
         valid = (source >= 0) & (source < SPAN) & (lane + first < SPAN)
-        window = jnp.where(valid, pltpu.roll(merged, (-shift) & (LANES - 1), 1), 0.0)
-        slot = mine * across + index
+        moved = pltpu.roll(merged, (-shift) % LANES, 1) if shift else merged
+        window = jnp.where(valid, moved, 0.0)
         right = pltpu.roll(window[PACK // 2 :], HALF, 1)
         slots_ref[slot, 0 : PACK // 2, :] = jnp.where(half_lane < HALF, window[0 : PACK // 2], right)
         rest = jnp.zeros((SUB, LANES), F32)
-        for group in range(PACK // SUB):
-            moved = pltpu.roll(window[group * SUB : (group + 1) * SUB], HALF + 3 * group, 1)
-            rest = jnp.where((tile_lane >= 3 * group) & (tile_lane < 3 * group + 3), moved, rest)
+        if away not in (2, 3):
+            for group in range(PACK // SUB):
+                moved = pltpu.roll(window[group * SUB : (group + 1) * SUB], HALF + 3 * group, 1)
+                rest = jnp.where((tile_lane >= 3 * group) & (tile_lane < 3 * group + 3), moved, rest)
         slots_ref[slot, PACK // 2 : PACK // 2 + SUB, :] = rest
-        slots_ref[slot, PACK // 2 + SUB : SLOT, :] = jnp.where(away > 0, up, down)
-        shift = CY * away
-        source = halo_lane + shift
-        valid = (source >= 0) & (source < SPAN) & (halo_lane < SPAN)
-        slot = (1 - mine) * across + index
-        slots_ref[slot, 0 : 2 * SUB, :] = jnp.where(valid, pltpu.roll(halo, (-shift) & (LANES - 1), 1), 0.0)
-        slots_ref[slot, 2 * SUB : SLOT, :] = jnp.zeros((SLOT - 2 * SUB, LANES), F32)
+        slots_ref[slot, PACK // 2 + SUB : SLOT, :] = up if away > 0 else down
 
 
 def put_velocity(row, x, node_y, velocity_ref):
@@ -463,11 +470,18 @@
     from_low = jnp.zeros((part, LANES), F32)
     from_high = jnp.zeros((part, LANES), F32)
     halo = jnp.zeros((2 * SUB, LANES), F32)
-    for index in range(across):
-        value = slots_ref[mine * across + index, 0:part, :]
-        from_low = from_low + jnp.where(index < gy, value, 0.0)
-        from_high = from_high + jnp.where(index > gy, value, 0.0)
-        halo = halo + slots_ref[(1 - mine) * across + index, 0 : 2 * SUB, :]
+    for away in REACH:
+        index = gy + away
+        there = (index >= 0) & (index < across)
+        index = jnp.clip(index, 0, across - 1)
+        halo = halo + jnp.where(there, slots_ref[(1 - mine) * across + index, 0 : 2 * SUB, :], 0.0)
+        if away == 0:
+            continue
+        value = jnp.where(there, slots_ref[mine * across + index, 0:part, :], 0.0)
+        if away < 0:
+            from_low = from_low + value
+        else:
+            from_high = from_high + value
     half_lane = iota((PACK // 2, LANES), 1)
     tile_lane = iota((SUB, LANES), 1)
     total = merged_ref[...]
@@ -763,10 +777,11 @@
 
 
 def settle(
-    advanced_ref, stays_ref, velocity_ref, turned_ref, new_meta_ref, tables_ref, slots_ref, cross_ref, tags_ref,
+    advanced_ref, stays_ref, velocity_ref, from_near_ref, from_far_ref, tables_ref, slots_ref, cross_ref, tags_ref,
     rows_ref, tail_ref,
-    wide_ref, middle_ref, out_ref, small_ref,
+    wide_ref, middle_ref, out_ref, small_ref, turned_ref, new_meta_ref, other_wide_ref,
 ):
+    arrange_depth(from_near_ref, from_far_ref, turned_ref, new_meta_ref, other_wide_ref)
     stays = stays_ref[...] > 0.5
     for piece in range(PIECES):
         columns = slice(piece * LANES, (piece + 1) * LANES)
@@ -971,9 +986,6 @@
     merged, slots = call(
         merge_far, (packed_form, slots_form), (), (IN_VMEM,) * 4, own, from_far, near_nodes, cross_tags
     )
-    turned, new_meta = call(
-        arrange_depth, (quarter_form, tags), (scratch(turned_form),), (IN_VMEM,) * 2, from_near, from_far
-    )
     slots = lax.all_to_all(slots, ("gx", "gy"), 0, 0, axis_index_groups=chip_columns())
     advanced, velocity, far, near = call(
         advance_two,
@@ -992,9 +1004,12 @@
             scratch(half_form),
             scratch(half_form),
             scratch(quarter_form),
+            scratch(quarter_form),
+            scratch(tags),
+            scratch(turned_form),
         ),
         (IN_VMEM,) * 9,
-        advanced, stays, velocity, turned, new_meta, tables, slots, cross, cross_tags,
+        advanced, stays, velocity, from_near, from_far, tables, slots, cross, cross_tags,
     )
     final_points, final_cells, final_mats = call(
         assemble,

time: 61.1 us -> 60.9 us (level)
    pallas_call x17 -> x16, Pallas kernels: 7.88 us -> 7.57 us  [call(): pl.pallas_call(kernel, out_shape=tuple((jax.ShapeDtypeStruct(shape, dtype...]
where the time goes in v8:
time: 60.9 us; the launch traced here: 60.5 us
  starting transfers between devices  26.4 us (43%)
  blocking collectives  14.8 us (24%)
  waiting for transfers between devices  9.89 us (16%)
  Pallas kernels  7.57 us (12%)
  local copies, waits for them, and re-layouts  0.91 us (1%)
  between operations  0.9 us (1%)
    ppermute x8, starting transfers between devices, swap(): return lax.ppermute(value, axis, pairs)  26.4 us
    all_to_all x1, blocking collectives, shards(): lax.all_to_all(slots, ('gx', 'gy'), 0, 0, axis_index_groups=chip_columns())  14.8 us
    ppermute x8, waiting for transfers between devices, swap(): return lax.ppermute(value, axis, pairs)  9.89 us
    pallas_call x16, Pallas kernels, call(): pl.pallas_call(kernel, out_shape=tuple((jax.ShapeDtypeStruct(shape, dtype...  7.57 us
  transfers between devices with their start and end apart: 8, of which 5 were waited for; matrix products, arithmetic and copies ran while one was open for 0% of the time, Pallas kernels for 5%

profile of v8, /device:TPU:384, one launch (start us, length us, event | category | flops | bytes accessed | tf_op | source)
XLA Modules:
  0.0 60.5 jit_solution(12226463245183440464)
XLA Ops:
  0.8 0.6 copy-done.4
  1.3 0.0 copy-done.5
  1.5 0.1 shard_map.140
  1.6 0.1 copy-done
  1.8 0.5 shard_map.141
  2.3 0.3 shard_map.142
  2.5 6.2 %collective-permute-start = (f32[24,128]{1,0:T(8,128)S(1)}, f32[24,128]{1,0:T(8,128)S(1)}, u32[]{:S(2)}, u32[]{:S(2)}) collective-permute-start(f32[24,128]{1,0:T(8,128)S(1)} %get-tuple-element.49), channel_id=1, source_target_pairs={{8,16},{16,8},{24,32},{32,24},{40,48},{48,40},{56,64},{64,56},{72,... | collective-permute-start | bytes 36872 | tf_op jit(solution)/shard_map/ppermute | solution.py:62
  8.7 1.9 %collective-permute-start.1 = (f32[24,128]{1,0:T(8,128)S(1)}, f32[24,128]{1,0:T(8,128)S(1)}, u32[]{:S(2)}, u32[]{:S(2)}) collective-permute-start(f32[24,128]{1,0:T(8,128)S(1)} %get-tuple-element.50), channel_id=1, source_target_pairs={{0,8},{8,0},{16,24},{24,16},{32,40},{40,32},{48,56},{56,48},{64,72... | collective-permute-start | bytes 36872 | tf_op jit(solution)/shard_map/ppermute | solution.py:62
  10.7 0.5 shard_map.143
  11.2 0.6 %collective-permute-done.1.from_inner_ref = f32[24,128]{1,0:T(8,128)S(1)} collective-permute-done((f32[24,128]{1,0:T(8,128)S(1)}, f32[24,128]{1,0:T(8,128)S(1)}, u32[]{:S(2)}, u32[]{:S(2)}) %collective-permute-start.1) | collective-permute-done | bytes 12320 | tf_op jit(solution)/shard_map/ppermute | solution.py:62
  11.8 0.1 shard_map.144
  11.9 0.7 %collective-permute-start.2 = (f32[144,128]{1,0:T(8,128)S(1)}, f32[144,128]{1,0:T(8,128)S(1)}, u32[]{:S(2)}, u32[]{:S(2)}) collective-permute-start(f32[144,128]{1,0:T(8,128)S(1)} %get-tuple-element.55), channel_id=1, source_target_pairs={{1,2},{2,1},{3,4},{4,3},{5,6},{6,5},{9,10},{10,9},{11,12},{12,11},... | collective-permute-start | bytes 221192 | tf_op jit(solution)/shard_map/ppermute | solution.py:62
  12.6 6.1 %collective-permute-start.3 = (f32[144,128]{1,0:T(8,128)S(1)}, f32[144,128]{1,0:T(8,128)S(1)}, u32[]{:S(2)}, u32[]{:S(2)}) collective-permute-start(f32[144,128]{1,0:T(8,128)S(1)} %get-tuple-element.56), channel_id=1, source_target_pairs={{0,1},{1,0},{2,3},{3,2},{4,5},{5,4},{6,7},{7,6},{8,9},{9,8},{10,11... | collective-permute-start | bytes 221192 | tf_op jit(solution)/shard_map/ppermute | solution.py:62
  18.7 0.7 %shard_map.145 = (f32[32,128]{1,0:T(8,128)S(1)}, f32[32,128]{1,0:T(8,128)S(1)}, f32[8,128]{1,0:T(8,128)S(1)}, f32[8,128]{1,0:T(8,128)S(1)}, s32[8,128]{1,0:T(8,1...) custom-call(s32[8,128]{1,0:T(8,128)S(1)} %get-tuple-element.44.meta_ref, ...), custom_call_target="tpu_custom_call" | custom-call | flops 4194304 | bytes 524288 | tf_op jit(solution)/shard_map/pallas_call | solution.py:46
  19.4 1.6 %collective-permute-done.3.yi_ref = f32[144,128]{1,0:T(8,128)S(1)} collective-permute-done((f32[144,128]{1,0:T(8,128)S(1)}, f32[144,128]{1,0:T(8,128)S(1)}, u32[]{:S(2)}, u32[]{:S(2)}) %collective-permute-start.3) | collective-permute-done | bytes 73760 | tf_op jit(solution)/shard_map/ppermute | solution.py:62
  21.0 0.8 %shard_map.146 = (f32[512,128]{1,0:T(8,128)S(1)}, f32[32,128]{1,0:T(8,128)S(1)}, f32[72,128]{1,0:T(8,128)S(1)}, f32[72,128]{1,0:T(8,128)S(1)}) custom-call(f32[512,128]{1,0:T(8,128)S(1)} %get-tuple-element.45.turned_ref, s32[8,128]{1,0:T(8,128)S(1)} %get-tuple-element.44.meta_ref, f32[160,128]{1,0:T(8,128)S(1)} %get-tuple-element.54.merged_ref, ...), custom_call_target="tpu_custom_call" | custom-call | flops 4194304 | bytes 524288 | tf_op jit(solution)/shard_map/pallas_call | solution.py:46
  21.9 1.9 %collective-permute-start.4 = (f32[72,128]{1,0:T(8,128)S(1)}, f32[72,128]{1,0:T(8,128)S(1)}, u32[]{:S(2)}, u32[]{:S(2)}) collective-permute-start(f32[72,128]{1,0:T(8,128)S(1)} %get-tuple-element.62), channel_id=1, source_target_pairs={{0,8},{8,0},{16,24},{24,16},{32,40},{40,32},{48,56},{56,48},{64,72... | collective-permute-start | bytes 110600 | tf_op jit(solution)/shard_map/ppermute | solution.py:62
  23.8 0.7 %shard_map.147.kept_sums_ref = f32[288,128]{1,0:T(8,128)S(1)} custom-call(f32[512,128]{1,0:T(8,128)S(1)} %get-tuple-element.59.fresh_ref.kept_ref, s32[8,128]{1,0:T(8,128)S(1)} %get-tuple-element.61.target_ref, f32[24,128]{1,0:T(8,128)S(1)} %get-tuple-element.47.tables_ref), custom_call_target="tpu_custom_call" | custom-call | flops 4194304 | bytes 524288 | tf_op jit(solution)/shard_map/pallas_call | solution.py:46
  24.5 0.5 collective-permute-done.4.from_near_ref
  25.0 0.6 %shard_map.148 = (f32[64,128]{1,0:T(8,128)S(1)}, f32[136,128]{1,0:T(8,128)S(1)}) custom-call(f32[288,128]{1,0:T(8,128)S(1)} %shard_map.147.kept_sums_ref, f32[72,128]{1,0:T(8,128)S(1)} %collective-permute-done.4.from_near_ref, f32[72,128]{1,0:T(8,128)S(1)} %get-tuple-element.63.to_far_ref, f32[24,128]{1,0:T(8,128)S(1)} %get-tuple-element.47.tables_ref), custom_call_target="tpu_custom_call" | custom-call | flops 4194304 | bytes 524288 | tf_op jit(solution)/shard_map/pallas_call | solution.py:46
  25.6 4.4 %collective-permute-start.5 = (f32[136,128]{1,0:T(8,128)S(1)}, f32[136,128]{1,0:T(8,128)S(1)}, u32[]{:S(2)}, u32[]{:S(2)}) collective-permute-start(f32[136,128]{1,0:T(8,128)S(1)} %get-tuple-element.65), channel_id=1, source_target_pairs={{8,16},{16,8},{24,32},{32,24},{40,48},{48,40},{56,64},{64,56},{72,... | collective-permute-start | bytes 208904 | tf_op jit(solution)/shard_map/ppermute | solution.py:62
  30.0 0.1 shard_map.149.near_ref
  30.1 0.2 shard_map.150
  30.4 4.5 %collective-permute-done.5.from_far_ref = f32[136,128]{1,0:T(8,128)S(1)} collective-permute-done((f32[136,128]{1,0:T(8,128)S(1)}, f32[136,128]{1,0:T(8,128)S(1)}, u32[]{:S(2)}, u32[]{:S(2)}) %collective-permute-start.5) | collective-permute-done | bytes 69664 | tf_op jit(solution)/shard_map/ppermute | solution.py:62
  34.8 0.2 shard_map.151
  35.1 14.8 %all_to_all.5.slots_ref = f32[16,48,128]{2,1,0:T(8,128)S(1)} all-to-all(f32[16,48,128]{2,1,0:T(8,128)S(1)} %get-tuple-element.69), channel_id=1, replica_groups={{0,1,2,3,4,5,6,7,8,9,10,11,12,13,14,15},{16,17,18,19,20,21,22,23,24,25,..., dimensions={0} | all-to-all | bytes 786432 | tf_op jit(solution)/shard_map/all_to_all | solution.py:989
  49.9 0.9 %shard_map.152 = (f32[128,512]{1,0:T(8,128)S(1)}, f32[160,128]{1,0:T(8,128)S(1)}, f32[72,128]{1,0:T(8,128)S(1)}, f32[72,128]{1,0:T(8,128)S(1)}) custom-call(f32[512,128]{1,0:T(8,128)S(1)} %get-tuple-element.59.fresh_ref.kept_ref, s32[8,128]{1,0:T(8,128)S(1)} %get-tuple-element.60.meta_ref, f32[16,48,128]{2,1,0:T(8,128)S(1)} %all_to_all.5.slots_ref, ...), custom_call_target="tpu_custom_call" | custom-call | flops 4194304 | bytes 524288 | tf_op jit(solution)/shard_map/pallas_call | solution.py:46
  50.8 3.3 %collective-permute-start.6 = (f32[72,128]{1,0:T(8,128)S(1)}, f32[72,128]{1,0:T(8,128)S(1)}, u32[]{:S(2)}, u32[]{:S(2)}) collective-permute-start(f32[72,128]{1,0:T(8,128)S(1)} %get-tuple-element.80), channel_id=1, source_target_pairs={{8,16},{16,8},{24,32},{32,24},{40,48},{48,40},{56,64},{64,56},{72,... | collective-permute-start | bytes 110600 | tf_op jit(solution)/shard_map/ppermute | solution.py:62
  54.1 1.9 %collective-permute-start.7 = (f32[72,128]{1,0:T(8,128)S(1)}, f32[72,128]{1,0:T(8,128)S(1)}, u32[]{:S(2)}, u32[]{:S(2)}) collective-permute-start(f32[72,128]{1,0:T(8,128)S(1)} %get-tuple-element.81), channel_id=1, source_target_pairs={{0,8},{8,0},{16,24},{24,16},{32,40},{40,32},{48,56},{56,48},{64,72... | collective-permute-start | bytes 110600 | tf_op jit(solution)/shard_map/ppermute | solution.py:62
  56.0 1.0 %shard_map.153 = (f32[256,512]{1,0:T(8,128)S(1)}, s32[8,128]{1,0:T(8,128)S(1)}) custom-call(f32[128,512]{1,0:T(8,128)S(1)} %get-tuple-element.73.advanced_ref, f32[128,128]{1,0:T(8,128)S(1)} %get-tuple-element.74.stays_ref, f32[160,128]{1,0:T(8,128)S(1)} %get-tuple-element.75.velocity_ref, f32[72,128]{1,0:T(8,128)S(1)} %collective-permute-done.4.from_near_ref, ...), custom_call_target="tpu_custom_call" | custom-call | flops 4194304 | bytes 524288 | tf_op jit(solution)/shard_map/pallas_call | solution.py:46
  57.0 2.7 %collective-permute-done.6.xo_ref = f32[72,128]{1,0:T(8,128)S(1)} collective-permute-done((f32[72,128]{1,0:T(8,128)S(1)}, f32[72,128]{1,0:T(8,128)S(1)}, u32[]{:S(2)}, u32[]{:S(2)}) %collective-permute-start.6) | collective-permute-done | bytes 36896 | tf_op jit(solution)/shard_map/ppermute | solution.py:62
  59.7 0.8 %shard_map.154 = (f32[256,512]{1,0:T(8,128)}, s32[2,128]{1,0:T(2,128)}, s32[2,128]{1,0:T(2,128)}) custom-call(f32[256,512]{1,0:T(8,128)S(1)} %get-tuple-element.77.part_ref, s32[8,128]{1,0:T(8,128)S(1)} %get-tuple-element.78.old_meta_ref, s32[8,128]{1,0:T(8,128)S(1)} %get-tuple-element.79.tail_ref, f32[72,128]{1,0:T(8,128)S(1)} %collective-permute-done.6.xo_ref, ...), custom_call_target="tpu_custom_call" | custom-call | flops 4194304 | bytes 524288 | tf_op jit(solution)/shard_map/pallas_call | solution.py:46
  (25 shorter events, 0.2 us)
Async XLA Ops:
  0.6 1.1 %copy-start = (f32[128,512]{1,0:T(8,128)S(1)}, f32[128,512]{1,0:T(8,128)}, u32[]{:S(2)}) copy-start(f32[128,512]{1,0:T(8,128)} %points_ref.3) | copy-start | bytes 786436
  0.6 0.7 %copy-start.4 = (f32[8]{0:T(128)S(1)}, f32[8]{0:T(128)}, u32[]{:S(2)}) copy-start(f32[8]{0:T(128)} %param.16) | copy-start | bytes 100
  0.7 0.7 %copy-start.5 = (f32[8]{0:T(128)S(1)}, f32[8]{0:T(128)}, u32[]{:S(2)}) copy-start(f32[8]{0:T(128)} %param.17) | copy-start | bytes 100
  0.7 0.7 %copy-start.6 = (s32[64]{0:T(128)S(1)}, s32[64]{0:T(128)}, u32[]{:S(2)}) copy-start(s32[64]{0:T(128)} %param.18) | copy-start | bytes 772
  0.7 0.7 %copy-start.7 = (s32[64]{0:T(128)S(1)}, s32[64]{0:T(128)}, u32[]{:S(2)}) copy-start(s32[64]{0:T(128)} %param.19) | copy-start | bytes 772
  0.7 0.7 %copy-start.8 = (s32[64]{0:T(128)S(1)}, s32[64]{0:T(128)}, u32[]{:S(2)}) copy-start(s32[64]{0:T(128)} %param.20) | copy-start | bytes 772
  0.7 0.7 %copy-start.9 = (s32[64]{0:T(128)S(1)}, s32[64]{0:T(128)}, u32[]{:S(2)}) copy-start(s32[64]{0:T(128)} %param.21) | copy-start | bytes 772
  0.7 0.7 %copy-start.10 = (s32[64]{0:T(128)S(1)}, s32[64]{0:T(128)}, u32[]{:S(2)}) copy-start(s32[64]{0:T(128)} %param.22) | copy-start | bytes 772
  0.7 0.7 %copy-start.11 = (s32[64]{0:T(128)S(1)}, s32[64]{0:T(128)}, u32[]{:S(2)}) copy-start(s32[64]{0:T(128)} %param.23) | copy-start | bytes 772
  0.7 0.7 %copy-start.1 = (s32[128]{0:T(128)S(1)}, s32[128]{0:T(128)}, u32[]{:S(2)}) copy-start(s32[128]{0:T(128)} %param.13) | copy-start | bytes 1540
  0.8 0.7 %copy-start.2 = (s32[128]{0:T(128)S(1)}, s32[128]{0:T(128)}, u32[]{:S(2)}) copy-start(s32[128]{0:T(128)} %param.14) | copy-start | bytes 1540
  0.8 0.7 %copy-start.3 = (f32[8]{0:T(128)S(1)}, f32[8]{0:T(128)}, u32[]{:S(2)}) copy-start(f32[8]{0:T(128)} %param.15) | copy-start | bytes 100
  2.5 8.6 %collective-permute-start = (f32[24,128]{1,0:T(8,128)S(1)}, f32[24,128]{1,0:T(8,128)S(1)}, u32[]{:S(2)}, u32[]{:S(2)}) collective-permute-start(f32[24,128]{1,0:T(8,128)S(1)} %get-tuple-element.49), channel_id=1, source_target_pairs={{8,16},{16,8},{24,32},{32,24},{40,48},{48,40},{56,64},{64,56},{72,... | collective-permute-start | bytes 36872 | tf_op jit(solution)/shard_map/ppermute | solution.py:62
  8.7 3.1 %collective-permute-start.1 = (f32[24,128]{1,0:T(8,128)S(1)}, f32[24,128]{1,0:T(8,128)S(1)}, u32[]{:S(2)}, u32[]{:S(2)}) collective-permute-start(f32[24,128]{1,0:T(8,128)S(1)} %get-tuple-element.50), channel_id=1, source_target_pairs={{0,8},{8,0},{16,24},{24,16},{32,40},{40,32},{48,56},{56,48},{64,72... | collective-permute-start | bytes 36872 | tf_op jit(solution)/shard_map/ppermute | solution.py:62
  11.9 7.5 %collective-permute-start.2 = (f32[144,128]{1,0:T(8,128)S(1)}, f32[144,128]{1,0:T(8,128)S(1)}, u32[]{:S(2)}, u32[]{:S(2)}) collective-permute-start(f32[144,128]{1,0:T(8,128)S(1)} %get-tuple-element.55), channel_id=1, source_target_pairs={{1,2},{2,1},{3,4},{4,3},{5,6},{6,5},{9,10},{10,9},{11,12},{12,11},... | collective-permute-start | bytes 221192 | tf_op jit(solution)/shard_map/ppermute | solution.py:62
  12.6 8.4 %collective-permute-start.3 = (f32[144,128]{1,0:T(8,128)S(1)}, f32[144,128]{1,0:T(8,128)S(1)}, u32[]{:S(2)}, u32[]{:S(2)}) collective-permute-start(f32[144,128]{1,0:T(8,128)S(1)} %get-tuple-element.56), channel_id=1, source_target_pairs={{0,1},{1,0},{2,3},{3,2},{4,5},{5,4},{6,7},{7,6},{8,9},{9,8},{10,11... | collective-permute-start | bytes 221192 | tf_op jit(solution)/shard_map/ppermute | solution.py:62
  21.9 3.1 %collective-permute-start.4 = (f32[72,128]{1,0:T(8,128)S(1)}, f32[72,128]{1,0:T(8,128)S(1)}, u32[]{:S(2)}, u32[]{:S(2)}) collective-permute-start(f32[72,128]{1,0:T(8,128)S(1)} %get-tuple-element.62), channel_id=1, source_target_pairs={{0,8},{8,0},{16,24},{24,16},{32,40},{40,32},{48,56},{56,48},{64,72... | collective-permute-start | bytes 110600 | tf_op jit(solution)/shard_map/ppermute | solution.py:62
  25.6 9.2 %collective-permute-start.5 = (f32[136,128]{1,0:T(8,128)S(1)}, f32[136,128]{1,0:T(8,128)S(1)}, u32[]{:S(2)}, u32[]{:S(2)}) collective-permute-start(f32[136,128]{1,0:T(8,128)S(1)} %get-tuple-element.65), channel_id=1, source_target_pairs={{8,16},{16,8},{24,32},{32,24},{40,48},{48,40},{56,64},{64,56},{72,... | collective-permute-start | bytes 208904 | tf_op jit(solution)/shard_map/ppermute | solution.py:62
  50.8 8.9 %collective-permute-start.6 = (f32[72,128]{1,0:T(8,128)S(1)}, f32[72,128]{1,0:T(8,128)S(1)}, u32[]{:S(2)}, u32[]{:S(2)}) collective-permute-start(f32[72,128]{1,0:T(8,128)S(1)} %get-tuple-element.80), channel_id=1, source_target_pairs={{8,16},{16,8},{24,32},{32,24},{40,48},{48,40},{56,64},{64,56},{72,... | collective-permute-start | bytes 110600 | tf_op jit(solution)/shard_map/ppermute | solution.py:62
  54.1 5.6 %collective-permute-start.7 = (f32[72,128]{1,0:T(8,128)S(1)}, f32[72,128]{1,0:T(8,128)S(1)}, u32[]{:S(2)}, u32[]{:S(2)}) collective-permute-start(f32[72,128]{1,0:T(8,128)S(1)} %get-tuple-element.81), channel_id=1, source_target_pairs={{0,8},{8,0},{16,24},{24,16},{32,40},{40,32},{48,56},{56,48},{64,72... | collective-permute-start | bytes 110600 | tf_op jit(solution)/shard_map/ppermute | solution.py:62
